TPU v7x, 128 devices: a whole 4x4x4 slice. The times are simulated.
128 devices in a mesh: pairs: 32 (over x, z, core), ga: 4 (over y).
Axes of the slice: x: 4, y: 4, z: 4, core: 2. Of those that a mesh axis runs over, the one named last changes fastest.
Arguments:
- densities: bfloat16 [8192, 12000], P('pairs', 'ga'), may hold values from -0.0546875 to 0.0546875
- coulomb: float32 [12000], P('ga'), may hold values from 0.1 to 10
- pair_list: int32 [64, 2], replicated, may hold values from 0 to 7, as said below
- owner: int32 [64, 1], replicated, may hold values from 0 to 31; in each aligned block of 64 rows (0 to 63, 64 to 127, ...) at most 4 rows name the same one
Outputs:
- kernel: float32 [128, 1024, 1024], P('pairs', 'ga')
Inputs may be any that keep to these rules, and one draw needn't show every extreme that they name: `pair_list`: each row is a tile pair I <= J; rows are ordered by J - I, never falling. No owner holds more than 4 entries; some owner holds exactly 4.
All inputs are finite; a program needn't handle non-finite values.
Results may differ from a plain program's by a relative error of at most 0.0026.
Values may be sent and summed in bfloat16 or wider, within the bound.
No kernel may reach another device: no remote copies, remote signals or barrier semaphores. Data moves between devices by JAX's collectives and lax.ppermute only.
A program may use at most 192 MiB of HBM per device.

v0:
```python
import jax
import jax.numpy as jnp
from jax import lax
from jax.sharding import PartitionSpec as P

TILE = 1024
CAP = 4


def on_device(densities, coulomb, pair_list, owner):
    groups = lax.axis_size("pairs")
    device = lax.axis_index("pairs")
    listed = pair_list.shape[0]
    everyone = lax.all_gather(densities, "pairs", axis=0, tiled=True)
    owner_ids = owner[:, 0]
    onehot = (owner_ids[:, None] == jnp.arange(groups, dtype=jnp.int32)[None, :]).astype(jnp.int32)
    rank = jnp.sum((jnp.cumsum(onehot, 0) - onehot) * onehot, 1)
    slot_ids = jnp.arange(CAP, dtype=jnp.int32)
    match = ((owner_ids[None, :] == device) & (rank[None, :] == slot_ids[:, None])).astype(
        jnp.int32
    )
    entry = jnp.sum(match * jnp.arange(listed, dtype=jnp.int32)[None, :], 1)
    valid = jnp.sum(match, 1).astype(jnp.float32)
    first = pair_list[entry, 0]
    second = pair_list[entry, 1]

    def single(items):
        rows = lax.dynamic_slice_in_dim(everyone, items[0] * TILE + 0, TILE, 0)
        left = (rows.astype(jnp.float32) * coulomb[None, :]).astype(jnp.bfloat16)
        right = lax.dynamic_slice_in_dim(everyone, items[1] * TILE, TILE, 0)
        return jnp.einsum("ix,jx->ij", left, right, preferred_element_type=jnp.float32)

    partial_value = lax.map(single, (first, second)) * valid[:, None, None]
    return lax.psum_scatter(partial_value, "ga", scatter_dimension=1, tiled=True)


def solution(mesh):
    in_specs = (P("pairs", "ga"), P("ga"), P(), P())
    out_specs = P("pairs", "ga", None)
    return jax.shard_map(
        on_device, mesh=mesh, in_specs=in_specs, out_specs=out_specs, check_vma=False
    )
```

profile of v0, /device:TPU:1, one launch (start us, length us, event | category | flops | bytes accessed | tf_op | source)
XLA Modules:
  0.0 397.2 jit_solution(2553237053676441415)
XLA Ops:
  6.5 2.6 copy.7
  9.3 0.7 fusion.7
  10.0 0.1 reduce_window_sum.11
  10.1 0.8 select_reduce_fusion
  10.9 0.7 broadcast_compare_fusion
  11.6 0.1 convert_reduce_fusion
  11.8 0.6 gather_fusion
  12.4 0.6 gather_fusion.1
  13.1 157.8 %all-gather.2.cloned.1.call-done = bf16[8192,3000]{1,0:T(8,128)(2,1)} async-done(((bf16[256,3000]{1,0:T(8,128)(2,1)}), bf16[8192,3000]{1,0:T(8,128)(2,1)}) %all-gather.2.cloned.1.call-update) | async-done | bytes 49152016 | tf_op jit(solution)/shard_map/all_gather | solution.py:14
  170.8 60.7 %while.10 = (s32[]{:T(128)}, f32[4,1024,1024]{2,1,0:T(8,128)}, s32[4]{0:T(128)S(1)}, bf16[8192,3000]{1,0:T(8,128)(2,1)}, f32[3000]{0:T(1024)}, /*index=5*/s32[4]...) while((s32[]{:T(128)}, f32[4,1024,1024]{2,1,0:T(8,128)}, s32[4]{0:T(128)S(1)}, ...), condition=%wide.region_4.5_spmd, body=%wide.region_3.4_spmd.sunk | while | flops 6300672000 | bytes 16790240 | solution.py:33
  170.8 0.6 dynamic_slice.30
  172.1 0.6 dynamic_slice.29
  173.3 13.0 %bitcast_dynamic-update-slice_fusion.2 = f32[4,1024,1024]{2,1,0:T(8,128)} fusion(f32[4,1024,1024]{2,1,0:T(8,128)} %get-tuple-element.102, s32[]{:T(128)} %get-tuple-element.101, bf16[8192,3000]{1,0:T(8,128)(2,1)} %get-tuple-element.114, s32[]{:T(128)S(6)} %select_n.29, f32[3000]{0:T(1024)} %get-tuple-element.115, s32[]{:T(128)S(6)} %select_n.30), kind=kOutput, calls=%fused_computation.7.clone.1 | convolution fusion | flops 6300672000 | bytes 16790024 | tf_op jit(solution)/shard_map/while/body/eval_jaxpr/ix,jx->ij/dot_general | solution.py:31
  186.3 0.6 dynamic_slice.30
  187.6 0.6 dynamic_slice.29
  188.8 12.1 %bitcast_dynamic-update-slice_fusion.2 = f32[4,1024,1024]{2,1,0:T(8,128)} fusion(f32[4,1024,1024]{2,1,0:T(8,128)} %get-tuple-element.102, s32[]{:T(128)} %get-tuple-element.101, bf16[8192,3000]{1,0:T(8,128)(2,1)} %get-tuple-element.114, s32[]{:T(128)S(6)} %select_n.29, f32[3000]{0:T(1024)} %get-tuple-element.115, s32[]{:T(128)S(6)} %select_n.30), kind=kOutput, calls=%fused_computation.7.clone.1 | convolution fusion | flops 6300672000 | bytes 16790024 | tf_op jit(solution)/shard_map/while/body/eval_jaxpr/ix,jx->ij/dot_general | solution.py:31
  200.9 0.6 dynamic_slice.30
  202.1 0.6 dynamic_slice.29
  203.4 12.8 %bitcast_dynamic-update-slice_fusion.2 = f32[4,1024,1024]{2,1,0:T(8,128)} fusion(f32[4,1024,1024]{2,1,0:T(8,128)} %get-tuple-element.102, s32[]{:T(128)} %get-tuple-element.101, bf16[8192,3000]{1,0:T(8,128)(2,1)} %get-tuple-element.114, s32[]{:T(128)S(6)} %select_n.29, f32[3000]{0:T(1024)} %get-tuple-element.115, s32[]{:T(128)S(6)} %select_n.30), kind=kOutput, calls=%fused_computation.7.clone.1 | convolution fusion | flops 6300672000 | bytes 16790024 | tf_op jit(solution)/shard_map/while/body/eval_jaxpr/ix,jx->ij/dot_general | solution.py:31
  216.2 0.6 dynamic_slice.30
  217.4 0.6 dynamic_slice.29
  218.7 12.8 %bitcast_dynamic-update-slice_fusion.2 = f32[4,1024,1024]{2,1,0:T(8,128)} fusion(f32[4,1024,1024]{2,1,0:T(8,128)} %get-tuple-element.102, s32[]{:T(128)} %get-tuple-element.101, bf16[8192,3000]{1,0:T(8,128)(2,1)} %get-tuple-element.114, s32[]{:T(128)S(6)} %select_n.29, f32[3000]{0:T(1024)} %get-tuple-element.115, s32[]{:T(128)S(6)} %select_n.30), kind=kOutput, calls=%fused_computation.7.clone.1 | convolution fusion | flops 6300672000 | bytes 16790024 | tf_op jit(solution)/shard_map/while/body/eval_jaxpr/ix,jx->ij/dot_general | solution.py:31
  231.5 12.3 %broadcast_multiply_fusion = f32[4,1024,1024]{2,1,0:T(8,128)} fusion(f32[4,1024,1024]{2,1,0:T(8,128)} %get-tuple-element.37, f32[4]{0:T(128)S(1)} %convert_element_type.21), kind=kLoop, calls=%fused_computation.9 | loop fusion | flops 4194304 | bytes 33554448 | tf_op jit(solution)/shard_map/mul | solution.py:33
  243.8 146.5 %reduce-scatter.2.cloned.1.call-done = f32[4,256,1024]{2,1,0:T(8,128)} async-done(((f32[4,1024,1024]{2,1,0:T(8,128)}), f32[4,256,1024]{2,1,0:T(8,128)}) %reduce-scatter.2.cloned.1.call-update) | async-done | bytes 4194320 | tf_op jit(solution)/shard_map/reduce_scatter | solution.py:34
  (11 shorter events, 0.1 us)
Async XLA Ops:
  6.5 5.2 %copy-start = (s32[64,2]{0,1:T(2,128)S(1)}, s32[64,2]{0,1:T(2,128)}, u32[]{:S(2)}) copy-start(s32[64,2]{0,1:T(2,128)} %param.8) | copy-start | bytes 1540
  6.5 164.3 %all-gather.2.cloned.1.call-start = ((), (), s32[]{:S(2)}) async-start(), calls=%async_computation.1 | async-start | bytes 51904512 | tf_op jit(solution)/shard_map/all_gather | solution.py:14
  9.2 381.2 %reduce-scatter.2.cloned.1.call-start = ((), (), s32[]{:S(2)}) async-start(), calls=%async_computation.2 | async-start | bytes 20971520 | tf_op jit(solution)/shard_map/reduce_scatter | solution.py:34
  231.5 158.8 %copy-start.1 = (s32[64,2]{0,1:T(2,128)S(1)}, s32[64,2]{0,1:T(2,128)}, u32[]{:S(2)}) copy-start(s32[64,2]{0,1:T(2,128)} %param.8) | copy-start | bytes 1540
Sparse Core Ops, SparseCore 0:
  9.6 161.1 all-gather.1
  243.9 146.3 reduce-scatter.1
where the time goes:
time: 398 us; the launch traced here: 397 us
  waiting for transfers between devices  304 us (76%)
  matrix products  50.7 us (13%)
  other arithmetic  14.8 us (4%)
  between operations  13.4 us (3%)
  local copies, waits for them, and re-layouts  8.62 us (2%)
  loops' own time  5.26 us (1%)
    all_gather x1, waiting for transfers between devices, on_device(): everyone = lax.all_gather(densities, 'pairs', axis=0, tiled=True)  158 us
    reduce_scatter x1, waiting for transfers between devices, on_device(): lax.psum_scatter(partial_value, 'ga', scatter_dimension=1, tiled=True)  147 us
    dot_general x4, matrix products, single(): jnp.einsum('ix,jx->ij', left, right, preferred_element_type=jnp.float32)  50.7 us
    mul x1, other arithmetic, on_device(): partial_value = lax.map(single, (first, second)) * valid[:, None, None]  12.3 us
  transfers between devices with their start and end apart: 2, of which 2 were waited for; matrix products, arithmetic and copies ran while one was open for 1% of the time, Pallas kernels for 0%

commit v1 on v0

v1 whole, which is shorter than its diff:
```python
import jax
import jax.numpy as jnp
from jax import lax
from jax.experimental import pallas as pl
from jax.experimental.pallas import tpu as pltpu
from jax.sharding import Mesh
from jax.sharding import PartitionSpec as P

TILES = 8
CAP = 4
NP = TILES * (TILES + 1) // 2
BF = jnp.bfloat16
F32 = jnp.float32
STEPS = [(i, j) for j in range(4) for i in range(j + 1)]
MIB = 1 << 20


def shift(a, axis, d):
    return lax.ppermute(a, axis, [(i, (i + d) % 4) for i in range(4)])


def gather4(a, axis):
    half = a.shape[0] // 2
    low, high = shift(a, axis, 1), shift(a, axis, -1)
    far0 = shift(low[:half], axis, 1)
    far1 = shift(high[half:], axis, -1)
    return a, high, far0, far1, low


def gram_kernel(meta, steps_i, steps_j, *refs):
    lefts, rights = refs[:10], refs[10:20]
    own, s1, s2, s3 = refs[20:24]
    lbuf, rbuf, sems = refs[24:]
    x, z, c, y = meta[0], meta[1], meta[2], meta[3]
    copies = []

    def copy(src, dst):
        copies.append(pltpu.make_async_copy(src, dst, sems.at[len(copies)]))
        copies[-1].start()

    for half in range(2):
        parity = (z // 2 + half) % 2
        mine = rights[5 * half : 5 * half + 5]
        for dx, ref, lo in ((0, mine[0], 0), (1, mine[1], 0), (2, mine[2], 0), (2, mine[3], 64), (3, mine[4], 0)):
            tile = 2 * ((x + dx) % 4) + parity
            copy(ref, rbuf.at[tile, pl.ds(lo, ref.shape[0])])
    for dc in range(2):
        mine = lefts[5 * dc : 5 * dc + 5]
        for dz, ref, first in ((0, mine[0], 0), (1, mine[1], 0), (2, mine[2], 0), (2, mine[3], 2), (3, mine[4], 0)):
            zz = (z + dz) % 4
            quarter = 2 * (zz % 2) + (c + dc) % 2
            for k in range(ref.shape[0]):
                tile = 2 * ((x + first + k) % 4) + zz // 2
                copy(ref.at[k], lbuf.at[tile, (quarter - y + 4) % 4])
    for item in copies:
        item.wait()

    def step(t, _):
        ip, jp = steps_i[t], steps_j[t]
        left = lbuf[pl.ds(2 * ip, 2)].reshape(512, lbuf.shape[-1])
        right = rbuf[pl.ds(2 * jp, 2)].reshape(256, rbuf.shape[-1])
        out = lax.dot_general(left, right, (((1,), (1,)), ((), ())), preferred_element_type=F32)
        for a in range(2):
            for b in range(2):
                i, j = 2 * ip + a, 2 * jp + b

                @pl.when(i <= j)
                def _():
                    at = j * (j + 1) // 2 + i
                    part = out[256 * a : 256 * a + 256, 128 * b : 128 * b + 128]
                    own[at] = part[0:64]
                    s1[at] = part[64:128].astype(BF)
                    s2[at] = part[128:192].astype(BF)
                    s3[at] = part[192:256].astype(BF)

        return 0

    lax.fori_loop(0, len(STEPS), step, 0)


def grams(meta, lefts, rights):
    width = rights[0].shape[-1]
    any_ = pl.BlockSpec(memory_space=pl.ANY)
    smem = pl.BlockSpec(memory_space=pltpu.SMEM)
    vmem = pl.BlockSpec(memory_space=pltpu.VMEM)
    piece = (NP, 64, 128)
    return pl.pallas_call(
        gram_kernel,
        out_shape=[jax.ShapeDtypeStruct(piece, F32)] + [jax.ShapeDtypeStruct(piece, BF)] * 3,
        in_specs=[smem] * 3 + [any_] * 20,
        out_specs=[vmem] * 4,
        scratch_shapes=[
            pltpu.VMEM((TILES, 4, 64, width), BF),
            pltpu.VMEM((TILES, 128, width), BF),
            pltpu.SemaphoreType.DMA((42,)),
        ],
        compiler_params=pltpu.CompilerParams(vmem_limit_bytes=48 * MIB),
        cost_estimate=pl.CostEstimate(
            flops=2 * 10 * 512 * 256 * width, bytes_accessed=20 * MIB, transcendentals=0
        ),
        name="grams",
    )(
        meta,
        jnp.array([s[0] for s in STEPS], jnp.int32),
        jnp.array([s[1] for s in STEPS], jnp.int32),
        *lefts,
        *rights,
    )


def route_kernel(index, valid, own, a, b, c, out, total):
    total[...] = (
        own[...] + a[...].astype(F32) + b[...].astype(F32) + c[...].astype(F32)
    ).astype(BF)

    def one(k, _):
        @pl.when(valid[k] > 0)
        def _():
            out[k] = total[index[k]]

        @pl.when(valid[k] == 0)
        def _():
            out[k] = jnp.zeros(out.shape[1:], BF)

        return 0

    lax.fori_loop(0, out.shape[0], one, 0)


def route(index, valid, own, parts):
    smem = pl.BlockSpec(memory_space=pltpu.SMEM)
    vmem = pl.BlockSpec(memory_space=pltpu.VMEM)
    return pl.pallas_call(
        route_kernel,
        out_shape=jax.ShapeDtypeStruct((index.shape[0], 64, 128), BF),
        in_specs=[smem, smem] + [vmem] * 4,
        out_specs=vmem,
        scratch_shapes=[pltpu.VMEM((NP, 64, 128), BF)],
        compiler_params=pltpu.CompilerParams(vmem_limit_bytes=32 * MIB),
        name="route",
    )(index, valid, own, *parts)


def place_kernel(got, out):
    for src in range(32):
        x, z1, z0, c = src // 8, (src // 4) % 2, (src // 2) % 2, src % 2
        col = (4 * z0 + 2 * c + z1) * 128
        for h in range(2):
            row = h * 128 + x * 32
            out[0, row : row + 32, col : col + 128] = got[src, 0, 32 * h : 32 * h + 32].astype(F32)


def place(got):
    return pl.pallas_call(
        place_kernel,
        grid=(CAP,),
        out_shape=jax.ShapeDtypeStruct((CAP, 256, 1024), F32),
        in_specs=[pl.BlockSpec((32, 1, 64, 128), lambda s: (0, s, 0, 0))],
        out_specs=pl.BlockSpec((1, 256, 1024), lambda s: (s, 0, 0)),
        name="place",
    )(got)


def on_device(densities, coulomb, pair_list, owner):
    x, z, c, y = (lax.axis_index(n) for n in ("x", "z", "c", "y"))
    z1 = z // 2
    rows, k = densities.shape
    width = -(-k // 128) * 128
    dens = jnp.pad(densities, ((0, 0), (0, width - k)))
    weights = jnp.pad(coulomb, (0, width - k))

    keep = lax.dynamic_slice_in_dim(dens, z1 * 128, 128, 0)
    send = lax.dynamic_slice_in_dim(dens, (1 - z1) * 128, 128, 0)
    got = shift(send, "z", 2)

    quarter = dens.reshape(2, 4, 32, width)

    def weighted_part(to):
        part = lax.dynamic_slice_in_dim(quarter, to, 1, 1).reshape(1, 64, width)
        return (part.astype(F32) * weights).astype(BF)

    mine = [weighted_part(lax.rem(x + d, 4)) for d in range(4)]
    left = jnp.concatenate(
        [mine[0], shift(mine[3], "x", 3), shift(mine[2], "x", 2), shift(mine[1], "x", 1)], 0
    )
    rights = gather4(keep, "x") + gather4(got, "x")
    lefts = gather4(left, "z")
    lefts = lefts + tuple(lax.ppermute(a, "c", [(0, 1), (1, 0)]) for a in lefts)
    meta = jnp.stack([x, z, c, y]).astype(jnp.int32)
    own, s1, s2, s3 = grams(meta, lefts, rights)
    parts = [shift(s1, "y", 1), shift(s2, "y", 2), shift(s3, "y", 3)]

    owners = 32
    owner_ids = owner[:, 0]
    onehot = (owner_ids[:, None] == jnp.arange(owners, dtype=jnp.int32)[None, :]).astype(jnp.int32)
    rank = jnp.sum((jnp.cumsum(onehot, 0) - onehot) * onehot, 1)
    slot = owner_ids * CAP + rank
    match = (slot[None, :] == jnp.arange(owners * CAP, dtype=jnp.int32)[:, None]).astype(jnp.int32)
    second = pair_list[:, 1]
    which = second * (second + 1) // 2 + pair_list[:, 0]
    index = jnp.sum(match * which[None, :], 1)
    valid = jnp.sum(match, 1)

    routed = route(index, valid, own, parts).reshape(owners, CAP, 64, 128)
    arrived = lax.all_to_all(routed, ("x", "z", "c"), 0, 0, tiled=True)
    return place(arrived)


def solution(mesh):
    grid = Mesh(mesh.devices.reshape(4, 4, 2, 4), ("x", "z", "c", "y"))
    pairs = ("x", "z", "c")
    return jax.shard_map(
        on_device,
        mesh=grid,
        in_specs=(P(pairs, "y"), P("y"), P(), P()),
        out_specs=P(pairs, "y", None),
        check_vma=False,
    )
```

time: 398 us -> 244 us (0.61)
  waiting for transfers between devices: 304 us -> 136 us
  matrix products: 50.7 us -> 0 us
  blocking collectives: 0 us -> 34.9 us
  starting transfers between devices: 0.04 us -> 33 us
  Pallas kernels: 0 us -> 26.3 us
  other arithmetic: 14.8 us -> 1.06 us
  between operations: 13.4 us -> 0.38 us
  loops' own time: 5.26 us -> 0 us
    all_gather x1 -> x0, waiting for transfers between devices: 158 us -> none  [on_device(): everyone = lax.all_gather(densities, 'pairs', axis=0, tiled=True)]
    reduce_scatter x1 -> x0, waiting for transfers between devices: 147 us -> none  [on_device(): lax.psum_scatter(partial_value, 'ga', scatter_dimension=1, tiled=True)]
    ppermute x0 -> x24, waiting for transfers between devices: none -> 136 us  [the longest x19 136 us: shift(): return lax.ppermute(a, axis, [(i, (i + d) % 4) for i in range(4)])]
    dot_general x4 -> x0, matrix products: 50.7 us -> none  [single(): jnp.einsum('ix,jx->ij', left, right, preferred_element_type=jnp.float32)]
    all_to_all x0 -> x1, blocking collectives: none -> 34.9 us  [on_device(): arrived = lax.all_to_all(routed, ('x', 'z', 'c'), 0, 0, tiled=True)]
    ppermute x0 -> x24, starting transfers between devices: none -> 33 us  [the longest x19 26.7 us: shift(): return lax.ppermute(a, axis, [(i, (i + d) % 4) for i in range(4)])]
    pallas_call x0 -> x3, Pallas kernels: none -> 26.3 us  [the longest x1 18.3 us: grams(): pl.pallas_call(gram_kernel, out_shape=[jax.ShapeDtypeStruct(piece, F32)]...]
    mul x1 -> x0, other arithmetic: 12.3 us -> none  [on_device(): partial_value = lax.map(single, (first, second)) * valid[:, None, None]]
  transfers between devices with their start and end apart: 2 -> 24, of which waited for: 2 -> 9; matrix products, arithmetic and copies ran while one was open for 1% -> 1% of each run, Pallas kernels for 0% -> 0%
where the time goes in v1:
time: 244 us; the launch traced here: 243 us
  waiting for transfers between devices  136 us (56%)
  blocking collectives  34.9 us (14%)
  starting transfers between devices  33 us (14%)
  Pallas kernels  26.3 us (11%)
  local copies, waits for them, and re-layouts  12 us (5%)
    ppermute x19, waiting for transfers between devices, shift(): return lax.ppermute(a, axis, [(i, (i + d) % 4) for i in range(4)])  136 us
    all_to_all x1, blocking collectives, on_device(): arrived = lax.all_to_all(routed, ('x', 'z', 'c'), 0, 0, tiled=True)  34.9 us
    ppermute x19, starting transfers between devices, shift(): return lax.ppermute(a, axis, [(i, (i + d) % 4) for i in range(4)])  26.7 us
    pallas_call x1, Pallas kernels, grams(): pl.pallas_call(gram_kernel, out_shape=[jax.ShapeDtypeStruct(piece, F32)]...  18.3 us
    unnamed x45, local copies, waits for them, and re-layouts  9.17 us
    ppermute x5, starting transfers between devices, on_device(): lax.ppermute(a, 'c', [(0, 1), (1, 0)])  6.31 us
  transfers between devices with their start and end apart: 24, of which 9 were waited for; matrix products, arithmetic and copies ran while one was open for 1% of the time, Pallas kernels for 0%

profile of v1, /device:TPU:1, one launch (start us, length us, event | category | flops | bytes accessed | tf_op | source)
XLA Modules:
  0.0 243.4 jit_solution(6941591802918431408)
XLA Ops:
  0.0 1.8 copy.8
  3.0 3.4 %collective-permute-start = (bf16[1,64,3072]{2,1,0:T(8,128)(2,1)S(1)}, bf16[1,64,3072]{2,1,0:T(8,128)(2,1)S(1)}, u32[]{:S(2)}, u32[]{:S(2)}) collective-permute-start(bf16[1,64,3072]{2,1,0:T(8,128)(2,1)S(1)} %get-tuple-element.22), channel_id=1, source_target_pairs={{0,96},{32,0},{64,32},{96,64},{1,97},{33,1},{65,33},{97,65},{2,98}... | collective-permute-start | bytes 1179656 | tf_op jit(solution)/shard_map/ppermute | solution.py:19
  7.5 7.9 %collective-permute-done = bf16[1,64,3072]{2,1,0:T(8,128)(2,1)S(1)} collective-permute-done((bf16[1,64,3072]{2,1,0:T(8,128)(2,1)S(1)}, bf16[1,64,3072]{2,1,0:T(8,128)(2,1)S(1)}, u32[]{:S(2)}, u32[]{:S(2)}) %collective-permute-start) | collective-permute-done | bytes 393248 | tf_op jit(solution)/shard_map/ppermute | solution.py:19
  15.4 2.2 collective-permute-done.1
  17.6 9.8 %collective-permute-done.2 = bf16[1,64,3072]{2,1,0:T(8,128)(2,1)S(1)} collective-permute-done((bf16[1,64,3072]{2,1,0:T(8,128)(2,1)S(1)}, bf16[1,64,3072]{2,1,0:T(8,128)(2,1)S(1)}, u32[]{:S(2)}, u32[]{:S(2)}) %collective-permute-start.2) | collective-permute-done | bytes 393248 | tf_op jit(solution)/shard_map/ppermute | solution.py:19
  27.6 3.8 %collective-permute-start.3 = (bf16[4,64,3072]{2,1,0:T(8,128)(2,1)S(1)}, bf16[4,64,3072]{2,1,0:T(8,128)(2,1)}, u32[]{:S(2)}, u32[]{:S(2)}) collective-permute-start(bf16[4,64,3072]{2,1,0:T(8,128)(2,1)S(1)} %pad_maximum_fusion.refs_0_), channel_id=1, source_target_pairs={{0,24},{8,0},{16,8},{24,16},{1,25},{9,1},{17,9},{25,17},{2,26},{10... | collective-permute-start | bytes 4718600 | tf_op jit(solution)/shard_map/ppermute | solution.py:19
  32.9 2.7 %collective-permute-start.12 = (bf16[128,3072]{1,0:T(8,128)(2,1)S(1)}, bf16[128,3072]{1,0:T(8,128)(2,1)S(1)}, u32[]{:S(2)}, u32[]{:S(2)}) collective-permute-start(bf16[128,3072]{1,0:T(8,128)(2,1)S(1)} %get-tuple-element.16.refs_10_), channel_id=1, source_target_pairs={{0,96},{32,0},{64,32},{96,64},{1,97},{33,1},{65,33},{97,65},{2,98}... | collective-permute-start | bytes 2359304 | tf_op jit(solution)/shard_map/ppermute | solution.py:19
  35.6 47.7 %collective-permute-done.16.refs_15_ = bf16[128,3072]{1,0:T(8,128)(2,1)S(1)} collective-permute-done((bf16[128,3072]{1,0:T(8,128)(2,1)S(1)}, bf16[128,3072]{1,0:T(8,128)(2,1)S(1)}, u32[]{:S(2)}, u32[]{:S(2)}) %collective-permute-start.16) | collective-permute-done | bytes 786464 | tf_op jit(solution)/shard_map/ppermute | solution.py:19
  83.3 1.7 collective-permute-start.7
  85.0 2.7 %collective-permute-start.17 = (bf16[128,3072]{1,0:T(8,128)(2,1)S(1)}, bf16[128,3072]{1,0:T(8,128)(2,1)S(1)}, u32[]{:S(2)}, u32[]{:S(2)}) collective-permute-start(bf16[128,3072]{1,0:T(8,128)(2,1)S(1)} %collective-permute-done.16.refs_15_), channel_id=1, source_target_pairs={{0,96},{32,0},{64,32},{96,64},{1,97},{33,1},{65,33},{97,65},{2,98}... | collective-permute-start | bytes 2359304 | tf_op jit(solution)/shard_map/ppermute | solution.py:19
  87.9 2.7 %collective-permute-start.15 = (bf16[64,3072]{1,0:T(8,128)(2,1)S(1)}, bf16[64,3072]{1,0:T(8,128)(2,1)S(1)}, u32[]{:S(2)}, u32[]{:S(2)}) collective-permute-start(bf16[64,3072]{1,0:T(8,128)(2,1)S(1)} %slice.35), channel_id=1, source_target_pairs={{0,96},{32,0},{64,32},{96,64},{1,97},{33,1},{65,33},{97,65},{2,98}... | collective-permute-start | bytes 1179656 | tf_op jit(solution)/shard_map/ppermute | solution.py:19
  93.0 20.7 %collective-permute-done.14.refs_12_ = bf16[64,3072]{1,0:T(8,128)(2,1)S(1)} collective-permute-done((bf16[64,3072]{1,0:T(8,128)(2,1)S(1)}, bf16[64,3072]{1,0:T(8,128)(2,1)S(1)}, u32[]{:S(2)}, u32[]{:S(2)}) %collective-permute-start.14) | collective-permute-done | bytes 393248 | tf_op jit(solution)/shard_map/ppermute | solution.py:19
  113.8 1.5 collective-permute-start.5
  116.9 15.0 %collective-permute-done.6.refs_3_ = bf16[2,64,3072]{2,1,0:T(8,128)(2,1)S(1)} collective-permute-done((bf16[2,64,3072]{2,1,0:T(8,128)(2,1)S(1)}, bf16[2,64,3072]{2,1,0:T(8,128)(2,1)S(1)}, u32[]{:S(2)}, u32[]{:S(2)}) %collective-permute-start.6) | collective-permute-done | bytes 786464 | tf_op jit(solution)/shard_map/ppermute | solution.py:19
  131.9 1.8 collective-permute-start.10
  135.9 2.3 collective-permute-start.20
  138.2 8.5 %collective-permute-done.20.refs_18_ = bf16[64,3072]{1,0:T(8,128)(2,1)S(1)} collective-permute-done((bf16[64,3072]{1,0:T(8,128)(2,1)S(1)}, bf16[64,3072]{1,0:T(8,128)(2,1)S(1)}, u32[]{:S(2)}, u32[]{:S(2)}) %collective-permute-start.20) | collective-permute-done | bytes 393248 | tf_op jit(solution)/shard_map/ppermute | solution.py:19
  151.5 18.3 %grams.1 = (f32[36,64,128]{2,1,0:T(8,128)}, bf16[36,64,128]{2,1,0:T(8,128)(2,1)}, bf16[36,64,128]{2,1,0:T(8,128)(2,1)S(1)}, bf16[36,64,128]{2,1,0:T(8,128)(2,1)S(1)}) custom-call(s32[4]{0:T(128)S(1)} %pad_add_fusion.meta, s32[10]{0:T(128)S(1)} %copy-done.9, s32[10]{0:T(128)S(1)} %copy-done.10, bf16[4,64,3072]{2,1,0:T(8,128)(2,1)} %copy-done.11, ...), custom_call_target="tpu_custom_call" | custom-call | flops 8053063680 | bytes 20971520 | tf_op jit(solution)/shard_map/grams/pallas_call | solution.py:87
  171.2 2.6 %collective-permute-start.22 = (bf16[36,64,128]{2,1,0:T(8,128)(2,1)S(1)}, bf16[36,64,128]{2,1,0:T(8,128)(2,1)S(1)}, u32[]{:S(2)}, u32[]{:S(2)}) collective-permute-start(bf16[36,64,128]{2,1,0:T(8,128)(2,1)S(1)} %get-tuple-element.11), channel_id=1, source_target_pairs={{0,2},{1,3},{2,0},{3,1},{4,6},{5,7},{6,4},{7,5},{8,10},{9,11},{10,... | collective-permute-start | bytes 1769480 | tf_op jit(solution)/shard_map/ppermute | solution.py:19
  175.3 10.2 %collective-permute-done.21.a = bf16[36,64,128]{2,1,0:T(8,128)(2,1)S(1)} collective-permute-done((bf16[36,64,128]{2,1,0:T(8,128)(2,1)}, bf16[36,64,128]{2,1,0:T(8,128)(2,1)S(1)}, u32[]{:S(2)}, u32[]{:S(2)}) %collective-permute-start.21) | collective-permute-done | bytes 589856 | tf_op jit(solution)/shard_map/ppermute | solution.py:19
  185.5 13.7 %collective-permute-done.22.b = bf16[36,64,128]{2,1,0:T(8,128)(2,1)S(1)} collective-permute-done((bf16[36,64,128]{2,1,0:T(8,128)(2,1)S(1)}, bf16[36,64,128]{2,1,0:T(8,128)(2,1)S(1)}, u32[]{:S(2)}, u32[]{:S(2)}) %collective-permute-start.22) | collective-permute-done | bytes 589856 | tf_op jit(solution)/shard_map/ppermute | solution.py:19
  200.5 3.7 %route.1 = bf16[128,64,128]{2,1,0:T(8,128)(2,1)S(1)} custom-call(s32[128]{0:T(128)S(1)} %get-tuple-element.14.index, s32[128]{0:T(128)S(1)} %get-tuple-element.13.valid, f32[36,64,128]{2,1,0:T(8,128)S(1)} %copy-done, bf16[36,64,128]{2,1,0:T(8,128)(2,1)S(1)} %collective-permute-done.21.a, bf16[36,64,128]{2,1,0:T(8,128)(2,1)S(1)} %collective-permute-done.22.b, ...), custom_call_target="tpu_custom_call" | custom-call | tf_op jit(solution)/shard_map/route/pallas_call | solution.py:133
  204.2 34.9 %all_to_all.5.got = bf16[32,4,64,128]{3,2,1,0:T(8,128)(2,1)} all-to-all(bf16[32,4,64,128]{3,2,1,0:T(8,128)(2,1)S(1)} %bitcast.22), channel_id=1, replica_groups=mesh['x'=4,'z'=4,'c'=2,'y'=4] {'x','z','c'}, dimensions={0} | all-to-all | bytes 4194304 | tf_op jit(solution)/shard_map/all_to_all | solution.py:205
  239.1 4.2 %place.1 = f32[4,256,1024]{2,1,0:T(8,128)} custom-call(bf16[32,4,64,128]{3,2,1,0:T(8,128)(2,1)} %all_to_all.5.got), custom_call_target="tpu_custom_call" | custom-call | tf_op jit(solution)/shard_map/place/pallas_call | solution.py:154
  (91 shorter events, 19.3 us)
Async XLA Ops:
  3.0 12.4 %collective-permute-start = (bf16[1,64,3072]{2,1,0:T(8,128)(2,1)S(1)}, bf16[1,64,3072]{2,1,0:T(8,128)(2,1)S(1)}, u32[]{:S(2)}, u32[]{:S(2)}) collective-permute-start(bf16[1,64,3072]{2,1,0:T(8,128)(2,1)S(1)} %get-tuple-element.22), channel_id=1, source_target_pairs={{0,96},{32,0},{64,32},{96,64},{1,97},{33,1},{65,33},{97,65},{2,98}... | collective-permute-start | bytes 1179656 | tf_op jit(solution)/shard_map/ppermute | solution.py:19
  6.4 11.2 %collective-permute-start.1 = (bf16[1,64,3072]{2,1,0:T(8,128)(2,1)S(1)}, bf16[1,64,3072]{2,1,0:T(8,128)(2,1)S(1)}, u32[]{:S(2)}, u32[]{:S(2)}) collective-permute-start(bf16[1,64,3072]{2,1,0:T(8,128)(2,1)S(1)} %get-tuple-element.23), channel_id=1, source_target_pairs={{0,64},{32,96},{64,0},{96,32},{1,65},{33,97},{65,1},{97,33},{2,66}... | collective-permute-start | bytes 1179656 | tf_op jit(solution)/shard_map/ppermute | solution.py:19
  6.9 20.4 %collective-permute-start.2 = (bf16[1,64,3072]{2,1,0:T(8,128)(2,1)S(1)}, bf16[1,64,3072]{2,1,0:T(8,128)(2,1)S(1)}, u32[]{:S(2)}, u32[]{:S(2)}) collective-permute-start(bf16[1,64,3072]{2,1,0:T(8,128)(2,1)S(1)} %get-tuple-element.24), channel_id=1, source_target_pairs={{0,32},{32,64},{64,96},{96,0},{1,33},{33,65},{65,97},{97,1},{2,34}... | collective-permute-start | bytes 1179656 | tf_op jit(solution)/shard_map/ppermute | solution.py:19
  27.6 60.2 %collective-permute-start.3 = (bf16[4,64,3072]{2,1,0:T(8,128)(2,1)S(1)}, bf16[4,64,3072]{2,1,0:T(8,128)(2,1)}, u32[]{:S(2)}, u32[]{:S(2)}) collective-permute-start(bf16[4,64,3072]{2,1,0:T(8,128)(2,1)S(1)} %pad_maximum_fusion.refs_0_), channel_id=1, source_target_pairs={{0,24},{8,0},{16,8},{24,16},{1,25},{9,1},{17,9},{25,17},{2,26},{10... | collective-permute-start | bytes 4718600 | tf_op jit(solution)/shard_map/ppermute | solution.py:19
  31.4 56.5 %collective-permute-start.4 = (bf16[4,64,3072]{2,1,0:T(8,128)(2,1)S(1)}, bf16[4,64,3072]{2,1,0:T(8,128)(2,1)}, u32[]{:S(2)}, u32[]{:S(2)}) collective-permute-start(bf16[4,64,3072]{2,1,0:T(8,128)(2,1)S(1)} %pad_maximum_fusion.refs_0_), channel_id=1, source_target_pairs={{0,8},{8,16},{16,24},{24,0},{1,9},{9,17},{17,25},{25,1},{2,10},{10... | collective-permute-start | bytes 4718600 | tf_op jit(solution)/shard_map/ppermute | solution.py:19
  31.5 51.8 %collective-permute-start.16 = (bf16[128,3072]{1,0:T(8,128)(2,1)S(1)}, bf16[128,3072]{1,0:T(8,128)(2,1)S(1)}, u32[]{:S(2)}, u32[]{:S(2)}) collective-permute-start(bf16[128,3072]{1,0:T(8,128)(2,1)S(1)} %get-tuple-element.15), channel_id=1, source_target_pairs={{0,16},{8,24},{16,0},{24,8},{1,17},{9,25},{17,1},{25,9},{2,18},{10... | collective-permute-start | bytes 2359304 | tf_op jit(solution)/shard_map/ppermute | solution.py:19
  32.9 52.1 %collective-permute-start.13 = (bf16[128,3072]{1,0:T(8,128)(2,1)S(1)}, bf16[128,3072]{1,0:T(8,128)(2,1)S(1)}, u32[]{:S(2)}, u32[]{:S(2)}) collective-permute-start(bf16[128,3072]{1,0:T(8,128)(2,1)S(1)} %get-tuple-element.16.refs_10_), channel_id=1, source_target_pairs={{0,32},{32,64},{64,96},{96,0},{1,33},{33,65},{65,97},{97,1},{2,34}... | collective-permute-start | bytes 2359304 | tf_op jit(solution)/shard_map/ppermute | solution.py:19
  32.9 52.1 %collective-permute-start.12 = (bf16[128,3072]{1,0:T(8,128)(2,1)S(1)}, bf16[128,3072]{1,0:T(8,128)(2,1)S(1)}, u32[]{:S(2)}, u32[]{:S(2)}) collective-permute-start(bf16[128,3072]{1,0:T(8,128)(2,1)S(1)} %get-tuple-element.16.refs_10_), channel_id=1, source_target_pairs={{0,96},{32,0},{64,32},{96,64},{1,97},{33,1},{65,33},{97,65},{2,98}... | collective-permute-start | bytes 2359304 | tf_op jit(solution)/shard_map/ppermute | solution.py:19
  83.3 33.5 %collective-permute-start.7 = (bf16[4,64,3072]{2,1,0:T(8,128)(2,1)S(1)}, bf16[4,64,3072]{2,1,0:T(8,128)(2,1)S(1)}, u32[]{:S(2)}, u32[]{:S(2)}) collective-permute-start(bf16[4,64,3072]{2,1,0:T(8,128)(2,1)S(1)} %pad_maximum_fusion.refs_0_), channel_id=1, source_target_pairs={{0,4},{4,0},{1,5},{5,1},{2,6},{6,2},{3,7},{7,3},{8,12},{12,8},{9,1... | collective-permute-start | bytes 4718600 | tf_op jit(solution)/shard_map/ppermute | solution.py:188
  85.0 30.2 %collective-permute-start.18 = (bf16[128,3072]{1,0:T(8,128)(2,1)S(1)}, bf16[128,3072]{1,0:T(8,128)(2,1)S(1)}, u32[]{:S(2)}, u32[]{:S(2)}) collective-permute-start(bf16[128,3072]{1,0:T(8,128)(2,1)S(1)} %collective-permute-done.16.refs_15_), channel_id=1, source_target_pairs={{0,32},{32,64},{64,96},{96,0},{1,33},{33,65},{65,97},{97,1},{2,34}... | collective-permute-start | bytes 2359304 | tf_op jit(solution)/shard_map/ppermute | solution.py:19
  85.0 31.6 %collective-permute-start.17 = (bf16[128,3072]{1,0:T(8,128)(2,1)S(1)}, bf16[128,3072]{1,0:T(8,128)(2,1)S(1)}, u32[]{:S(2)}, u32[]{:S(2)}) collective-permute-start(bf16[128,3072]{1,0:T(8,128)(2,1)S(1)} %collective-permute-done.16.refs_15_), channel_id=1, source_target_pairs={{0,96},{32,0},{64,32},{96,64},{1,97},{33,1},{65,33},{97,65},{2,98}... | collective-permute-start | bytes 2359304 | tf_op jit(solution)/shard_map/ppermute | solution.py:19
  87.8 26.0 %collective-permute-start.14 = (bf16[64,3072]{1,0:T(8,128)(2,1)S(1)}, bf16[64,3072]{1,0:T(8,128)(2,1)S(1)}, u32[]{:S(2)}, u32[]{:S(2)}) collective-permute-start(bf16[64,3072]{1,0:T(8,128)(2,1)S(1)} %slice.34), channel_id=1, source_target_pairs={{0,32},{32,64},{64,96},{96,0},{1,33},{33,65},{65,97},{97,1},{2,34}... | collective-permute-start | bytes 1179656 | tf_op jit(solution)/shard_map/ppermute | solution.py:19
  87.9 25.9 %collective-permute-start.15 = (bf16[64,3072]{1,0:T(8,128)(2,1)S(1)}, bf16[64,3072]{1,0:T(8,128)(2,1)S(1)}, u32[]{:S(2)}, u32[]{:S(2)}) collective-permute-start(bf16[64,3072]{1,0:T(8,128)(2,1)S(1)} %slice.35), channel_id=1, source_target_pairs={{0,96},{32,0},{64,32},{96,64},{1,97},{33,1},{65,33},{97,65},{2,98}... | collective-permute-start | bytes 1179656 | tf_op jit(solution)/shard_map/ppermute | solution.py:19
  113.7 18.2 %collective-permute-start.6 = (bf16[2,64,3072]{2,1,0:T(8,128)(2,1)S(1)}, bf16[2,64,3072]{2,1,0:T(8,128)(2,1)S(1)}, u32[]{:S(2)}, u32[]{:S(2)}) collective-permute-start(bf16[2,64,3072]{2,1,0:T(8,128)(2,1)S(1)} %slice.33), channel_id=1, source_target_pairs={{0,24},{8,0},{16,8},{24,16},{1,25},{9,1},{17,9},{25,17},{2,26},{10... | collective-permute-start | bytes 2359304 | tf_op jit(solution)/shard_map/ppermute | solution.py:19
  113.8 19.9 %collective-permute-start.5 = (bf16[2,64,3072]{2,1,0:T(8,128)(2,1)S(1)}, bf16[2,64,3072]{2,1,0:T(8,128)(2,1)S(1)}, u32[]{:S(2)}, u32[]{:S(2)}) collective-permute-start(bf16[2,64,3072]{2,1,0:T(8,128)(2,1)S(1)} %slice.32), channel_id=1, source_target_pairs={{0,8},{8,16},{16,24},{24,0},{1,9},{9,17},{17,25},{25,1},{2,10},{10... | collective-permute-start | bytes 2359304 | tf_op jit(solution)/shard_map/ppermute | solution.py:19
  115.2 32.2 %collective-permute-start.11 = (bf16[4,64,3072]{2,1,0:T(8,128)(2,1)}, bf16[4,64,3072]{2,1,0:T(8,128)(2,1)}, u32[]{:S(2)}, u32[]{:S(2)}) collective-permute-start(bf16[4,64,3072]{2,1,0:T(8,128)(2,1)} %collective-permute-done.4.refs_4_), channel_id=1, source_target_pairs={{0,4},{4,0},{1,5},{5,1},{2,6},{6,2},{3,7},{7,3},{8,12},{12,8},{9,1... | collective-permute-start | bytes 4718600 | tf_op jit(solution)/shard_map/ppermute | solution.py:188
  116.7 30.8 %collective-permute-start.8 = (bf16[4,64,3072]{2,1,0:T(8,128)(2,1)}, bf16[4,64,3072]{2,1,0:T(8,128)(2,1)}, u32[]{:S(2)}, u32[]{:S(2)}) collective-permute-start(bf16[4,64,3072]{2,1,0:T(8,128)(2,1)} %collective-permute-done.3.refs_1_), channel_id=1, source_target_pairs={{0,4},{4,0},{1,5},{5,1},{2,6},{6,2},{3,7},{7,3},{8,12},{12,8},{9,1... | collective-permute-start | bytes 4718600 | tf_op jit(solution)/shard_map/ppermute | solution.py:188
  116.8 18.2 %collective-permute-start.19 = (bf16[64,3072]{1,0:T(8,128)(2,1)S(1)}, bf16[64,3072]{1,0:T(8,128)(2,1)S(1)}, u32[]{:S(2)}, u32[]{:S(2)}) collective-permute-start(bf16[64,3072]{1,0:T(8,128)(2,1)S(1)} %slice.36), channel_id=1, source_target_pairs={{0,32},{32,64},{64,96},{96,0},{1,33},{33,65},{65,97},{97,1},{2,34}... | collective-permute-start | bytes 1179656 | tf_op jit(solution)/shard_map/ppermute | solution.py:19
  131.9 15.5 %collective-permute-start.10 = (bf16[2,64,3072]{2,1,0:T(8,128)(2,1)S(1)}, bf16[2,64,3072]{2,1,0:T(8,128)(2,1)}, u32[]{:S(2)}, u32[]{:S(2)}) collective-permute-start(bf16[2,64,3072]{2,1,0:T(8,128)(2,1)S(1)} %collective-permute-done.6.refs_3_), channel_id=1, source_target_pairs={{0,4},{4,0},{1,5},{5,1},{2,6},{6,2},{3,7},{7,3},{8,12},{12,8},{9,1... | collective-permute-start | bytes 2359304 | tf_op jit(solution)/shard_map/ppermute | solution.py:188
  133.7 13.7 %collective-permute-start.9 = (bf16[2,64,3072]{2,1,0:T(8,128)(2,1)S(1)}, bf16[2,64,3072]{2,1,0:T(8,128)(2,1)S(1)}, u32[]{:S(2)}, u32[]{:S(2)}) collective-permute-start(bf16[2,64,3072]{2,1,0:T(8,128)(2,1)S(1)} %collective-permute-done.5.refs_2_), channel_id=1, source_target_pairs={{0,4},{4,0},{1,5},{5,1},{2,6},{6,2},{3,7},{7,3},{8,12},{12,8},{9,1... | collective-permute-start | bytes 2359304 | tf_op jit(solution)/shard_map/ppermute | solution.py:188
  135.9 10.8 %collective-permute-start.20 = (bf16[64,3072]{1,0:T(8,128)(2,1)S(1)}, bf16[64,3072]{1,0:T(8,128)(2,1)S(1)}, u32[]{:S(2)}, u32[]{:S(2)}) collective-permute-start(bf16[64,3072]{1,0:T(8,128)(2,1)S(1)} %slice.37), channel_id=1, source_target_pairs={{0,96},{32,0},{64,32},{96,64},{1,97},{33,1},{65,33},{97,65},{2,98}... | collective-permute-start | bytes 1179656 | tf_op jit(solution)/shard_map/ppermute | solution.py:19
  169.8 15.7 %collective-permute-start.21 = (bf16[36,64,128]{2,1,0:T(8,128)(2,1)}, bf16[36,64,128]{2,1,0:T(8,128)(2,1)S(1)}, u32[]{:S(2)}, u32[]{:S(2)}) collective-permute-start(bf16[36,64,128]{2,1,0:T(8,128)(2,1)} %get-tuple-element.10), channel_id=1, source_target_pairs={{0,1},{1,2},{2,3},{3,0},{4,5},{5,6},{6,7},{7,4},{8,9},{9,10},{10,1... | collective-permute-start | bytes 1769480 | tf_op jit(solution)/shard_map/ppermute | solution.py:19
  171.2 28.0 %collective-permute-start.22 = (bf16[36,64,128]{2,1,0:T(8,128)(2,1)S(1)}, bf16[36,64,128]{2,1,0:T(8,128)(2,1)S(1)}, u32[]{:S(2)}, u32[]{:S(2)}) collective-permute-start(bf16[36,64,128]{2,1,0:T(8,128)(2,1)S(1)} %get-tuple-element.11), channel_id=1, source_target_pairs={{0,2},{1,3},{2,0},{3,1},{4,6},{5,7},{6,4},{7,5},{8,10},{9,11},{10,... | collective-permute-start | bytes 1769480 | tf_op jit(solution)/shard_map/ppermute | solution.py:19
  173.8 25.4 %collective-permute-start.23 = (bf16[36,64,128]{2,1,0:T(8,128)(2,1)S(1)}, bf16[36,64,128]{2,1,0:T(8,128)(2,1)S(1)}, u32[]{:S(2)}, u32[]{:S(2)}) collective-permute-start(bf16[36,64,128]{2,1,0:T(8,128)(2,1)S(1)} %get-tuple-element.12), channel_id=1, source_target_pairs={{0,3},{1,0},{2,1},{3,2},{4,7},{5,4},{6,5},{7,6},{8,11},{9,8},{10,9... | collective-permute-start | bytes 1769480 | tf_op jit(solution)/shard_map/ppermute | solution.py:19
  (22 other events, 463.9 us)

commit v2 on v1

--- a/solution.py
+++ b/solution.py
@@ -11,7 +11,6 @@
 NP = TILES * (TILES + 1) // 2
 BF = jnp.bfloat16
 F32 = jnp.float32
-STEPS = [(i, j) for j in range(4) for i in range(j + 1)]
 MIB = 1 << 20
 
 
@@ -19,93 +18,145 @@
     return lax.ppermute(a, axis, [(i, (i + d) % 4) for i in range(4)])
 
 
-def gather4(a, axis):
-    half = a.shape[0] // 2
-    low, high = shift(a, axis, 1), shift(a, axis, -1)
-    far0 = shift(low[:half], axis, 1)
-    far1 = shift(high[half:], axis, -1)
-    return a, high, far0, far1, low
-
-
-def gram_kernel(meta, steps_i, steps_j, *refs):
-    lefts, rights = refs[:10], refs[10:20]
-    own, s1, s2, s3 = refs[20:24]
-    lbuf, rbuf, sems = refs[24:]
-    x, z, c, y = meta[0], meta[1], meta[2], meta[3]
+def tie(*arrays):
+    return lax.optimization_barrier(arrays)
+
+
+def left_slot(z, c, zz, cc):
+    own = zz // 2 == z // 2
+    near = jnp.where(zz % 2 == z % 2, 6, 4) + cc
+    return jnp.where(own, 2 * (zz % 2) + cc, near)
+
+
+def load(meta, lefts, rights, lbuf, rbuf, sems):
+    x, z, c = meta[0], meta[1], meta[2]
     copies = []
 
     def copy(src, dst):
         copies.append(pltpu.make_async_copy(src, dst, sems.at[len(copies)]))
         copies[-1].start()
 
-    for half in range(2):
-        parity = (z // 2 + half) % 2
-        mine = rights[5 * half : 5 * half + 5]
-        for dx, ref, lo in ((0, mine[0], 0), (1, mine[1], 0), (2, mine[2], 0), (2, mine[3], 64), (3, mine[4], 0)):
-            tile = 2 * ((x + dx) % 4) + parity
-            copy(ref, rbuf.at[tile, pl.ds(lo, ref.shape[0])])
-    for dc in range(2):
-        mine = lefts[5 * dc : 5 * dc + 5]
-        for dz, ref, first in ((0, mine[0], 0), (1, mine[1], 0), (2, mine[2], 0), (2, mine[3], 2), (3, mine[4], 0)):
-            zz = (z + dz) % 4
-            quarter = 2 * (zz % 2) + (c + dc) % 2
-            for k in range(ref.shape[0]):
-                tile = 2 * ((x + first + k) % 4) + zz // 2
-                copy(ref.at[k], lbuf.at[tile, (quarter - y + 4) % 4])
+    for (half, dx), ref in rights:
+        copy(ref, rbuf.at[(x + dx) % 4, (z // 2 + half) % 2])
+    for (dc, dz, first), ref in lefts:
+        zz = (z + dz) % 4
+        slot = left_slot(z, c, zz, (c + dc) % 2)
+        for k in range(ref.shape[0]):
+            copy(ref.at[k], lbuf.at[(x + first + k) % 4, slot])
     for item in copies:
         item.wait()
 
-    def step(t, _):
-        ip, jp = steps_i[t], steps_j[t]
-        left = lbuf[pl.ds(2 * ip, 2)].reshape(512, lbuf.shape[-1])
-        right = rbuf[pl.ds(2 * jp, 2)].reshape(256, rbuf.shape[-1])
-        out = lax.dot_general(left, right, (((1,), (1,)), ((), ())), preferred_element_type=F32)
-        for a in range(2):
-            for b in range(2):
-                i, j = 2 * ip + a, 2 * jp + b
-
-                @pl.when(i <= j)
-                def _():
-                    at = j * (j + 1) // 2 + i
-                    part = out[256 * a : 256 * a + 256, 128 * b : 128 * b + 128]
-                    own[at] = part[0:64]
-                    s1[at] = part[64:128].astype(BF)
-                    s2[at] = part[128:192].astype(BF)
-                    s3[at] = part[192:256].astype(BF)
-
+
+def product(left, right):
+    return lax.dot_general(left, right, (((1,), (1,)), ((), ())), preferred_element_type=F32)
+
+
+def store(meta, outs, part, i, j, slot_quarter):
+    dy = (slot_quarter - meta[3] + 4) % 4
+    at = j * (j + 1) // 2 + i
+    for k in range(4):
+
+        @pl.when((i <= j) & (dy == k))
+        def _():
+            outs[k][at] = part.astype(outs[k].dtype)
+
+
+def store_slots(meta, outs, out, ip, jp, slots, row):
+    z = meta[1]
+    z1, z0 = z // 2, z % 2
+    for n, slot in enumerate(slots):
+        if slot < 4:
+            i, quarter = 2 * ip + z1, slot
+        elif slot < 6:
+            i, quarter = 2 * ip + 1 - z1, 2 * (1 - z0) + slot - 4
+        else:
+            i, quarter = 2 * ip + 1 - z1, 2 * z0 + slot - 6
+        for b in range(2):
+            part = out[row + 64 * n : row + 64 * n + 64, 128 * b : 128 * b + 128]
+            store(meta, outs, part, i, 2 * jp + b, quarter)
+
+
+EARLY_L = [(dc, dz, 0) for dc in range(2) for dz in (0, 1, 3)]
+LATE_L = [(dc, 2, first) for dc in range(2) for first in (0, 2)]
+EARLY_R = [(half, dx) for half in range(2) for dx in (0, 1, 3)]
+LATE_R = [(half, 2) for half in range(2)]
+
+
+def early_kernel(meta, *refs):
+    n = len(EARLY_L) + len(EARLY_R)
+    lefts = list(zip(EARLY_L, refs))
+    rights = list(zip(EARLY_R, refs[len(EARLY_L) :]))
+    outs, (lbuf, rbuf, sems) = refs[n : n + 4], refs[n + 4 :]
+    load(meta, lefts, rights, lbuf, rbuf, sems)
+    x = meta[0]
+    width = lbuf.shape[-1]
+
+    for dx in (0, 1, 3):
+        jp = (x + dx) % 4
+
+        def step(ip, _):
+            out = product(lbuf[ip].reshape(384, width), rbuf[jp].reshape(256, width))
+            store_slots(meta, outs, out, ip, jp, range(6), 0)
+            return 0
+
+        lax.fori_loop(0, jp + 1, step, 0)
+
+
+def late_kernel(meta, *refs):
+    keys_l, keys_r = EARLY_L + LATE_L, EARLY_R + LATE_R
+    n = len(keys_l) + len(keys_r)
+    lefts = list(zip(keys_l, refs))
+    rights = list(zip(keys_r, refs[len(keys_l) :]))
+    done, outs = refs[n : n + 4], refs[n + 4 : n + 8]
+    lbuf, rbuf, sems = refs[n + 8 :]
+    for a, b in zip(done, outs):
+        b[...] = a[...]
+    load(meta, lefts, rights, lbuf, rbuf, sems)
+    x = meta[0]
+    width = lbuf.shape[-1]
+
+    def near(k, _):
+        jp = (x + jnp.where(k == 2, 3, k)) % 4
+        left = lbuf[:, 6:8].reshape(512, width)
+        out = product(left, rbuf[jp].reshape(256, width))
+        for ip in range(4):
+            store_slots(meta, outs, out, ip, jp, (6, 7), 128 * ip)
         return 0
 
-    lax.fori_loop(0, len(STEPS), step, 0)
-
-
-def grams(meta, lefts, rights):
+    lax.fori_loop(0, 3, near, 0)
+    jp = (x + 2) % 4
+
+    def far(ip, _):
+        out = product(lbuf[ip].reshape(512, width), rbuf[jp].reshape(256, width))
+        store_slots(meta, outs, out, ip, jp, range(8), 0)
+        return 0
+
+    lax.fori_loop(0, jp + 1, far, 0)
+
+
+def grams(meta, lefts, rights, done):
     width = rights[0].shape[-1]
     any_ = pl.BlockSpec(memory_space=pl.ANY)
     smem = pl.BlockSpec(memory_space=pltpu.SMEM)
     vmem = pl.BlockSpec(memory_space=pltpu.VMEM)
     piece = (NP, 64, 128)
+    slots = 8 if done else 6
     return pl.pallas_call(
-        gram_kernel,
+        late_kernel if done else early_kernel,
         out_shape=[jax.ShapeDtypeStruct(piece, F32)] + [jax.ShapeDtypeStruct(piece, BF)] * 3,
-        in_specs=[smem] * 3 + [any_] * 20,
+        in_specs=[smem] + [any_] * (len(lefts) + len(rights)) + [vmem] * len(done),
         out_specs=[vmem] * 4,
         scratch_shapes=[
-            pltpu.VMEM((TILES, 4, 64, width), BF),
-            pltpu.VMEM((TILES, 128, width), BF),
-            pltpu.SemaphoreType.DMA((42,)),
+            pltpu.VMEM((4, slots, 64, width), BF),
+            pltpu.VMEM((4, 2, 128, width), BF),
+            pltpu.SemaphoreType.DMA((40,)),
         ],
         compiler_params=pltpu.CompilerParams(vmem_limit_bytes=48 * MIB),
         cost_estimate=pl.CostEstimate(
-            flops=2 * 10 * 512 * 256 * width, bytes_accessed=20 * MIB, transcendentals=0
+            flops=2 * 8 * 384 * 256 * width, bytes_accessed=20 * MIB, transcendentals=0
         ),
-        name="grams",
-    )(
-        meta,
-        jnp.array([s[0] for s in STEPS], jnp.int32),
-        jnp.array([s[1] for s in STEPS], jnp.int32),
-        *lefts,
-        *rights,
-    )
+        name="late_grams" if done else "early_grams",
+    )(meta, *lefts, *rights, *done)
 
 
 def route_kernel(index, valid, own, a, b, c, out, total):
@@ -180,14 +231,32 @@
         return (part.astype(F32) * weights).astype(BF)
 
     mine = [weighted_part(lax.rem(x + d, 4)) for d in range(4)]
-    left = jnp.concatenate(
-        [mine[0], shift(mine[3], "x", 3), shift(mine[2], "x", 2), shift(mine[1], "x", 1)], 0
-    )
-    rights = gather4(keep, "x") + gather4(got, "x")
-    lefts = gather4(left, "z")
-    lefts = lefts + tuple(lax.ppermute(a, "c", [(0, 1), (1, 0)]) for a in lefts)
+    other = [(0, 1), (1, 0)]
+    got, e1, e2, e3 = tie(
+        got, shift(mine[3], "x", 3), shift(mine[2], "x", 2), shift(mine[1], "x", 1)
+    )
+    left = jnp.concatenate([mine[0], e1, e2, e3], 0)
+    keep, got, left = tie(keep, got, left)
+
+    keep3, keep1 = shift(keep, "x", 1), shift(keep, "x", -1)
+    got3, got1 = shift(got, "x", 1), shift(got, "x", -1)
+    left3, left1 = shift(left, "z", 1), shift(left, "z", -1)
+    swap0 = lax.ppermute(left, "c", other)
+    keep3, keep1, got3, got1, left3, left1, swap0 = tie(
+        keep3, keep1, got3, got1, left3, left1, swap0
+    )
+
+    keep2, got2 = shift(keep3, "x", 1), shift(got1, "x", -1)
+    left2a, left2b = shift(left3[:2], "z", 1), shift(left1[2:], "z", -1)
+    swap1, swap3 = lax.ppermute(left1, "c", other), lax.ppermute(left3, "c", other)
     meta = jnp.stack([x, z, c, y]).astype(jnp.int32)
-    own, s1, s2, s3 = grams(meta, lefts, rights)
+    lefts = [left, left1, left3, swap0, swap1, swap3]
+    rights = [keep, keep1, keep3, got, got1, got3]
+    done = grams(meta, lefts, rights, [])
+    swap2a, swap2b = lax.ppermute(left2a, "c", other), lax.ppermute(left2b, "c", other)
+    own, s1, s2, s3 = grams(
+        meta, lefts + [left2a, left2b, swap2a, swap2b], rights + [keep2, got2], done
+    )
     parts = [shift(s1, "y", 1), shift(s2, "y", 2), shift(s3, "y", 3)]
 
     owners = 32

time: 244 us -> 208 us (0.85)
  waiting for transfers between devices: 136 us -> 90.2 us
  Pallas kernels: 26.3 us -> 40.9 us
  starting transfers between devices: 33 us -> 29.7 us
  local copies, waits for them, and re-layouts: 12 us -> 9.27 us
  other arithmetic: 1.06 us -> 3.77 us
    ppermute x19 -> x17, waiting for transfers between devices: 136 us -> 90.2 us  [shift(): return lax.ppermute(a, axis, [(i, (i + d) % 4) for i in range(4)])]
    pallas_call x1 -> x2, Pallas kernels: 18.3 us -> 33 us  [grams(): pl.pallas_call(late_kernel if done else early_kernel, out_shape=[jax.Shap...]
    unnamed x45 -> x27, local copies, waits for them, and re-layouts: 9.17 us -> 4.29 us
    ppermute x19 -> x17, starting transfers between devices: 26.7 us -> 25.5 us  [shift(): return lax.ppermute(a, axis, [(i, (i + d) % 4) for i in range(4)])]
  transfers between devices with their start and end apart: 24 -> 22, of which waited for: 9 -> 9; matrix products, arithmetic and copies ran while one was open for 1% -> 4% of each run, Pallas kernels for 0% -> 7%
where the time goes in v2:
time: 208 us; the launch traced here: 207 us
  waiting for transfers between devices  90.2 us (43%)
  Pallas kernels  40.9 us (20%)
  blocking collectives  33.1 us (16%)
  starting transfers between devices  29.7 us (14%)
  local copies, waits for them, and re-layouts  9.27 us (4%)
  other arithmetic  3.77 us (2%)
    ppermute x17, waiting for transfers between devices, shift(): return lax.ppermute(a, axis, [(i, (i + d) % 4) for i in range(4)])  90.2 us
    all_to_all x1, blocking collectives, on_device(): arrived = lax.all_to_all(routed, ('x', 'z', 'c'), 0, 0, tiled=True)  33.1 us
    pallas_call x2, Pallas kernels, grams(): pl.pallas_call(late_kernel if done else early_kernel, out_shape=[jax.Shap...  33 us
    ppermute x17, starting transfers between devices, shift(): return lax.ppermute(a, axis, [(i, (i + d) % 4) for i in range(4)])  25.5 us
    unnamed x27, local copies, waits for them, and re-layouts  4.29 us
    pallas_call x1, Pallas kernels, place(): pl.pallas_call(place_kernel, grid=(CAP,), out_shape=jax.ShapeDtypeStruct(...  4.24 us
  transfers between devices with their start and end apart: 22, of which 9 were waited for; matrix products, arithmetic and copies ran while one was open for 4% of the time, Pallas kernels for 7%

profile of v2, /device:TPU:1, one launch (start us, length us, event | category | flops | bytes accessed | tf_op | source)
XLA Modules:
  0.0 207.2 jit_solution(5551278092394519884)
XLA Ops:
  0.0 1.8 copy.6
  2.8 4.4 %collective-permute-start = (bf16[128,3072]{1,0:T(8,128)(2,1)}, bf16[128,3072]{1,0:T(8,128)(2,1)S(1)}, u32[]{:S(2)}, u32[]{:S(2)}) collective-permute-start(bf16[128,3072]{1,0:T(8,128)(2,1)} %get-tuple-element.55), channel_id=1, source_target_pairs={{0,16},{8,24},{16,0},{24,8},{1,17},{9,25},{17,1},{25,9},{2,18},{10... | collective-permute-start | bytes 2359304 | tf_op jit(solution)/shard_map/ppermute | solution.py:18
  10.3 2.5 %collective-permute-start.1 = (bf16[1,64,3072]{2,1,0:T(8,128)(2,1)S(1)}, bf16[1,64,3072]{2,1,0:T(8,128)(2,1)S(1)}, u32[]{:S(2)}, u32[]{:S(2)}) collective-permute-start(bf16[1,64,3072]{2,1,0:T(8,128)(2,1)S(1)} %get-tuple-element.60), channel_id=1, source_target_pairs={{0,96},{32,0},{64,32},{96,64},{1,97},{33,1},{65,33},{97,65},{2,98}... | collective-permute-start | bytes 1179656 | tf_op jit(solution)/shard_map/ppermute | solution.py:18
  14.0 7.1 %collective-permute-done.1 = bf16[1,64,3072]{2,1,0:T(8,128)(2,1)S(1)} collective-permute-done((bf16[1,64,3072]{2,1,0:T(8,128)(2,1)S(1)}, bf16[1,64,3072]{2,1,0:T(8,128)(2,1)S(1)}, u32[]{:S(2)}, u32[]{:S(2)}) %collective-permute-start.1) | collective-permute-done | bytes 393248 | tf_op jit(solution)/shard_map/ppermute | solution.py:18
  21.1 2.7 %collective-permute-done.2 = bf16[1,64,3072]{2,1,0:T(8,128)(2,1)S(1)} collective-permute-done((bf16[1,64,3072]{2,1,0:T(8,128)(2,1)S(1)}, bf16[1,64,3072]{2,1,0:T(8,128)(2,1)S(1)}, u32[]{:S(2)}, u32[]{:S(2)}) %collective-permute-start.2) | collective-permute-done | bytes 393248 | tf_op jit(solution)/shard_map/ppermute | solution.py:18
  23.8 10.1 %collective-permute-done.3 = bf16[1,64,3072]{2,1,0:T(8,128)(2,1)S(1)} collective-permute-done((bf16[1,64,3072]{2,1,0:T(8,128)(2,1)S(1)}, bf16[1,64,3072]{2,1,0:T(8,128)(2,1)S(1)}, u32[]{:S(2)}, u32[]{:S(2)}) %collective-permute-start.3) | collective-permute-done | bytes 393248 | tf_op jit(solution)/shard_map/ppermute | solution.py:18
  34.1 2.7 %collective-permute-start.5 = (bf16[128,3072]{1,0:T(8,128)(2,1)S(1)}, bf16[128,3072]{1,0:T(8,128)(2,1)S(1)}, u32[]{:S(2)}, u32[]{:S(2)}) collective-permute-start(bf16[128,3072]{1,0:T(8,128)(2,1)S(1)} %get-tuple-element.32.refs_6_.refs_10_), channel_id=1, source_target_pairs={{0,96},{32,0},{64,32},{96,64},{1,97},{33,1},{65,33},{97,65},{2,98}... | collective-permute-start | bytes 2359304 | tf_op jit(solution)/shard_map/ppermute | solution.py:18
  38.6 1.9 collective-permute-start.9
  40.5 13.5 %collective-permute-done.4.refs_8_.refs_12_ = bf16[128,3072]{1,0:T(8,128)(2,1)S(1)} collective-permute-done((bf16[128,3072]{1,0:T(8,128)(2,1)S(1)}, bf16[128,3072]{1,0:T(8,128)(2,1)S(1)}, u32[]{:S(2)}, u32[]{:S(2)}) %collective-permute-start.4) | collective-permute-done | bytes 786464 | tf_op jit(solution)/shard_map/ppermute | solution.py:18
  54.1 2.7 %collective-permute-start.7 = (bf16[128,3072]{1,0:T(8,128)(2,1)S(1)}, bf16[128,3072]{1,0:T(8,128)(2,1)}, u32[]{:S(2)}, u32[]{:S(2)}) collective-permute-start(bf16[128,3072]{1,0:T(8,128)(2,1)S(1)} %collective-permute-done.refs_9_.refs_13_), channel_id=1, source_target_pairs={{0,96},{32,0},{64,32},{96,64},{1,97},{33,1},{65,33},{97,65},{2,98}... | collective-permute-start | bytes 2359304 | tf_op jit(solution)/shard_map/ppermute | solution.py:18
  56.7 16.4 %collective-permute-done.6.refs_11_.refs_15_ = bf16[128,3072]{1,0:T(8,128)(2,1)S(1)} collective-permute-done((bf16[128,3072]{1,0:T(8,128)(2,1)S(1)}, bf16[128,3072]{1,0:T(8,128)(2,1)S(1)}, u32[]{:S(2)}, u32[]{:S(2)}) %collective-permute-start.6) | collective-permute-done | bytes 786464 | tf_op jit(solution)/shard_map/ppermute | solution.py:18
  73.2 2.0 collective-permute-done.8.refs_2_
  78.2 2.1 %collective-permute-start.14 = (bf16[2,64,3072]{2,1,0:T(8,128)(2,1)S(1)}, bf16[2,64,3072]{2,1,0:T(8,128)(2,1)}, u32[]{:S(2)}, u32[]{:S(2)}) collective-permute-start(bf16[2,64,3072]{2,1,0:T(8,128)(2,1)S(1)} %slice.15), channel_id=1, source_target_pairs={{0,24},{8,0},{16,8},{24,16},{1,25},{9,1},{17,9},{25,17},{2,26},{10... | collective-permute-start | bytes 2359304 | tf_op jit(solution)/shard_map/ppermute | solution.py:18
  80.3 17.2 %collective-permute-done.13.refs_6_ = bf16[2,64,3072]{2,1,0:T(8,128)(2,1)} collective-permute-done((bf16[2,64,3072]{2,1,0:T(8,128)(2,1)S(1)}, bf16[2,64,3072]{2,1,0:T(8,128)(2,1)}, u32[]{:S(2)}, u32[]{:S(2)}) %collective-permute-start.13) | collective-permute-done | bytes 786464 | tf_op jit(solution)/shard_map/ppermute | solution.py:18
  97.5 1.5 collective-permute-start.18
  99.0 2.1 collective-permute-start.15
  102.4 14.7 %early_grams.1 = (f32[36,64,128]{2,1,0:T(8,128)}, bf16[36,64,128]{2,1,0:T(8,128)(2,1)S(1)}, bf16[36,64,128]{2,1,0:T(8,128)(2,1)S(1)}, bf16[36,64,128]{2,1,0:T(8,128)(2,1)S(1)}) custom-call(s32[4]{0:T(128)S(1)} %pad_add_fusion.meta, bf16[4,64,3072]{2,1,0:T(8,128)(2,1)} %copy-done.5, bf16[4,64,3072]{2,1,0:T(8,128)(2,1)} %copy-done.6, ...), custom_call_target="tpu_custom_call" | custom-call | flops 4831838208 | bytes 20971520 | tf_op jit(solution)/shard_map/early_grams/pallas_call | solution.py:144
  117.2 18.3 %late_grams.1 = (f32[36,64,128]{2,1,0:T(8,128)}, bf16[36,64,128]{2,1,0:T(8,128)(2,1)S(1)}, bf16[36,64,128]{2,1,0:T(8,128)(2,1)S(1)}, bf16[36,64,128]{2,1,0:T(8,128)(2,1)S(1)}) custom-call(s32[4]{0:T(128)S(1)} %pad_add_fusion.meta, bf16[4,64,3072]{2,1,0:T(8,128)(2,1)} %copy-done.5, bf16[4,64,3072]{2,1,0:T(8,128)(2,1)} %copy-done.6, ...), custom_call_target="tpu_custom_call" | custom-call | flops 4831838208 | bytes 20971520 | tf_op jit(solution)/shard_map/late_grams/pallas_call | solution.py:144
  136.8 2.6 %collective-permute-start.20 = (bf16[36,64,128]{2,1,0:T(8,128)(2,1)S(1)}, bf16[36,64,128]{2,1,0:T(8,128)(2,1)S(1)}, u32[]{:S(2)}, u32[]{:S(2)}) collective-permute-start(bf16[36,64,128]{2,1,0:T(8,128)(2,1)S(1)} %get-tuple-element.47), channel_id=1, source_target_pairs={{0,2},{1,3},{2,0},{3,1},{4,6},{5,7},{6,4},{7,5},{8,10},{9,11},{10,... | collective-permute-start | bytes 1769480 | tf_op jit(solution)/shard_map/ppermute | solution.py:18
  143.7 7.4 %collective-permute-done.19.a = bf16[36,64,128]{2,1,0:T(8,128)(2,1)S(1)} collective-permute-done((bf16[36,64,128]{2,1,0:T(8,128)(2,1)S(1)}, bf16[36,64,128]{2,1,0:T(8,128)(2,1)S(1)}, u32[]{:S(2)}, u32[]{:S(2)}) %collective-permute-start.19) | collective-permute-done | bytes 589856 | tf_op jit(solution)/shard_map/ppermute | solution.py:18
  151.1 13.8 %collective-permute-done.20.b = bf16[36,64,128]{2,1,0:T(8,128)(2,1)S(1)} collective-permute-done((bf16[36,64,128]{2,1,0:T(8,128)(2,1)S(1)}, bf16[36,64,128]{2,1,0:T(8,128)(2,1)S(1)}, u32[]{:S(2)}, u32[]{:S(2)}) %collective-permute-start.20) | collective-permute-done | bytes 589856 | tf_op jit(solution)/shard_map/ppermute | solution.py:18
  166.1 3.7 %route.1 = bf16[128,64,128]{2,1,0:T(8,128)(2,1)S(1)} custom-call(s32[128]{0:T(128)S(1)} %get-tuple-element.50.index, s32[128]{0:T(128)S(1)} %get-tuple-element.49.valid, f32[36,64,128]{2,1,0:T(8,128)S(1)} %copy-done.1, bf16[36,64,128]{2,1,0:T(8,128)(2,1)S(1)} %collective-permute-done.19.a, bf16[36,64,128]{2,1,0:T(8,128)(2,1)S(1)} %collective-permute-done.20.b, ...), custom_call_target="tpu_custom_call" | custom-call | tf_op jit(solution)/shard_map/route/pallas_call | solution.py:184
  169.8 33.1 %all_to_all.5.got = bf16[32,4,64,128]{3,2,1,0:T(8,128)(2,1)} all-to-all(bf16[32,4,64,128]{3,2,1,0:T(8,128)(2,1)S(1)} %bitcast.22), channel_id=1, replica_groups=mesh['x'=4,'z'=4,'c'=2,'y'=4] {'x','z','c'}, dimensions={0} | all-to-all | bytes 4194304 | tf_op jit(solution)/shard_map/all_to_all | solution.py:274
  203.0 4.2 %place.1 = f32[4,256,1024]{2,1,0:T(8,128)} custom-call(bf16[32,4,64,128]{3,2,1,0:T(8,128)(2,1)} %all_to_all.5.got), custom_call_target="tpu_custom_call" | custom-call | tf_op jit(solution)/shard_map/place/pallas_call | solution.py:205
  (66 shorter events, 18.5 us)
Async XLA Ops:
  2.8 99.5 %copy-start = (bf16[128,3072]{1,0:T(8,128)(2,1)}, bf16[128,3072]{1,0:T(8,128)(2,1)S(1)}, u32[]{:S(2)}) copy-start(bf16[128,3072]{1,0:T(8,128)(2,1)S(1)} %get-tuple-element.32.refs_6_.refs_10_) | copy-start | bytes 2359300
  2.8 31.0 %collective-permute-start = (bf16[128,3072]{1,0:T(8,128)(2,1)}, bf16[128,3072]{1,0:T(8,128)(2,1)S(1)}, u32[]{:S(2)}, u32[]{:S(2)}) collective-permute-start(bf16[128,3072]{1,0:T(8,128)(2,1)} %get-tuple-element.55), channel_id=1, source_target_pairs={{0,16},{8,24},{16,0},{24,8},{1,17},{9,25},{17,1},{25,9},{2,18},{10... | collective-permute-start | bytes 2359304 | tf_op jit(solution)/shard_map/ppermute | solution.py:18
  10.3 10.8 %collective-permute-start.1 = (bf16[1,64,3072]{2,1,0:T(8,128)(2,1)S(1)}, bf16[1,64,3072]{2,1,0:T(8,128)(2,1)S(1)}, u32[]{:S(2)}, u32[]{:S(2)}) collective-permute-start(bf16[1,64,3072]{2,1,0:T(8,128)(2,1)S(1)} %get-tuple-element.60), channel_id=1, source_target_pairs={{0,96},{32,0},{64,32},{96,64},{1,97},{33,1},{65,33},{97,65},{2,98}... | collective-permute-start | bytes 1179656 | tf_op jit(solution)/shard_map/ppermute | solution.py:18
  12.9 10.9 %collective-permute-start.2 = (bf16[1,64,3072]{2,1,0:T(8,128)(2,1)S(1)}, bf16[1,64,3072]{2,1,0:T(8,128)(2,1)S(1)}, u32[]{:S(2)}, u32[]{:S(2)}) collective-permute-start(bf16[1,64,3072]{2,1,0:T(8,128)(2,1)S(1)} %get-tuple-element.58), channel_id=1, source_target_pairs={{0,64},{32,96},{64,0},{96,32},{1,65},{33,97},{65,1},{97,33},{2,66}... | collective-permute-start | bytes 1179656 | tf_op jit(solution)/shard_map/ppermute | solution.py:18
  13.4 20.4 %collective-permute-start.3 = (bf16[1,64,3072]{2,1,0:T(8,128)(2,1)S(1)}, bf16[1,64,3072]{2,1,0:T(8,128)(2,1)S(1)}, u32[]{:S(2)}, u32[]{:S(2)}) collective-permute-start(bf16[1,64,3072]{2,1,0:T(8,128)(2,1)S(1)} %get-tuple-element.59), channel_id=1, source_target_pairs={{0,32},{32,64},{64,96},{96,0},{1,33},{33,65},{65,97},{97,1},{2,34}... | collective-permute-start | bytes 1179656 | tf_op jit(solution)/shard_map/ppermute | solution.py:18
  33.8 68.5 %copy-start.2 = (bf16[128,3072]{1,0:T(8,128)(2,1)}, bf16[128,3072]{1,0:T(8,128)(2,1)S(1)}, u32[]{:S(2)}) copy-start(bf16[128,3072]{1,0:T(8,128)(2,1)S(1)} %collective-permute-done.refs_9_.refs_13_) | copy-start | bytes 2359300
  34.0 20.0 %collective-permute-start.4 = (bf16[128,3072]{1,0:T(8,128)(2,1)S(1)}, bf16[128,3072]{1,0:T(8,128)(2,1)S(1)}, u32[]{:S(2)}, u32[]{:S(2)}) collective-permute-start(bf16[128,3072]{1,0:T(8,128)(2,1)S(1)} %get-tuple-element.32.refs_6_.refs_10_), channel_id=1, source_target_pairs={{0,32},{32,64},{64,96},{96,0},{1,33},{33,65},{65,97},{97,1},{2,34}... | collective-permute-start | bytes 2359304 | tf_op jit(solution)/shard_map/ppermute | solution.py:18
  34.1 19.9 %collective-permute-start.5 = (bf16[128,3072]{1,0:T(8,128)(2,1)S(1)}, bf16[128,3072]{1,0:T(8,128)(2,1)S(1)}, u32[]{:S(2)}, u32[]{:S(2)}) collective-permute-start(bf16[128,3072]{1,0:T(8,128)(2,1)S(1)} %get-tuple-element.32.refs_6_.refs_10_), channel_id=1, source_target_pairs={{0,96},{32,0},{64,32},{96,64},{1,97},{33,1},{65,33},{97,65},{2,98}... | collective-permute-start | bytes 2359304 | tf_op jit(solution)/shard_map/ppermute | solution.py:18
  36.8 36.4 %collective-permute-start.10 = (bf16[4,64,3072]{2,1,0:T(8,128)(2,1)S(1)}, bf16[4,64,3072]{2,1,0:T(8,128)(2,1)S(1)}, u32[]{:S(2)}, u32[]{:S(2)}) collective-permute-start(bf16[4,64,3072]{2,1,0:T(8,128)(2,1)S(1)} %pad_maximum_fusion.refs_0_), channel_id=1, source_target_pairs={{0,4},{4,0},{1,5},{5,1},{2,6},{6,2},{3,7},{7,3},{8,12},{12,8},{9,1... | collective-permute-start | bytes 4718600 | tf_op jit(solution)/shard_map/ppermute | solution.py:244
  37.8 37.3 %collective-permute-start.8 = (bf16[4,64,3072]{2,1,0:T(8,128)(2,1)S(1)}, bf16[4,64,3072]{2,1,0:T(8,128)(2,1)}, u32[]{:S(2)}, u32[]{:S(2)}) collective-permute-start(bf16[4,64,3072]{2,1,0:T(8,128)(2,1)S(1)} %pad_maximum_fusion.refs_0_), channel_id=1, source_target_pairs={{0,8},{8,16},{16,24},{24,0},{1,9},{9,17},{17,25},{25,1},{2,10},{10... | collective-permute-start | bytes 4718600 | tf_op jit(solution)/shard_map/ppermute | solution.py:18
  38.6 36.6 %collective-permute-start.9 = (bf16[4,64,3072]{2,1,0:T(8,128)(2,1)S(1)}, bf16[4,64,3072]{2,1,0:T(8,128)(2,1)S(1)}, u32[]{:S(2)}, u32[]{:S(2)}) collective-permute-start(bf16[4,64,3072]{2,1,0:T(8,128)(2,1)S(1)} %pad_maximum_fusion.refs_0_), channel_id=1, source_target_pairs={{0,24},{8,0},{16,8},{24,16},{1,25},{9,1},{17,9},{25,17},{2,26},{10... | collective-permute-start | bytes 4718600 | tf_op jit(solution)/shard_map/ppermute | solution.py:18
  54.0 19.1 %collective-permute-start.6 = (bf16[128,3072]{1,0:T(8,128)(2,1)S(1)}, bf16[128,3072]{1,0:T(8,128)(2,1)S(1)}, u32[]{:S(2)}, u32[]{:S(2)}) collective-permute-start(bf16[128,3072]{1,0:T(8,128)(2,1)S(1)} %collective-permute-done.refs_9_.refs_13_), channel_id=1, source_target_pairs={{0,32},{32,64},{64,96},{96,0},{1,33},{33,65},{65,97},{97,1},{2,34}... | collective-permute-start | bytes 2359304 | tf_op jit(solution)/shard_map/ppermute | solution.py:18
  54.1 19.1 %collective-permute-start.7 = (bf16[128,3072]{1,0:T(8,128)(2,1)S(1)}, bf16[128,3072]{1,0:T(8,128)(2,1)}, u32[]{:S(2)}, u32[]{:S(2)}) collective-permute-start(bf16[128,3072]{1,0:T(8,128)(2,1)S(1)} %collective-permute-done.refs_9_.refs_13_), channel_id=1, source_target_pairs={{0,96},{32,0},{64,32},{96,64},{1,97},{33,1},{65,33},{97,65},{2,98}... | collective-permute-start | bytes 2359304 | tf_op jit(solution)/shard_map/ppermute | solution.py:18
  75.2 25.8 %collective-permute-start.11 = (bf16[4,64,3072]{2,1,0:T(8,128)(2,1)S(1)}, bf16[4,64,3072]{2,1,0:T(8,128)(2,1)S(1)}, u32[]{:S(2)}, u32[]{:S(2)}) collective-permute-start(bf16[4,64,3072]{2,1,0:T(8,128)(2,1)S(1)} %collective-permute-done.9.refs_1_), channel_id=1, source_target_pairs={{0,4},{4,0},{1,5},{5,1},{2,6},{6,2},{3,7},{7,3},{8,12},{12,8},{9,1... | collective-permute-start | bytes 4718600 | tf_op jit(solution)/shard_map/ppermute | solution.py:251
  76.2 26.2 %collective-permute-start.12 = (bf16[4,64,3072]{2,1,0:T(8,128)(2,1)}, bf16[4,64,3072]{2,1,0:T(8,128)(2,1)}, u32[]{:S(2)}, u32[]{:S(2)}) collective-permute-start(bf16[4,64,3072]{2,1,0:T(8,128)(2,1)} %collective-permute-done.8.refs_2_), channel_id=1, source_target_pairs={{0,4},{4,0},{1,5},{5,1},{2,6},{6,2},{3,7},{7,3},{8,12},{12,8},{9,1... | collective-permute-start | bytes 4718600 | tf_op jit(solution)/shard_map/ppermute | solution.py:251
  77.4 20.0 %collective-permute-start.13 = (bf16[2,64,3072]{2,1,0:T(8,128)(2,1)S(1)}, bf16[2,64,3072]{2,1,0:T(8,128)(2,1)}, u32[]{:S(2)}, u32[]{:S(2)}) collective-permute-start(bf16[2,64,3072]{2,1,0:T(8,128)(2,1)S(1)} %slice.14), channel_id=1, source_target_pairs={{0,8},{8,16},{16,24},{24,0},{1,9},{9,17},{17,25},{25,1},{2,10},{10... | collective-permute-start | bytes 2359304 | tf_op jit(solution)/shard_map/ppermute | solution.py:18
  78.2 20.8 %collective-permute-start.14 = (bf16[2,64,3072]{2,1,0:T(8,128)(2,1)S(1)}, bf16[2,64,3072]{2,1,0:T(8,128)(2,1)}, u32[]{:S(2)}, u32[]{:S(2)}) collective-permute-start(bf16[2,64,3072]{2,1,0:T(8,128)(2,1)S(1)} %slice.15), channel_id=1, source_target_pairs={{0,24},{8,0},{16,8},{24,16},{1,25},{9,1},{17,9},{25,17},{2,26},{10... | collective-permute-start | bytes 2359304 | tf_op jit(solution)/shard_map/ppermute | solution.py:18
  80.3 36.8 %collective-permute-start.17 = (bf16[128,3072]{1,0:T(8,128)(2,1)S(1)}, bf16[128,3072]{1,0:T(8,128)(2,1)}, u32[]{:S(2)}, u32[]{:S(2)}) collective-permute-start(bf16[128,3072]{1,0:T(8,128)(2,1)S(1)} %collective-permute-done.4.refs_8_.refs_12_), channel_id=1, source_target_pairs={{0,32},{32,64},{64,96},{96,0},{1,33},{33,65},{65,97},{97,1},{2,34}... | collective-permute-start | bytes 2359304 | tf_op jit(solution)/shard_map/ppermute | solution.py:18
  97.5 19.6 %collective-permute-start.18 = (bf16[128,3072]{1,0:T(8,128)(2,1)}, bf16[128,3072]{1,0:T(8,128)(2,1)}, u32[]{:S(2)}, u32[]{:S(2)}) collective-permute-start(bf16[128,3072]{1,0:T(8,128)(2,1)} %collective-permute-done.7.refs_10_.refs_14_), channel_id=1, source_target_pairs={{0,96},{32,0},{64,32},{96,64},{1,97},{33,1},{65,33},{97,65},{2,98}... | collective-permute-start | bytes 2359304 | tf_op jit(solution)/shard_map/ppermute | solution.py:18
  99.0 18.1 %collective-permute-start.15 = (bf16[2,64,3072]{2,1,0:T(8,128)(2,1)}, bf16[2,64,3072]{2,1,0:T(8,128)(2,1)}, u32[]{:S(2)}, u32[]{:S(2)}) collective-permute-start(bf16[2,64,3072]{2,1,0:T(8,128)(2,1)} %collective-permute-done.13.refs_6_), channel_id=1, source_target_pairs={{0,4},{4,0},{1,5},{5,1},{2,6},{6,2},{3,7},{7,3},{8,12},{12,8},{9,1... | collective-permute-start | bytes 2359304 | tf_op jit(solution)/shard_map/ppermute | solution.py:256
  102.2 14.9 %collective-permute-start.16 = (bf16[2,64,3072]{2,1,0:T(8,128)(2,1)}, bf16[2,64,3072]{2,1,0:T(8,128)(2,1)}, u32[]{:S(2)}, u32[]{:S(2)}) collective-permute-start(bf16[2,64,3072]{2,1,0:T(8,128)(2,1)} %collective-permute-done.14.refs_7_), channel_id=1, source_target_pairs={{0,4},{4,0},{1,5},{5,1},{2,6},{6,2},{3,7},{7,3},{8,12},{12,8},{9,1... | collective-permute-start | bytes 2359304 | tf_op jit(solution)/shard_map/ppermute | solution.py:256
  135.4 15.7 %collective-permute-start.19 = (bf16[36,64,128]{2,1,0:T(8,128)(2,1)S(1)}, bf16[36,64,128]{2,1,0:T(8,128)(2,1)S(1)}, u32[]{:S(2)}, u32[]{:S(2)}) collective-permute-start(bf16[36,64,128]{2,1,0:T(8,128)(2,1)S(1)} %get-tuple-element.46), channel_id=1, source_target_pairs={{0,1},{1,2},{2,3},{3,0},{4,5},{5,6},{6,7},{7,4},{8,9},{9,10},{10,1... | collective-permute-start | bytes 1769480 | tf_op jit(solution)/shard_map/ppermute | solution.py:18
  136.8 28.0 %collective-permute-start.20 = (bf16[36,64,128]{2,1,0:T(8,128)(2,1)S(1)}, bf16[36,64,128]{2,1,0:T(8,128)(2,1)S(1)}, u32[]{:S(2)}, u32[]{:S(2)}) collective-permute-start(bf16[36,64,128]{2,1,0:T(8,128)(2,1)S(1)} %get-tuple-element.47), channel_id=1, source_target_pairs={{0,2},{1,3},{2,0},{3,1},{4,6},{5,7},{6,4},{7,5},{8,10},{9,11},{10,... | collective-permute-start | bytes 1769480 | tf_op jit(solution)/shard_map/ppermute | solution.py:18
  139.4 25.4 %collective-permute-start.21 = (bf16[36,64,128]{2,1,0:T(8,128)(2,1)S(1)}, bf16[36,64,128]{2,1,0:T(8,128)(2,1)S(1)}, u32[]{:S(2)}, u32[]{:S(2)}) collective-permute-start(bf16[36,64,128]{2,1,0:T(8,128)(2,1)S(1)} %get-tuple-element.48), channel_id=1, source_target_pairs={{0,3},{1,0},{2,1},{3,2},{4,7},{5,4},{6,5},{7,6},{8,11},{9,8},{10,9... | collective-permute-start | bytes 1769480 | tf_op jit(solution)/shard_map/ppermute | solution.py:18
  (11 other events, 229.3 us)

commit v3 on v2

v3 whole, which is shorter than its diff:
```python
import jax
import jax.numpy as jnp
from jax import lax
from jax.experimental import pallas as pl
from jax.experimental.pallas import tpu as pltpu
from jax.sharding import Mesh
from jax.sharding import PartitionSpec as P

TILES = 8
CAP = 4
NP = TILES * (TILES + 1) // 2
BF = jnp.bfloat16
F32 = jnp.float32
MIB = 1 << 20


def shift(a, axis, d):
    return lax.ppermute(a, axis, [(i, (i + d) % 4) for i in range(4)])


def tie(*arrays):
    return lax.optimization_barrier(arrays)


EARLY_L = [(dc, dz) for dc in range(2) for dz in (0, 1, 3)]
LATE_L = [(dc, 2) for dc in range(2)]


def product(lefts, rights):
    return lax.dot_general(
        jnp.concatenate(lefts, 0),
        jnp.concatenate(rights, 0),
        (((1,), (1,)), ((), ())),
        preferred_element_type=F32,
    )


def store(meta, sums, out, ip, jp, sources, row):
    z, c, y = meta[1], meta[2], meta[3]
    for n, (dc, dz) in enumerate(sources):
        zz, cc = (z + dz) % 4, (c + dc) % 2
        i = 2 * ip + zz // 2
        dy = (2 * (zz % 2) + cc - y + 4) % 4
        for half in range(2):
            j = 2 * jp + (z // 2 + half) % 2
            at = jnp.where(i <= j, j * (j + 1) // 2 + i, NP)
            sums[dy, at] = out[row + 64 * n : row + 64 * n + 64, 128 * half : 128 * half + 128]


def early_kernel(meta, *refs):
    lefts, rights, sums = refs[:6], refs[6:12], refs[12]
    x = meta[0]
    for n, dx in enumerate((0, 1, 3)):
        jp = (x + dx) % 4
        right = [rights[n], rights[3 + n]]

        def step(k, _):
            ip = (x + k) % 4

            @pl.when(ip <= jp)
            def _():
                out = product([ref[k] for ref in lefts], [ref[...] for ref in right])
                store(meta, sums, out, ip, jp, EARLY_L, 0)

            return 0

        lax.fori_loop(0, 4, step, 0)


def late_kernel(meta, *refs):
    lefts, rights, late, far = refs[:6], refs[6:12], refs[12:16], refs[16:18]
    own, s1, s2, s3, sums = refs[19:24]
    x = meta[0]

    def late_of(k):
        return [late[2 * dc + k // 2][k % 2] for dc in range(2)]

    for n, dx in enumerate((0, 1, 3)):
        jp = (x + dx) % 4
        rows = [block for k in range(4) for block in late_of(k)]
        out = product(rows, [rights[n][...], rights[3 + n][...]])
        for k in range(4):
            store(meta, sums, out, (x + k) % 4, jp, LATE_L, 128 * k)
    jp = (x + 2) % 4
    for k in range(4):
        ip = (x + k) % 4

        @pl.when(ip <= jp)
        def _():
            rows = [ref[k] for ref in lefts] + late_of(k)
            out = product(rows, [ref[...] for ref in far])
            store(meta, sums, out, ip, jp, EARLY_L + LATE_L, 0)

    own[...] = sums[0, :NP]
    for k, ref in enumerate((s1, s2, s3)):
        ref[...] = sums[k + 1, :NP].astype(BF)


def grams(meta, lefts, rights, late=(), far=(), sums=()):
    width = rights[0].shape[-1]
    smem = pl.BlockSpec(memory_space=pltpu.SMEM)
    vmem = pl.BlockSpec(memory_space=pltpu.VMEM)
    piece = (NP, 64, 128)
    given = [*lefts, *rights, *late, *far, *sums]
    shapes = [jax.ShapeDtypeStruct((4, NP + 1, 64, 128), F32)]
    if late:
        shapes = [jax.ShapeDtypeStruct(piece, F32)] + [jax.ShapeDtypeStruct(piece, BF)] * 3 + shapes
    return pl.pallas_call(
        late_kernel if late else early_kernel,
        out_shape=shapes,
        in_specs=[smem] + [vmem] * len(given),
        out_specs=[vmem] * len(shapes),
        input_output_aliases={len(given): 4} if late else {},
        compiler_params=pltpu.CompilerParams(vmem_limit_bytes=16 * MIB),
        cost_estimate=pl.CostEstimate(
            flops=2 * 8 * 384 * 256 * width, bytes_accessed=20 * MIB, transcendentals=0
        ),
        name="late_grams" if late else "early_grams",
    )(meta, *given)


def prepare_kernel(meta, dens, weights, keep, send, *parts):
    k, width = dens.shape[1], keep.shape[1]
    x, z1 = meta[0], meta[1] // 2
    edge = k // 128 * 128
    for ref in (keep, send):
        ref[:, edge:] = jnp.zeros((128, width - edge), BF)
    keep[:, :k] = dens[pl.ds(pl.multiple_of(z1 * 128, 128), 128), :]
    send[:, :k] = dens[pl.ds(pl.multiple_of((1 - z1) * 128, 128), 128), :]
    for d, ref in enumerate(parts):
        ref[0, :, edge:] = jnp.zeros((64, width - edge), BF)
        for h in range(2):
            row = pl.multiple_of(h * 128 + (x + d) % 4 * 32, 32)
            part = dens[pl.ds(row, 32), :].astype(F32) * weights[...]
            ref[0, 32 * h : 32 * h + 32, :k] = part.astype(BF)


def prepare(meta, dens, weights, width):
    smem = pl.BlockSpec(memory_space=pltpu.SMEM)
    vmem = pl.BlockSpec(memory_space=pltpu.VMEM)
    shapes = [jax.ShapeDtypeStruct((128, width), BF)] * 2
    shapes += [jax.ShapeDtypeStruct((1, 64, width), BF)] * 4
    return pl.pallas_call(
        prepare_kernel,
        out_shape=shapes,
        in_specs=[smem, vmem, vmem],
        out_specs=[vmem] * 6,
        compiler_params=pltpu.CompilerParams(vmem_limit_bytes=16 * MIB),
        name="prepare",
    )(meta, dens, weights)


def route_kernel(index, valid, own, a, b, c, out, total):
    total[...] = (
        own[...] + a[...].astype(F32) + b[...].astype(F32) + c[...].astype(F32)
    ).astype(BF)

    def one(k, _):
        @pl.when(valid[k] > 0)
        def _():
            out[k] = total[index[k]]

        @pl.when(valid[k] == 0)
        def _():
            out[k] = jnp.zeros(out.shape[1:], BF)

        return 0

    lax.fori_loop(0, out.shape[0], one, 0)


def route(index, valid, own, parts):
    smem = pl.BlockSpec(memory_space=pltpu.SMEM)
    vmem = pl.BlockSpec(memory_space=pltpu.VMEM)
    return pl.pallas_call(
        route_kernel,
        out_shape=jax.ShapeDtypeStruct((index.shape[0], 64, 128), BF),
        in_specs=[smem, smem] + [vmem] * 4,
        out_specs=vmem,
        scratch_shapes=[pltpu.VMEM((NP, 64, 128), BF)],
        compiler_params=pltpu.CompilerParams(vmem_limit_bytes=32 * MIB),
        name="route",
    )(index, valid, own, *parts)


def place_kernel(got, out):
    for src in range(32):
        x, z1, z0, c = src // 8, (src // 4) % 2, (src // 2) % 2, src % 2
        col = (4 * z0 + 2 * c + z1) * 128
        for h in range(2):
            row = h * 128 + x * 32
            out[0, row : row + 32, col : col + 128] = got[src, 0, 32 * h : 32 * h + 32].astype(F32)


def place(got):
    return pl.pallas_call(
        place_kernel,
        grid=(CAP,),
        out_shape=jax.ShapeDtypeStruct((CAP, 256, 1024), F32),
        in_specs=[pl.BlockSpec((32, 1, 64, 128), lambda s: (0, s, 0, 0))],
        out_specs=pl.BlockSpec((1, 256, 1024), lambda s: (s, 0, 0)),
        name="place",
    )(got)


def on_device(densities, coulomb, pair_list, owner):
    x, z, c, y = (lax.axis_index(n) for n in ("x", "z", "c", "y"))
    k = densities.shape[1]
    meta = jnp.stack([x, z, c, y]).astype(jnp.int32)
    keep, send, *mine = prepare(meta, densities, coulomb[None, :], -(-k // 128) * 128)
    got = shift(send, "z", 2)
    other = [(0, 1), (1, 0)]
    got, e1, e2, e3 = tie(
        got, shift(mine[3], "x", 3), shift(mine[2], "x", 2), shift(mine[1], "x", 1)
    )
    left = jnp.concatenate([mine[0], e1, e2, e3], 0)
    keep, got, left = tie(keep, got, left)

    keep3, keep1 = shift(keep, "x", 1), shift(keep, "x", -1)
    got3, got1 = shift(got, "x", 1), shift(got, "x", -1)
    left3, left1 = shift(left, "z", 1), shift(left, "z", -1)
    swap0 = lax.ppermute(left, "c", other)
    keep3, keep1, got3, got1, left3, left1, swap0 = tie(
        keep3, keep1, got3, got1, left3, left1, swap0
    )

    keep2, got2 = shift(keep3, "x", 1), shift(got1, "x", -1)
    left2a, left2b = shift(left3[:2], "z", 1), shift(left1[2:], "z", -1)
    swap1, swap3 = lax.ppermute(left1, "c", other), lax.ppermute(left3, "c", other)
    lefts = [left, left1, left3, swap0, swap1, swap3]
    rights = [keep, keep1, keep3, got, got1, got3]
    (sums,) = grams(meta, lefts, rights)
    left2a, left2b, sums = tie(left2a, left2b, sums)
    swap2a, swap2b = lax.ppermute(left2a, "c", other), lax.ppermute(left2b, "c", other)
    late = [left2a, left2b, swap2a, swap2b]
    own, s1, s2, s3, _ = grams(meta, lefts, rights, late, [keep2, got2], [sums])
    parts = [shift(s1, "y", 1), shift(s2, "y", 2), shift(s3, "y", 3)]

    owners = 32
    owner_ids = owner[:, 0]
    onehot = (owner_ids[:, None] == jnp.arange(owners, dtype=jnp.int32)[None, :]).astype(jnp.int32)
    rank = jnp.sum((jnp.cumsum(onehot, 0) - onehot) * onehot, 1)
    slot = owner_ids * CAP + rank
    match = (slot[None, :] == jnp.arange(owners * CAP, dtype=jnp.int32)[:, None]).astype(jnp.int32)
    second = pair_list[:, 1]
    which = second * (second + 1) // 2 + pair_list[:, 0]
    index = jnp.sum(match * which[None, :], 1)
    valid = jnp.sum(match, 1)

    routed = route(index, valid, own, parts).reshape(owners, CAP, 64, 128)
    arrived = lax.all_to_all(routed, ("x", "z", "c"), 0, 0, tiled=True)
    return place(arrived)


def solution(mesh):
    grid = Mesh(mesh.devices.reshape(4, 4, 2, 4), ("x", "z", "c", "y"))
    pairs = ("x", "z", "c")
    return jax.shard_map(
        on_device,
        mesh=grid,
        in_specs=(P(pairs, "y"), P("y"), P(), P()),
        out_specs=P(pairs, "y", None),
        check_vma=False,
    )
```

time: 208 us -> 177 us (0.85)
  Pallas kernels: 40.9 us -> 23.1 us
  local copies, waits for them, and re-layouts: 9.27 us -> 1.9 us
  waiting for transfers between devices: 90.2 us -> 84.3 us
    pallas_call x2 -> x3, Pallas kernels: 33 us -> 15.1 us  [the longest x2 14.2 us: grams(): pl.pallas_call(late_kernel if late else early_kernel, out_shape=shapes, i...]
    ppermute x17, waiting for transfers between devices: 90.2 us -> 82.1 us  [shift(): return lax.ppermute(a, axis, [(i, (i + d) % 4) for i in range(4)])]
    unnamed x27 -> x7, local copies, waits for them, and re-layouts: 4.29 us -> 1.79 us
    dynamic_slice x2 -> x0, local copies, waits for them, and re-layouts: 2.49 us -> none  [the longest x1 1.46 us: weighted_part(): part = lax.dynamic_slice_in_dim(quarter, to, 1, 1).reshape(1, 64, width)]
  transfers between devices with their start and end apart: 22 -> 22, of which waited for: 9 -> 13; matrix products, arithmetic and copies ran while one was open for 4% -> 2% of each run, Pallas kernels for 7% -> 4%
where the time goes in v3:
time: 177 us
  waiting for transfers between devices  84.3 us (48%)
  blocking collectives  34.5 us (19%)
  starting transfers between devices  29.8 us (17%)
  Pallas kernels  23.1 us (13%)
  other arithmetic  3.44 us (2%)
  local copies, waits for them, and re-layouts  1.9 us (1%)
    ppermute x17, waiting for transfers between devices, shift(): return lax.ppermute(a, axis, [(i, (i + d) % 4) for i in range(4)])  82.1 us
    all_to_all x1, blocking collectives, on_device(): arrived = lax.all_to_all(routed, ('x', 'z', 'c'), 0, 0, tiled=True)  34.5 us
    ppermute x17, starting transfers between devices, shift(): return lax.ppermute(a, axis, [(i, (i + d) % 4) for i in range(4)])  26.6 us
    pallas_call x2, Pallas kernels, grams(): pl.pallas_call(late_kernel if late else early_kernel, out_shape=shapes, i...  14.2 us
    pallas_call x1, Pallas kernels, place(): pl.pallas_call(place_kernel, grid=(CAP,), out_shape=jax.ShapeDtypeStruct(...  4.24 us
    pallas_call x1, Pallas kernels, route(): pl.pallas_call(route_kernel, out_shape=jax.ShapeDtypeStruct((index.shape[...  3.69 us
  transfers between devices with their start and end apart: 22, of which 13 were waited for; matrix products, arithmetic and copies ran while one was open for 2% of the time, Pallas kernels for 4%

profile of v3, /device:TPU:1, one launch (start us, length us, event | category | flops | bytes accessed | tf_op | source)
XLA Modules:
  0.0 177.1 jit_solution(7968446243933052232)
XLA Ops:
  0.0 1.8 %copy.7.dens = bf16[256,3000]{1,0:T(8,128)(2,1)S(1)} copy(bf16[256,3000]{0,1:T(8,128)(2,1)} %param.4) | data formatting | bytes 3072000 | tf_op args[0]
  2.8 4.5 %collective-permute-start = (bf16[128,3072]{1,0:T(8,128)(2,1)S(1)}, bf16[128,3072]{1,0:T(8,128)(2,1)S(1)}, u32[]{:S(2)}, u32[]{:S(2)}) collective-permute-start(bf16[128,3072]{1,0:T(8,128)(2,1)S(1)} %get-tuple-element.33), channel_id=1, source_target_pairs={{0,16},{8,24},{16,0},{24,8},{1,17},{9,25},{17,1},{25,9},{2,18},{10... | collective-permute-start | bytes 2359304 | tf_op jit(solution)/shard_map/ppermute | solution.py:18
  7.3 2.5 %collective-permute-start.1 = (bf16[1,64,3072]{2,1,0:T(8,128)(2,1)S(1)}, bf16[1,64,3072]{2,1,0:T(8,128)(2,1)S(1)}, u32[]{:S(2)}, u32[]{:S(2)}) collective-permute-start(bf16[1,64,3072]{2,1,0:T(8,128)(2,1)S(1)} %get-tuple-element.34), channel_id=1, source_target_pairs={{0,96},{32,0},{64,32},{96,64},{1,97},{33,1},{65,33},{97,65},{2,98}... | collective-permute-start | bytes 1179656 | tf_op jit(solution)/shard_map/ppermute | solution.py:18
  10.9 7.1 %collective-permute-done.1 = bf16[1,64,3072]{2,1,0:T(8,128)(2,1)S(1)} collective-permute-done((bf16[1,64,3072]{2,1,0:T(8,128)(2,1)S(1)}, bf16[1,64,3072]{2,1,0:T(8,128)(2,1)S(1)}, u32[]{:S(2)}, u32[]{:S(2)}) %collective-permute-start.1) | collective-permute-done | bytes 393248 | tf_op jit(solution)/shard_map/ppermute | solution.py:18
  18.1 2.7 %collective-permute-done.2 = bf16[1,64,3072]{2,1,0:T(8,128)(2,1)S(1)} collective-permute-done((bf16[1,64,3072]{2,1,0:T(8,128)(2,1)S(1)}, bf16[1,64,3072]{2,1,0:T(8,128)(2,1)S(1)}, u32[]{:S(2)}, u32[]{:S(2)}) %collective-permute-start.2) | collective-permute-done | bytes 393248 | tf_op jit(solution)/shard_map/ppermute | solution.py:18
  20.7 10.1 %collective-permute-done.3 = bf16[1,64,3072]{2,1,0:T(8,128)(2,1)S(1)} collective-permute-done((bf16[1,64,3072]{2,1,0:T(8,128)(2,1)S(1)}, bf16[1,64,3072]{2,1,0:T(8,128)(2,1)S(1)}, u32[]{:S(2)}, u32[]{:S(2)}) %collective-permute-start.3) | collective-permute-done | bytes 393248 | tf_op jit(solution)/shard_map/ppermute | solution.py:18
  31.0 2.7 %collective-permute-start.5 = (bf16[128,3072]{1,0:T(8,128)(2,1)S(1)}, bf16[128,3072]{1,0:T(8,128)(2,1)S(1)}, u32[]{:S(2)}, u32[]{:S(2)}) collective-permute-start(bf16[128,3072]{1,0:T(8,128)(2,1)S(1)} %get-tuple-element.43.refs_6_), channel_id=1, source_target_pairs={{0,96},{32,0},{64,32},{96,64},{1,97},{33,1},{65,33},{97,65},{2,98}... | collective-permute-start | bytes 2359304 | tf_op jit(solution)/shard_map/ppermute | solution.py:18
  35.5 1.9 %collective-permute-start.9 = (bf16[4,64,3072]{2,1,0:T(8,128)(2,1)S(1)}, bf16[4,64,3072]{2,1,0:T(8,128)(2,1)S(1)}, u32[]{:S(2)}, u32[]{:S(2)}) collective-permute-start(bf16[4,64,3072]{2,1,0:T(8,128)(2,1)S(1)} %pad_maximum_fusion.refs_0_), channel_id=1, source_target_pairs={{0,24},{8,0},{16,8},{24,16},{1,25},{9,1},{17,9},{25,17},{2,26},{10... | collective-permute-start | bytes 4718600 | tf_op jit(solution)/shard_map/ppermute | solution.py:18
  37.4 13.4 %collective-permute-done.4.refs_8_ = bf16[128,3072]{1,0:T(8,128)(2,1)S(1)} collective-permute-done((bf16[128,3072]{1,0:T(8,128)(2,1)S(1)}, bf16[128,3072]{1,0:T(8,128)(2,1)S(1)}, u32[]{:S(2)}, u32[]{:S(2)}) %collective-permute-start.4) | collective-permute-done | bytes 786464 | tf_op jit(solution)/shard_map/ppermute | solution.py:18
  50.9 2.7 %collective-permute-start.7 = (bf16[128,3072]{1,0:T(8,128)(2,1)S(1)}, bf16[128,3072]{1,0:T(8,128)(2,1)S(1)}, u32[]{:S(2)}, u32[]{:S(2)}) collective-permute-start(bf16[128,3072]{1,0:T(8,128)(2,1)S(1)} %collective-permute-done.refs_9_), channel_id=1, source_target_pairs={{0,96},{32,0},{64,32},{96,64},{1,97},{33,1},{65,33},{97,65},{2,98}... | collective-permute-start | bytes 2359304 | tf_op jit(solution)/shard_map/ppermute | solution.py:18
  53.5 16.2 %collective-permute-done.6.refs_11_ = bf16[128,3072]{1,0:T(8,128)(2,1)S(1)} collective-permute-done((bf16[128,3072]{1,0:T(8,128)(2,1)S(1)}, bf16[128,3072]{1,0:T(8,128)(2,1)S(1)}, u32[]{:S(2)}, u32[]{:S(2)}) %collective-permute-start.6) | collective-permute-done | bytes 786464 | tf_op jit(solution)/shard_map/ppermute | solution.py:18
  69.8 2.2 %collective-permute-done.8.refs_2_ = bf16[4,64,3072]{2,1,0:T(8,128)(2,1)S(1)} collective-permute-done((bf16[4,64,3072]{2,1,0:T(8,128)(2,1)S(1)}, bf16[4,64,3072]{2,1,0:T(8,128)(2,1)S(1)}, u32[]{:S(2)}, u32[]{:S(2)}) %collective-permute-start.8) | collective-permute-done | bytes 1572896 | tf_op jit(solution)/shard_map/ppermute | solution.py:18
  73.1 2.6 %collective-permute-start.14 = (bf16[2,64,3072]{2,1,0:T(8,128)(2,1)S(1)}, bf16[2,64,3072]{2,1,0:T(8,128)(2,1)S(1)}, u32[]{:S(2)}, u32[]{:S(2)}) collective-permute-start(bf16[2,64,3072]{2,1,0:T(8,128)(2,1)S(1)} %slice.15), channel_id=1, source_target_pairs={{0,24},{8,0},{16,8},{24,16},{1,25},{9,1},{17,9},{25,17},{2,26},{10... | collective-permute-start | bytes 2359304 | tf_op jit(solution)/shard_map/ppermute | solution.py:18
  75.8 2.6 %collective-permute-start.18 = (bf16[128,3072]{1,0:T(8,128)(2,1)S(1)}, bf16[128,3072]{1,0:T(8,128)(2,1)S(1)}, u32[]{:S(2)}, u32[]{:S(2)}) collective-permute-start(bf16[128,3072]{1,0:T(8,128)(2,1)S(1)} %collective-permute-done.7.refs_10_), channel_id=1, source_target_pairs={{0,96},{32,0},{64,32},{96,64},{1,97},{33,1},{65,33},{97,65},{2,98}... | collective-permute-start | bytes 2359304 | tf_op jit(solution)/shard_map/ppermute | solution.py:18
  78.4 6.5 %early_grams.1.refs_18_ = f32[4,37,64,128]{3,2,1,0:T(8,128)S(1)} custom-call(s32[4]{0:T(128)S(1)} %pad_add_fusion.meta, bf16[4,64,3072]{2,1,0:T(8,128)(2,1)S(1)} %pad_maximum_fusion.refs_0_, bf16[4,64,3072]{2,1,0:T(8,128)(2,1)S(1)} %collective-permute-done.9.refs_1_, bf16[4,64,3072]{2,1,0:T(8,128)(2,1)S(1)} %collective-permute-done.8.refs_2_, ...), custom_call_target="tpu_custom_call" | custom-call | flops 4831838208 | bytes 20971520 | tf_op jit(solution)/shard_map/early_grams/pallas_call | solution.py:108
  85.0 7.8 %collective-permute-done.13.refs_12_ = bf16[2,64,3072]{2,1,0:T(8,128)(2,1)S(1)} collective-permute-done((bf16[2,64,3072]{2,1,0:T(8,128)(2,1)S(1)}, bf16[2,64,3072]{2,1,0:T(8,128)(2,1)S(1)}, u32[]{:S(2)}, u32[]{:S(2)}) %collective-permute-start.13) | collective-permute-done | bytes 786464 | tf_op jit(solution)/shard_map/ppermute | solution.py:18
  97.2 7.7 %late_grams.1 = (f32[36,64,128]{2,1,0:T(8,128)S(1)}, bf16[36,64,128]{2,1,0:T(8,128)(2,1)}, bf16[36,64,128]{2,1,0:T(8,128)(2,1)}, bf16[36,64,128]{2,1,0:T(8,128)(2,1)S(1)}, f32[4,37,64,128]{3,2,1,0:T(8,128)S(1)}) custom-call(s32[4]{0:T(128)S(1)} %pad_add_fusion.meta, ...), custom_call_target="tpu_custom_call", output_to_operand_aliasing={{4}: (19, {})} | custom-call | flops 4831838208 | bytes 20971520 | tf_op jit(solution)/shard_map/late_grams/pallas_call | solution.py:108
  106.2 2.6 %collective-permute-start.20 = (bf16[36,64,128]{2,1,0:T(8,128)(2,1)}, bf16[36,64,128]{2,1,0:T(8,128)(2,1)S(1)}, u32[]{:S(2)}, u32[]{:S(2)}) collective-permute-start(bf16[36,64,128]{2,1,0:T(8,128)(2,1)} %get-tuple-element.57), channel_id=1, source_target_pairs={{0,2},{1,3},{2,0},{3,1},{4,6},{5,7},{6,4},{7,5},{8,10},{9,11},{10,... | collective-permute-start | bytes 1769480 | tf_op jit(solution)/shard_map/ppermute | solution.py:18
  110.6 1.4 reduce_window_sum.11
  113.1 7.9 %collective-permute-done.19.a = bf16[36,64,128]{2,1,0:T(8,128)(2,1)S(1)} collective-permute-done((bf16[36,64,128]{2,1,0:T(8,128)(2,1)}, bf16[36,64,128]{2,1,0:T(8,128)(2,1)S(1)}, u32[]{:S(2)}, u32[]{:S(2)}) %collective-permute-start.19) | collective-permute-done | bytes 589856 | tf_op jit(solution)/shard_map/ppermute | solution.py:18
  121.0 13.7 %collective-permute-done.20.b = bf16[36,64,128]{2,1,0:T(8,128)(2,1)S(1)} collective-permute-done((bf16[36,64,128]{2,1,0:T(8,128)(2,1)}, bf16[36,64,128]{2,1,0:T(8,128)(2,1)S(1)}, u32[]{:S(2)}, u32[]{:S(2)}) %collective-permute-start.20) | collective-permute-done | bytes 589856 | tf_op jit(solution)/shard_map/ppermute | solution.py:18
  134.7 3.7 %route.1 = bf16[128,64,128]{2,1,0:T(8,128)(2,1)S(1)} custom-call(s32[128]{0:T(128)S(1)} %get-tuple-element.60.index, s32[128]{0:T(128)S(1)} %get-tuple-element.59.valid, f32[36,64,128]{2,1,0:T(8,128)S(1)} %get-tuple-element.55.own, bf16[36,64,128]{2,1,0:T(8,128)(2,1)S(1)} %collective-permute-done.19.a, bf16[36,64,128]{2,1,0:T(8,128)(2,1)S(1)} %collective-permute-done.20.b, ...), custom_call_target="tpu_custom_call" | custom-call | tf_op jit(solution)/shard_map/route/pallas_call | solution.py:175
  138.4 34.5 %all_to_all.5.got = bf16[32,4,64,128]{3,2,1,0:T(8,128)(2,1)} all-to-all(bf16[32,4,64,128]{3,2,1,0:T(8,128)(2,1)S(1)} %bitcast.14), channel_id=1, replica_groups=mesh['x'=4,'z'=4,'c'=2,'y'=4] {'x','z','c'}, dimensions={0} | all-to-all | bytes 4194304 | tf_op jit(solution)/shard_map/all_to_all | solution.py:251
  172.9 4.2 %place.1 = f32[4,256,1024]{2,1,0:T(8,128)} custom-call(bf16[32,4,64,128]{3,2,1,0:T(8,128)(2,1)} %all_to_all.5.got), custom_call_target="tpu_custom_call" | custom-call | tf_op jit(solution)/shard_map/place/pallas_call | solution.py:196
  (42 shorter events, 13.9 us)
Async XLA Ops:
  2.8 28.0 %collective-permute-start = (bf16[128,3072]{1,0:T(8,128)(2,1)S(1)}, bf16[128,3072]{1,0:T(8,128)(2,1)S(1)}, u32[]{:S(2)}, u32[]{:S(2)}) collective-permute-start(bf16[128,3072]{1,0:T(8,128)(2,1)S(1)} %get-tuple-element.33), channel_id=1, source_target_pairs={{0,16},{8,24},{16,0},{24,8},{1,17},{9,25},{17,1},{25,9},{2,18},{10... | collective-permute-start | bytes 2359304 | tf_op jit(solution)/shard_map/ppermute | solution.py:18
  7.3 10.7 %collective-permute-start.1 = (bf16[1,64,3072]{2,1,0:T(8,128)(2,1)S(1)}, bf16[1,64,3072]{2,1,0:T(8,128)(2,1)S(1)}, u32[]{:S(2)}, u32[]{:S(2)}) collective-permute-start(bf16[1,64,3072]{2,1,0:T(8,128)(2,1)S(1)} %get-tuple-element.34), channel_id=1, source_target_pairs={{0,96},{32,0},{64,32},{96,64},{1,97},{33,1},{65,33},{97,65},{2,98}... | collective-permute-start | bytes 1179656 | tf_op jit(solution)/shard_map/ppermute | solution.py:18
  9.8 10.9 %collective-permute-start.2 = (bf16[1,64,3072]{2,1,0:T(8,128)(2,1)S(1)}, bf16[1,64,3072]{2,1,0:T(8,128)(2,1)S(1)}, u32[]{:S(2)}, u32[]{:S(2)}) collective-permute-start(bf16[1,64,3072]{2,1,0:T(8,128)(2,1)S(1)} %get-tuple-element.35), channel_id=1, source_target_pairs={{0,64},{32,96},{64,0},{96,32},{1,65},{33,97},{65,1},{97,33},{2,66}... | collective-permute-start | bytes 1179656 | tf_op jit(solution)/shard_map/ppermute | solution.py:18
  10.3 20.4 %collective-permute-start.3 = (bf16[1,64,3072]{2,1,0:T(8,128)(2,1)S(1)}, bf16[1,64,3072]{2,1,0:T(8,128)(2,1)S(1)}, u32[]{:S(2)}, u32[]{:S(2)}) collective-permute-start(bf16[1,64,3072]{2,1,0:T(8,128)(2,1)S(1)} %get-tuple-element.36), channel_id=1, source_target_pairs={{0,32},{32,64},{64,96},{96,0},{1,33},{33,65},{65,97},{97,1},{2,34}... | collective-permute-start | bytes 1179656 | tf_op jit(solution)/shard_map/ppermute | solution.py:18
  31.0 19.9 %collective-permute-start.4 = (bf16[128,3072]{1,0:T(8,128)(2,1)S(1)}, bf16[128,3072]{1,0:T(8,128)(2,1)S(1)}, u32[]{:S(2)}, u32[]{:S(2)}) collective-permute-start(bf16[128,3072]{1,0:T(8,128)(2,1)S(1)} %get-tuple-element.43.refs_6_), channel_id=1, source_target_pairs={{0,32},{32,64},{64,96},{96,0},{1,33},{33,65},{65,97},{97,1},{2,34}... | collective-permute-start | bytes 2359304 | tf_op jit(solution)/shard_map/ppermute | solution.py:18
  31.0 19.8 %collective-permute-start.5 = (bf16[128,3072]{1,0:T(8,128)(2,1)S(1)}, bf16[128,3072]{1,0:T(8,128)(2,1)S(1)}, u32[]{:S(2)}, u32[]{:S(2)}) collective-permute-start(bf16[128,3072]{1,0:T(8,128)(2,1)S(1)} %get-tuple-element.43.refs_6_), channel_id=1, source_target_pairs={{0,96},{32,0},{64,32},{96,64},{1,97},{33,1},{65,33},{97,65},{2,98}... | collective-permute-start | bytes 2359304 | tf_op jit(solution)/shard_map/ppermute | solution.py:18
  33.7 36.1 %collective-permute-start.10 = (bf16[4,64,3072]{2,1,0:T(8,128)(2,1)S(1)}, bf16[4,64,3072]{2,1,0:T(8,128)(2,1)S(1)}, u32[]{:S(2)}, u32[]{:S(2)}) collective-permute-start(bf16[4,64,3072]{2,1,0:T(8,128)(2,1)S(1)} %pad_maximum_fusion.refs_0_), channel_id=1, source_target_pairs={{0,4},{4,0},{1,5},{5,1},{2,6},{6,2},{3,7},{7,3},{8,12},{12,8},{9,1... | collective-permute-start | bytes 4718600 | tf_op jit(solution)/shard_map/ppermute | solution.py:222
  34.8 37.2 %collective-permute-start.8 = (bf16[4,64,3072]{2,1,0:T(8,128)(2,1)S(1)}, bf16[4,64,3072]{2,1,0:T(8,128)(2,1)S(1)}, u32[]{:S(2)}, u32[]{:S(2)}) collective-permute-start(bf16[4,64,3072]{2,1,0:T(8,128)(2,1)S(1)} %pad_maximum_fusion.refs_0_), channel_id=1, source_target_pairs={{0,8},{8,16},{16,24},{24,0},{1,9},{9,17},{17,25},{25,1},{2,10},{10... | collective-permute-start | bytes 4718600 | tf_op jit(solution)/shard_map/ppermute | solution.py:18
  35.5 36.5 %collective-permute-start.9 = (bf16[4,64,3072]{2,1,0:T(8,128)(2,1)S(1)}, bf16[4,64,3072]{2,1,0:T(8,128)(2,1)S(1)}, u32[]{:S(2)}, u32[]{:S(2)}) collective-permute-start(bf16[4,64,3072]{2,1,0:T(8,128)(2,1)S(1)} %pad_maximum_fusion.refs_0_), channel_id=1, source_target_pairs={{0,24},{8,0},{16,8},{24,16},{1,25},{9,1},{17,9},{25,17},{2,26},{10... | collective-permute-start | bytes 4718600 | tf_op jit(solution)/shard_map/ppermute | solution.py:18
  50.9 18.9 %collective-permute-start.6 = (bf16[128,3072]{1,0:T(8,128)(2,1)S(1)}, bf16[128,3072]{1,0:T(8,128)(2,1)S(1)}, u32[]{:S(2)}, u32[]{:S(2)}) collective-permute-start(bf16[128,3072]{1,0:T(8,128)(2,1)S(1)} %collective-permute-done.refs_9_), channel_id=1, source_target_pairs={{0,32},{32,64},{64,96},{96,0},{1,33},{33,65},{65,97},{97,1},{2,34}... | collective-permute-start | bytes 2359304 | tf_op jit(solution)/shard_map/ppermute | solution.py:18
  50.9 18.9 %collective-permute-start.7 = (bf16[128,3072]{1,0:T(8,128)(2,1)S(1)}, bf16[128,3072]{1,0:T(8,128)(2,1)S(1)}, u32[]{:S(2)}, u32[]{:S(2)}) collective-permute-start(bf16[128,3072]{1,0:T(8,128)(2,1)S(1)} %collective-permute-done.refs_9_), channel_id=1, source_target_pairs={{0,96},{32,0},{64,32},{96,64},{1,97},{33,1},{65,33},{97,65},{2,98}... | collective-permute-start | bytes 2359304 | tf_op jit(solution)/shard_map/ppermute | solution.py:18
  72.0 3.8 %collective-permute-start.11 = (bf16[4,64,3072]{2,1,0:T(8,128)(2,1)S(1)}, bf16[4,64,3072]{2,1,0:T(8,128)(2,1)S(1)}, u32[]{:S(2)}, u32[]{:S(2)}) collective-permute-start(bf16[4,64,3072]{2,1,0:T(8,128)(2,1)S(1)} %collective-permute-done.9.refs_1_), channel_id=1, source_target_pairs={{0,4},{4,0},{1,5},{5,1},{2,6},{6,2},{3,7},{7,3},{8,12},{12,8},{9,1... | collective-permute-start | bytes 4718600 | tf_op jit(solution)/shard_map/ppermute | solution.py:229
  72.8 5.6 %collective-permute-start.12 = (bf16[4,64,3072]{2,1,0:T(8,128)(2,1)S(1)}, bf16[4,64,3072]{2,1,0:T(8,128)(2,1)S(1)}, u32[]{:S(2)}, u32[]{:S(2)}) collective-permute-start(bf16[4,64,3072]{2,1,0:T(8,128)(2,1)S(1)} %collective-permute-done.8.refs_2_), channel_id=1, source_target_pairs={{0,4},{4,0},{1,5},{5,1},{2,6},{6,2},{3,7},{7,3},{8,12},{12,8},{9,1... | collective-permute-start | bytes 4718600 | tf_op jit(solution)/shard_map/ppermute | solution.py:229
  72.9 19.9 %collective-permute-start.13 = (bf16[2,64,3072]{2,1,0:T(8,128)(2,1)S(1)}, bf16[2,64,3072]{2,1,0:T(8,128)(2,1)S(1)}, u32[]{:S(2)}, u32[]{:S(2)}) collective-permute-start(bf16[2,64,3072]{2,1,0:T(8,128)(2,1)S(1)} %slice.14), channel_id=1, source_target_pairs={{0,8},{8,16},{16,24},{24,0},{1,9},{9,17},{17,25},{25,1},{2,10},{10... | collective-permute-start | bytes 2359304 | tf_op jit(solution)/shard_map/ppermute | solution.py:18
  73.1 19.6 %collective-permute-start.14 = (bf16[2,64,3072]{2,1,0:T(8,128)(2,1)S(1)}, bf16[2,64,3072]{2,1,0:T(8,128)(2,1)S(1)}, u32[]{:S(2)}, u32[]{:S(2)}) collective-permute-start(bf16[2,64,3072]{2,1,0:T(8,128)(2,1)S(1)} %slice.15), channel_id=1, source_target_pairs={{0,24},{8,0},{16,8},{24,16},{1,25},{9,1},{17,9},{25,17},{2,26},{10... | collective-permute-start | bytes 2359304 | tf_op jit(solution)/shard_map/ppermute | solution.py:18
  75.7 19.3 %collective-permute-start.17 = (bf16[128,3072]{1,0:T(8,128)(2,1)S(1)}, bf16[128,3072]{1,0:T(8,128)(2,1)S(1)}, u32[]{:S(2)}, u32[]{:S(2)}) collective-permute-start(bf16[128,3072]{1,0:T(8,128)(2,1)S(1)} %collective-permute-done.4.refs_8_), channel_id=1, source_target_pairs={{0,32},{32,64},{64,96},{96,0},{1,33},{33,65},{65,97},{97,1},{2,34}... | collective-permute-start | bytes 2359304 | tf_op jit(solution)/shard_map/ppermute | solution.py:18
  75.8 19.2 %collective-permute-start.18 = (bf16[128,3072]{1,0:T(8,128)(2,1)S(1)}, bf16[128,3072]{1,0:T(8,128)(2,1)S(1)}, u32[]{:S(2)}, u32[]{:S(2)}) collective-permute-start(bf16[128,3072]{1,0:T(8,128)(2,1)S(1)} %collective-permute-done.7.refs_10_), channel_id=1, source_target_pairs={{0,96},{32,0},{64,32},{96,64},{1,97},{33,1},{65,33},{97,65},{2,98}... | collective-permute-start | bytes 2359304 | tf_op jit(solution)/shard_map/ppermute | solution.py:18
  84.9 25.0 %copy-start.1 = (s32[64,1]{0,1:T(1,128)S(1)}, s32[64,1]{0,1:T(1,128)}, u32[]{:S(2)}) copy-start(s32[64,1]{0,1:T(1,128)} %param.7) | copy-start | bytes 772
  84.9 28.0 %copy-start.2 = (s32[64,2]{0,1:T(2,128)S(1)}, s32[64,2]{0,1:T(2,128)}, u32[]{:S(2)}) copy-start(s32[64,2]{0,1:T(2,128)} %param.6) | copy-start | bytes 1540
  92.8 3.3 %collective-permute-start.15 = (bf16[2,64,3072]{2,1,0:T(8,128)(2,1)S(1)}, bf16[2,64,3072]{2,1,0:T(8,128)(2,1)S(1)}, u32[]{:S(2)}, u32[]{:S(2)}) collective-permute-start(bf16[2,64,3072]{2,1,0:T(8,128)(2,1)S(1)} %collective-permute-done.13.refs_12_), channel_id=1, source_target_pairs={{0,4},{4,0},{1,5},{5,1},{2,6},{6,2},{3,7},{7,3},{8,12},{12,8},{9,1... | collective-permute-start | bytes 2359304 | tf_op jit(solution)/shard_map/ppermute | solution.py:234
  94.2 3.0 %collective-permute-start.16 = (bf16[2,64,3072]{2,1,0:T(8,128)(2,1)S(1)}, bf16[2,64,3072]{2,1,0:T(8,128)(2,1)S(1)}, u32[]{:S(2)}, u32[]{:S(2)}) collective-permute-start(bf16[2,64,3072]{2,1,0:T(8,128)(2,1)S(1)} %collective-permute-done.14.refs_13_), channel_id=1, source_target_pairs={{0,4},{4,0},{1,5},{5,1},{2,6},{6,2},{3,7},{7,3},{8,12},{12,8},{9,1... | collective-permute-start | bytes 2359304 | tf_op jit(solution)/shard_map/ppermute | solution.py:234
  104.9 16.1 %collective-permute-start.19 = (bf16[36,64,128]{2,1,0:T(8,128)(2,1)}, bf16[36,64,128]{2,1,0:T(8,128)(2,1)S(1)}, u32[]{:S(2)}, u32[]{:S(2)}) collective-permute-start(bf16[36,64,128]{2,1,0:T(8,128)(2,1)} %get-tuple-element.56), channel_id=1, source_target_pairs={{0,1},{1,2},{2,3},{3,0},{4,5},{5,6},{6,7},{7,4},{8,9},{9,10},{10,1... | collective-permute-start | bytes 1769480 | tf_op jit(solution)/shard_map/ppermute | solution.py:18
  106.2 28.5 %collective-permute-start.20 = (bf16[36,64,128]{2,1,0:T(8,128)(2,1)}, bf16[36,64,128]{2,1,0:T(8,128)(2,1)S(1)}, u32[]{:S(2)}, u32[]{:S(2)}) collective-permute-start(bf16[36,64,128]{2,1,0:T(8,128)(2,1)} %get-tuple-element.57), channel_id=1, source_target_pairs={{0,2},{1,3},{2,0},{3,1},{4,6},{5,7},{6,4},{7,5},{8,10},{9,11},{10,... | collective-permute-start | bytes 1769480 | tf_op jit(solution)/shard_map/ppermute | solution.py:18
  108.8 25.9 %collective-permute-start.21 = (bf16[36,64,128]{2,1,0:T(8,128)(2,1)S(1)}, bf16[36,64,128]{2,1,0:T(8,128)(2,1)S(1)}, u32[]{:S(2)}, u32[]{:S(2)}) collective-permute-start(bf16[36,64,128]{2,1,0:T(8,128)(2,1)S(1)} %get-tuple-element.58), channel_id=1, source_target_pairs={{0,3},{1,0},{2,1},{3,2},{4,7},{5,4},{6,5},{7,6},{8,11},{9,8},{10,9... | collective-permute-start | bytes 1769480 | tf_op jit(solution)/shard_map/ppermute | solution.py:18
  (1 other events, 1.9 us)

commit v4 on v3

v4 whole, which is shorter than its diff:
```python
import jax
import jax.numpy as jnp
from jax import lax
from jax.experimental import pallas as pl
from jax.experimental.pallas import tpu as pltpu
from jax.sharding import Mesh
from jax.sharding import PartitionSpec as P

TILES = 8
CAP = 4
NP = TILES * (TILES + 1) // 2
BF = jnp.bfloat16
F32 = jnp.float32
MIB = 1 << 20


def shift(a, axis, d):
    return lax.ppermute(a, axis, [(i, (i + d) % 4) for i in range(4)])


def tie(*arrays):
    return lax.optimization_barrier(arrays)


EARLY_L = [(dc, dz) for dc in range(2) for dz in (0, 1, 3)]
LATE_L = [(dc, 2) for dc in range(2)]


def product(lefts, rights):
    return lax.dot_general(
        jnp.concatenate(lefts, 0),
        jnp.concatenate(rights, 0),
        (((1,), (1,)), ((), ())),
        preferred_element_type=F32,
    )


def store(meta, sums, out, ip, jp, sources, row):
    z, c, y = meta[1], meta[2], meta[3]
    for n, (dc, dz) in enumerate(sources):
        zz, cc = (z + dz) % 4, (c + dc) % 2
        i = 2 * ip + zz // 2
        dy = (2 * (zz % 2) + cc - y + 4) % 4
        for half in range(2):
            j = 2 * jp + (z // 2 + half) % 2
            at = jnp.where(i <= j, j * (j + 1) // 2 + i, NP)
            sums[dy, at] = out[row + 64 * n : row + 64 * n + 64, 128 * half : 128 * half + 128]


def early_kernel(meta, *refs):
    lefts, rights, sums = refs[:6], refs[6:9], refs[9]
    x = meta[0]
    for n, dx in enumerate((0, 1, 3)):
        near_step(meta, lefts, [rights[n]], (x + dx) % 4, sums)


def near_step(meta, lefts, right, jp, sums):
    x = meta[0]

    def step(k, _):
        ip = (x + k) % 4

        @pl.when(ip <= jp)
        def _():
            out = product([ref[k] for ref in lefts], [ref[...] for ref in right])
            store(meta, sums, out, ip, jp, EARLY_L, 0)

        return 0

    lax.fori_loop(0, 4, step, 0)


def middle_kernel(meta, *refs):
    near_step(meta, refs[:6], refs[6:8], (meta[0] + 2) % 4, refs[9])


def late_kernel(meta, *refs):
    late, rights = refs[:4], [refs[4:5], refs[5:6], refs[7:9], refs[6:7]]
    s1, s2, s3, sums = refs[10:14]
    x = meta[0]
    rows = [late[2 * dc + k // 2][k % 2] for k in range(4) for dc in range(2)]
    for dx, right in enumerate(rights):
        jp = (x + dx) % 4
        out = product(rows, [ref[...] for ref in right])
        for k in range(4):
            store(meta, sums, out, (x + k) % 4, jp, LATE_L, 128 * k)
    for k, ref in enumerate((s1, s2, s3)):
        ref[...] = sums[k + 1, :NP].astype(BF)


def grams(kernel, meta, given, sums=None, parts=False):
    width = given[0].shape[-1]
    smem = pl.BlockSpec(memory_space=pltpu.SMEM)
    vmem = pl.BlockSpec(memory_space=pltpu.VMEM)
    shapes = [jax.ShapeDtypeStruct((NP, 64, 128), BF)] * 3 if parts else []
    shapes += [jax.ShapeDtypeStruct((4, NP + 1, 64, 128), F32)]
    aliases = {}
    if sums is not None:
        given = [*given, sums]
        aliases = {len(given): len(shapes) - 1}
    return pl.pallas_call(
        kernel,
        out_shape=shapes,
        in_specs=[smem] + [vmem] * len(given),
        out_specs=[vmem] * len(shapes),
        input_output_aliases=aliases,
        compiler_params=pltpu.CompilerParams(vmem_limit_bytes=16 * MIB),
        cost_estimate=pl.CostEstimate(
            flops=2 * 4 * 512 * 256 * width, bytes_accessed=16 * MIB, transcendentals=0
        ),
        name=kernel.__name__,
    )(meta, *given)


def prepare_kernel(meta, dens, weights, keep, send, *parts):
    k, width = dens.shape[1], keep.shape[1]
    x, z1 = meta[0], meta[1] // 2
    edge = k // 128 * 128
    for ref in (keep, send):
        ref[:, edge:] = jnp.zeros((128, width - edge), BF)
    keep[:, :k] = dens[pl.ds(pl.multiple_of(z1 * 128, 128), 128), :]
    send[:, :k] = dens[pl.ds(pl.multiple_of((1 - z1) * 128, 128), 128), :]
    for d, ref in enumerate(parts):
        ref[0, :, edge:] = jnp.zeros((64, width - edge), BF)
        for h in range(2):
            row = pl.multiple_of(h * 128 + (x + d) % 4 * 32, 32)
            part = dens[pl.ds(row, 32), :].astype(F32) * weights[...]
            ref[0, 32 * h : 32 * h + 32, :k] = part.astype(BF)


def prepare(meta, dens, weights, width):
    smem = pl.BlockSpec(memory_space=pltpu.SMEM)
    vmem = pl.BlockSpec(memory_space=pltpu.VMEM)
    shapes = [jax.ShapeDtypeStruct((128, width), BF)] * 2
    shapes += [jax.ShapeDtypeStruct((1, 64, width), BF)] * 4
    return pl.pallas_call(
        prepare_kernel,
        out_shape=shapes,
        in_specs=[smem, vmem, vmem],
        out_specs=[vmem] * 6,
        compiler_params=pltpu.CompilerParams(vmem_limit_bytes=16 * MIB),
        name="prepare",
    )(meta, dens, weights)


def route_kernel(index, sums, a, b, c, out, total):
    total[:NP] = (
        sums[0, :NP] + a[...].astype(F32) + b[...].astype(F32) + c[...].astype(F32)
    ).astype(BF)
    total[NP] = jnp.zeros(total.shape[1:], BF)

    def some(k, _):
        for n in range(8):
            out[8 * k + n] = total[index[8 * k + n]]
        return 0

    lax.fori_loop(0, out.shape[0] // 8, some, 0)


def route(index, sums, parts):
    smem = pl.BlockSpec(memory_space=pltpu.SMEM)
    vmem = pl.BlockSpec(memory_space=pltpu.VMEM)
    return pl.pallas_call(
        route_kernel,
        out_shape=jax.ShapeDtypeStruct((index.shape[0], 64, 128), BF),
        in_specs=[smem] + [vmem] * 4,
        out_specs=vmem,
        scratch_shapes=[pltpu.VMEM((NP + 1, 64, 128), BF)],
        compiler_params=pltpu.CompilerParams(vmem_limit_bytes=16 * MIB),
        name="route",
    )(index, sums, *parts)


def place_kernel(got, out):
    for src in range(32):
        x, z1, z0, c = src // 8, (src // 4) % 2, (src // 2) % 2, src % 2
        col = (4 * z0 + 2 * c + z1) * 128
        out[0, 32 * x : 32 * x + 32, col : col + 128] = got[src, 0].astype(F32)


def place(got):
    return pl.pallas_call(
        place_kernel,
        grid=(CAP, 2),
        out_shape=jax.ShapeDtypeStruct((CAP, 256, 1024), F32),
        in_specs=[pl.BlockSpec((32, 1, 32, 128), lambda s, h: (0, s, h, 0))],
        out_specs=pl.BlockSpec((1, 128, 1024), lambda s, h: (s, h, 0)),
        name="place",
    )(got)


def on_device(densities, coulomb, pair_list, owner):
    x, z, c, y = (lax.axis_index(n) for n in ("x", "z", "c", "y"))
    k = densities.shape[1]
    meta = jnp.stack([x, z, c, y]).astype(jnp.int32)
    keep, send, *mine = prepare(meta, densities, coulomb[None, :], -(-k // 128) * 128)
    got = shift(send, "z", 2)
    other = [(0, 1), (1, 0)]
    got, e1, e2, e3 = tie(
        got, shift(mine[3], "x", 3), shift(mine[2], "x", 2), shift(mine[1], "x", 1)
    )
    right = jnp.concatenate([keep, got], 0)
    left = jnp.concatenate([mine[0], e1, e2, e3], 0)
    right, left = tie(right, left)

    left3, left1 = shift(left, "z", 1), shift(left, "z", -1)
    right3, right1 = shift(right, "x", 1), shift(right, "x", -1)
    swap0 = lax.ppermute(left, "c", other)
    right3, right1, left3, left1, swap0 = tie(right3, right1, left3, left1, swap0)

    left2a, left2b = shift(left3[:2], "z", 1), shift(left1[2:], "z", -1)
    right2a, right2b = shift(right3[:128], "x", 1), shift(right1[128:], "x", -1)
    swap1, swap3 = lax.ppermute(left1, "c", other), lax.ppermute(left3, "c", other)
    lefts = [left, left1, left3, swap0, swap1, swap3]
    rights = [right, right1, right3]
    (sums,) = grams(early_kernel, meta, lefts + rights)
    left2a, left2b, sums = tie(left2a, left2b, sums)
    swap2a, swap2b = lax.ppermute(left2a, "c", other), lax.ppermute(left2b, "c", other)
    far = [right2a, right2b]
    (sums,) = grams(middle_kernel, meta, lefts + far, sums)
    late = [left2a, left2b, swap2a, swap2b]
    s1, s2, s3, sums = grams(late_kernel, meta, late + rights + far, sums, True)
    parts = [shift(s1, "y", 1), shift(s2, "y", 2), shift(s3, "y", 3)]

    owners = 32
    owner_ids = owner[:, 0]
    onehot = (owner_ids[:, None] == jnp.arange(owners, dtype=jnp.int32)[None, :]).astype(jnp.int32)
    rank = jnp.sum((jnp.cumsum(onehot, 0) - onehot) * onehot, 1)
    slot = owner_ids * CAP + rank
    match = (slot[None, :] == jnp.arange(owners * CAP, dtype=jnp.int32)[:, None]).astype(jnp.int32)
    second = pair_list[:, 1]
    which = second * (second + 1) // 2 + pair_list[:, 0]
    index = NP + jnp.sum(match * (which - NP)[None, :], 1)

    routed = route(index, sums, parts).reshape(owners, CAP, 64, 128)
    arrived = lax.all_to_all(routed, ("x", "z", "c"), 0, 0, tiled=True)
    return place(arrived)


def solution(mesh):
    grid = Mesh(mesh.devices.reshape(4, 4, 2, 4), ("x", "z", "c", "y"))
    pairs = ("x", "z", "c")
    return jax.shard_map(
        on_device,
        mesh=grid,
        in_specs=(P(pairs, "y"), P("y"), P(), P()),
        out_specs=P(pairs, "y", None),
        check_vma=False,
    )
```

time: 177 us -> 197 us (1.11)
  local copies, waits for them, and re-layouts: 1.9 us -> 25.6 us
  waiting for transfers between devices: 84.3 us -> 80.3 us
  other arithmetic: 3.44 us -> 0.84 us
    unnamed x7 -> x47, local copies, waits for them, and re-layouts: 1.79 us -> 23.6 us
    pallas_call x3 -> x4, Pallas kernels: 18.5 us -> 22.5 us  [the longest x3 16.5 us: grams(): pl.pallas_call(kernel, out_shape=shapes, in_specs=[smem] + [vmem] * len(g...]
    ppermute x17 -> x15, starting transfers between devices: 26.6 us -> 23.8 us  [shift(): return lax.ppermute(a, axis, [(i, (i + d) % 4) for i in range(4)])]
    pallas_call x1, Pallas kernels: 3.69 us -> 1.06 us  [route(): pl.pallas_call(route_kernel, out_shape=jax.ShapeDtypeStruct((index.shape[...]
    ppermute x17 -> x15, waiting for transfers between devices: 82.1 us -> 80.2 us  [shift(): return lax.ppermute(a, axis, [(i, (i + d) % 4) for i in range(4)])]
  transfers between devices with their start and end apart: 22 -> 20, of which waited for: 13 -> 9; matrix products, arithmetic and copies ran while one was open for 2% -> 1% of each run, Pallas kernels for 4% -> 5%
where the time goes in v4:
time: 197 us
  waiting for transfers between devices  80.3 us (41%)
  blocking collectives  35.9 us (18%)
  starting transfers between devices  29.2 us (15%)
  local copies, waits for them, and re-layouts  25.6 us (13%)
  Pallas kernels  24.5 us (12%)
    ppermute x15, waiting for transfers between devices, shift(): return lax.ppermute(a, axis, [(i, (i + d) % 4) for i in range(4)])  80.2 us
    all_to_all x1, blocking collectives, on_device(): arrived = lax.all_to_all(routed, ('x', 'z', 'c'), 0, 0, tiled=True)  35.9 us
    ppermute x15, starting transfers between devices, shift(): return lax.ppermute(a, axis, [(i, (i + d) % 4) for i in range(4)])  23.8 us
    unnamed x47, local copies, waits for them, and re-layouts  23.6 us
    pallas_call x3, Pallas kernels, grams(): pl.pallas_call(kernel, out_shape=shapes, in_specs=[smem] + [vmem] * len(g...  16.5 us
    pallas_call x1, Pallas kernels, place(): pl.pallas_call(place_kernel, grid=(CAP, 2), out_shape=jax.ShapeDtypeStruc...  6.02 us
  transfers between devices with their start and end apart: 20, of which 9 were waited for; matrix products, arithmetic and copies ran while one was open for 1% of the time, Pallas kernels for 5%

profile of v4, /device:TPU:1, one launch (start us, length us, event | category | flops | bytes accessed | tf_op | source)
XLA Modules:
  0.0 196.5 jit_solution(10313236754903394044)
XLA Ops:
  2.8 4.5 %collective-permute-start = (bf16[128,3072]{1,0:T(8,128)(2,1)S(1)}, bf16[128,3072]{1,0:T(8,128)(2,1)S(1)}, u32[]{:S(2)}, u32[]{:S(2)}) collective-permute-start(bf16[128,3072]{1,0:T(8,128)(2,1)S(1)} %get-tuple-element.30), channel_id=1, source_target_pairs={{0,16},{8,24},{16,0},{24,8},{1,17},{9,25},{17,1},{25,9},{2,18},{10... | collective-permute-start | bytes 2359304 | tf_op jit(solution)/shard_map/ppermute | solution.py:18
  7.3 2.5 %collective-permute-start.1 = (bf16[1,64,3072]{2,1,0:T(8,128)(2,1)S(1)}, bf16[1,64,3072]{2,1,0:T(8,128)(2,1)S(1)}, u32[]{:S(2)}, u32[]{:S(2)}) collective-permute-start(bf16[1,64,3072]{2,1,0:T(8,128)(2,1)S(1)} %get-tuple-element.31), channel_id=1, source_target_pairs={{0,96},{32,0},{64,32},{96,64},{1,97},{33,1},{65,33},{97,65},{2,98}... | collective-permute-start | bytes 1179656 | tf_op jit(solution)/shard_map/ppermute | solution.py:18
  10.9 7.1 %collective-permute-done.1 = bf16[1,64,3072]{2,1,0:T(8,128)(2,1)S(1)} collective-permute-done((bf16[1,64,3072]{2,1,0:T(8,128)(2,1)S(1)}, bf16[1,64,3072]{2,1,0:T(8,128)(2,1)S(1)}, u32[]{:S(2)}, u32[]{:S(2)}) %collective-permute-start.1) | collective-permute-done | bytes 393248 | tf_op jit(solution)/shard_map/ppermute | solution.py:18
  18.0 2.7 %collective-permute-done.2 = bf16[1,64,3072]{2,1,0:T(8,128)(2,1)S(1)} collective-permute-done((bf16[1,64,3072]{2,1,0:T(8,128)(2,1)S(1)}, bf16[1,64,3072]{2,1,0:T(8,128)(2,1)S(1)}, u32[]{:S(2)}, u32[]{:S(2)}) %collective-permute-start.2) | collective-permute-done | bytes 393248 | tf_op jit(solution)/shard_map/ppermute | solution.py:18
  20.7 10.1 %collective-permute-done.3 = bf16[1,64,3072]{2,1,0:T(8,128)(2,1)S(1)} collective-permute-done((bf16[1,64,3072]{2,1,0:T(8,128)(2,1)S(1)}, bf16[1,64,3072]{2,1,0:T(8,128)(2,1)S(1)}, u32[]{:S(2)}, u32[]{:S(2)}) %collective-permute-start.3) | collective-permute-done | bytes 393248 | tf_op jit(solution)/shard_map/ppermute | solution.py:18
  31.1 2.7 %collective-permute-start.5 = (bf16[256,3072]{1,0:T(8,128)(2,1)S(1)}, bf16[256,3072]{1,0:T(8,128)(2,1)S(1)}, u32[]{:S(2)}, u32[]{:S(2)}) collective-permute-start(bf16[256,3072]{1,0:T(8,128)(2,1)S(1)} %pad_maximum_fusion.refs_6_.refs_4_), channel_id=1, source_target_pairs={{0,96},{32,0},{64,32},{96,64},{1,97},{33,1},{65,33},{97,65},{2,98}... | collective-permute-start | bytes 4718600 | tf_op jit(solution)/shard_map/ppermute | solution.py:18
  38.1 29.7 %collective-permute-done.4.refs_8_.refs_6_ = bf16[256,3072]{1,0:T(8,128)(2,1)S(1)} collective-permute-done((bf16[256,3072]{1,0:T(8,128)(2,1)S(1)}, bf16[256,3072]{1,0:T(8,128)(2,1)S(1)}, u32[]{:S(2)}, u32[]{:S(2)}) %collective-permute-start.4) | collective-permute-done | bytes 1572896 | tf_op jit(solution)/shard_map/ppermute | solution.py:18
  72.1 2.6 %collective-permute-start.10 = (bf16[2,64,3072]{2,1,0:T(8,128)(2,1)S(1)}, bf16[2,64,3072]{2,1,0:T(8,128)(2,1)}, u32[]{:S(2)}, u32[]{:S(2)}) collective-permute-start(bf16[2,64,3072]{2,1,0:T(8,128)(2,1)S(1)} %slice.21), channel_id=1, source_target_pairs={{0,24},{8,0},{16,8},{24,16},{1,25},{9,1},{17,9},{25,17},{2,26},{10... | collective-permute-start | bytes 2359304 | tf_op jit(solution)/shard_map/ppermute | solution.py:18
  76.7 2.7 %collective-permute-start.16 = (bf16[128,3072]{1,0:T(8,128)(2,1)}, bf16[128,3072]{1,0:T(8,128)(2,1)}, u32[]{:S(2)}, u32[]{:S(2)}) collective-permute-start(bf16[128,3072]{1,0:T(8,128)(2,1)} %slice.23), channel_id=1, source_target_pairs={{0,96},{32,0},{64,32},{96,64},{1,97},{33,1},{65,33},{97,65},{2,98}... | collective-permute-start | bytes 2359304 | tf_op jit(solution)/shard_map/ppermute | solution.py:18
  79.4 6.5 %early_kernel.1.refs_8_ = f32[4,37,64,128]{3,2,1,0:T(8,128)S(1)} custom-call(s32[4]{0:T(128)S(1)} %pad_add_fusion.meta, bf16[4,64,3072]{2,1,0:T(8,128)(2,1)S(1)} %pad_maximum_fusion.1.refs_0_, bf16[4,64,3072]{2,1,0:T(8,128)(2,1)S(1)} %collective-permute-done.7.refs_1_, bf16[4,64,3072]{2,1,0:T(8,128)(2,1)S(1)} %collective-permute-done.6.refs_2_, ...), custom_call_target="tpu_custom_call" | custom-call | flops 3221225472 | bytes 16777216 | tf_op jit(solution)/shard_map/early_kernel/pallas_call | solution.py:101
  85.9 2.2 %copy-done = f32[4,37,64,128]{3,2,1,0:T(8,128)} copy-done((f32[4,37,64,128]{3,2,1,0:T(8,128)}, f32[4,37,64,128]{3,2,1,0:T(8,128)S(1)}, u32[]{:S(2)}) %copy-start) | copy-done | bytes 4849688
  91.3 3.2 %collective-permute-done.9.refs_0_ = bf16[2,64,3072]{2,1,0:T(8,128)(2,1)} collective-permute-done((bf16[2,64,3072]{2,1,0:T(8,128)(2,1)S(1)}, bf16[2,64,3072]{2,1,0:T(8,128)(2,1)}, u32[]{:S(2)}, u32[]{:S(2)}) %collective-permute-start.9) | collective-permute-done | bytes 786464 | tf_op jit(solution)/shard_map/ppermute | solution.py:18
  96.3 2.4 %copy-done.1 = f32[4,37,64,128]{3,2,1,0:T(8,128)S(1)} copy-done((f32[4,37,64,128]{3,2,1,0:T(8,128)S(1)}, f32[4,37,64,128]{3,2,1,0:T(8,128)}, u32[]{:S(2)}) %copy-start.1) | copy-done | bytes 4849688
  105.7 4.0 %middle_kernel.1.refs_9_ = f32[4,37,64,128]{3,2,1,0:T(8,128)S(1)} custom-call(s32[4]{0:T(128)S(1)} %pad_add_fusion.meta, bf16[4,64,3072]{2,1,0:T(8,128)(2,1)S(1)} %pad_maximum_fusion.1.refs_0_, bf16[4,64,3072]{2,1,0:T(8,128)(2,1)S(1)} %copy-done.9, bf16[4,64,3072]{2,1,0:T(8,128)(2,1)S(1)} %copy-done.7, ...), custom_call_target="tpu_custom_call", output_to_operand_aliasing={{}: (9, {})} | custom-call | flops 3221225472 | bytes 16777216 | tf_op jit(solution)/shard_map/middle_kernel/pallas_call | solution.py:101
  109.7 2.2 %copy-done.2 = f32[4,37,64,128]{3,2,1,0:T(8,128)} copy-done((f32[4,37,64,128]{3,2,1,0:T(8,128)}, f32[4,37,64,128]{3,2,1,0:T(8,128)S(1)}, u32[]{:S(2)}) %copy-start.2) | copy-done | bytes 4849688
  111.9 2.4 %copy-done.3 = f32[4,37,64,128]{3,2,1,0:T(8,128)S(1)} copy-done((f32[4,37,64,128]{3,2,1,0:T(8,128)S(1)}, f32[4,37,64,128]{3,2,1,0:T(8,128)}, u32[]{:S(2)}) %copy-start.3) | copy-done | bytes 4849688
  114.3 6.0 %late_kernel.1 = (bf16[36,64,128]{2,1,0:T(8,128)(2,1)S(1)}, bf16[36,64,128]{2,1,0:T(8,128)(2,1)S(1)}, bf16[36,64,128]{2,1,0:T(8,128)(2,1)S(1)}, f32[4,37,64,128]{3,2,1,0:T(8,128)S(1)}) custom-call(s32[4]{0:T(128)S(1)} %pad_add_fusion.meta, bf16[2,64,3072]{2,1,0:T(8,128)(2,1)} %collective-permute-done.9.refs_0_, ...), custom_call_target="tpu_custom_call", output_to_operand_aliasing={{3}: (10, {})} | custom-call | flops 3221225472 | bytes 16777216 | tf_op jit(solution)/shard_map/late_kernel/pallas_call | solution.py:101
  120.3 2.2 %copy-done.4 = f32[4,37,64,128]{3,2,1,0:T(8,128)} copy-done((f32[4,37,64,128]{3,2,1,0:T(8,128)}, f32[4,37,64,128]{3,2,1,0:T(8,128)S(1)}, u32[]{:S(2)}) %copy-start.4) | copy-done | bytes 4849688
  123.8 2.6 %collective-permute-start.18 = (bf16[36,64,128]{2,1,0:T(8,128)(2,1)S(1)}, bf16[36,64,128]{2,1,0:T(8,128)(2,1)S(1)}, u32[]{:S(2)}, u32[]{:S(2)}) collective-permute-start(bf16[36,64,128]{2,1,0:T(8,128)(2,1)S(1)} %get-tuple-element.51), channel_id=1, source_target_pairs={{0,2},{1,3},{2,0},{3,1},{4,6},{5,7},{6,4},{7,5},{8,10},{9,11},{10,... | collective-permute-start | bytes 1769480 | tf_op jit(solution)/shard_map/ppermute | solution.py:18
  127.8 9.7 %collective-permute-done.17.a = bf16[36,64,128]{2,1,0:T(8,128)(2,1)S(1)} collective-permute-done((bf16[36,64,128]{2,1,0:T(8,128)(2,1)S(1)}, bf16[36,64,128]{2,1,0:T(8,128)(2,1)S(1)}, u32[]{:S(2)}, u32[]{:S(2)}) %collective-permute-start.17) | collective-permute-done | bytes 589856 | tf_op jit(solution)/shard_map/ppermute | solution.py:18
  137.4 13.8 %collective-permute-done.18.b = bf16[36,64,128]{2,1,0:T(8,128)(2,1)S(1)} collective-permute-done((bf16[36,64,128]{2,1,0:T(8,128)(2,1)S(1)}, bf16[36,64,128]{2,1,0:T(8,128)(2,1)S(1)}, u32[]{:S(2)}, u32[]{:S(2)}) %collective-permute-start.18) | collective-permute-done | bytes 589856 | tf_op jit(solution)/shard_map/ppermute | solution.py:18
  151.2 2.4 %copy-done.5 = f32[4,37,64,128]{3,2,1,0:T(8,128)S(1)} copy-done((f32[4,37,64,128]{3,2,1,0:T(8,128)S(1)}, f32[4,37,64,128]{3,2,1,0:T(8,128)}, u32[]{:S(2)}) %copy-start.5) | copy-done | bytes 4849688
  154.7 35.9 %all_to_all.5.got = bf16[32,4,64,128]{3,2,1,0:T(8,128)(2,1)} all-to-all(bf16[32,4,64,128]{3,2,1,0:T(8,128)(2,1)S(1)} %bitcast.16), channel_id=1, replica_groups=mesh['x'=4,'z'=4,'c'=2,'y'=4] {'x','z','c'}, dimensions={0} | all-to-all | bytes 4194304 | tf_op jit(solution)/shard_map/all_to_all | solution.py:236
  190.5 6.0 %place.1 = f32[4,256,1024]{2,1,0:T(8,128)} custom-call(bf16[32,4,64,128]{3,2,1,0:T(8,128)(2,1)} %all_to_all.5.got), custom_call_target="tpu_custom_call" | custom-call | tf_op jit(solution)/shard_map/place/pallas_call | solution.py:182
  (83 shorter events, 30.5 us)
Async XLA Ops:
  2.8 28.0 %collective-permute-start = (bf16[128,3072]{1,0:T(8,128)(2,1)S(1)}, bf16[128,3072]{1,0:T(8,128)(2,1)S(1)}, u32[]{:S(2)}, u32[]{:S(2)}) collective-permute-start(bf16[128,3072]{1,0:T(8,128)(2,1)S(1)} %get-tuple-element.30), channel_id=1, source_target_pairs={{0,16},{8,24},{16,0},{24,8},{1,17},{9,25},{17,1},{25,9},{2,18},{10... | collective-permute-start | bytes 2359304 | tf_op jit(solution)/shard_map/ppermute | solution.py:18
  7.3 10.7 %collective-permute-start.1 = (bf16[1,64,3072]{2,1,0:T(8,128)(2,1)S(1)}, bf16[1,64,3072]{2,1,0:T(8,128)(2,1)S(1)}, u32[]{:S(2)}, u32[]{:S(2)}) collective-permute-start(bf16[1,64,3072]{2,1,0:T(8,128)(2,1)S(1)} %get-tuple-element.31), channel_id=1, source_target_pairs={{0,96},{32,0},{64,32},{96,64},{1,97},{33,1},{65,33},{97,65},{2,98}... | collective-permute-start | bytes 1179656 | tf_op jit(solution)/shard_map/ppermute | solution.py:18
  9.8 10.9 %collective-permute-start.2 = (bf16[1,64,3072]{2,1,0:T(8,128)(2,1)S(1)}, bf16[1,64,3072]{2,1,0:T(8,128)(2,1)S(1)}, u32[]{:S(2)}, u32[]{:S(2)}) collective-permute-start(bf16[1,64,3072]{2,1,0:T(8,128)(2,1)S(1)} %get-tuple-element.32), channel_id=1, source_target_pairs={{0,64},{32,96},{64,0},{96,32},{1,65},{33,97},{65,1},{97,33},{2,66}... | collective-permute-start | bytes 1179656 | tf_op jit(solution)/shard_map/ppermute | solution.py:18
  10.3 20.4 %collective-permute-start.3 = (bf16[1,64,3072]{2,1,0:T(8,128)(2,1)S(1)}, bf16[1,64,3072]{2,1,0:T(8,128)(2,1)S(1)}, u32[]{:S(2)}, u32[]{:S(2)}) collective-permute-start(bf16[1,64,3072]{2,1,0:T(8,128)(2,1)S(1)} %get-tuple-element.33), channel_id=1, source_target_pairs={{0,32},{32,64},{64,96},{96,0},{1,33},{33,65},{65,97},{97,1},{2,34}... | collective-permute-start | bytes 1179656 | tf_op jit(solution)/shard_map/ppermute | solution.py:18
  31.1 36.8 %collective-permute-start.4 = (bf16[256,3072]{1,0:T(8,128)(2,1)S(1)}, bf16[256,3072]{1,0:T(8,128)(2,1)S(1)}, u32[]{:S(2)}, u32[]{:S(2)}) collective-permute-start(bf16[256,3072]{1,0:T(8,128)(2,1)S(1)} %pad_maximum_fusion.refs_6_.refs_4_), channel_id=1, source_target_pairs={{0,32},{32,64},{64,96},{96,0},{1,33},{33,65},{65,97},{97,1},{2,34}... | collective-permute-start | bytes 4718600 | tf_op jit(solution)/shard_map/ppermute | solution.py:18
  31.1 36.7 %collective-permute-start.5 = (bf16[256,3072]{1,0:T(8,128)(2,1)S(1)}, bf16[256,3072]{1,0:T(8,128)(2,1)S(1)}, u32[]{:S(2)}, u32[]{:S(2)}) collective-permute-start(bf16[256,3072]{1,0:T(8,128)(2,1)S(1)} %pad_maximum_fusion.refs_6_.refs_4_), channel_id=1, source_target_pairs={{0,96},{32,0},{64,32},{96,64},{1,97},{33,1},{65,33},{97,65},{2,98}... | collective-permute-start | bytes 4718600 | tf_op jit(solution)/shard_map/ppermute | solution.py:18
  33.8 36.0 %collective-permute-start.6 = (bf16[4,64,3072]{2,1,0:T(8,128)(2,1)S(1)}, bf16[4,64,3072]{2,1,0:T(8,128)(2,1)S(1)}, u32[]{:S(2)}, u32[]{:S(2)}) collective-permute-start(bf16[4,64,3072]{2,1,0:T(8,128)(2,1)S(1)} %pad_maximum_fusion.1.refs_0_), channel_id=1, source_target_pairs={{0,8},{8,16},{16,24},{24,0},{1,9},{9,17},{17,25},{25,1},{2,10},{10... | collective-permute-start | bytes 4718600 | tf_op jit(solution)/shard_map/ppermute | solution.py:18
  34.5 35.3 %collective-permute-start.7 = (bf16[4,64,3072]{2,1,0:T(8,128)(2,1)S(1)}, bf16[4,64,3072]{2,1,0:T(8,128)(2,1)S(1)}, u32[]{:S(2)}, u32[]{:S(2)}) collective-permute-start(bf16[4,64,3072]{2,1,0:T(8,128)(2,1)S(1)} %pad_maximum_fusion.1.refs_0_), channel_id=1, source_target_pairs={{0,24},{8,0},{16,8},{24,16},{1,25},{9,1},{17,9},{25,17},{2,26},{10... | collective-permute-start | bytes 4718600 | tf_op jit(solution)/shard_map/ppermute | solution.py:18
  36.5 33.4 %collective-permute-start.8 = (bf16[4,64,3072]{2,1,0:T(8,128)(2,1)S(1)}, bf16[4,64,3072]{2,1,0:T(8,128)(2,1)S(1)}, u32[]{:S(2)}, u32[]{:S(2)}) collective-permute-start(bf16[4,64,3072]{2,1,0:T(8,128)(2,1)S(1)} %pad_maximum_fusion.1.refs_0_), channel_id=1, source_target_pairs={{0,4},{4,0},{1,5},{5,1},{2,6},{6,2},{3,7},{7,3},{8,12},{12,8},{9,1... | collective-permute-start | bytes 4718600 | tf_op jit(solution)/shard_map/ppermute | solution.py:208
  67.8 11.5 %copy-start.10 = (bf16[256,3072]{1,0:T(8,128)(2,1)}, bf16[256,3072]{1,0:T(8,128)(2,1)S(1)}, u32[]{:S(2)}) copy-start(bf16[256,3072]{1,0:T(8,128)(2,1)S(1)} %collective-permute-done.4.refs_8_.refs_6_) | copy-start | bytes 4718596
  67.8 11.5 %copy-start.12 = (bf16[256,3072]{1,0:T(8,128)(2,1)}, bf16[256,3072]{1,0:T(8,128)(2,1)S(1)}, u32[]{:S(2)}) copy-start(bf16[256,3072]{1,0:T(8,128)(2,1)S(1)} %collective-permute-done.5.refs_7_.refs_5_) | copy-start | bytes 4718596
  69.9 6.8 %collective-permute-start.11 = (bf16[4,64,3072]{2,1,0:T(8,128)(2,1)S(1)}, bf16[4,64,3072]{2,1,0:T(8,128)(2,1)S(1)}, u32[]{:S(2)}, u32[]{:S(2)}) collective-permute-start(bf16[4,64,3072]{2,1,0:T(8,128)(2,1)S(1)} %collective-permute-done.7.refs_1_), channel_id=1, source_target_pairs={{0,4},{4,0},{1,5},{5,1},{2,6},{6,2},{3,7},{7,3},{8,12},{12,8},{9,1... | collective-permute-start | bytes 4718600 | tf_op jit(solution)/shard_map/ppermute | solution.py:213
  71.9 7.4 %collective-permute-start.12 = (bf16[4,64,3072]{2,1,0:T(8,128)(2,1)S(1)}, bf16[4,64,3072]{2,1,0:T(8,128)(2,1)S(1)}, u32[]{:S(2)}, u32[]{:S(2)}) collective-permute-start(bf16[4,64,3072]{2,1,0:T(8,128)(2,1)S(1)} %collective-permute-done.6.refs_2_), channel_id=1, source_target_pairs={{0,4},{4,0},{1,5},{5,1},{2,6},{6,2},{3,7},{7,3},{8,12},{12,8},{9,1... | collective-permute-start | bytes 4718600 | tf_op jit(solution)/shard_map/ppermute | solution.py:213
  72.1 19.1 %collective-permute-start.10 = (bf16[2,64,3072]{2,1,0:T(8,128)(2,1)S(1)}, bf16[2,64,3072]{2,1,0:T(8,128)(2,1)}, u32[]{:S(2)}, u32[]{:S(2)}) collective-permute-start(bf16[2,64,3072]{2,1,0:T(8,128)(2,1)S(1)} %slice.21), channel_id=1, source_target_pairs={{0,24},{8,0},{16,8},{24,16},{1,25},{9,1},{17,9},{25,17},{2,26},{10... | collective-permute-start | bytes 2359304 | tf_op jit(solution)/shard_map/ppermute | solution.py:18
  74.8 19.7 %collective-permute-start.9 = (bf16[2,64,3072]{2,1,0:T(8,128)(2,1)S(1)}, bf16[2,64,3072]{2,1,0:T(8,128)(2,1)}, u32[]{:S(2)}, u32[]{:S(2)}) collective-permute-start(bf16[2,64,3072]{2,1,0:T(8,128)(2,1)S(1)} %slice.20), channel_id=1, source_target_pairs={{0,8},{8,16},{16,24},{24,0},{1,9},{9,17},{17,25},{25,1},{2,10},{10... | collective-permute-start | bytes 2359304 | tf_op jit(solution)/shard_map/ppermute | solution.py:18
  75.7 20.5 %collective-permute-start.15 = (bf16[128,3072]{1,0:T(8,128)(2,1)}, bf16[128,3072]{1,0:T(8,128)(2,1)}, u32[]{:S(2)}, u32[]{:S(2)}) collective-permute-start(bf16[128,3072]{1,0:T(8,128)(2,1)} %slice.22), channel_id=1, source_target_pairs={{0,32},{32,64},{64,96},{96,0},{1,33},{33,65},{65,97},{97,1},{2,34}... | collective-permute-start | bytes 2359304 | tf_op jit(solution)/shard_map/ppermute | solution.py:18
  76.7 19.4 %copy-start.21 = (s32[64,1]{0,1:T(1,128)S(1)}, s32[64,1]{0,1:T(1,128)}, u32[]{:S(2)}) copy-start(s32[64,1]{0,1:T(1,128)} %param.7) | copy-start | bytes 772
  76.7 19.6 %collective-permute-start.16 = (bf16[128,3072]{1,0:T(8,128)(2,1)}, bf16[128,3072]{1,0:T(8,128)(2,1)}, u32[]{:S(2)}, u32[]{:S(2)}) collective-permute-start(bf16[128,3072]{1,0:T(8,128)(2,1)} %slice.23), channel_id=1, source_target_pairs={{0,96},{32,0},{64,32},{96,64},{1,97},{33,1},{65,33},{97,65},{2,98}... | collective-permute-start | bytes 2359304 | tf_op jit(solution)/shard_map/ppermute | solution.py:18
  94.5 17.4 %collective-permute-start.13 = (bf16[2,64,3072]{2,1,0:T(8,128)(2,1)}, bf16[2,64,3072]{2,1,0:T(8,128)(2,1)}, u32[]{:S(2)}, u32[]{:S(2)}) collective-permute-start(bf16[2,64,3072]{2,1,0:T(8,128)(2,1)} %collective-permute-done.9.refs_0_), channel_id=1, source_target_pairs={{0,4},{4,0},{1,5},{5,1},{2,6},{6,2},{3,7},{7,3},{8,12},{12,8},{9,1... | collective-permute-start | bytes 2359304 | tf_op jit(solution)/shard_map/ppermute | solution.py:218
  96.1 15.8 %collective-permute-start.14 = (bf16[2,64,3072]{2,1,0:T(8,128)(2,1)}, bf16[2,64,3072]{2,1,0:T(8,128)(2,1)}, u32[]{:S(2)}, u32[]{:S(2)}) collective-permute-start(bf16[2,64,3072]{2,1,0:T(8,128)(2,1)} %collective-permute-done.10.refs_1_), channel_id=1, source_target_pairs={{0,4},{4,0},{1,5},{5,1},{2,6},{6,2},{3,7},{7,3},{8,12},{12,8},{9,1... | collective-permute-start | bytes 2359304 | tf_op jit(solution)/shard_map/ppermute | solution.py:218
  105.7 22.0 %copy-start.22 = (s32[64,2]{0,1:T(2,128)S(1)}, s32[64,2]{0,1:T(2,128)}, u32[]{:S(2)}) copy-start(s32[64,2]{0,1:T(2,128)} %param.6) | copy-start | bytes 1540
  122.5 15.0 %collective-permute-start.17 = (bf16[36,64,128]{2,1,0:T(8,128)(2,1)S(1)}, bf16[36,64,128]{2,1,0:T(8,128)(2,1)S(1)}, u32[]{:S(2)}, u32[]{:S(2)}) collective-permute-start(bf16[36,64,128]{2,1,0:T(8,128)(2,1)S(1)} %get-tuple-element.50), channel_id=1, source_target_pairs={{0,1},{1,2},{2,3},{3,0},{4,5},{5,6},{6,7},{7,4},{8,9},{9,10},{10,1... | collective-permute-start | bytes 1769480 | tf_op jit(solution)/shard_map/ppermute | solution.py:18
  123.8 27.4 %collective-permute-start.18 = (bf16[36,64,128]{2,1,0:T(8,128)(2,1)S(1)}, bf16[36,64,128]{2,1,0:T(8,128)(2,1)S(1)}, u32[]{:S(2)}, u32[]{:S(2)}) collective-permute-start(bf16[36,64,128]{2,1,0:T(8,128)(2,1)S(1)} %get-tuple-element.51), channel_id=1, source_target_pairs={{0,2},{1,3},{2,0},{3,1},{4,6},{5,7},{6,4},{7,5},{8,10},{9,11},{10,... | collective-permute-start | bytes 1769480 | tf_op jit(solution)/shard_map/ppermute | solution.py:18
  126.4 24.8 %collective-permute-start.19 = (bf16[36,64,128]{2,1,0:T(8,128)(2,1)S(1)}, bf16[36,64,128]{2,1,0:T(8,128)(2,1)S(1)}, u32[]{:S(2)}, u32[]{:S(2)}) collective-permute-start(bf16[36,64,128]{2,1,0:T(8,128)(2,1)S(1)} %get-tuple-element.52), channel_id=1, source_target_pairs={{0,3},{1,0},{2,1},{3,2},{4,7},{5,4},{6,5},{7,6},{8,11},{9,8},{10,9... | collective-permute-start | bytes 1769480 | tf_op jit(solution)/shard_map/ppermute | solution.py:18
  (19 other events, 71.0 us)

commit v5 on v4

--- a/solution.py
+++ b/solution.py
@@ -1,3 +1,5 @@
+import functools
+
 import jax
 import jax.numpy as jnp
 from jax import lax
@@ -11,6 +13,7 @@
 NP = TILES * (TILES + 1) // 2
 BF = jnp.bfloat16
 F32 = jnp.float32
+FIRST, SECOND = 18, 20
 MIB = 1 << 20
 
 
@@ -70,46 +73,54 @@
     lax.fori_loop(0, 4, step, 0)
 
 
-def middle_kernel(meta, *refs):
-    near_step(meta, refs[:6], refs[6:8], (meta[0] + 2) % 4, refs[9])
-
-
-def late_kernel(meta, *refs):
-    late, rights = refs[:4], [refs[4:5], refs[5:6], refs[7:9], refs[6:7]]
-    s1, s2, s3, sums = refs[10:14]
+def pack(order, sums, outs):
+    for p in range(outs[0].shape[0]):
+        at = order[p]
+        for k, ref in enumerate(outs):
+            ref[p] = sums[k + 1, at].astype(BF)
+
+
+def middle_kernel(meta, order, *refs):
+    near_step(meta, refs[:6], refs[6:8], (meta[0] + 2) % 4, refs[12])
+    pack(order, refs[12], refs[9:12])
+
+
+def late_kernel(dc, meta, order, *refs):
+    late, rights = refs[:2], [refs[2:3], refs[3:4], refs[5:7], refs[4:5]]
+    sums = refs[-1]
     x = meta[0]
-    rows = [late[2 * dc + k // 2][k % 2] for k in range(4) for dc in range(2)]
+    rows = [late[k // 2][k % 2] for k in range(4)]
     for dx, right in enumerate(rights):
         jp = (x + dx) % 4
         out = product(rows, [ref[...] for ref in right])
         for k in range(4):
-            store(meta, sums, out, (x + k) % 4, jp, LATE_L, 128 * k)
-    for k, ref in enumerate((s1, s2, s3)):
-        ref[...] = sums[k + 1, :NP].astype(BF)
-
-
-def grams(kernel, meta, given, sums=None, parts=False):
+            store(meta, sums, out, (x + k) % 4, jp, [(dc, 2)], 64 * k)
+    if dc:
+        pack(order, sums, refs[8:11])
+
+
+def grams(kernel, name, scalars, given, sums=None, parts=0):
     width = given[0].shape[-1]
     smem = pl.BlockSpec(memory_space=pltpu.SMEM)
     vmem = pl.BlockSpec(memory_space=pltpu.VMEM)
-    shapes = [jax.ShapeDtypeStruct((NP, 64, 128), BF)] * 3 if parts else []
+    shapes = [jax.ShapeDtypeStruct((parts, 64, 128), BF)] * 3 if parts else []
     shapes += [jax.ShapeDtypeStruct((4, NP + 1, 64, 128), F32)]
     aliases = {}
     if sums is not None:
         given = [*given, sums]
-        aliases = {len(given): len(shapes) - 1}
+        aliases = {len(scalars) + len(given) - 1: len(shapes) - 1}
     return pl.pallas_call(
         kernel,
         out_shape=shapes,
-        in_specs=[smem] + [vmem] * len(given),
+        in_specs=[smem] * len(scalars) + [vmem] * len(given),
         out_specs=[vmem] * len(shapes),
         input_output_aliases=aliases,
         compiler_params=pltpu.CompilerParams(vmem_limit_bytes=16 * MIB),
         cost_estimate=pl.CostEstimate(
-            flops=2 * 4 * 512 * 256 * width, bytes_accessed=16 * MIB, transcendentals=0
+            flops=2 * 4 * 512 * 256 * width, bytes_accessed=MIB, transcendentals=0
         ),
-        name=kernel.__name__,
-    )(meta, *given)
+        name=name,
+    )(*scalars, *given)
 
 
 def prepare_kernel(meta, dens, weights, keep, send, *parts):
@@ -143,10 +154,15 @@
     )(meta, dens, weights)
 
 
-def route_kernel(index, sums, a, b, c, out, total):
-    total[:NP] = (
-        sums[0, :NP] + a[...].astype(F32) + b[...].astype(F32) + c[...].astype(F32)
-    ).astype(BF)
+def route_kernel(index, order1, order2, sums, *refs):
+    out, total = refs[6], refs[7]
+    for order, parts in ((order1, refs[:3]), (order2, refs[3:6])):
+        for p in range(parts[0].shape[0]):
+            at = order[p]
+            value = sums[0, at]
+            for part in parts:
+                value = value + part[p].astype(F32)
+            total[at] = value.astype(BF)
     total[NP] = jnp.zeros(total.shape[1:], BF)
 
     def some(k, _):
@@ -157,34 +173,81 @@
     lax.fori_loop(0, out.shape[0] // 8, some, 0)
 
 
-def route(index, sums, parts):
+def route(scalars, sums, parts):
     smem = pl.BlockSpec(memory_space=pltpu.SMEM)
     vmem = pl.BlockSpec(memory_space=pltpu.VMEM)
     return pl.pallas_call(
         route_kernel,
-        out_shape=jax.ShapeDtypeStruct((index.shape[0], 64, 128), BF),
-        in_specs=[smem] + [vmem] * 4,
+        out_shape=jax.ShapeDtypeStruct((scalars[0].shape[0], 64, 128), BF),
+        in_specs=[smem] * 3 + [vmem] * 7,
         out_specs=vmem,
         scratch_shapes=[pltpu.VMEM((NP + 1, 64, 128), BF)],
         compiler_params=pltpu.CompilerParams(vmem_limit_bytes=16 * MIB),
         name="route",
-    )(index, sums, *parts)
+    )(*scalars, sums, *parts)
+
+
+def plan_kernel(meta, first, second, owner, index, order1, order2, count):
+    def clear(k, _):
+        index[k] = NP
+        return 0
+
+    def reset(k, _):
+        count[k] = 0
+        order1[lax.rem(k, FIRST + 1)] = NP
+        order2[lax.rem(k, SECOND + 1)] = NP
+        return 0
+
+    def entry(e, _):
+        who = owner[e]
+        rank = count[who]
+        count[who] = rank + 1
+        j = second[e]
+        index[who * CAP + rank] = j * (j + 1) // 2 + first[e]
+        return 0
+
+    lax.fori_loop(0, index.shape[0], clear, 0)
+    lax.fori_loop(0, count.shape[0], reset, 0)
+    lax.fori_loop(0, owner.shape[0], entry, 0)
+    z1 = meta[1] // 2
+    n1 = n2 = jnp.int32(0)
+    for j in range(TILES):
+        for i in range(j + 1):
+            one = jnp.where((z1 == i % 2) & (n1 < FIRST), 1, 0)
+            order1[jnp.where(one == 1, n1, FIRST)] = j * (j + 1) // 2 + i
+            order2[jnp.where(one == 1, SECOND, n2)] = j * (j + 1) // 2 + i
+            n1, n2 = n1 + one, n2 + 1 - one
+
+
+def plan(meta, pair_list, owner, slots):
+    smem = pl.BlockSpec(memory_space=pltpu.SMEM)
+    return pl.pallas_call(
+        plan_kernel,
+        out_shape=[jax.ShapeDtypeStruct((n,), jnp.int32) for n in (slots, FIRST + 1, SECOND + 1)],
+        in_specs=[smem] * 4,
+        out_specs=[smem] * 3,
+        scratch_shapes=[pltpu.SMEM((slots // CAP,), jnp.int32)],
+        compiler_params=pltpu.CompilerParams(vmem_limit_bytes=MIB),
+        name="plan",
+    )(meta, pair_list[:, 0], pair_list[:, 1], owner[:, 0])
 
 
 def place_kernel(got, out):
     for src in range(32):
         x, z1, z0, c = src // 8, (src // 4) % 2, (src // 2) % 2, src % 2
         col = (4 * z0 + 2 * c + z1) * 128
-        out[0, 32 * x : 32 * x + 32, col : col + 128] = got[src, 0].astype(F32)
+        for h in range(2):
+            row = h * 128 + x * 32
+            out[0, row : row + 32, col : col + 128] = got[src, 0, 32 * h : 32 * h + 32].astype(F32)
 
 
 def place(got):
     return pl.pallas_call(
         place_kernel,
-        grid=(CAP, 2),
+        grid=(CAP,),
         out_shape=jax.ShapeDtypeStruct((CAP, 256, 1024), F32),
-        in_specs=[pl.BlockSpec((32, 1, 32, 128), lambda s, h: (0, s, h, 0))],
-        out_specs=pl.BlockSpec((1, 128, 1024), lambda s, h: (s, h, 0)),
+        in_specs=[pl.BlockSpec((32, 1, 64, 128), lambda s: (0, s, 0, 0))],
+        out_specs=pl.BlockSpec((1, 256, 1024), lambda s: (s, 0, 0)),
         name="place",
     )(got)
 
@@ -210,29 +273,31 @@
 
     left2a, left2b = shift(left3[:2], "z", 1), shift(left1[2:], "z", -1)
     right2a, right2b = shift(right3[:128], "x", 1), shift(right1[128:], "x", -1)
-    swap1, swap3 = lax.ppermute(left1, "c", other), lax.ppermute(left3, "c", other)
+    index, order1, order2 = plan(meta, pair_list, owner, 32 * CAP)
+    index, near1, near3 = tie(index, left1, left3)
+    swap1, swap3 = lax.ppermute(near1, "c", other), lax.ppermute(near3, "c", other)
     lefts = [left, left1, left3, swap0, swap1, swap3]
     rights = [right, right1, right3]
-    (sums,) = grams(early_kernel, meta, lefts + rights)
+    (sums,) = grams(early_kernel, "early", [meta], lefts + rights)
     left2a, left2b, sums = tie(left2a, left2b, sums)
     swap2a, swap2b = lax.ppermute(left2a, "c", other), lax.ppermute(left2b, "c", other)
     far = [right2a, right2b]
-    (sums,) = grams(middle_kernel, meta, lefts + far, sums)
-    late = [left2a, left2b, swap2a, swap2b]
-    s1, s2, s3, sums = grams(late_kernel, meta, late + rights + far, sums, True)
-    parts = [shift(s1, "y", 1), shift(s2, "y", 2), shift(s3, "y", 3)]
-
-    owners = 32
-    owner_ids = owner[:, 0]
-    onehot = (owner_ids[:, None] == jnp.arange(owners, dtype=jnp.int32)[None, :]).astype(jnp.int32)
-    rank = jnp.sum((jnp.cumsum(onehot, 0) - onehot) * onehot, 1)
-    slot = owner_ids * CAP + rank
-    match = (slot[None, :] == jnp.arange(owners * CAP, dtype=jnp.int32)[:, None]).astype(jnp.int32)
-    second = pair_list[:, 1]
-    which = second * (second + 1) // 2 + pair_list[:, 0]
-    index = NP + jnp.sum(match * (which - NP)[None, :], 1)
-
-    routed = route(index, sums, parts).reshape(owners, CAP, 64, 128)
+
+    def over_y(blocks):
+        return [shift(block, "y", k + 1) for k, block in enumerate(blocks)]
+
+    *blocks, sums = grams(middle_kernel, "middle", [meta, order1], lefts + far, sums, FIRST)
+    parts = over_y(blocks)
+    late = functools.partial(late_kernel, 0)
+    (sums,) = grams(late, "late_own", [meta, order2], [left2a, left2b] + rights + far, sums)
+    late = functools.partial(late_kernel, 1)
+    *blocks, sums = grams(
+        late, "late_other", [meta, order2], [swap2a, swap2b] + rights + far, sums, SECOND
+    )
+    blocks[1], parts[0], parts[2] = tie(blocks[1], parts[0], parts[2])
+    parts += over_y(blocks)
+
+    routed = route([index, order1, order2], sums, parts).reshape(32, CAP, 64, 128)
     arrived = lax.all_to_all(routed, ("x", "z", "c"), 0, 0, tiled=True)
     return place(arrived)
 

time: 197 us -> 169 us (0.86)
  local copies, waits for them, and re-layouts: 25.6 us -> 2 us
  waiting for transfers between devices: 80.3 us -> 77.1 us
    unnamed x47 -> x7, local copies, waits for them, and re-layouts: 23.6 us -> 1.79 us
    ppermute x15 -> x18, waiting for transfers between devices: 80.2 us -> 77.1 us  [shift(): return lax.ppermute(a, axis, [(i, (i + d) % 4) for i in range(4)])]
    ppermute x15 -> x18, starting transfers between devices: 23.8 us -> 24.8 us  [shift(): return lax.ppermute(a, axis, [(i, (i + d) % 4) for i in range(4)])]
    pallas_call x5 -> x7, Pallas kernels: 23.6 us -> 23.1 us  [the longest x4 14.5 us: grams(): pl.pallas_call(kernel, out_shape=shapes, in_specs=[smem] * len(scalars) +...]
  transfers between devices with their start and end apart: 20 -> 23, of which waited for: 9 -> 10; matrix products, arithmetic and copies ran while one was open for 1% -> 0% of each run, Pallas kernels for 5% -> 11%
where the time goes in v5:
time: 169 us
  waiting for transfers between devices  77.1 us (46%)
  blocking collectives  37.2 us (22%)
  starting transfers between devices  28.3 us (17%)
  Pallas kernels  24 us (14%)
  local copies, waits for them, and re-layouts  2 us (1%)
    ppermute x18, waiting for transfers between devices, shift(): return lax.ppermute(a, axis, [(i, (i + d) % 4) for i in range(4)])  77.1 us
    all_to_all x1, blocking collectives, on_device(): arrived = lax.all_to_all(routed, ('x', 'z', 'c'), 0, 0, tiled=True)  37.2 us
    ppermute x18, starting transfers between devices, shift(): return lax.ppermute(a, axis, [(i, (i + d) % 4) for i in range(4)])  24.8 us
    pallas_call x4, Pallas kernels, grams(): pl.pallas_call(kernel, out_shape=shapes, in_specs=[smem] * len(scalars) +...  14.5 us
    pallas_call x1, Pallas kernels, place(): pl.pallas_call(place_kernel, grid=(CAP,), out_shape=jax.ShapeDtypeStruct(...  4.24 us
  transfers between devices with their start and end apart: 23, of which 10 were waited for; matrix products, arithmetic and copies ran while one was open for 0% of the time, Pallas kernels for 11%

profile of v5, /device:TPU:1, one launch (start us, length us, event | category | flops | bytes accessed | tf_op | source)
XLA Modules:
  0.0 169.2 jit_solution(3729755496584171997)
XLA Ops:
  0.0 1.8 %copy.8.dens = bf16[256,3000]{1,0:T(8,128)(2,1)S(1)} copy(bf16[256,3000]{0,1:T(8,128)(2,1)} %param.4) | data formatting | bytes 3072000 | tf_op args[0]
  2.8 4.5 %collective-permute-start = (bf16[128,3072]{1,0:T(8,128)(2,1)S(1)}, bf16[128,3072]{1,0:T(8,128)(2,1)S(1)}, u32[]{:S(2)}, u32[]{:S(2)}) collective-permute-start(bf16[128,3072]{1,0:T(8,128)(2,1)S(1)} %get-tuple-element.44), channel_id=1, source_target_pairs={{0,16},{8,24},{16,0},{24,8},{1,17},{9,25},{17,1},{25,9},{2,18},{10... | collective-permute-start | bytes 2359304 | tf_op jit(solution)/shard_map/ppermute | solution.py:21
  7.3 2.5 %collective-permute-start.1 = (bf16[1,64,3072]{2,1,0:T(8,128)(2,1)S(1)}, bf16[1,64,3072]{2,1,0:T(8,128)(2,1)S(1)}, u32[]{:S(2)}, u32[]{:S(2)}) collective-permute-start(bf16[1,64,3072]{2,1,0:T(8,128)(2,1)S(1)} %get-tuple-element.45), channel_id=1, source_target_pairs={{0,96},{32,0},{64,32},{96,64},{1,97},{33,1},{65,33},{97,65},{2,98}... | collective-permute-start | bytes 1179656 | tf_op jit(solution)/shard_map/ppermute | solution.py:21
  10.9 7.1 %collective-permute-done.1 = bf16[1,64,3072]{2,1,0:T(8,128)(2,1)S(1)} collective-permute-done((bf16[1,64,3072]{2,1,0:T(8,128)(2,1)S(1)}, bf16[1,64,3072]{2,1,0:T(8,128)(2,1)S(1)}, u32[]{:S(2)}, u32[]{:S(2)}) %collective-permute-start.1) | collective-permute-done | bytes 393248 | tf_op jit(solution)/shard_map/ppermute | solution.py:21
  18.0 2.7 %collective-permute-done.2 = bf16[1,64,3072]{2,1,0:T(8,128)(2,1)S(1)} collective-permute-done((bf16[1,64,3072]{2,1,0:T(8,128)(2,1)S(1)}, bf16[1,64,3072]{2,1,0:T(8,128)(2,1)S(1)}, u32[]{:S(2)}, u32[]{:S(2)}) %collective-permute-start.2) | collective-permute-done | bytes 393248 | tf_op jit(solution)/shard_map/ppermute | solution.py:21
  20.7 10.1 %collective-permute-done.3 = bf16[1,64,3072]{2,1,0:T(8,128)(2,1)S(1)} collective-permute-done((bf16[1,64,3072]{2,1,0:T(8,128)(2,1)S(1)}, bf16[1,64,3072]{2,1,0:T(8,128)(2,1)S(1)}, u32[]{:S(2)}, u32[]{:S(2)}) %collective-permute-start.3) | collective-permute-done | bytes 393248 | tf_op jit(solution)/shard_map/ppermute | solution.py:21
  31.2 1.5 collective-permute-start.4
  35.2 3.3 %plan.1 = (s32[128]{0:T(128)S(1)}, s32[19]{0:T(128)S(1)}, s32[21]{0:T(128)S(1)}) custom-call(s32[4]{0:T(128)S(1)} %pad_add_fusion.meta, s32[64]{0:T(128)S(1)} %get-tuple-element.80.first, s32[64]{0:T(128)S(1)} %get-tuple-element.79.second, s32[64]{0:T(128)S(1)} %bitcast.13), custom_call_target="tpu_custom_call" | custom-call | tf_op jit(solution)/shard_map/plan/pallas_call | solution.py:224
  38.5 28.2 %collective-permute-done.5.refs_7_.refs_3_ = bf16[256,3072]{1,0:T(8,128)(2,1)S(1)} collective-permute-done((bf16[256,3072]{1,0:T(8,128)(2,1)S(1)}, bf16[256,3072]{1,0:T(8,128)(2,1)S(1)}, u32[]{:S(2)}, u32[]{:S(2)}) %collective-permute-start.5) | collective-permute-done | bytes 1572896 | tf_op jit(solution)/shard_map/ppermute | solution.py:21
  67.3 2.4 %collective-permute-done.7.refs_1_ = bf16[4,64,3072]{2,1,0:T(8,128)(2,1)S(1)} collective-permute-done((bf16[4,64,3072]{2,1,0:T(8,128)(2,1)S(1)}, bf16[4,64,3072]{2,1,0:T(8,128)(2,1)S(1)}, u32[]{:S(2)}, u32[]{:S(2)}) %collective-permute-start.7) | collective-permute-done | bytes 1572896 | tf_op jit(solution)/shard_map/ppermute | solution.py:21
  72.3 2.7 %collective-permute-start.10 = (bf16[2,64,3072]{2,1,0:T(8,128)(2,1)S(1)}, bf16[2,64,3072]{2,1,0:T(8,128)(2,1)S(1)}, u32[]{:S(2)}, u32[]{:S(2)}) collective-permute-start(bf16[2,64,3072]{2,1,0:T(8,128)(2,1)S(1)} %slice.21), channel_id=1, source_target_pairs={{0,24},{8,0},{16,8},{24,16},{1,25},{9,1},{17,9},{25,17},{2,26},{10... | collective-permute-start | bytes 2359304 | tf_op jit(solution)/shard_map/ppermute | solution.py:21
  75.2 2.7 %collective-permute-start.16 = (bf16[128,3072]{1,0:T(8,128)(2,1)S(1)}, bf16[128,3072]{1,0:T(8,128)(2,1)S(1)}, u32[]{:S(2)}, u32[]{:S(2)}) collective-permute-start(bf16[128,3072]{1,0:T(8,128)(2,1)S(1)} %slice.23), channel_id=1, source_target_pairs={{0,96},{32,0},{64,32},{96,64},{1,97},{33,1},{65,33},{97,65},{2,98}... | collective-permute-start | bytes 2359304 | tf_op jit(solution)/shard_map/ppermute | solution.py:21
  77.9 6.5 %early.1.refs_8_ = f32[4,37,64,128]{3,2,1,0:T(8,128)S(1)} custom-call(s32[4]{0:T(128)S(1)} %pad_add_fusion.meta, bf16[4,64,3072]{2,1,0:T(8,128)(2,1)S(1)} %pad_maximum_fusion.1.refs_0_, bf16[4,64,3072]{2,1,0:T(8,128)(2,1)S(1)} %collective-permute-done.7.refs_1_, bf16[4,64,3072]{2,1,0:T(8,128)(2,1)S(1)} %collective-permute-done.6.refs_2_, ...), custom_call_target="tpu_custom_call" | custom-call | flops 3221225472 | bytes 1048576 | tf_op jit(solution)/shard_map/early/pallas_call | solution.py:112
  84.4 7.8 %collective-permute-done.9.refs_0_ = bf16[2,64,3072]{2,1,0:T(8,128)(2,1)S(1)} collective-permute-done((bf16[2,64,3072]{2,1,0:T(8,128)(2,1)S(1)}, bf16[2,64,3072]{2,1,0:T(8,128)(2,1)S(1)}, u32[]{:S(2)}, u32[]{:S(2)}) %collective-permute-start.9) | collective-permute-done | bytes 786464 | tf_op jit(solution)/shard_map/ppermute | solution.py:21
  92.1 1.4 collective-permute-start.13
  94.4 3.2 %middle.1 = (bf16[18,64,128]{2,1,0:T(8,128)(2,1)S(1)}, bf16[18,64,128]{2,1,0:T(8,128)(2,1)S(1)}, bf16[18,64,128]{2,1,0:T(8,128)(2,1)S(1)}, f32[4,37,64,128]{3,2,1,0:T(8,128)S(1)}) custom-call(s32[4]{0:T(128)S(1)} %pad_add_fusion.meta, s32[19]{0:T(128)S(1)} %get-tuple-element.58.order.order1, ...), custom_call_target="tpu_custom_call", output_to_operand_aliasing={{3}: (10, {})} | custom-call | flops 3221225472 | bytes 1048576 | tf_op jit(solution)/shard_map/middle/pallas_call | solution.py:112
  98.9 1.7 %collective-permute-start.18 = (bf16[18,64,128]{2,1,0:T(8,128)(2,1)S(1)}, bf16[18,64,128]{2,1,0:T(8,128)(2,1)S(1)}, u32[]{:S(2)}, u32[]{:S(2)}) collective-permute-start(bf16[18,64,128]{2,1,0:T(8,128)(2,1)S(1)} %get-tuple-element.72), channel_id=1, source_target_pairs={{0,3},{1,0},{2,1},{3,2},{4,7},{5,4},{6,5},{7,6},{8,11},{9,8},{10,9... | collective-permute-start | bytes 884744 | tf_op jit(solution)/shard_map/ppermute | solution.py:21
  100.6 2.4 %late_own.1.refs_7_ = f32[4,37,64,128]{3,2,1,0:T(8,128)S(1)} custom-call(s32[4]{0:T(128)S(1)} %pad_add_fusion.meta, s32[21]{0:T(128)S(1)} %get-tuple-element.59.order.order2, bf16[2,64,3072]{2,1,0:T(8,128)(2,1)S(1)} %collective-permute-done.9.refs_0_, bf16[2,64,3072]{2,1,0:T(8,128)(2,1)S(1)} %collective-permute-done.10.refs_1_, ...), custom_call_target="tpu_custom_call", output_to_operand_aliasing={{}: (9, {})} | custom-call | flops 3221225472 | bytes 1048576 | tf_op jit(solution)/shard_map/late_own/pallas_call | solution.py:112
  103.0 2.5 %late_other.1 = (bf16[20,64,128]{2,1,0:T(8,128)(2,1)S(1)}, bf16[20,64,128]{2,1,0:T(8,128)(2,1)S(1)}, bf16[20,64,128]{2,1,0:T(8,128)(2,1)S(1)}, f32[4,37,64,128]{3,2,1,0:T(8,128)S(1)}) custom-call(s32[4]{0:T(128)S(1)} %pad_add_fusion.meta, s32[21]{0:T(128)S(1)} %get-tuple-element.59.order.order2, ...), custom_call_target="tpu_custom_call", output_to_operand_aliasing={{3}: (9, {})} | custom-call | flops 3221225472 | bytes 1048576 | tf_op jit(solution)/shard_map/late_other/pallas_call | solution.py:112
  105.5 2.2 %collective-permute-start.21 = (bf16[20,64,128]{2,1,0:T(8,128)(2,1)S(1)}, bf16[20,64,128]{2,1,0:T(8,128)(2,1)S(1)}, u32[]{:S(2)}, u32[]{:S(2)}) collective-permute-start(bf16[20,64,128]{2,1,0:T(8,128)(2,1)S(1)} %get-tuple-element.77), channel_id=1, source_target_pairs={{0,2},{1,3},{2,0},{3,1},{4,6},{5,7},{6,4},{7,5},{8,10},{9,11},{10,... | collective-permute-start | bytes 983048 | tf_op jit(solution)/shard_map/ppermute | solution.py:21
  108.9 1.5 collective-permute-start.22
  110.7 16.0 %collective-permute-done.19.refs_1_ = bf16[18,64,128]{2,1,0:T(8,128)(2,1)S(1)} collective-permute-done((bf16[18,64,128]{2,1,0:T(8,128)(2,1)S(1)}, bf16[18,64,128]{2,1,0:T(8,128)(2,1)S(1)}, u32[]{:S(2)}, u32[]{:S(2)}) %collective-permute-start.19) | collective-permute-done | bytes 294944 | tf_op jit(solution)/shard_map/ppermute | solution.py:21
  127.8 37.2 %all_to_all.5.got = bf16[32,4,64,128]{3,2,1,0:T(8,128)(2,1)} all-to-all(bf16[32,4,64,128]{3,2,1,0:T(8,128)(2,1)S(1)} %bitcast.11), channel_id=1, replica_groups=mesh['x'=4,'z'=4,'c'=2,'y'=4] {'x','z','c'}, dimensions={0} | all-to-all | bytes 4194304 | tf_op jit(solution)/shard_map/all_to_all | solution.py:301
  164.9 4.2 %place.1 = f32[4,256,1024]{2,1,0:T(8,128)} custom-call(bf16[32,4,64,128]{3,2,1,0:T(8,128)(2,1)} %all_to_all.5.got), custom_call_target="tpu_custom_call" | custom-call | tf_op jit(solution)/shard_map/place/pallas_call | solution.py:245
  (46 shorter events, 13.2 us)
Async XLA Ops:
  2.8 28.0 %collective-permute-start = (bf16[128,3072]{1,0:T(8,128)(2,1)S(1)}, bf16[128,3072]{1,0:T(8,128)(2,1)S(1)}, u32[]{:S(2)}, u32[]{:S(2)}) collective-permute-start(bf16[128,3072]{1,0:T(8,128)(2,1)S(1)} %get-tuple-element.44), channel_id=1, source_target_pairs={{0,16},{8,24},{16,0},{24,8},{1,17},{9,25},{17,1},{25,9},{2,18},{10... | collective-permute-start | bytes 2359304 | tf_op jit(solution)/shard_map/ppermute | solution.py:21
  7.3 10.7 %collective-permute-start.1 = (bf16[1,64,3072]{2,1,0:T(8,128)(2,1)S(1)}, bf16[1,64,3072]{2,1,0:T(8,128)(2,1)S(1)}, u32[]{:S(2)}, u32[]{:S(2)}) collective-permute-start(bf16[1,64,3072]{2,1,0:T(8,128)(2,1)S(1)} %get-tuple-element.45), channel_id=1, source_target_pairs={{0,96},{32,0},{64,32},{96,64},{1,97},{33,1},{65,33},{97,65},{2,98}... | collective-permute-start | bytes 1179656 | tf_op jit(solution)/shard_map/ppermute | solution.py:21
  9.8 10.9 %collective-permute-start.2 = (bf16[1,64,3072]{2,1,0:T(8,128)(2,1)S(1)}, bf16[1,64,3072]{2,1,0:T(8,128)(2,1)S(1)}, u32[]{:S(2)}, u32[]{:S(2)}) collective-permute-start(bf16[1,64,3072]{2,1,0:T(8,128)(2,1)S(1)} %get-tuple-element.46), channel_id=1, source_target_pairs={{0,64},{32,96},{64,0},{96,32},{1,65},{33,97},{65,1},{97,33},{2,66}... | collective-permute-start | bytes 1179656 | tf_op jit(solution)/shard_map/ppermute | solution.py:21
  10.3 20.4 %collective-permute-start.3 = (bf16[1,64,3072]{2,1,0:T(8,128)(2,1)S(1)}, bf16[1,64,3072]{2,1,0:T(8,128)(2,1)S(1)}, u32[]{:S(2)}, u32[]{:S(2)}) collective-permute-start(bf16[1,64,3072]{2,1,0:T(8,128)(2,1)S(1)} %get-tuple-element.47), channel_id=1, source_target_pairs={{0,32},{32,64},{64,96},{96,0},{1,33},{33,65},{65,97},{97,1},{2,34}... | collective-permute-start | bytes 1179656 | tf_op jit(solution)/shard_map/ppermute | solution.py:21
  30.9 4.3 %copy-start.2 = (s32[64,2]{0,1:T(2,128)S(1)}, s32[64,2]{0,1:T(2,128)}, u32[]{:S(2)}) copy-start(s32[64,2]{0,1:T(2,128)} %param.6) | copy-start | bytes 1540
  31.1 35.5 %collective-permute-start.5 = (bf16[256,3072]{1,0:T(8,128)(2,1)S(1)}, bf16[256,3072]{1,0:T(8,128)(2,1)S(1)}, u32[]{:S(2)}, u32[]{:S(2)}) collective-permute-start(bf16[256,3072]{1,0:T(8,128)(2,1)S(1)} %pad_maximum_fusion.refs_6_.refs_2_), channel_id=1, source_target_pairs={{0,96},{32,0},{64,32},{96,64},{1,97},{33,1},{65,33},{97,65},{2,98}... | collective-permute-start | bytes 4718600 | tf_op jit(solution)/shard_map/ppermute | solution.py:21
  31.2 36.1 %collective-permute-start.4 = (bf16[256,3072]{1,0:T(8,128)(2,1)S(1)}, bf16[256,3072]{1,0:T(8,128)(2,1)S(1)}, u32[]{:S(2)}, u32[]{:S(2)}) collective-permute-start(bf16[256,3072]{1,0:T(8,128)(2,1)S(1)} %pad_maximum_fusion.refs_6_.refs_2_), channel_id=1, source_target_pairs={{0,32},{32,64},{64,96},{96,0},{1,33},{33,65},{65,97},{97,1},{2,34}... | collective-permute-start | bytes 4718600 | tf_op jit(solution)/shard_map/ppermute | solution.py:21
  32.6 34.7 %collective-permute-start.8 = (bf16[4,64,3072]{2,1,0:T(8,128)(2,1)S(1)}, bf16[4,64,3072]{2,1,0:T(8,128)(2,1)S(1)}, u32[]{:S(2)}, u32[]{:S(2)}) collective-permute-start(bf16[4,64,3072]{2,1,0:T(8,128)(2,1)S(1)} %pad_maximum_fusion.1.refs_0_), channel_id=1, source_target_pairs={{0,4},{4,0},{1,5},{5,1},{2,6},{6,2},{3,7},{7,3},{8,12},{12,8},{9,1... | collective-permute-start | bytes 4718600 | tf_op jit(solution)/shard_map/ppermute | solution.py:271
  33.7 36.0 %collective-permute-start.7 = (bf16[4,64,3072]{2,1,0:T(8,128)(2,1)S(1)}, bf16[4,64,3072]{2,1,0:T(8,128)(2,1)S(1)}, u32[]{:S(2)}, u32[]{:S(2)}) collective-permute-start(bf16[4,64,3072]{2,1,0:T(8,128)(2,1)S(1)} %pad_maximum_fusion.1.refs_0_), channel_id=1, source_target_pairs={{0,24},{8,0},{16,8},{24,16},{1,25},{9,1},{17,9},{25,17},{2,26},{10... | collective-permute-start | bytes 4718600 | tf_op jit(solution)/shard_map/ppermute | solution.py:21
  34.1 36.9 %collective-permute-start.6 = (bf16[4,64,3072]{2,1,0:T(8,128)(2,1)S(1)}, bf16[4,64,3072]{2,1,0:T(8,128)(2,1)S(1)}, u32[]{:S(2)}, u32[]{:S(2)}) collective-permute-start(bf16[4,64,3072]{2,1,0:T(8,128)(2,1)S(1)} %pad_maximum_fusion.1.refs_0_), channel_id=1, source_target_pairs={{0,8},{8,16},{16,24},{24,0},{1,9},{9,17},{17,25},{25,1},{2,10},{10... | collective-permute-start | bytes 4718600 | tf_op jit(solution)/shard_map/ppermute | solution.py:21
  71.0 4.2 %collective-permute-start.11 = (bf16[4,64,3072]{2,1,0:T(8,128)(2,1)S(1)}, bf16[4,64,3072]{2,1,0:T(8,128)(2,1)S(1)}, u32[]{:S(2)}, u32[]{:S(2)}) collective-permute-start(bf16[4,64,3072]{2,1,0:T(8,128)(2,1)S(1)} %collective-permute-done.7.refs_1_), channel_id=1, source_target_pairs={{0,4},{4,0},{1,5},{5,1},{2,6},{6,2},{3,7},{7,3},{8,12},{12,8},{9,1... | collective-permute-start | bytes 4718600 | tf_op jit(solution)/shard_map/ppermute | solution.py:278
  72.1 5.7 %collective-permute-start.12 = (bf16[4,64,3072]{2,1,0:T(8,128)(2,1)S(1)}, bf16[4,64,3072]{2,1,0:T(8,128)(2,1)S(1)}, u32[]{:S(2)}, u32[]{:S(2)}) collective-permute-start(bf16[4,64,3072]{2,1,0:T(8,128)(2,1)S(1)} %collective-permute-done.6.refs_2_), channel_id=1, source_target_pairs={{0,4},{4,0},{1,5},{5,1},{2,6},{6,2},{3,7},{7,3},{8,12},{12,8},{9,1... | collective-permute-start | bytes 4718600 | tf_op jit(solution)/shard_map/ppermute | solution.py:278
  72.3 19.9 %collective-permute-start.9 = (bf16[2,64,3072]{2,1,0:T(8,128)(2,1)S(1)}, bf16[2,64,3072]{2,1,0:T(8,128)(2,1)S(1)}, u32[]{:S(2)}, u32[]{:S(2)}) collective-permute-start(bf16[2,64,3072]{2,1,0:T(8,128)(2,1)S(1)} %slice.20), channel_id=1, source_target_pairs={{0,8},{8,16},{16,24},{24,0},{1,9},{9,17},{17,25},{25,1},{2,10},{10... | collective-permute-start | bytes 2359304 | tf_op jit(solution)/shard_map/ppermute | solution.py:21
  72.3 19.8 %collective-permute-start.10 = (bf16[2,64,3072]{2,1,0:T(8,128)(2,1)S(1)}, bf16[2,64,3072]{2,1,0:T(8,128)(2,1)S(1)}, u32[]{:S(2)}, u32[]{:S(2)}) collective-permute-start(bf16[2,64,3072]{2,1,0:T(8,128)(2,1)S(1)} %slice.21), channel_id=1, source_target_pairs={{0,24},{8,0},{16,8},{24,16},{1,25},{9,1},{17,9},{25,17},{2,26},{10... | collective-permute-start | bytes 2359304 | tf_op jit(solution)/shard_map/ppermute | solution.py:21
  75.1 19.2 %collective-permute-start.15 = (bf16[128,3072]{1,0:T(8,128)(2,1)S(1)}, bf16[128,3072]{1,0:T(8,128)(2,1)S(1)}, u32[]{:S(2)}, u32[]{:S(2)}) collective-permute-start(bf16[128,3072]{1,0:T(8,128)(2,1)S(1)} %slice.22), channel_id=1, source_target_pairs={{0,32},{32,64},{64,96},{96,0},{1,33},{33,65},{65,97},{97,1},{2,34}... | collective-permute-start | bytes 2359304 | tf_op jit(solution)/shard_map/ppermute | solution.py:21
  75.2 19.2 %collective-permute-start.16 = (bf16[128,3072]{1,0:T(8,128)(2,1)S(1)}, bf16[128,3072]{1,0:T(8,128)(2,1)S(1)}, u32[]{:S(2)}, u32[]{:S(2)}) collective-permute-start(bf16[128,3072]{1,0:T(8,128)(2,1)S(1)} %slice.23), channel_id=1, source_target_pairs={{0,96},{32,0},{64,32},{96,64},{1,97},{33,1},{65,33},{97,65},{2,98}... | collective-permute-start | bytes 2359304 | tf_op jit(solution)/shard_map/ppermute | solution.py:21
  92.1 10.8 %collective-permute-start.13 = (bf16[2,64,3072]{2,1,0:T(8,128)(2,1)S(1)}, bf16[2,64,3072]{2,1,0:T(8,128)(2,1)S(1)}, u32[]{:S(2)}, u32[]{:S(2)}) collective-permute-start(bf16[2,64,3072]{2,1,0:T(8,128)(2,1)S(1)} %collective-permute-done.9.refs_0_), channel_id=1, source_target_pairs={{0,4},{4,0},{1,5},{5,1},{2,6},{6,2},{3,7},{7,3},{8,12},{12,8},{9,1... | collective-permute-start | bytes 2359304 | tf_op jit(solution)/shard_map/ppermute | solution.py:283
  93.5 9.5 %collective-permute-start.14 = (bf16[2,64,3072]{2,1,0:T(8,128)(2,1)S(1)}, bf16[2,64,3072]{2,1,0:T(8,128)(2,1)S(1)}, u32[]{:S(2)}, u32[]{:S(2)}) collective-permute-start(bf16[2,64,3072]{2,1,0:T(8,128)(2,1)S(1)} %collective-permute-done.10.refs_1_), channel_id=1, source_target_pairs={{0,4},{4,0},{1,5},{5,1},{2,6},{6,2},{3,7},{7,3},{8,12},{12,8},{9,1... | collective-permute-start | bytes 2359304 | tf_op jit(solution)/shard_map/ppermute | solution.py:283
  97.5 8.0 %collective-permute-start.17 = (bf16[18,64,128]{2,1,0:T(8,128)(2,1)S(1)}, bf16[18,64,128]{2,1,0:T(8,128)(2,1)S(1)}, u32[]{:S(2)}, u32[]{:S(2)}) collective-permute-start(bf16[18,64,128]{2,1,0:T(8,128)(2,1)S(1)} %get-tuple-element.71), channel_id=1, source_target_pairs={{0,1},{1,2},{2,3},{3,0},{4,5},{5,6},{6,7},{7,4},{8,9},{9,10},{10,1... | collective-permute-start | bytes 884744 | tf_op jit(solution)/shard_map/ppermute | solution.py:21
  98.9 6.6 %collective-permute-start.18 = (bf16[18,64,128]{2,1,0:T(8,128)(2,1)S(1)}, bf16[18,64,128]{2,1,0:T(8,128)(2,1)S(1)}, u32[]{:S(2)}, u32[]{:S(2)}) collective-permute-start(bf16[18,64,128]{2,1,0:T(8,128)(2,1)S(1)} %get-tuple-element.72), channel_id=1, source_target_pairs={{0,3},{1,0},{2,1},{3,2},{4,7},{5,4},{6,5},{7,6},{8,11},{9,8},{10,9... | collective-permute-start | bytes 884744 | tf_op jit(solution)/shard_map/ppermute | solution.py:21
  105.5 21.2 %collective-permute-start.21 = (bf16[20,64,128]{2,1,0:T(8,128)(2,1)S(1)}, bf16[20,64,128]{2,1,0:T(8,128)(2,1)S(1)}, u32[]{:S(2)}, u32[]{:S(2)}) collective-permute-start(bf16[20,64,128]{2,1,0:T(8,128)(2,1)S(1)} %get-tuple-element.77), channel_id=1, source_target_pairs={{0,2},{1,3},{2,0},{3,1},{4,6},{5,7},{6,4},{7,5},{8,10},{9,11},{10,... | collective-permute-start | bytes 983048 | tf_op jit(solution)/shard_map/ppermute | solution.py:21
  107.7 19.0 %collective-permute-start.20 = (bf16[20,64,128]{2,1,0:T(8,128)(2,1)S(1)}, bf16[20,64,128]{2,1,0:T(8,128)(2,1)S(1)}, u32[]{:S(2)}, u32[]{:S(2)}) collective-permute-start(bf16[20,64,128]{2,1,0:T(8,128)(2,1)S(1)} %get-tuple-element.76), channel_id=1, source_target_pairs={{0,1},{1,2},{2,3},{3,0},{4,5},{5,6},{6,7},{7,4},{8,9},{9,10},{10,1... | collective-permute-start | bytes 983048 | tf_op jit(solution)/shard_map/ppermute | solution.py:21
  108.9 17.8 %collective-permute-start.22 = (bf16[20,64,128]{2,1,0:T(8,128)(2,1)S(1)}, bf16[20,64,128]{2,1,0:T(8,128)(2,1)S(1)}, u32[]{:S(2)}, u32[]{:S(2)}) collective-permute-start(bf16[20,64,128]{2,1,0:T(8,128)(2,1)S(1)} %get-tuple-element.78), channel_id=1, source_target_pairs={{0,3},{1,0},{2,1},{3,2},{4,7},{5,4},{6,5},{7,6},{8,11},{9,8},{10,9... | collective-permute-start | bytes 983048 | tf_op jit(solution)/shard_map/ppermute | solution.py:21
  110.4 16.3 %collective-permute-start.19 = (bf16[18,64,128]{2,1,0:T(8,128)(2,1)S(1)}, bf16[18,64,128]{2,1,0:T(8,128)(2,1)S(1)}, u32[]{:S(2)}, u32[]{:S(2)}) collective-permute-start(bf16[18,64,128]{2,1,0:T(8,128)(2,1)S(1)} %get-tuple-element.74), channel_id=1, source_target_pairs={{0,2},{1,3},{2,0},{3,1},{4,6},{5,7},{6,4},{7,5},{8,10},{9,11},{10,... | collective-permute-start | bytes 884744 | tf_op jit(solution)/shard_map/ppermute | solution.py:21
  (2 other events, 6.2 us)

commit v6 on v5

--- a/solution.py
+++ b/solution.py
@@ -14,6 +14,7 @@
 BF = jnp.bfloat16
 F32 = jnp.float32
 FIRST, SECOND = 18, 20
+NEAR = 9
 MIB = 1 << 20
 
 
@@ -50,11 +51,12 @@
             sums[dy, at] = out[row + 64 * n : row + 64 * n + 64, 128 * half : 128 * half + 128]
 
 
-def early_kernel(meta, *refs):
-    lefts, rights, sums = refs[:6], refs[6:9], refs[9]
+def early_kernel(meta, order, *refs):
+    lefts, rights, sums = refs[:6], refs[6:9], refs[10]
     x = meta[0]
     for n, dx in enumerate((0, 1, 3)):
         near_step(meta, lefts, [rights[n]], (x + dx) % 4, sums)
+    pack(order, sums, {2: refs[9]})
 
 
 def near_step(meta, lefts, right, jp, sums):
@@ -73,16 +75,16 @@
     lax.fori_loop(0, 4, step, 0)
 
 
-def pack(order, sums, outs):
-    for p in range(outs[0].shape[0]):
-        at = order[p]
-        for k, ref in enumerate(outs):
-            ref[p] = sums[k + 1, at].astype(BF)
+def pack(order, sums, outs, first=0):
+    for k, ref in outs.items():
+        for p in range(ref.shape[0]):
+            ref[p] = sums[k, order[first + p]].astype(BF)
 
 
 def middle_kernel(meta, order, *refs):
     near_step(meta, refs[:6], refs[6:8], (meta[0] + 2) % 4, refs[12])
-    pack(order, refs[12], refs[9:12])
+    pack(order, refs[12], {1: refs[9], 3: refs[11]})
+    pack(order, refs[12], {2: refs[10]}, NEAR)
 
 
 def late_kernel(dc, meta, order, *refs):
@@ -96,14 +98,14 @@
         for k in range(4):
             store(meta, sums, out, (x + k) % 4, jp, [(dc, 2)], 64 * k)
     if dc:
-        pack(order, sums, refs[8:11])
-
-
-def grams(kernel, name, scalars, given, sums=None, parts=0):
+        pack(order, sums, dict(zip((1, 2, 3), refs[8:11])))
+
+
+def grams(kernel, name, scalars, given, sums=None, parts=()):
     width = given[0].shape[-1]
     smem = pl.BlockSpec(memory_space=pltpu.SMEM)
     vmem = pl.BlockSpec(memory_space=pltpu.VMEM)
-    shapes = [jax.ShapeDtypeStruct((parts, 64, 128), BF)] * 3 if parts else []
+    shapes = [jax.ShapeDtypeStruct((n, 64, 128), BF) for n in parts]
     shapes += [jax.ShapeDtypeStruct((4, NP + 1, 64, 128), F32)]
     aliases = {}
     if sums is not None:
@@ -155,14 +157,16 @@
 
 
 def route_kernel(index, order1, order2, sums, *refs):
-    out, total = refs[6], refs[7]
-    for order, parts in ((order1, refs[:3]), (order2, refs[3:6])):
-        for p in range(parts[0].shape[0]):
-            at = order[p]
-            value = sums[0, at]
-            for part in parts:
-                value = value + part[p].astype(F32)
-            total[at] = value.astype(BF)
+    near2, one1, one2, one3, two1, two2, two3, out, total = refs
+    for p in range(FIRST):
+        at = order1[p]
+        opposite = near2[p] if p < NEAR else one2[p - NEAR]
+        value = sums[0, at] + one1[p].astype(F32) + opposite.astype(F32)
+        total[at] = (value + one3[p].astype(F32)).astype(BF)
+    for p in range(SECOND):
+        at = order2[p]
+        value = sums[0, at] + two1[p].astype(F32) + two2[p].astype(F32)
+        total[at] = (value + two3[p].astype(F32)).astype(BF)
     total[NP] = jnp.zeros(total.shape[1:], BF)
 
     def some(k, _):
@@ -179,7 +183,7 @@
     return pl.pallas_call(
         route_kernel,
         out_shape=jax.ShapeDtypeStruct((scalars[0].shape[0], 64, 128), BF),
-        in_specs=[smem] * 3 + [vmem] * 7,
+        in_specs=[smem] * 3 + [vmem] * 8,
         out_specs=vmem,
         scratch_shapes=[pltpu.VMEM((NP + 1, 64, 128), BF)],
         compiler_params=pltpu.CompilerParams(vmem_limit_bytes=16 * MIB),
@@ -209,14 +213,17 @@
     lax.fori_loop(0, index.shape[0], clear, 0)
     lax.fori_loop(0, count.shape[0], reset, 0)
     lax.fori_loop(0, owner.shape[0], entry, 0)
-    z1 = meta[1] // 2
-    n1 = n2 = jnp.int32(0)
+    far, z1 = (meta[0] + 2) % 4, meta[1] // 2
+    n0, n1, n2 = jnp.int32(0), jnp.int32(NEAR), jnp.int32(0)
     for j in range(TILES):
         for i in range(j + 1):
-            one = jnp.where((z1 == i % 2) & (n1 < FIRST), 1, 0)
-            order1[jnp.where(one == 1, n1, FIRST)] = j * (j + 1) // 2 + i
-            order2[jnp.where(one == 1, SECOND, n2)] = j * (j + 1) // 2 + i
-            n1, n2 = n1 + one, n2 + 1 - one
+            mine = z1 == i % 2
+            zero = jnp.where(mine & (far != j // 2) & (n0 < NEAR), 1, 0)
+            one = jnp.where(mine & (zero == 0) & (n1 < FIRST), 1, 0)
+            at = jnp.where(zero == 1, n0, jnp.where(one == 1, n1, FIRST))
+            order1[at] = j * (j + 1) // 2 + i
+            order2[jnp.where(zero + one == 1, SECOND, n2)] = j * (j + 1) // 2 + i
+            n0, n1, n2 = n0 + zero, n1 + one, n2 + 1 - zero - one
 
 
 def plan(meta, pair_list, owner, slots):
@@ -269,35 +276,38 @@
     left3, left1 = shift(left, "z", 1), shift(left, "z", -1)
     right3, right1 = shift(right, "x", 1), shift(right, "x", -1)
     swap0 = lax.ppermute(left, "c", other)
-    right3, right1, left3, left1, swap0 = tie(right3, right1, left3, left1, swap0)
-
+    right3, right1 = tie(right3, right1)
+
+    right2a, right2b = shift(right3[:128], "x", 1), shift(right1[128:], "x", -1)
     left2a, left2b = shift(left3[:2], "z", 1), shift(left1[2:], "z", -1)
-    right2a, right2b = shift(right3[:128], "x", 1), shift(right1[128:], "x", -1)
     index, order1, order2 = plan(meta, pair_list, owner, 32 * CAP)
     index, near1, near3 = tie(index, left1, left3)
     swap1, swap3 = lax.ppermute(near1, "c", other), lax.ppermute(near3, "c", other)
     lefts = [left, left1, left3, swap0, swap1, swap3]
     rights = [right, right1, right3]
-    (sums,) = grams(early_kernel, "early", [meta], lefts + rights)
-    left2a, left2b, sums = tie(left2a, left2b, sums)
+    near2, sums = grams(early_kernel, "early", [meta, order1], lefts + rights, parts=[NEAR])
+    near2 = shift(near2, "y", 2)
+    left2a, left2b, sums, near2 = tie(left2a, left2b, sums, near2)
     swap2a, swap2b = lax.ppermute(left2a, "c", other), lax.ppermute(left2b, "c", other)
     far = [right2a, right2b]
 
     def over_y(blocks):
         return [shift(block, "y", k + 1) for k, block in enumerate(blocks)]
 
-    *blocks, sums = grams(middle_kernel, "middle", [meta, order1], lefts + far, sums, FIRST)
+    *blocks, sums = grams(
+        middle_kernel, "middle", [meta, order1], lefts + far, sums, [FIRST, FIRST - NEAR, FIRST]
+    )
     parts = over_y(blocks)
     late = functools.partial(late_kernel, 0)
     (sums,) = grams(late, "late_own", [meta, order2], [left2a, left2b] + rights + far, sums)
     late = functools.partial(late_kernel, 1)
     *blocks, sums = grams(
-        late, "late_other", [meta, order2], [swap2a, swap2b] + rights + far, sums, SECOND
+        late, "late_other", [meta, order2], [swap2a, swap2b] + rights + far, sums, [SECOND] * 3
     )
     blocks[1], parts[0], parts[2] = tie(blocks[1], parts[0], parts[2])
     parts += over_y(blocks)
 
-    routed = route([index, order1, order2], sums, parts).reshape(32, CAP, 64, 128)
+    routed = route([index, order1, order2], sums, [near2] + parts).reshape(32, CAP, 64, 128)
     arrived = lax.all_to_all(routed, ("x", "z", "c"), 0, 0, tiled=True)
     return place(arrived)
 

time: 169 us -> 163 us (0.964)
  waiting for transfers between devices: 77.1 us -> 65.4 us
  starting transfers between devices: 28.3 us -> 33.8 us
    ppermute x18 -> x19, waiting for transfers between devices: 77.1 us -> 65.4 us  [shift(): return lax.ppermute(a, axis, [(i, (i + d) % 4) for i in range(4)])]
    ppermute x18 -> x19, starting transfers between devices: 24.8 us -> 28.5 us  [shift(): return lax.ppermute(a, axis, [(i, (i + d) % 4) for i in range(4)])]
  transfers between devices with their start and end apart: 23 -> 24, of which waited for: 10 -> 8; matrix products, arithmetic and copies ran while one was open for 0% -> 0% of each run, Pallas kernels for 11% -> 11%
where the time goes in v6:
time: 163 us; the launch traced here: 162 us
  waiting for transfers between devices  65.4 us (40%)
  blocking collectives  36.5 us (22%)
  starting transfers between devices  33.8 us (21%)
  Pallas kernels  24.2 us (15%)
  local copies, waits for them, and re-layouts  2 us (1%)
    ppermute x19, waiting for transfers between devices, shift(): return lax.ppermute(a, axis, [(i, (i + d) % 4) for i in range(4)])  65.4 us
    all_to_all x1, blocking collectives, on_device(): arrived = lax.all_to_all(routed, ('x', 'z', 'c'), 0, 0, tiled=True)  36.5 us
    ppermute x19, starting transfers between devices, shift(): return lax.ppermute(a, axis, [(i, (i + d) % 4) for i in range(4)])  28.5 us
    pallas_call x4, Pallas kernels, grams(): pl.pallas_call(kernel, out_shape=shapes, in_specs=[smem] * len(scalars) +...  14.5 us
    pallas_call x1, Pallas kernels, place(): pl.pallas_call(place_kernel, grid=(CAP,), out_shape=jax.ShapeDtypeStruct(...  4.24 us
    pallas_call x1, Pallas kernels, plan(): pl.pallas_call(plan_kernel, out_shape=[jax.ShapeDtypeStruct((n,), jnp.int...  3.47 us
  transfers between devices with their start and end apart: 24, of which 8 were waited for; matrix products, arithmetic and copies ran while one was open for 0% of the time, Pallas kernels for 11%

profile of v6, /device:TPU:1, one launch (start us, length us, event | category | flops | bytes accessed | tf_op | source)
XLA Modules:
  0.0 162.4 jit_solution(15612359605023161521)
XLA Ops:
  0.0 1.8 %copy.8.dens = bf16[256,3000]{1,0:T(8,128)(2,1)S(1)} copy(bf16[256,3000]{0,1:T(8,128)(2,1)} %param.4) | data formatting | bytes 3072000 | tf_op args[0]
  2.8 4.5 %collective-permute-start = (bf16[128,3072]{1,0:T(8,128)(2,1)S(1)}, bf16[128,3072]{1,0:T(8,128)(2,1)S(1)}, u32[]{:S(2)}, u32[]{:S(2)}) collective-permute-start(bf16[128,3072]{1,0:T(8,128)(2,1)S(1)} %get-tuple-element.44), channel_id=1, source_target_pairs={{0,16},{8,24},{16,0},{24,8},{1,17},{9,25},{17,1},{25,9},{2,18},{10... | collective-permute-start | bytes 2359304 | tf_op jit(solution)/shard_map/ppermute | solution.py:22
  7.3 2.5 %collective-permute-start.1 = (bf16[1,64,3072]{2,1,0:T(8,128)(2,1)S(1)}, bf16[1,64,3072]{2,1,0:T(8,128)(2,1)S(1)}, u32[]{:S(2)}, u32[]{:S(2)}) collective-permute-start(bf16[1,64,3072]{2,1,0:T(8,128)(2,1)S(1)} %get-tuple-element.45), channel_id=1, source_target_pairs={{0,96},{32,0},{64,32},{96,64},{1,97},{33,1},{65,33},{97,65},{2,98}... | collective-permute-start | bytes 1179656 | tf_op jit(solution)/shard_map/ppermute | solution.py:22
  10.9 7.1 %collective-permute-done.1 = bf16[1,64,3072]{2,1,0:T(8,128)(2,1)S(1)} collective-permute-done((bf16[1,64,3072]{2,1,0:T(8,128)(2,1)S(1)}, bf16[1,64,3072]{2,1,0:T(8,128)(2,1)S(1)}, u32[]{:S(2)}, u32[]{:S(2)}) %collective-permute-start.1) | collective-permute-done | bytes 393248 | tf_op jit(solution)/shard_map/ppermute | solution.py:22
  18.0 2.7 %collective-permute-done.2 = bf16[1,64,3072]{2,1,0:T(8,128)(2,1)S(1)} collective-permute-done((bf16[1,64,3072]{2,1,0:T(8,128)(2,1)S(1)}, bf16[1,64,3072]{2,1,0:T(8,128)(2,1)S(1)}, u32[]{:S(2)}, u32[]{:S(2)}) %collective-permute-start.2) | collective-permute-done | bytes 393248 | tf_op jit(solution)/shard_map/ppermute | solution.py:22
  20.7 10.1 %collective-permute-done.3 = bf16[1,64,3072]{2,1,0:T(8,128)(2,1)S(1)} collective-permute-done((bf16[1,64,3072]{2,1,0:T(8,128)(2,1)S(1)}, bf16[1,64,3072]{2,1,0:T(8,128)(2,1)S(1)}, u32[]{:S(2)}, u32[]{:S(2)}) %collective-permute-start.3) | collective-permute-done | bytes 393248 | tf_op jit(solution)/shard_map/ppermute | solution.py:22
  31.9 1.9 %collective-permute-start.4 = (bf16[4,64,3072]{2,1,0:T(8,128)(2,1)S(1)}, bf16[4,64,3072]{2,1,0:T(8,128)(2,1)S(1)}, u32[]{:S(2)}, u32[]{:S(2)}) collective-permute-start(bf16[4,64,3072]{2,1,0:T(8,128)(2,1)S(1)} %pad_maximum_fusion.1.refs_0_), channel_id=1, source_target_pairs={{0,24},{8,0},{16,8},{24,16},{1,25},{9,1},{17,9},{25,17},{2,26},{10... | collective-permute-start | bytes 4718600 | tf_op jit(solution)/shard_map/ppermute | solution.py:22
  35.3 3.5 %plan.1 = (s32[128]{0:T(128)S(1)}, s32[19]{0:T(128)S(1)}, s32[21]{0:T(128)S(1)}) custom-call(s32[4]{0:T(128)S(1)} %pad_add_fusion.meta, s32[64]{0:T(128)S(1)} %get-tuple-element.80.first, s32[64]{0:T(128)S(1)} %get-tuple-element.79.second, s32[64]{0:T(128)S(1)} %bitcast.13), custom_call_target="tpu_custom_call" | custom-call | tf_op jit(solution)/shard_map/plan/pallas_call | solution.py:231
  38.8 1.7 %collective-permute-start.8 = (bf16[4,64,3072]{2,1,0:T(8,128)(2,1)S(1)}, bf16[4,64,3072]{2,1,0:T(8,128)(2,1)S(1)}, u32[]{:S(2)}, u32[]{:S(2)}) collective-permute-start(bf16[4,64,3072]{2,1,0:T(8,128)(2,1)S(1)} %pad_maximum_fusion.1.refs_0_), channel_id=1, source_target_pairs={{0,4},{4,0},{1,5},{5,1},{2,6},{6,2},{3,7},{7,3},{8,12},{12,8},{9,1... | collective-permute-start | bytes 4718600 | tf_op jit(solution)/shard_map/ppermute | solution.py:278
  40.5 27.4 %collective-permute-done.5.refs_2_ = bf16[4,64,3072]{2,1,0:T(8,128)(2,1)S(1)} collective-permute-done((bf16[4,64,3072]{2,1,0:T(8,128)(2,1)S(1)}, bf16[4,64,3072]{2,1,0:T(8,128)(2,1)S(1)}, u32[]{:S(2)}, u32[]{:S(2)}) %collective-permute-start.5) | collective-permute-done | bytes 1572896 | tf_op jit(solution)/shard_map/ppermute | solution.py:22
  69.4 2.7 %collective-permute-start.7 = (bf16[2,64,3072]{2,1,0:T(8,128)(2,1)S(1)}, bf16[2,64,3072]{2,1,0:T(8,128)(2,1)S(1)}, u32[]{:S(2)}, u32[]{:S(2)}) collective-permute-start(bf16[2,64,3072]{2,1,0:T(8,128)(2,1)S(1)} %slice.25), channel_id=1, source_target_pairs={{0,24},{8,0},{16,8},{24,16},{1,25},{9,1},{17,9},{25,17},{2,26},{10... | collective-permute-start | bytes 2359304 | tf_op jit(solution)/shard_map/ppermute | solution.py:22
  72.4 2.7 %collective-permute-start.17 = (bf16[128,3072]{1,0:T(8,128)(2,1)S(1)}, bf16[128,3072]{1,0:T(8,128)(2,1)S(1)}, u32[]{:S(2)}, u32[]{:S(2)}) collective-permute-start(bf16[128,3072]{1,0:T(8,128)(2,1)S(1)} %slice.23), channel_id=1, source_target_pairs={{0,96},{32,0},{64,32},{96,64},{1,97},{33,1},{65,33},{97,65},{2,98}... | collective-permute-start | bytes 2359304 | tf_op jit(solution)/shard_map/ppermute | solution.py:22
  75.0 6.5 %early.1 = (bf16[9,64,128]{2,1,0:T(8,128)(2,1)S(1)}, f32[4,37,64,128]{3,2,1,0:T(8,128)S(1)}) custom-call(s32[4]{0:T(128)S(1)} %pad_add_fusion.meta, s32[19]{0:T(128)S(1)} %get-tuple-element.55.order.order1, bf16[4,64,3072]{2,1,0:T(8,128)(2,1)S(1)} %pad_maximum_fusion.1.refs_0_, bf16[4,64,3072]{2,1,0:T(8,128)(2,1)S(1)} %collective-permute-done.4.refs_1_, ...), custom_call_target="tpu_custom_call" | custom-call | flops 3221225472 | bytes 1048576 | tf_op jit(solution)/shard_map/early/pallas_call | solution.py:114
  81.5 3.0 %collective-permute-start.13 = (bf16[9,64,128]{2,1,0:T(8,128)(2,1)S(1)}, bf16[9,64,128]{2,1,0:T(8,128)(2,1)S(1)}, u32[]{:S(2)}, u32[]{:S(2)}) collective-permute-start(bf16[9,64,128]{2,1,0:T(8,128)(2,1)S(1)} %get-tuple-element.63), channel_id=1, source_target_pairs={{0,2},{1,3},{2,0},{3,1},{4,6},{5,7},{6,4},{7,5},{8,10},{9,11},{10,... | collective-permute-start | bytes 442376 | tf_op jit(solution)/shard_map/ppermute | solution.py:22
  84.5 3.8 %collective-permute-done.6.refs_0_ = bf16[2,64,3072]{2,1,0:T(8,128)(2,1)S(1)} collective-permute-done((bf16[2,64,3072]{2,1,0:T(8,128)(2,1)S(1)}, bf16[2,64,3072]{2,1,0:T(8,128)(2,1)S(1)}, u32[]{:S(2)}, u32[]{:S(2)}) %collective-permute-start.6) | collective-permute-done | bytes 786464 | tf_op jit(solution)/shard_map/ppermute | solution.py:22
  88.4 2.2 %collective-permute-start.14 = (bf16[2,64,3072]{2,1,0:T(8,128)(2,1)S(1)}, bf16[2,64,3072]{2,1,0:T(8,128)(2,1)S(1)}, u32[]{:S(2)}, u32[]{:S(2)}) collective-permute-start(bf16[2,64,3072]{2,1,0:T(8,128)(2,1)S(1)} %collective-permute-done.6.refs_0_), channel_id=1, source_target_pairs={{0,4},{4,0},{1,5},{5,1},{2,6},{6,2},{3,7},{7,3},{8,12},{12,8},{9,1... | collective-permute-start | bytes 2359304 | tf_op jit(solution)/shard_map/ppermute | solution.py:291
  90.9 3.1 %middle.1 = (bf16[18,64,128]{2,1,0:T(8,128)(2,1)S(1)}, bf16[9,64,128]{2,1,0:T(8,128)(2,1)S(1)}, bf16[18,64,128]{2,1,0:T(8,128)(2,1)S(1)}, f32[4,37,64,128]{3,2,1,0:T(8,128)S(1)}) custom-call(s32[4]{0:T(128)S(1)} %pad_add_fusion.meta, s32[19]{0:T(128)S(1)} %get-tuple-element.55.order.order1, ...), custom_call_target="tpu_custom_call", output_to_operand_aliasing={{3}: (10, {})} | custom-call | flops 3221225472 | bytes 1048576 | tf_op jit(solution)/shard_map/middle/pallas_call | solution.py:114
  97.1 2.4 %late_own.1.refs_7_ = f32[4,37,64,128]{3,2,1,0:T(8,128)S(1)} custom-call(s32[4]{0:T(128)S(1)} %pad_add_fusion.meta, s32[21]{0:T(128)S(1)} %get-tuple-element.56.order.order2, bf16[2,64,3072]{2,1,0:T(8,128)(2,1)S(1)} %collective-permute-done.6.refs_0_, bf16[2,64,3072]{2,1,0:T(8,128)(2,1)S(1)} %collective-permute-done.7.refs_1_, ...), custom_call_target="tpu_custom_call", output_to_operand_aliasing={{}: (9, {})} | custom-call | flops 3221225472 | bytes 1048576 | tf_op jit(solution)/shard_map/late_own/pallas_call | solution.py:114
  99.5 2.5 %late_other.1 = (bf16[20,64,128]{2,1,0:T(8,128)(2,1)S(1)}, bf16[20,64,128]{2,1,0:T(8,128)(2,1)S(1)}, bf16[20,64,128]{2,1,0:T(8,128)(2,1)S(1)}, f32[4,37,64,128]{3,2,1,0:T(8,128)S(1)}) custom-call(s32[4]{0:T(128)S(1)} %pad_add_fusion.meta, s32[21]{0:T(128)S(1)} %get-tuple-element.56.order.order2, ...), custom_call_target="tpu_custom_call", output_to_operand_aliasing={{3}: (9, {})} | custom-call | flops 3221225472 | bytes 1048576 | tf_op jit(solution)/shard_map/late_other/pallas_call | solution.py:114
  102.0 1.8 %collective-permute-start.22 = (bf16[20,64,128]{2,1,0:T(8,128)(2,1)S(1)}, bf16[20,64,128]{2,1,0:T(8,128)(2,1)S(1)}, u32[]{:S(2)}, u32[]{:S(2)}) collective-permute-start(bf16[20,64,128]{2,1,0:T(8,128)(2,1)S(1)} %get-tuple-element.77), channel_id=1, source_target_pairs={{0,2},{1,3},{2,0},{3,1},{4,6},{5,7},{6,4},{7,5},{8,10},{9,11},{10,... | collective-permute-start | bytes 983048 | tf_op jit(solution)/shard_map/ppermute | solution.py:22
  104.4 2.1 %collective-permute-start.23 = (bf16[20,64,128]{2,1,0:T(8,128)(2,1)S(1)}, bf16[20,64,128]{2,1,0:T(8,128)(2,1)S(1)}, u32[]{:S(2)}, u32[]{:S(2)}) collective-permute-start(bf16[20,64,128]{2,1,0:T(8,128)(2,1)S(1)} %get-tuple-element.78), channel_id=1, source_target_pairs={{0,3},{1,0},{2,1},{3,2},{4,7},{5,4},{6,5},{7,6},{8,11},{9,8},{10,9... | collective-permute-start | bytes 983048 | tf_op jit(solution)/shard_map/ppermute | solution.py:22
  106.5 13.3 %collective-permute-done.20.refs_2_ = bf16[9,64,128]{2,1,0:T(8,128)(2,1)S(1)} collective-permute-done((bf16[9,64,128]{2,1,0:T(8,128)(2,1)S(1)}, bf16[9,64,128]{2,1,0:T(8,128)(2,1)S(1)}, u32[]{:S(2)}, u32[]{:S(2)}) %collective-permute-start.20) | collective-permute-done | bytes 147488 | tf_op jit(solution)/shard_map/ppermute | solution.py:22
  121.7 36.5 %all_to_all.5.got = bf16[32,4,64,128]{3,2,1,0:T(8,128)(2,1)} all-to-all(bf16[32,4,64,128]{3,2,1,0:T(8,128)(2,1)S(1)} %bitcast.11), channel_id=1, replica_groups=mesh['x'=4,'z'=4,'c'=2,'y'=4] {'x','z','c'}, dimensions={0} | all-to-all | bytes 4194304 | tf_op jit(solution)/shard_map/all_to_all | solution.py:311
  158.2 4.2 %place.1 = f32[4,256,1024]{2,1,0:T(8,128)} custom-call(bf16[32,4,64,128]{3,2,1,0:T(8,128)(2,1)} %all_to_all.5.got), custom_call_target="tpu_custom_call" | custom-call | tf_op jit(solution)/shard_map/place/pallas_call | solution.py:252
  (48 shorter events, 12.2 us)
Async XLA Ops:
  2.8 28.0 %collective-permute-start = (bf16[128,3072]{1,0:T(8,128)(2,1)S(1)}, bf16[128,3072]{1,0:T(8,128)(2,1)S(1)}, u32[]{:S(2)}, u32[]{:S(2)}) collective-permute-start(bf16[128,3072]{1,0:T(8,128)(2,1)S(1)} %get-tuple-element.44), channel_id=1, source_target_pairs={{0,16},{8,24},{16,0},{24,8},{1,17},{9,25},{17,1},{25,9},{2,18},{10... | collective-permute-start | bytes 2359304 | tf_op jit(solution)/shard_map/ppermute | solution.py:22
  7.3 10.7 %collective-permute-start.1 = (bf16[1,64,3072]{2,1,0:T(8,128)(2,1)S(1)}, bf16[1,64,3072]{2,1,0:T(8,128)(2,1)S(1)}, u32[]{:S(2)}, u32[]{:S(2)}) collective-permute-start(bf16[1,64,3072]{2,1,0:T(8,128)(2,1)S(1)} %get-tuple-element.45), channel_id=1, source_target_pairs={{0,96},{32,0},{64,32},{96,64},{1,97},{33,1},{65,33},{97,65},{2,98}... | collective-permute-start | bytes 1179656 | tf_op jit(solution)/shard_map/ppermute | solution.py:22
  9.8 10.9 %collective-permute-start.2 = (bf16[1,64,3072]{2,1,0:T(8,128)(2,1)S(1)}, bf16[1,64,3072]{2,1,0:T(8,128)(2,1)S(1)}, u32[]{:S(2)}, u32[]{:S(2)}) collective-permute-start(bf16[1,64,3072]{2,1,0:T(8,128)(2,1)S(1)} %get-tuple-element.46), channel_id=1, source_target_pairs={{0,64},{32,96},{64,0},{96,32},{1,65},{33,97},{65,1},{97,33},{2,66}... | collective-permute-start | bytes 1179656 | tf_op jit(solution)/shard_map/ppermute | solution.py:22
  10.3 20.4 %collective-permute-start.3 = (bf16[1,64,3072]{2,1,0:T(8,128)(2,1)S(1)}, bf16[1,64,3072]{2,1,0:T(8,128)(2,1)S(1)}, u32[]{:S(2)}, u32[]{:S(2)}) collective-permute-start(bf16[1,64,3072]{2,1,0:T(8,128)(2,1)S(1)} %get-tuple-element.47), channel_id=1, source_target_pairs={{0,32},{32,64},{64,96},{96,0},{1,33},{33,65},{65,97},{97,1},{2,34}... | collective-permute-start | bytes 1179656 | tf_op jit(solution)/shard_map/ppermute | solution.py:22
  31.1 36.8 %collective-permute-start.5 = (bf16[4,64,3072]{2,1,0:T(8,128)(2,1)S(1)}, bf16[4,64,3072]{2,1,0:T(8,128)(2,1)S(1)}, u32[]{:S(2)}, u32[]{:S(2)}) collective-permute-start(bf16[4,64,3072]{2,1,0:T(8,128)(2,1)S(1)} %pad_maximum_fusion.1.refs_0_), channel_id=1, source_target_pairs={{0,8},{8,16},{16,24},{24,0},{1,9},{9,17},{17,25},{25,1},{2,10},{10... | collective-permute-start | bytes 4718600 | tf_op jit(solution)/shard_map/ppermute | solution.py:22
  31.9 35.9 %collective-permute-start.4 = (bf16[4,64,3072]{2,1,0:T(8,128)(2,1)S(1)}, bf16[4,64,3072]{2,1,0:T(8,128)(2,1)S(1)}, u32[]{:S(2)}, u32[]{:S(2)}) collective-permute-start(bf16[4,64,3072]{2,1,0:T(8,128)(2,1)S(1)} %pad_maximum_fusion.1.refs_0_), channel_id=1, source_target_pairs={{0,24},{8,0},{16,8},{24,16},{1,25},{9,1},{17,9},{25,17},{2,26},{10... | collective-permute-start | bytes 4718600 | tf_op jit(solution)/shard_map/ppermute | solution.py:22
  33.8 35.5 %collective-permute-start.12 = (bf16[256,3072]{1,0:T(8,128)(2,1)S(1)}, bf16[256,3072]{1,0:T(8,128)(2,1)S(1)}, u32[]{:S(2)}, u32[]{:S(2)}) collective-permute-start(bf16[256,3072]{1,0:T(8,128)(2,1)S(1)} %pad_maximum_fusion.refs_6_.refs_2_), channel_id=1, source_target_pairs={{0,96},{32,0},{64,32},{96,64},{1,97},{33,1},{65,33},{97,65},{2,98}... | collective-permute-start | bytes 4718600 | tf_op jit(solution)/shard_map/ppermute | solution.py:22
  33.8 35.6 %collective-permute-start.11 = (bf16[256,3072]{1,0:T(8,128)(2,1)S(1)}, bf16[256,3072]{1,0:T(8,128)(2,1)S(1)}, u32[]{:S(2)}, u32[]{:S(2)}) collective-permute-start(bf16[256,3072]{1,0:T(8,128)(2,1)S(1)} %pad_maximum_fusion.refs_6_.refs_2_), channel_id=1, source_target_pairs={{0,32},{32,64},{64,96},{96,0},{1,33},{33,65},{65,97},{97,1},{2,34}... | collective-permute-start | bytes 4718600 | tf_op jit(solution)/shard_map/ppermute | solution.py:22
  38.8 33.5 %collective-permute-start.8 = (bf16[4,64,3072]{2,1,0:T(8,128)(2,1)S(1)}, bf16[4,64,3072]{2,1,0:T(8,128)(2,1)S(1)}, u32[]{:S(2)}, u32[]{:S(2)}) collective-permute-start(bf16[4,64,3072]{2,1,0:T(8,128)(2,1)S(1)} %pad_maximum_fusion.1.refs_0_), channel_id=1, source_target_pairs={{0,4},{4,0},{1,5},{5,1},{2,6},{6,2},{3,7},{7,3},{8,12},{12,8},{9,1... | collective-permute-start | bytes 4718600 | tf_op jit(solution)/shard_map/ppermute | solution.py:278
  67.8 4.5 %collective-permute-start.9 = (bf16[4,64,3072]{2,1,0:T(8,128)(2,1)S(1)}, bf16[4,64,3072]{2,1,0:T(8,128)(2,1)S(1)}, u32[]{:S(2)}, u32[]{:S(2)}) collective-permute-start(bf16[4,64,3072]{2,1,0:T(8,128)(2,1)S(1)} %collective-permute-done.4.refs_1_), channel_id=1, source_target_pairs={{0,4},{4,0},{1,5},{5,1},{2,6},{6,2},{3,7},{7,3},{8,12},{12,8},{9,1... | collective-permute-start | bytes 4718600 | tf_op jit(solution)/shard_map/ppermute | solution.py:285
  69.2 5.8 %collective-permute-start.10 = (bf16[4,64,3072]{2,1,0:T(8,128)(2,1)S(1)}, bf16[4,64,3072]{2,1,0:T(8,128)(2,1)S(1)}, u32[]{:S(2)}, u32[]{:S(2)}) collective-permute-start(bf16[4,64,3072]{2,1,0:T(8,128)(2,1)S(1)} %collective-permute-done.5.refs_2_), channel_id=1, source_target_pairs={{0,4},{4,0},{1,5},{5,1},{2,6},{6,2},{3,7},{7,3},{8,12},{12,8},{9,1... | collective-permute-start | bytes 4718600 | tf_op jit(solution)/shard_map/ppermute | solution.py:285
  69.3 19.1 %collective-permute-start.6 = (bf16[2,64,3072]{2,1,0:T(8,128)(2,1)S(1)}, bf16[2,64,3072]{2,1,0:T(8,128)(2,1)S(1)}, u32[]{:S(2)}, u32[]{:S(2)}) collective-permute-start(bf16[2,64,3072]{2,1,0:T(8,128)(2,1)S(1)} %slice.24), channel_id=1, source_target_pairs={{0,8},{8,16},{16,24},{24,0},{1,9},{9,17},{17,25},{25,1},{2,10},{10... | collective-permute-start | bytes 2359304 | tf_op jit(solution)/shard_map/ppermute | solution.py:22
  69.4 19.0 %collective-permute-start.7 = (bf16[2,64,3072]{2,1,0:T(8,128)(2,1)S(1)}, bf16[2,64,3072]{2,1,0:T(8,128)(2,1)S(1)}, u32[]{:S(2)}, u32[]{:S(2)}) collective-permute-start(bf16[2,64,3072]{2,1,0:T(8,128)(2,1)S(1)} %slice.25), channel_id=1, source_target_pairs={{0,24},{8,0},{16,8},{24,16},{1,25},{9,1},{17,9},{25,17},{2,26},{10... | collective-permute-start | bytes 2359304 | tf_op jit(solution)/shard_map/ppermute | solution.py:22
  72.3 18.6 %collective-permute-start.16 = (bf16[128,3072]{1,0:T(8,128)(2,1)S(1)}, bf16[128,3072]{1,0:T(8,128)(2,1)S(1)}, u32[]{:S(2)}, u32[]{:S(2)}) collective-permute-start(bf16[128,3072]{1,0:T(8,128)(2,1)S(1)} %slice.22), channel_id=1, source_target_pairs={{0,32},{32,64},{64,96},{96,0},{1,33},{33,65},{65,97},{97,1},{2,34}... | collective-permute-start | bytes 2359304 | tf_op jit(solution)/shard_map/ppermute | solution.py:22
  72.4 18.5 %collective-permute-start.17 = (bf16[128,3072]{1,0:T(8,128)(2,1)S(1)}, bf16[128,3072]{1,0:T(8,128)(2,1)S(1)}, u32[]{:S(2)}, u32[]{:S(2)}) collective-permute-start(bf16[128,3072]{1,0:T(8,128)(2,1)S(1)} %slice.23), channel_id=1, source_target_pairs={{0,96},{32,0},{64,32},{96,64},{1,97},{33,1},{65,33},{97,65},{2,98}... | collective-permute-start | bytes 2359304 | tf_op jit(solution)/shard_map/ppermute | solution.py:22
  81.5 6.9 %collective-permute-start.13 = (bf16[9,64,128]{2,1,0:T(8,128)(2,1)S(1)}, bf16[9,64,128]{2,1,0:T(8,128)(2,1)S(1)}, u32[]{:S(2)}, u32[]{:S(2)}) collective-permute-start(bf16[9,64,128]{2,1,0:T(8,128)(2,1)S(1)} %get-tuple-element.63), channel_id=1, source_target_pairs={{0,2},{1,3},{2,0},{3,1},{4,6},{5,7},{6,4},{7,5},{8,10},{9,11},{10,... | collective-permute-start | bytes 442376 | tf_op jit(solution)/shard_map/ppermute | solution.py:22
  88.4 11.1 %collective-permute-start.14 = (bf16[2,64,3072]{2,1,0:T(8,128)(2,1)S(1)}, bf16[2,64,3072]{2,1,0:T(8,128)(2,1)S(1)}, u32[]{:S(2)}, u32[]{:S(2)}) collective-permute-start(bf16[2,64,3072]{2,1,0:T(8,128)(2,1)S(1)} %collective-permute-done.6.refs_0_), channel_id=1, source_target_pairs={{0,4},{4,0},{1,5},{5,1},{2,6},{6,2},{3,7},{7,3},{8,12},{12,8},{9,1... | collective-permute-start | bytes 2359304 | tf_op jit(solution)/shard_map/ppermute | solution.py:291
  90.6 8.9 %collective-permute-start.15 = (bf16[2,64,3072]{2,1,0:T(8,128)(2,1)S(1)}, bf16[2,64,3072]{2,1,0:T(8,128)(2,1)S(1)}, u32[]{:S(2)}, u32[]{:S(2)}) collective-permute-start(bf16[2,64,3072]{2,1,0:T(8,128)(2,1)S(1)} %collective-permute-done.7.refs_1_), channel_id=1, source_target_pairs={{0,4},{4,0},{1,5},{5,1},{2,6},{6,2},{3,7},{7,3},{8,12},{12,8},{9,1... | collective-permute-start | bytes 2359304 | tf_op jit(solution)/shard_map/ppermute | solution.py:291
  94.0 8.0 %collective-permute-start.18 = (bf16[18,64,128]{2,1,0:T(8,128)(2,1)S(1)}, bf16[18,64,128]{2,1,0:T(8,128)(2,1)S(1)}, u32[]{:S(2)}, u32[]{:S(2)}) collective-permute-start(bf16[18,64,128]{2,1,0:T(8,128)(2,1)S(1)} %get-tuple-element.71), channel_id=1, source_target_pairs={{0,1},{1,2},{2,3},{3,0},{4,5},{5,6},{6,7},{7,4},{8,9},{9,10},{10,1... | collective-permute-start | bytes 884744 | tf_op jit(solution)/shard_map/ppermute | solution.py:22
  95.4 6.6 %collective-permute-start.19 = (bf16[18,64,128]{2,1,0:T(8,128)(2,1)S(1)}, bf16[18,64,128]{2,1,0:T(8,128)(2,1)S(1)}, u32[]{:S(2)}, u32[]{:S(2)}) collective-permute-start(bf16[18,64,128]{2,1,0:T(8,128)(2,1)S(1)} %get-tuple-element.72), channel_id=1, source_target_pairs={{0,3},{1,0},{2,1},{3,2},{4,7},{5,4},{6,5},{7,6},{8,11},{9,8},{10,9... | collective-permute-start | bytes 884744 | tf_op jit(solution)/shard_map/ppermute | solution.py:22
  102.0 17.8 %collective-permute-start.22 = (bf16[20,64,128]{2,1,0:T(8,128)(2,1)S(1)}, bf16[20,64,128]{2,1,0:T(8,128)(2,1)S(1)}, u32[]{:S(2)}, u32[]{:S(2)}) collective-permute-start(bf16[20,64,128]{2,1,0:T(8,128)(2,1)S(1)} %get-tuple-element.77), channel_id=1, source_target_pairs={{0,2},{1,3},{2,0},{3,1},{4,6},{5,7},{6,4},{7,5},{8,10},{9,11},{10,... | collective-permute-start | bytes 983048 | tf_op jit(solution)/shard_map/ppermute | solution.py:22
  103.9 16.8 %collective-permute-start.21 = (bf16[20,64,128]{2,1,0:T(8,128)(2,1)S(1)}, bf16[20,64,128]{2,1,0:T(8,128)(2,1)S(1)}, u32[]{:S(2)}, u32[]{:S(2)}) collective-permute-start(bf16[20,64,128]{2,1,0:T(8,128)(2,1)S(1)} %get-tuple-element.76), channel_id=1, source_target_pairs={{0,1},{1,2},{2,3},{3,0},{4,5},{5,6},{6,7},{7,4},{8,9},{9,10},{10,1... | collective-permute-start | bytes 983048 | tf_op jit(solution)/shard_map/ppermute | solution.py:22
  104.4 16.2 %collective-permute-start.23 = (bf16[20,64,128]{2,1,0:T(8,128)(2,1)S(1)}, bf16[20,64,128]{2,1,0:T(8,128)(2,1)S(1)}, u32[]{:S(2)}, u32[]{:S(2)}) collective-permute-start(bf16[20,64,128]{2,1,0:T(8,128)(2,1)S(1)} %get-tuple-element.78), channel_id=1, source_target_pairs={{0,3},{1,0},{2,1},{3,2},{4,7},{5,4},{6,5},{7,6},{8,11},{9,8},{10,9... | collective-permute-start | bytes 983048 | tf_op jit(solution)/shard_map/ppermute | solution.py:22
  106.5 13.3 %collective-permute-start.20 = (bf16[9,64,128]{2,1,0:T(8,128)(2,1)S(1)}, bf16[9,64,128]{2,1,0:T(8,128)(2,1)S(1)}, u32[]{:S(2)}, u32[]{:S(2)}) collective-permute-start(bf16[9,64,128]{2,1,0:T(8,128)(2,1)S(1)} %get-tuple-element.74), channel_id=1, source_target_pairs={{0,2},{1,3},{2,0},{3,1},{4,6},{5,7},{6,4},{7,5},{8,10},{9,11},{10,... | collective-permute-start | bytes 442376 | tf_op jit(solution)/shard_map/ppermute | solution.py:22
  (3 other events, 10.8 us)

commit v7 on v6

--- a/solution.py
+++ b/solution.py
@@ -13,7 +13,7 @@
 NP = TILES * (TILES + 1) // 2
 BF = jnp.bfloat16
 F32 = jnp.float32
-FIRST, SECOND = 18, 20
+FIRST, SECOND = 16, 20
 NEAR = 9
 MIB = 1 << 20
 
@@ -56,7 +56,7 @@
     x = meta[0]
     for n, dx in enumerate((0, 1, 3)):
         near_step(meta, lefts, [rights[n]], (x + dx) % 4, sums)
-    pack(order, sums, {2: refs[9]})
+    pack(sums, 2, order, 0, NEAR, refs[9])
 
 
 def near_step(meta, lefts, right, jp, sums):
@@ -75,19 +75,18 @@
     lax.fori_loop(0, 4, step, 0)
 
 
-def pack(order, sums, outs, first=0):
-    for k, ref in outs.items():
-        for p in range(ref.shape[0]):
-            ref[p] = sums[k, order[first + p]].astype(BF)
+def pack(sums, dy, order, first, size, ref, at=0):
+    for p in range(size):
+        ref[at + p] = sums[dy, order[first + p]].astype(BF)
 
 
 def middle_kernel(meta, order, *refs):
-    near_step(meta, refs[:6], refs[6:8], (meta[0] + 2) % 4, refs[12])
-    pack(order, refs[12], {1: refs[9], 3: refs[11]})
-    pack(order, refs[12], {2: refs[10]}, NEAR)
-
-
-def late_kernel(dc, meta, order, *refs):
+    near_step(meta, refs[:6], refs[6:8], (meta[0] + 2) % 4, refs[11])
+    pack(refs[11], 1, order, 0, FIRST, refs[9])
+    pack(refs[11], 3, order, 0, FIRST, refs[10])
+
+
+def late_kernel(dc, meta, order1, order2, *refs):
     late, rights = refs[:2], [refs[2:3], refs[3:4], refs[5:7], refs[4:5]]
     sums = refs[-1]
     x = meta[0]
@@ -98,7 +97,10 @@
         for k in range(4):
             store(meta, sums, out, (x + k) % 4, jp, [(dc, 2)], 64 * k)
     if dc:
-        pack(order, sums, dict(zip((1, 2, 3), refs[8:11])))
+        pack(sums, 1, order2, 0, SECOND, refs[8])
+        pack(sums, 2, order1, NEAR, FIRST - NEAR, refs[9])
+        pack(sums, 2, order2, 0, SECOND, refs[9], FIRST - NEAR)
+        pack(sums, 3, order2, 0, SECOND, refs[10])
 
 
 def grams(kernel, name, scalars, given, sums=None, parts=()):
@@ -157,15 +159,15 @@
 
 
 def route_kernel(index, order1, order2, sums, *refs):
-    near2, one1, one2, one3, two1, two2, two3, out, total = refs
+    near2, one1, one3, two1, two2, two3, out, total = refs
     for p in range(FIRST):
         at = order1[p]
-        opposite = near2[p] if p < NEAR else one2[p - NEAR]
+        opposite = near2[p] if p < NEAR else two2[p - NEAR]
         value = sums[0, at] + one1[p].astype(F32) + opposite.astype(F32)
         total[at] = (value + one3[p].astype(F32)).astype(BF)
     for p in range(SECOND):
         at = order2[p]
-        value = sums[0, at] + two1[p].astype(F32) + two2[p].astype(F32)
+        value = sums[0, at] + two1[p].astype(F32) + two2[FIRST - NEAR + p].astype(F32)
         total[at] = (value + two3[p].astype(F32)).astype(BF)
     total[NP] = jnp.zeros(total.shape[1:], BF)
 
@@ -183,7 +185,7 @@
     return pl.pallas_call(
         route_kernel,
         out_shape=jax.ShapeDtypeStruct((scalars[0].shape[0], 64, 128), BF),
-        in_specs=[smem] * 3 + [vmem] * 8,
+        in_specs=[smem] * 3 + [vmem] * 7,
         out_specs=vmem,
         scratch_shapes=[pltpu.VMEM((NP + 1, 64, 128), BF)],
         compiler_params=pltpu.CompilerParams(vmem_limit_bytes=16 * MIB),
@@ -291,23 +293,20 @@
     swap2a, swap2b = lax.ppermute(left2a, "c", other), lax.ppermute(left2b, "c", other)
     far = [right2a, right2b]
 
-    def over_y(blocks):
-        return [shift(block, "y", k + 1) for k, block in enumerate(blocks)]
-
-    *blocks, sums = grams(
-        middle_kernel, "middle", [meta, order1], lefts + far, sums, [FIRST, FIRST - NEAR, FIRST]
+    one1, one3, sums = grams(middle_kernel, "middle", [meta, order1], lefts + far, sums, [FIRST] * 2)
+    one1, one3 = shift(one1, "y", 1), shift(one3, "y", 3)
+    scalars = [meta, order1, order2]
+    late = functools.partial(late_kernel, 0)
+    (sums,) = grams(late, "late_own", scalars, [left2a, left2b] + rights + far, sums)
+    late = functools.partial(late_kernel, 1)
+    sizes = [SECOND, FIRST - NEAR + SECOND, SECOND]
+    *two, sums = grams(
+        late, "late_other", scalars, [swap2a, swap2b] + rights + far, sums, sizes
     )
-    parts = over_y(blocks)
-    late = functools.partial(late_kernel, 0)
-    (sums,) = grams(late, "late_own", [meta, order2], [left2a, left2b] + rights + far, sums)
-    late = functools.partial(late_kernel, 1)
-    *blocks, sums = grams(
-        late, "late_other", [meta, order2], [swap2a, swap2b] + rights + far, sums, [SECOND] * 3
-    )
-    blocks[1], parts[0], parts[2] = tie(blocks[1], parts[0], parts[2])
-    parts += over_y(blocks)
-
-    routed = route([index, order1, order2], sums, [near2] + parts).reshape(32, CAP, 64, 128)
+    two[0], two[2], one1, one3 = tie(two[0], two[2], one1, one3)
+    two = [shift(block, "y", k + 1) for k, block in enumerate(two)]
+
+    routed = route([index, order1, order2], sums, [near2, one1, one3, *two]).reshape(32, CAP, 64, 128)
     arrived = lax.all_to_all(routed, ("x", "z", "c"), 0, 0, tiled=True)
     return place(arrived)
 

time: 163 us -> 162 us (level)
  blocking collectives: 36.5 us -> 33.6 us
  waiting for transfers between devices: 65.4 us -> 67.8 us
    all_to_all x1, blocking collectives: 36.5 us -> 33.6 us  [on_device(): arrived = lax.all_to_all(routed, ('x', 'z', 'c'), 0, 0, tiled=True)]
    ppermute x19 -> x18, waiting for transfers between devices: 65.4 us -> 67.8 us  [shift(): return lax.ppermute(a, axis, [(i, (i + d) % 4) for i in range(4)])]
    ppermute x19 -> x18, starting transfers between devices: 28.5 us -> 28.1 us  [shift(): return lax.ppermute(a, axis, [(i, (i + d) % 4) for i in range(4)])]
  transfers between devices with their start and end apart: 24 -> 23, of which waited for: 8 -> 7; matrix products, arithmetic and copies ran while one was open for 0% -> 0% of each run, Pallas kernels for 11% -> 11%
where the time goes in v7:
time: 162 us
  waiting for transfers between devices  67.8 us (42%)
  blocking collectives  33.6 us (21%)
  starting transfers between devices  33.4 us (21%)
  Pallas kernels  24.2 us (15%)
  local copies, waits for them, and re-layouts  2 us (1%)
    ppermute x18, waiting for transfers between devices, shift(): return lax.ppermute(a, axis, [(i, (i + d) % 4) for i in range(4)])  67.8 us
    all_to_all x1, blocking collectives, on_device(): arrived = lax.all_to_all(routed, ('x', 'z', 'c'), 0, 0, tiled=True)  33.6 us
    ppermute x18, starting transfers between devices, shift(): return lax.ppermute(a, axis, [(i, (i + d) % 4) for i in range(4)])  28.1 us
    pallas_call x4, Pallas kernels, grams(): pl.pallas_call(kernel, out_shape=shapes, in_specs=[smem] * len(scalars) +...  14.5 us
    pallas_call x1, Pallas kernels, place(): pl.pallas_call(place_kernel, grid=(CAP,), out_shape=jax.ShapeDtypeStruct(...  4.24 us
    pallas_call x1, Pallas kernels, plan(): pl.pallas_call(plan_kernel, out_shape=[jax.ShapeDtypeStruct((n,), jnp.int...  3.48 us
  transfers between devices with their start and end apart: 23, of which 7 were waited for; matrix products, arithmetic and copies ran while one was open for 0% of the time, Pallas kernels for 11%

profile of v7, /device:TPU:1, one launch (start us, length us, event | category | flops | bytes accessed | tf_op | source)
XLA Modules:
  0.0 161.7 jit_solution(1222771572013775997)
XLA Ops:
  0.0 1.8 %copy.8.dens = bf16[256,3000]{1,0:T(8,128)(2,1)S(1)} copy(bf16[256,3000]{0,1:T(8,128)(2,1)} %param.4) | data formatting | bytes 3072000 | tf_op args[0]
  2.8 4.5 %collective-permute-start = (bf16[128,3072]{1,0:T(8,128)(2,1)S(1)}, bf16[128,3072]{1,0:T(8,128)(2,1)S(1)}, u32[]{:S(2)}, u32[]{:S(2)}) collective-permute-start(bf16[128,3072]{1,0:T(8,128)(2,1)S(1)} %get-tuple-element.44), channel_id=1, source_target_pairs={{0,16},{8,24},{16,0},{24,8},{1,17},{9,25},{17,1},{25,9},{2,18},{10... | collective-permute-start | bytes 2359304 | tf_op jit(solution)/shard_map/ppermute | solution.py:22
  7.3 2.5 %collective-permute-start.1 = (bf16[1,64,3072]{2,1,0:T(8,128)(2,1)S(1)}, bf16[1,64,3072]{2,1,0:T(8,128)(2,1)S(1)}, u32[]{:S(2)}, u32[]{:S(2)}) collective-permute-start(bf16[1,64,3072]{2,1,0:T(8,128)(2,1)S(1)} %get-tuple-element.45), channel_id=1, source_target_pairs={{0,96},{32,0},{64,32},{96,64},{1,97},{33,1},{65,33},{97,65},{2,98}... | collective-permute-start | bytes 1179656 | tf_op jit(solution)/shard_map/ppermute | solution.py:22
  10.9 7.1 %collective-permute-done.1 = bf16[1,64,3072]{2,1,0:T(8,128)(2,1)S(1)} collective-permute-done((bf16[1,64,3072]{2,1,0:T(8,128)(2,1)S(1)}, bf16[1,64,3072]{2,1,0:T(8,128)(2,1)S(1)}, u32[]{:S(2)}, u32[]{:S(2)}) %collective-permute-start.1) | collective-permute-done | bytes 393248 | tf_op jit(solution)/shard_map/ppermute | solution.py:22
  18.0 2.7 %collective-permute-done.2 = bf16[1,64,3072]{2,1,0:T(8,128)(2,1)S(1)} collective-permute-done((bf16[1,64,3072]{2,1,0:T(8,128)(2,1)S(1)}, bf16[1,64,3072]{2,1,0:T(8,128)(2,1)S(1)}, u32[]{:S(2)}, u32[]{:S(2)}) %collective-permute-start.2) | collective-permute-done | bytes 393248 | tf_op jit(solution)/shard_map/ppermute | solution.py:22
  20.7 10.1 %collective-permute-done.3 = bf16[1,64,3072]{2,1,0:T(8,128)(2,1)S(1)} collective-permute-done((bf16[1,64,3072]{2,1,0:T(8,128)(2,1)S(1)}, bf16[1,64,3072]{2,1,0:T(8,128)(2,1)S(1)}, u32[]{:S(2)}, u32[]{:S(2)}) %collective-permute-start.3) | collective-permute-done | bytes 393248 | tf_op jit(solution)/shard_map/ppermute | solution.py:22
  31.9 1.9 %collective-permute-start.4 = (bf16[4,64,3072]{2,1,0:T(8,128)(2,1)S(1)}, bf16[4,64,3072]{2,1,0:T(8,128)(2,1)S(1)}, u32[]{:S(2)}, u32[]{:S(2)}) collective-permute-start(bf16[4,64,3072]{2,1,0:T(8,128)(2,1)S(1)} %pad_maximum_fusion.1.refs_0_), channel_id=1, source_target_pairs={{0,24},{8,0},{16,8},{24,16},{1,25},{9,1},{17,9},{25,17},{2,26},{10... | collective-permute-start | bytes 4718600 | tf_op jit(solution)/shard_map/ppermute | solution.py:22
  35.3 3.5 %plan.1 = (s32[128]{0:T(128)S(1)}, s32[17]{0:T(128)S(1)}, s32[21]{0:T(128)S(1)}) custom-call(s32[4]{0:T(128)S(1)} %pad_add_fusion.meta, s32[64]{0:T(128)S(1)} %get-tuple-element.80.first, s32[64]{0:T(128)S(1)} %get-tuple-element.79.second, s32[64]{0:T(128)S(1)} %bitcast.13), custom_call_target="tpu_custom_call" | custom-call | tf_op jit(solution)/shard_map/plan/pallas_call | solution.py:233
  38.8 1.7 %collective-permute-start.8 = (bf16[4,64,3072]{2,1,0:T(8,128)(2,1)S(1)}, bf16[4,64,3072]{2,1,0:T(8,128)(2,1)S(1)}, u32[]{:S(2)}, u32[]{:S(2)}) collective-permute-start(bf16[4,64,3072]{2,1,0:T(8,128)(2,1)S(1)} %pad_maximum_fusion.1.refs_0_), channel_id=1, source_target_pairs={{0,4},{4,0},{1,5},{5,1},{2,6},{6,2},{3,7},{7,3},{8,12},{12,8},{9,1... | collective-permute-start | bytes 4718600 | tf_op jit(solution)/shard_map/ppermute | solution.py:280
  40.5 27.3 %collective-permute-done.5.refs_2_ = bf16[4,64,3072]{2,1,0:T(8,128)(2,1)S(1)} collective-permute-done((bf16[4,64,3072]{2,1,0:T(8,128)(2,1)S(1)}, bf16[4,64,3072]{2,1,0:T(8,128)(2,1)S(1)}, u32[]{:S(2)}, u32[]{:S(2)}) %collective-permute-start.5) | collective-permute-done | bytes 1572896 | tf_op jit(solution)/shard_map/ppermute | solution.py:22
  69.4 2.7 %collective-permute-start.7 = (bf16[2,64,3072]{2,1,0:T(8,128)(2,1)S(1)}, bf16[2,64,3072]{2,1,0:T(8,128)(2,1)S(1)}, u32[]{:S(2)}, u32[]{:S(2)}) collective-permute-start(bf16[2,64,3072]{2,1,0:T(8,128)(2,1)S(1)} %slice.25), channel_id=1, source_target_pairs={{0,24},{8,0},{16,8},{24,16},{1,25},{9,1},{17,9},{25,17},{2,26},{10... | collective-permute-start | bytes 2359304 | tf_op jit(solution)/shard_map/ppermute | solution.py:22
  72.4 2.7 %collective-permute-start.17 = (bf16[128,3072]{1,0:T(8,128)(2,1)S(1)}, bf16[128,3072]{1,0:T(8,128)(2,1)S(1)}, u32[]{:S(2)}, u32[]{:S(2)}) collective-permute-start(bf16[128,3072]{1,0:T(8,128)(2,1)S(1)} %slice.23), channel_id=1, source_target_pairs={{0,96},{32,0},{64,32},{96,64},{1,97},{33,1},{65,33},{97,65},{2,98}... | collective-permute-start | bytes 2359304 | tf_op jit(solution)/shard_map/ppermute | solution.py:22
  75.0 6.5 %early.1 = (bf16[9,64,128]{2,1,0:T(8,128)(2,1)S(1)}, f32[4,37,64,128]{3,2,1,0:T(8,128)S(1)}) custom-call(s32[4]{0:T(128)S(1)} %pad_add_fusion.meta, s32[17]{0:T(128)S(1)} %get-tuple-element.55.order.order1, bf16[4,64,3072]{2,1,0:T(8,128)(2,1)S(1)} %pad_maximum_fusion.1.refs_0_, bf16[4,64,3072]{2,1,0:T(8,128)(2,1)S(1)} %collective-permute-done.4.refs_1_, ...), custom_call_target="tpu_custom_call" | custom-call | flops 3221225472 | bytes 1048576 | tf_op jit(solution)/shard_map/early/pallas_call | solution.py:116
  81.5 3.0 %collective-permute-start.13 = (bf16[9,64,128]{2,1,0:T(8,128)(2,1)S(1)}, bf16[9,64,128]{2,1,0:T(8,128)(2,1)S(1)}, u32[]{:S(2)}, u32[]{:S(2)}) collective-permute-start(bf16[9,64,128]{2,1,0:T(8,128)(2,1)S(1)} %get-tuple-element.63), channel_id=1, source_target_pairs={{0,2},{1,3},{2,0},{3,1},{4,6},{5,7},{6,4},{7,5},{8,10},{9,11},{10,... | collective-permute-start | bytes 442376 | tf_op jit(solution)/shard_map/ppermute | solution.py:22
  84.5 3.8 %collective-permute-done.6.refs_0_ = bf16[2,64,3072]{2,1,0:T(8,128)(2,1)S(1)} collective-permute-done((bf16[2,64,3072]{2,1,0:T(8,128)(2,1)S(1)}, bf16[2,64,3072]{2,1,0:T(8,128)(2,1)S(1)}, u32[]{:S(2)}, u32[]{:S(2)}) %collective-permute-start.6) | collective-permute-done | bytes 786464 | tf_op jit(solution)/shard_map/ppermute | solution.py:22
  88.4 2.2 %collective-permute-start.14 = (bf16[2,64,3072]{2,1,0:T(8,128)(2,1)S(1)}, bf16[2,64,3072]{2,1,0:T(8,128)(2,1)S(1)}, u32[]{:S(2)}, u32[]{:S(2)}) collective-permute-start(bf16[2,64,3072]{2,1,0:T(8,128)(2,1)S(1)} %collective-permute-done.6.refs_0_), channel_id=1, source_target_pairs={{0,4},{4,0},{1,5},{5,1},{2,6},{6,2},{3,7},{7,3},{8,12},{12,8},{9,1... | collective-permute-start | bytes 2359304 | tf_op jit(solution)/shard_map/ppermute | solution.py:293
  90.9 3.1 %middle.1 = (bf16[16,64,128]{2,1,0:T(8,128)(2,1)S(1)}, bf16[16,64,128]{2,1,0:T(8,128)(2,1)S(1)}, f32[4,37,64,128]{3,2,1,0:T(8,128)S(1)}) custom-call(s32[4]{0:T(128)S(1)} %pad_add_fusion.meta, s32[17]{0:T(128)S(1)} %get-tuple-element.55.order.order1, bf16[4,64,3072]{2,1,0:T(8,128)(2,1)S(1)} %pad_maximum_fusion.1.refs_0_, ...), custom_call_target="tpu_custom_call", output_to_operand_aliasing={{2}: (10, {})} | custom-call | flops 3221225472 | bytes 1048576 | tf_op jit(solution)/shard_map/middle/pallas_call | solution.py:116
  95.4 1.7 %collective-permute-start.19 = (bf16[16,64,128]{2,1,0:T(8,128)(2,1)S(1)}, bf16[16,64,128]{2,1,0:T(8,128)(2,1)S(1)}, u32[]{:S(2)}, u32[]{:S(2)}) collective-permute-start(bf16[16,64,128]{2,1,0:T(8,128)(2,1)S(1)} %get-tuple-element.73), channel_id=1, source_target_pairs={{0,3},{1,0},{2,1},{3,2},{4,7},{5,4},{6,5},{7,6},{8,11},{9,8},{10,9... | collective-permute-start | bytes 786440 | tf_op jit(solution)/shard_map/ppermute | solution.py:22
  97.0 2.4 %late_own.1.refs_7_ = f32[4,37,64,128]{3,2,1,0:T(8,128)S(1)} custom-call(s32[4]{0:T(128)S(1)} %pad_add_fusion.meta, s32[17]{0:T(128)S(1)} %get-tuple-element.55.order.order1, s32[21]{0:T(128)S(1)} %get-tuple-element.56.order2, bf16[2,64,3072]{2,1,0:T(8,128)(2,1)S(1)} %collective-permute-done.6.refs_0_, ...), custom_call_target="tpu_custom_call", output_to_operand_aliasing={{}: (10, {})} | custom-call | flops 3221225472 | bytes 1048576 | tf_op jit(solution)/shard_map/late_own/pallas_call | solution.py:116
  99.5 2.5 %late_other.1 = (bf16[20,64,128]{2,1,0:T(8,128)(2,1)S(1)}, bf16[27,64,128]{2,1,0:T(8,128)(2,1)S(1)}, bf16[20,64,128]{2,1,0:T(8,128)(2,1)S(1)}, f32[4,37,64,128]{3,2,1,0:T(8,128)S(1)}) custom-call(s32[4]{0:T(128)S(1)} %pad_add_fusion.meta, s32[17]{0:T(128)S(1)} %get-tuple-element.55.order.order1, ...), custom_call_target="tpu_custom_call", output_to_operand_aliasing={{3}: (10, {})} | custom-call | flops 3221225472 | bytes 1048576 | tf_op jit(solution)/shard_map/late_other/pallas_call | solution.py:116
  103.9 2.3 %collective-permute-start.22 = (bf16[20,64,128]{2,1,0:T(8,128)(2,1)S(1)}, bf16[20,64,128]{2,1,0:T(8,128)(2,1)S(1)}, u32[]{:S(2)}, u32[]{:S(2)}) collective-permute-start(bf16[20,64,128]{2,1,0:T(8,128)(2,1)S(1)} %get-tuple-element.78), channel_id=1, source_target_pairs={{0,3},{1,0},{2,1},{3,2},{4,7},{5,4},{6,5},{7,6},{8,11},{9,8},{10,9... | collective-permute-start | bytes 983048 | tf_op jit(solution)/shard_map/ppermute | solution.py:22
  106.2 16.5 %collective-permute-done.20.refs_3_ = bf16[20,64,128]{2,1,0:T(8,128)(2,1)S(1)} collective-permute-done((bf16[20,64,128]{2,1,0:T(8,128)(2,1)S(1)}, bf16[20,64,128]{2,1,0:T(8,128)(2,1)S(1)}, u32[]{:S(2)}, u32[]{:S(2)}) %collective-permute-start.20) | collective-permute-done | bytes 327712 | tf_op jit(solution)/shard_map/ppermute | solution.py:22
  123.8 33.6 %all_to_all.5.got = bf16[32,4,64,128]{3,2,1,0:T(8,128)(2,1)} all-to-all(bf16[32,4,64,128]{3,2,1,0:T(8,128)(2,1)S(1)} %bitcast.11), channel_id=1, replica_groups=mesh['x'=4,'z'=4,'c'=2,'y'=4] {'x','z','c'}, dimensions={0} | all-to-all | bytes 4194304 | tf_op jit(solution)/shard_map/all_to_all | solution.py:310
  157.4 4.2 %place.1 = f32[4,256,1024]{2,1,0:T(8,128)} custom-call(bf16[32,4,64,128]{3,2,1,0:T(8,128)(2,1)} %all_to_all.5.got), custom_call_target="tpu_custom_call" | custom-call | tf_op jit(solution)/shard_map/place/pallas_call | solution.py:254
  (46 shorter events, 11.0 us)
Async XLA Ops:
  2.8 28.0 %collective-permute-start = (bf16[128,3072]{1,0:T(8,128)(2,1)S(1)}, bf16[128,3072]{1,0:T(8,128)(2,1)S(1)}, u32[]{:S(2)}, u32[]{:S(2)}) collective-permute-start(bf16[128,3072]{1,0:T(8,128)(2,1)S(1)} %get-tuple-element.44), channel_id=1, source_target_pairs={{0,16},{8,24},{16,0},{24,8},{1,17},{9,25},{17,1},{25,9},{2,18},{10... | collective-permute-start | bytes 2359304 | tf_op jit(solution)/shard_map/ppermute | solution.py:22
  7.3 10.7 %collective-permute-start.1 = (bf16[1,64,3072]{2,1,0:T(8,128)(2,1)S(1)}, bf16[1,64,3072]{2,1,0:T(8,128)(2,1)S(1)}, u32[]{:S(2)}, u32[]{:S(2)}) collective-permute-start(bf16[1,64,3072]{2,1,0:T(8,128)(2,1)S(1)} %get-tuple-element.45), channel_id=1, source_target_pairs={{0,96},{32,0},{64,32},{96,64},{1,97},{33,1},{65,33},{97,65},{2,98}... | collective-permute-start | bytes 1179656 | tf_op jit(solution)/shard_map/ppermute | solution.py:22
  9.8 10.9 %collective-permute-start.2 = (bf16[1,64,3072]{2,1,0:T(8,128)(2,1)S(1)}, bf16[1,64,3072]{2,1,0:T(8,128)(2,1)S(1)}, u32[]{:S(2)}, u32[]{:S(2)}) collective-permute-start(bf16[1,64,3072]{2,1,0:T(8,128)(2,1)S(1)} %get-tuple-element.46), channel_id=1, source_target_pairs={{0,64},{32,96},{64,0},{96,32},{1,65},{33,97},{65,1},{97,33},{2,66}... | collective-permute-start | bytes 1179656 | tf_op jit(solution)/shard_map/ppermute | solution.py:22
  10.3 20.4 %collective-permute-start.3 = (bf16[1,64,3072]{2,1,0:T(8,128)(2,1)S(1)}, bf16[1,64,3072]{2,1,0:T(8,128)(2,1)S(1)}, u32[]{:S(2)}, u32[]{:S(2)}) collective-permute-start(bf16[1,64,3072]{2,1,0:T(8,128)(2,1)S(1)} %get-tuple-element.47), channel_id=1, source_target_pairs={{0,32},{32,64},{64,96},{96,0},{1,33},{33,65},{65,97},{97,1},{2,34}... | collective-permute-start | bytes 1179656 | tf_op jit(solution)/shard_map/ppermute | solution.py:22
  30.9 4.4 %copy-start.2 = (s32[64,2]{0,1:T(2,128)S(1)}, s32[64,2]{0,1:T(2,128)}, u32[]{:S(2)}) copy-start(s32[64,2]{0,1:T(2,128)} %param.6) | copy-start | bytes 1540
  31.1 36.8 %collective-permute-start.5 = (bf16[4,64,3072]{2,1,0:T(8,128)(2,1)S(1)}, bf16[4,64,3072]{2,1,0:T(8,128)(2,1)S(1)}, u32[]{:S(2)}, u32[]{:S(2)}) collective-permute-start(bf16[4,64,3072]{2,1,0:T(8,128)(2,1)S(1)} %pad_maximum_fusion.1.refs_0_), channel_id=1, source_target_pairs={{0,8},{8,16},{16,24},{24,0},{1,9},{9,17},{17,25},{25,1},{2,10},{10... | collective-permute-start | bytes 4718600 | tf_op jit(solution)/shard_map/ppermute | solution.py:22
  31.9 35.9 %collective-permute-start.4 = (bf16[4,64,3072]{2,1,0:T(8,128)(2,1)S(1)}, bf16[4,64,3072]{2,1,0:T(8,128)(2,1)S(1)}, u32[]{:S(2)}, u32[]{:S(2)}) collective-permute-start(bf16[4,64,3072]{2,1,0:T(8,128)(2,1)S(1)} %pad_maximum_fusion.1.refs_0_), channel_id=1, source_target_pairs={{0,24},{8,0},{16,8},{24,16},{1,25},{9,1},{17,9},{25,17},{2,26},{10... | collective-permute-start | bytes 4718600 | tf_op jit(solution)/shard_map/ppermute | solution.py:22
  33.8 35.5 %collective-permute-start.12 = (bf16[256,3072]{1,0:T(8,128)(2,1)S(1)}, bf16[256,3072]{1,0:T(8,128)(2,1)S(1)}, u32[]{:S(2)}, u32[]{:S(2)}) collective-permute-start(bf16[256,3072]{1,0:T(8,128)(2,1)S(1)} %pad_maximum_fusion.refs_6_.refs_2_), channel_id=1, source_target_pairs={{0,96},{32,0},{64,32},{96,64},{1,97},{33,1},{65,33},{97,65},{2,98}... | collective-permute-start | bytes 4718600 | tf_op jit(solution)/shard_map/ppermute | solution.py:22
  33.8 35.6 %collective-permute-start.11 = (bf16[256,3072]{1,0:T(8,128)(2,1)S(1)}, bf16[256,3072]{1,0:T(8,128)(2,1)S(1)}, u32[]{:S(2)}, u32[]{:S(2)}) collective-permute-start(bf16[256,3072]{1,0:T(8,128)(2,1)S(1)} %pad_maximum_fusion.refs_6_.refs_2_), channel_id=1, source_target_pairs={{0,32},{32,64},{64,96},{96,0},{1,33},{33,65},{65,97},{97,1},{2,34}... | collective-permute-start | bytes 4718600 | tf_op jit(solution)/shard_map/ppermute | solution.py:22
  38.8 33.5 %collective-permute-start.8 = (bf16[4,64,3072]{2,1,0:T(8,128)(2,1)S(1)}, bf16[4,64,3072]{2,1,0:T(8,128)(2,1)S(1)}, u32[]{:S(2)}, u32[]{:S(2)}) collective-permute-start(bf16[4,64,3072]{2,1,0:T(8,128)(2,1)S(1)} %pad_maximum_fusion.1.refs_0_), channel_id=1, source_target_pairs={{0,4},{4,0},{1,5},{5,1},{2,6},{6,2},{3,7},{7,3},{8,12},{12,8},{9,1... | collective-permute-start | bytes 4718600 | tf_op jit(solution)/shard_map/ppermute | solution.py:280
  67.8 4.5 %collective-permute-start.9 = (bf16[4,64,3072]{2,1,0:T(8,128)(2,1)S(1)}, bf16[4,64,3072]{2,1,0:T(8,128)(2,1)S(1)}, u32[]{:S(2)}, u32[]{:S(2)}) collective-permute-start(bf16[4,64,3072]{2,1,0:T(8,128)(2,1)S(1)} %collective-permute-done.4.refs_1_), channel_id=1, source_target_pairs={{0,4},{4,0},{1,5},{5,1},{2,6},{6,2},{3,7},{7,3},{8,12},{12,8},{9,1... | collective-permute-start | bytes 4718600 | tf_op jit(solution)/shard_map/ppermute | solution.py:287
  69.2 5.8 %collective-permute-start.10 = (bf16[4,64,3072]{2,1,0:T(8,128)(2,1)S(1)}, bf16[4,64,3072]{2,1,0:T(8,128)(2,1)S(1)}, u32[]{:S(2)}, u32[]{:S(2)}) collective-permute-start(bf16[4,64,3072]{2,1,0:T(8,128)(2,1)S(1)} %collective-permute-done.5.refs_2_), channel_id=1, source_target_pairs={{0,4},{4,0},{1,5},{5,1},{2,6},{6,2},{3,7},{7,3},{8,12},{12,8},{9,1... | collective-permute-start | bytes 4718600 | tf_op jit(solution)/shard_map/ppermute | solution.py:287
  69.3 19.1 %collective-permute-start.6 = (bf16[2,64,3072]{2,1,0:T(8,128)(2,1)S(1)}, bf16[2,64,3072]{2,1,0:T(8,128)(2,1)S(1)}, u32[]{:S(2)}, u32[]{:S(2)}) collective-permute-start(bf16[2,64,3072]{2,1,0:T(8,128)(2,1)S(1)} %slice.24), channel_id=1, source_target_pairs={{0,8},{8,16},{16,24},{24,0},{1,9},{9,17},{17,25},{25,1},{2,10},{10... | collective-permute-start | bytes 2359304 | tf_op jit(solution)/shard_map/ppermute | solution.py:22
  69.4 19.0 %collective-permute-start.7 = (bf16[2,64,3072]{2,1,0:T(8,128)(2,1)S(1)}, bf16[2,64,3072]{2,1,0:T(8,128)(2,1)S(1)}, u32[]{:S(2)}, u32[]{:S(2)}) collective-permute-start(bf16[2,64,3072]{2,1,0:T(8,128)(2,1)S(1)} %slice.25), channel_id=1, source_target_pairs={{0,24},{8,0},{16,8},{24,16},{1,25},{9,1},{17,9},{25,17},{2,26},{10... | collective-permute-start | bytes 2359304 | tf_op jit(solution)/shard_map/ppermute | solution.py:22
  72.3 18.6 %collective-permute-start.16 = (bf16[128,3072]{1,0:T(8,128)(2,1)S(1)}, bf16[128,3072]{1,0:T(8,128)(2,1)S(1)}, u32[]{:S(2)}, u32[]{:S(2)}) collective-permute-start(bf16[128,3072]{1,0:T(8,128)(2,1)S(1)} %slice.22), channel_id=1, source_target_pairs={{0,32},{32,64},{64,96},{96,0},{1,33},{33,65},{65,97},{97,1},{2,34}... | collective-permute-start | bytes 2359304 | tf_op jit(solution)/shard_map/ppermute | solution.py:22
  72.4 18.5 %collective-permute-start.17 = (bf16[128,3072]{1,0:T(8,128)(2,1)S(1)}, bf16[128,3072]{1,0:T(8,128)(2,1)S(1)}, u32[]{:S(2)}, u32[]{:S(2)}) collective-permute-start(bf16[128,3072]{1,0:T(8,128)(2,1)S(1)} %slice.23), channel_id=1, source_target_pairs={{0,96},{32,0},{64,32},{96,64},{1,97},{33,1},{65,33},{97,65},{2,98}... | collective-permute-start | bytes 2359304 | tf_op jit(solution)/shard_map/ppermute | solution.py:22
  81.5 6.9 %collective-permute-start.13 = (bf16[9,64,128]{2,1,0:T(8,128)(2,1)S(1)}, bf16[9,64,128]{2,1,0:T(8,128)(2,1)S(1)}, u32[]{:S(2)}, u32[]{:S(2)}) collective-permute-start(bf16[9,64,128]{2,1,0:T(8,128)(2,1)S(1)} %get-tuple-element.63), channel_id=1, source_target_pairs={{0,2},{1,3},{2,0},{3,1},{4,6},{5,7},{6,4},{7,5},{8,10},{9,11},{10,... | collective-permute-start | bytes 442376 | tf_op jit(solution)/shard_map/ppermute | solution.py:22
  88.4 11.1 %collective-permute-start.14 = (bf16[2,64,3072]{2,1,0:T(8,128)(2,1)S(1)}, bf16[2,64,3072]{2,1,0:T(8,128)(2,1)S(1)}, u32[]{:S(2)}, u32[]{:S(2)}) collective-permute-start(bf16[2,64,3072]{2,1,0:T(8,128)(2,1)S(1)} %collective-permute-done.6.refs_0_), channel_id=1, source_target_pairs={{0,4},{4,0},{1,5},{5,1},{2,6},{6,2},{3,7},{7,3},{8,12},{12,8},{9,1... | collective-permute-start | bytes 2359304 | tf_op jit(solution)/shard_map/ppermute | solution.py:293
  90.6 8.9 %collective-permute-start.15 = (bf16[2,64,3072]{2,1,0:T(8,128)(2,1)S(1)}, bf16[2,64,3072]{2,1,0:T(8,128)(2,1)S(1)}, u32[]{:S(2)}, u32[]{:S(2)}) collective-permute-start(bf16[2,64,3072]{2,1,0:T(8,128)(2,1)S(1)} %collective-permute-done.7.refs_1_), channel_id=1, source_target_pairs={{0,4},{4,0},{1,5},{5,1},{2,6},{6,2},{3,7},{7,3},{8,12},{12,8},{9,1... | collective-permute-start | bytes 2359304 | tf_op jit(solution)/shard_map/ppermute | solution.py:293
  94.0 9.5 %collective-permute-start.18 = (bf16[16,64,128]{2,1,0:T(8,128)(2,1)S(1)}, bf16[16,64,128]{2,1,0:T(8,128)(2,1)S(1)}, u32[]{:S(2)}, u32[]{:S(2)}) collective-permute-start(bf16[16,64,128]{2,1,0:T(8,128)(2,1)S(1)} %get-tuple-element.72), channel_id=1, source_target_pairs={{0,1},{1,2},{2,3},{3,0},{4,5},{5,6},{6,7},{7,4},{8,9},{9,10},{10,1... | collective-permute-start | bytes 786440 | tf_op jit(solution)/shard_map/ppermute | solution.py:22
  95.4 8.1 %collective-permute-start.19 = (bf16[16,64,128]{2,1,0:T(8,128)(2,1)S(1)}, bf16[16,64,128]{2,1,0:T(8,128)(2,1)S(1)}, u32[]{:S(2)}, u32[]{:S(2)}) collective-permute-start(bf16[16,64,128]{2,1,0:T(8,128)(2,1)S(1)} %get-tuple-element.73), channel_id=1, source_target_pairs={{0,3},{1,0},{2,1},{3,2},{4,7},{5,4},{6,5},{7,6},{8,11},{9,8},{10,9... | collective-permute-start | bytes 786440 | tf_op jit(solution)/shard_map/ppermute | solution.py:22
  102.0 20.7 %collective-permute-start.21 = (bf16[27,64,128]{2,1,0:T(8,128)(2,1)S(1)}, bf16[27,64,128]{2,1,0:T(8,128)(2,1)S(1)}, u32[]{:S(2)}, u32[]{:S(2)}) collective-permute-start(bf16[27,64,128]{2,1,0:T(8,128)(2,1)S(1)} %get-tuple-element.77), channel_id=1, source_target_pairs={{0,2},{1,3},{2,0},{3,1},{4,6},{5,7},{6,4},{7,5},{8,10},{9,11},{10,... | collective-permute-start | bytes 1327112 | tf_op jit(solution)/shard_map/ppermute | solution.py:22
  103.5 19.2 %collective-permute-start.20 = (bf16[20,64,128]{2,1,0:T(8,128)(2,1)S(1)}, bf16[20,64,128]{2,1,0:T(8,128)(2,1)S(1)}, u32[]{:S(2)}, u32[]{:S(2)}) collective-permute-start(bf16[20,64,128]{2,1,0:T(8,128)(2,1)S(1)} %get-tuple-element.76), channel_id=1, source_target_pairs={{0,1},{1,2},{2,3},{3,0},{4,5},{5,6},{6,7},{7,4},{8,9},{9,10},{10,1... | collective-permute-start | bytes 983048 | tf_op jit(solution)/shard_map/ppermute | solution.py:22
  103.9 18.8 %collective-permute-start.22 = (bf16[20,64,128]{2,1,0:T(8,128)(2,1)S(1)}, bf16[20,64,128]{2,1,0:T(8,128)(2,1)S(1)}, u32[]{:S(2)}, u32[]{:S(2)}) collective-permute-start(bf16[20,64,128]{2,1,0:T(8,128)(2,1)S(1)} %get-tuple-element.78), channel_id=1, source_target_pairs={{0,3},{1,0},{2,1},{3,2},{4,7},{5,4},{6,5},{7,6},{8,11},{9,8},{10,9... | collective-permute-start | bytes 983048 | tf_op jit(solution)/shard_map/ppermute | solution.py:22
  (2 other events, 6.3 us)

commit v8 on v7

--- a/solution.py
+++ b/solution.py
@@ -1,5 +1,3 @@
-import functools
-
 import jax
 import jax.numpy as jnp
 from jax import lax
@@ -27,7 +25,15 @@
 
 
 EARLY_L = [(dc, dz) for dc in range(2) for dz in (0, 1, 3)]
-LATE_L = [(dc, 2) for dc in range(2)]
+ORDER = [(0, 0), (0, 1), (1, 2), (0, 2), (0, 3), (1, 0), (1, 1), (1, 3)]
+SPLIT, END = 80, 160
+
+
+def place_of(half, k):
+    at = 0
+    for n, key in enumerate(ORDER):
+        at = jnp.where((half == key[0]) & (k == key[1]), 32 * n, at)
+    return pl.multiple_of(at, 32)
 
 
 def product(lefts, rights):
@@ -39,40 +45,17 @@
     )
 
 
-def store(meta, sums, out, ip, jp, sources, row):
-    z, c, y = meta[1], meta[2], meta[3]
-    for n, (dc, dz) in enumerate(sources):
+def store(meta, sums, out, jp, blocks):
+    x, z, c, y = meta[0], meta[1], meta[2], meta[3]
+    for n, (dc, dz, half, k) in enumerate(blocks):
         zz, cc = (z + dz) % 4, (c + dc) % 2
-        i = 2 * ip + zz // 2
+        i = 2 * ((x + k) % 4) + zz // 2
         dy = (2 * (zz % 2) + cc - y + 4) % 4
-        for half in range(2):
-            j = 2 * jp + (z // 2 + half) % 2
+        row = pl.multiple_of((zz // 2 + half) % 2 * 32, 32)
+        for b in range(2):
+            j = 2 * jp + (z // 2 + b) % 2
             at = jnp.where(i <= j, j * (j + 1) // 2 + i, NP)
-            sums[dy, at] = out[row + 64 * n : row + 64 * n + 64, 128 * half : 128 * half + 128]
-
-
-def early_kernel(meta, order, *refs):
-    lefts, rights, sums = refs[:6], refs[6:9], refs[10]
-    x = meta[0]
-    for n, dx in enumerate((0, 1, 3)):
-        near_step(meta, lefts, [rights[n]], (x + dx) % 4, sums)
-    pack(sums, 2, order, 0, NEAR, refs[9])
-
-
-def near_step(meta, lefts, right, jp, sums):
-    x = meta[0]
-
-    def step(k, _):
-        ip = (x + k) % 4
-
-        @pl.when(ip <= jp)
-        def _():
-            out = product([ref[k] for ref in lefts], [ref[...] for ref in right])
-            store(meta, sums, out, ip, jp, EARLY_L, 0)
-
-        return 0
-
-    lax.fori_loop(0, 4, step, 0)
+            sums[dy, at, pl.ds(row, 32)] = out[32 * n : 32 * n + 32, 128 * b : 128 * b + 128]
 
 
 def pack(sums, dy, order, first, size, ref, at=0):
@@ -80,27 +63,79 @@
         ref[at + p] = sums[dy, order[first + p]].astype(BF)
 
 
+def early_kernel(meta, order, *refs):
+    lefts, rights, outs, sums = refs[:6], refs[6:9], refs[9:10], refs[10]
+    x = meta[0]
+    for n, dx in enumerate((0, 1, 3)):
+        jp = (x + dx) % 4
+
+        def step(k, _):
+            @pl.when((x + k) % 4 <= jp)
+            def _():
+                rows = [ref[pl.ds(place_of(h, k), 32)] for ref in lefts for h in range(2)]
+                out = product(rows, [rights[n][...]])
+                store(meta, sums, out, jp, [(*key, h, k) for key in EARLY_L for h in range(2)])
+
+            return 0
+
+        lax.fori_loop(0, 4, step, 0)
+    pack(sums, 2, order, 0, NEAR, outs[0])
+
+
 def middle_kernel(meta, order, *refs):
-    near_step(meta, refs[:6], refs[6:8], (meta[0] + 2) % 4, refs[11])
-    pack(refs[11], 1, order, 0, FIRST, refs[9])
-    pack(refs[11], 3, order, 0, FIRST, refs[10])
-
-
-def late_kernel(dc, meta, order1, order2, *refs):
-    late, rights = refs[:2], [refs[2:3], refs[3:4], refs[5:7], refs[4:5]]
-    sums = refs[-1]
+    lefts, far, outs, sums = refs[:6], refs[6:8], refs[9:11], refs[11]
     x = meta[0]
-    rows = [late[k // 2][k % 2] for k in range(4)]
+    jp = (x + 2) % 4
+
+    def step(k, _):
+        @pl.when((x + k) % 4 <= jp)
+        def _():
+            rows = [ref[pl.ds(place_of(h, k), 32)] for ref in lefts for h in range(2)]
+            out = product(rows, [ref[...] for ref in far])
+            store(meta, sums, out, jp, [(*key, h, k) for key in EARLY_L for h in range(2)])
+
+        return 0
+
+    lax.fori_loop(0, 4, step, 0)
+    pack(sums, 1, order, 0, FIRST, outs[0])
+    pack(sums, 3, order, 0, FIRST, outs[1])
+
+
+def late_kernel(meta, order1, order2, *refs):
+    lates, outs, sums = refs[:2], refs[8:11], refs[11]
+    rights = [refs[2:3], refs[3:4], refs[5:7], refs[4:5]]
+    keys = [(dc, 2, h, k) for dc in range(2) for h, k in ORDER]
     for dx, right in enumerate(rights):
-        jp = (x + dx) % 4
-        out = product(rows, [ref[...] for ref in right])
-        for k in range(4):
-            store(meta, sums, out, (x + k) % 4, jp, [(dc, 2)], 64 * k)
-    if dc:
-        pack(sums, 1, order2, 0, SECOND, refs[8])
-        pack(sums, 2, order1, NEAR, FIRST - NEAR, refs[9])
-        pack(sums, 2, order2, 0, SECOND, refs[9], FIRST - NEAR)
-        pack(sums, 3, order2, 0, SECOND, refs[10])
+        out = product([ref[...] for ref in lates], [ref[...] for ref in right])
+        store(meta, sums, out, (meta[0] + dx) % 4, keys)
+    pack(sums, 1, order2, 0, SECOND, outs[0])
+    pack(sums, 2, order1, NEAR, FIRST - NEAR, outs[1])
+    pack(sums, 2, order2, 0, SECOND, outs[1], FIRST - NEAR)
+    pack(sums, 3, order2, 0, SECOND, outs[2])
+
+
+def derive_kernel(meta, weights, *refs):
+    out = refs[3]
+    k, width = weights.shape[1], out.shape[1]
+    edge = k // 128 * 128
+    out[:, edge:] = jnp.zeros((out.shape[0], width - edge), BF)
+    row = pl.multiple_of(128 + meta[0] * 32, 32)
+    for n, ref in enumerate(refs[:3]):
+        part = ref[pl.ds(row, 32), :k].astype(F32) * weights[...]
+        out[32 * n : 32 * n + 32, :k] = part.astype(BF)
+
+
+def derive(meta, weights, rights):
+    smem = pl.BlockSpec(memory_space=pltpu.SMEM)
+    vmem = pl.BlockSpec(memory_space=pltpu.VMEM)
+    return pl.pallas_call(
+        derive_kernel,
+        out_shape=jax.ShapeDtypeStruct((96, rights[0].shape[1]), BF),
+        in_specs=[smem] + [vmem] * 4,
+        out_specs=vmem,
+        compiler_params=pltpu.CompilerParams(vmem_limit_bytes=16 * MIB),
+        name="derive",
+    )(meta, weights, *rights)
 
 
 def grams(kernel, name, scalars, given, sums=None, parts=()):
@@ -136,18 +171,18 @@
     keep[:, :k] = dens[pl.ds(pl.multiple_of(z1 * 128, 128), 128), :]
     send[:, :k] = dens[pl.ds(pl.multiple_of((1 - z1) * 128, 128), 128), :]
     for d, ref in enumerate(parts):
-        ref[0, :, edge:] = jnp.zeros((64, width - edge), BF)
+        ref[:, edge:] = jnp.zeros((64, width - edge), BF)
         for h in range(2):
-            row = pl.multiple_of(h * 128 + (x + d) % 4 * 32, 32)
+            row = pl.multiple_of((z1 + h) % 2 * 128 + (x + d) % 4 * 32, 32)
             part = dens[pl.ds(row, 32), :].astype(F32) * weights[...]
-            ref[0, 32 * h : 32 * h + 32, :k] = part.astype(BF)
+            ref[32 * h : 32 * h + 32, :k] = part.astype(BF)
 
 
 def prepare(meta, dens, weights, width):
     smem = pl.BlockSpec(memory_space=pltpu.SMEM)
     vmem = pl.BlockSpec(memory_space=pltpu.VMEM)
     shapes = [jax.ShapeDtypeStruct((128, width), BF)] * 2
-    shapes += [jax.ShapeDtypeStruct((1, 64, width), BF)] * 4
+    shapes += [jax.ShapeDtypeStruct((64, width), BF)] * 4
     return pl.pallas_call(
         prepare_kernel,
         out_shape=shapes,
@@ -241,22 +276,39 @@
     )(meta, pair_list[:, 0], pair_list[:, 1], owner[:, 0])
 
 
-def place_kernel(got, out):
-    for src in range(32):
-        x, z1, z0, c = src // 8, (src // 4) % 2, (src // 2) % 2, src % 2
-        col = (4 * z0 + 2 * c + z1) * 128
-        for h in range(2):
-            row = h * 128 + x * 32
-            out[0, row : row + 32, col : col + 128] = got[src, 0, 32 * h : 32 * h + 32].astype(F32)
+def place_kernel(got, out, blocks, rows, came, went):
+    ins = [pltpu.make_async_copy(got.at[:, s], blocks.at[s], came.at[s]) for s in range(CAP)]
+    outs = [pltpu.make_async_copy(rows.at[s], out.at[s], went.at[s]) for s in range(CAP)]
+    for copy in ins:
+        copy.start()
+    for s in range(CAP):
+        ins[s].wait()
+        for src in range(32):
+            x, z1, z0, c = src // 8, (src // 4) % 2, (src // 2) % 2, src % 2
+            col = (4 * z0 + 2 * c + z1) * 128
+            for h in range(2):
+                row = h * 128 + x * 32
+                part = blocks[s, src, 32 * h : 32 * h + 32]
+                rows[s, row : row + 32, col : col + 128] = part.astype(F32)
+        outs[s].start()
+    for copy in outs:
+        copy.wait()
 
 
 def place(got):
+    any_ = pl.BlockSpec(memory_space=pl.ANY)
     return pl.pallas_call(
         place_kernel,
-        grid=(CAP,),
         out_shape=jax.ShapeDtypeStruct((CAP, 256, 1024), F32),
-        in_specs=[pl.BlockSpec((32, 1, 64, 128), lambda s: (0, s, 0, 0))],
-        out_specs=pl.BlockSpec((1, 256, 1024), lambda s: (s, 0, 0)),
+        in_specs=[any_],
+        out_specs=any_,
+        scratch_shapes=[
+            pltpu.VMEM((CAP, 32, 64, 128), BF),
+            pltpu.VMEM((CAP, 256, 1024), F32),
+            pltpu.SemaphoreType.DMA((CAP,)),
+            pltpu.SemaphoreType.DMA((CAP,)),
+        ],
+        compiler_params=pltpu.CompilerParams(vmem_limit_bytes=16 * MIB),
         name="place",
     )(got)
 
@@ -265,14 +317,16 @@
     x, z, c, y = (lax.axis_index(n) for n in ("x", "z", "c", "y"))
     k = densities.shape[1]
     meta = jnp.stack([x, z, c, y]).astype(jnp.int32)
-    keep, send, *mine = prepare(meta, densities, coulomb[None, :], -(-k // 128) * 128)
+    weights = coulomb[None, :]
+    keep, send, *mine = prepare(meta, densities, weights, -(-k // 128) * 128)
     got = shift(send, "z", 2)
     other = [(0, 1), (1, 0)]
     got, e1, e2, e3 = tie(
         got, shift(mine[3], "x", 3), shift(mine[2], "x", 2), shift(mine[1], "x", 1)
     )
     right = jnp.concatenate([keep, got], 0)
-    left = jnp.concatenate([mine[0], e1, e2, e3], 0)
+    pieces = [mine[0], e1, e2, e3]
+    left = jnp.concatenate([pieces[k][32 * h : 32 * h + 32] for h, k in ORDER], 0)
     right, left = tie(right, left)
 
     left3, left1 = shift(left, "z", 1), shift(left, "z", -1)
@@ -281,32 +335,31 @@
     right3, right1 = tie(right3, right1)
 
     right2a, right2b = shift(right3[:128], "x", 1), shift(right1[128:], "x", -1)
-    left2a, left2b = shift(left3[:2], "z", 1), shift(left1[2:], "z", -1)
+    late_a, late_b = shift(left3[:SPLIT], "z", 1), shift(left1[SPLIT:END], "z", -1)
     index, order1, order2 = plan(meta, pair_list, owner, 32 * CAP)
     index, near1, near3 = tie(index, left1, left3)
     swap1, swap3 = lax.ppermute(near1, "c", other), lax.ppermute(near3, "c", other)
     lefts = [left, left1, left3, swap0, swap1, swap3]
     rights = [right, right1, right3]
-    near2, sums = grams(early_kernel, "early", [meta, order1], lefts + rights, parts=[NEAR])
-    near2 = shift(near2, "y", 2)
-    left2a, left2b, sums, near2 = tie(left2a, left2b, sums, near2)
-    swap2a, swap2b = lax.ppermute(left2a, "c", other), lax.ppermute(left2b, "c", other)
+
+    held = derive(meta, weights, rights)
+    order1, held = tie(order1, held)
+    first, second = [meta, order1], [meta, order1, order2]
+    near, sums = grams(early_kernel, "early", first, lefts + rights, parts=[NEAR])
+    near = shift(near, "y", 2)
+    late_a, late_b, right2a, right2b, sums, near = tie(late_a, late_b, right2a, right2b, sums, near)
+    left2 = jnp.concatenate([late_a, late_b, held], 0)
+    swap2 = lax.ppermute(left2, "c", other)
     far = [right2a, right2b]
-
-    one1, one3, sums = grams(middle_kernel, "middle", [meta, order1], lefts + far, sums, [FIRST] * 2)
+    one1, one3, sums = grams(middle_kernel, "middle", first, lefts + far, sums, [FIRST] * 2)
     one1, one3 = shift(one1, "y", 1), shift(one3, "y", 3)
-    scalars = [meta, order1, order2]
-    late = functools.partial(late_kernel, 0)
-    (sums,) = grams(late, "late_own", scalars, [left2a, left2b] + rights + far, sums)
-    late = functools.partial(late_kernel, 1)
+    late = [left2, swap2]
     sizes = [SECOND, FIRST - NEAR + SECOND, SECOND]
-    *two, sums = grams(
-        late, "late_other", scalars, [swap2a, swap2b] + rights + far, sums, sizes
-    )
-    two[0], two[2], one1, one3 = tie(two[0], two[2], one1, one3)
+    *two, sums = grams(late_kernel, "late", second, late + rights + far, sums, sizes)
+    two[2], one1, one3 = tie(two[2], one1, one3)
     two = [shift(block, "y", k + 1) for k, block in enumerate(two)]
 
-    routed = route([index, order1, order2], sums, [near2, one1, one3, *two]).reshape(32, CAP, 64, 128)
+    routed = route([index, order1, order2], sums, [near, one1, one3, *two]).reshape(32, CAP, 64, 128)
     arrived = lax.all_to_all(routed, ("x", "z", "c"), 0, 0, tiled=True)
     return place(arrived)
 

time: 162 us -> 160 us (0.988)
  starting transfers between devices: 33.4 us -> 36.2 us
  Pallas kernels: 24.2 us -> 22.2 us
    ppermute x2 -> x1, starting transfers between devices: 2.27 us -> 4.94 us  [on_device(): swap2 = lax.ppermute(left2, 'c', other)]
    ppermute x18, waiting for transfers between devices: 67.8 us -> 66.2 us  [shift(): return lax.ppermute(a, axis, [(i, (i + d) % 4) for i in range(4)])]
    pallas_call x1 -> x2, Pallas kernels: 4.24 us -> 3 us  [the longest x1 2.35 us: place(): pl.pallas_call(place_kernel, out_shape=jax.ShapeDtypeStruct((CAP, 256, 10...]
    pallas_call x4 -> x3, Pallas kernels: 14.5 us -> 13.8 us  [grams(): pl.pallas_call(kernel, out_shape=shapes, in_specs=[smem] * len(scalars) +...]
  transfers between devices with their start and end apart: 23 -> 22, of which waited for: 7 -> 10; matrix products, arithmetic and copies ran while one was open for 0% -> 0% of each run, Pallas kernels for 11% -> 11%
where the time goes in v8:
time: 160 us
  waiting for transfers between devices  66.2 us (41%)
  starting transfers between devices  36.2 us (23%)
  blocking collectives  32.4 us (20%)
  Pallas kernels  22.2 us (14%)
  local copies, waits for them, and re-layouts  2.19 us (1%)
    ppermute x18, waiting for transfers between devices, shift(): return lax.ppermute(a, axis, [(i, (i + d) % 4) for i in range(4)])  66.2 us
    all_to_all x1, blocking collectives, on_device(): arrived = lax.all_to_all(routed, ('x', 'z', 'c'), 0, 0, tiled=True)  32.4 us
    ppermute x18, starting transfers between devices, shift(): return lax.ppermute(a, axis, [(i, (i + d) % 4) for i in range(4)])  28.2 us
    pallas_call x3, Pallas kernels, grams(): pl.pallas_call(kernel, out_shape=shapes, in_specs=[smem] * len(scalars) +...  13.8 us
    ppermute x1, starting transfers between devices, on_device(): swap2 = lax.ppermute(left2, 'c', other)  4.94 us
    pallas_call x1, Pallas kernels, plan(): pl.pallas_call(plan_kernel, out_shape=[jax.ShapeDtypeStruct((n,), jnp.int...  3.48 us
  transfers between devices with their start and end apart: 22, of which 10 were waited for; matrix products, arithmetic and copies ran while one was open for 0% of the time, Pallas kernels for 11%

profile of v8, /device:TPU:1, one launch (start us, length us, event | category | flops | bytes accessed | tf_op | source)
XLA Modules:
  0.0 159.7 jit_solution(12950143068347095847)
XLA Ops:
  0.0 1.8 %copy.7.dens = bf16[256,3000]{1,0:T(8,128)(2,1)S(1)} copy(bf16[256,3000]{0,1:T(8,128)(2,1)} %param.4) | data formatting | bytes 3072000 | tf_op args[0]
  2.8 4.5 %collective-permute-start = (bf16[128,3072]{1,0:T(8,128)(2,1)S(1)}, bf16[128,3072]{1,0:T(8,128)(2,1)S(1)}, u32[]{:S(2)}, u32[]{:S(2)}) collective-permute-start(bf16[128,3072]{1,0:T(8,128)(2,1)S(1)} %get-tuple-element.47), channel_id=1, source_target_pairs={{0,16},{8,24},{16,0},{24,8},{1,17},{9,25},{17,1},{25,9},{2,18},{10... | collective-permute-start | bytes 2359304 | tf_op jit(solution)/shard_map/ppermute | solution.py:20
  7.3 2.5 %collective-permute-start.1 = (bf16[64,3072]{1,0:T(8,128)(2,1)S(1)}, bf16[64,3072]{1,0:T(8,128)(2,1)S(1)}, u32[]{:S(2)}, u32[]{:S(2)}) collective-permute-start(bf16[64,3072]{1,0:T(8,128)(2,1)S(1)} %get-tuple-element.48), channel_id=1, source_target_pairs={{0,96},{32,0},{64,32},{96,64},{1,97},{33,1},{65,33},{97,65},{2,98}... | collective-permute-start | bytes 1179656 | tf_op jit(solution)/shard_map/ppermute | solution.py:20
  10.9 7.1 %collective-permute-done.1 = bf16[64,3072]{1,0:T(8,128)(2,1)S(1)} collective-permute-done((bf16[64,3072]{1,0:T(8,128)(2,1)S(1)}, bf16[64,3072]{1,0:T(8,128)(2,1)S(1)}, u32[]{:S(2)}, u32[]{:S(2)}) %collective-permute-start.1) | collective-permute-done | bytes 393248 | tf_op jit(solution)/shard_map/ppermute | solution.py:20
  18.0 2.7 %collective-permute-done.2 = bf16[64,3072]{1,0:T(8,128)(2,1)S(1)} collective-permute-done((bf16[64,3072]{1,0:T(8,128)(2,1)S(1)}, bf16[64,3072]{1,0:T(8,128)(2,1)S(1)}, u32[]{:S(2)}, u32[]{:S(2)}) %collective-permute-start.2) | collective-permute-done | bytes 393248 | tf_op jit(solution)/shard_map/ppermute | solution.py:20
  20.7 10.1 %collective-permute-done.3 = bf16[64,3072]{1,0:T(8,128)(2,1)S(1)} collective-permute-done((bf16[64,3072]{1,0:T(8,128)(2,1)S(1)}, bf16[64,3072]{1,0:T(8,128)(2,1)S(1)}, u32[]{:S(2)}, u32[]{:S(2)}) %collective-permute-start.3) | collective-permute-done | bytes 393248 | tf_op jit(solution)/shard_map/ppermute | solution.py:20
  31.9 1.9 %collective-permute-start.4 = (bf16[256,3072]{1,0:T(8,128)(2,1)S(1)}, bf16[256,3072]{1,0:T(8,128)(2,1)S(1)}, u32[]{:S(2)}, u32[]{:S(2)}) collective-permute-start(bf16[256,3072]{1,0:T(8,128)(2,1)S(1)} %slice_dynamic-update-slice_fusion.refs_0_), channel_id=1, source_target_pairs={{0,24},{8,0},{16,8},{24,16},{1,25},{9,1},{17,9},{25,17},{2,26},{10... | collective-permute-start | bytes 4718600 | tf_op jit(solution)/shard_map/ppermute | solution.py:20
  35.3 3.5 %plan.1 = (s32[128]{0:T(128)S(1)}, s32[17]{0:T(128)S(1)}, s32[21]{0:T(128)S(1)}) custom-call(s32[4]{0:T(128)S(1)} %pad_add_fusion.meta, s32[64]{0:T(128)S(1)} %get-tuple-element.86.first, s32[64]{0:T(128)S(1)} %get-tuple-element.85.second, s32[64]{0:T(128)S(1)} %bitcast.14), custom_call_target="tpu_custom_call" | custom-call | tf_op jit(solution)/shard_map/plan/pallas_call | solution.py:268
  38.8 1.7 %collective-permute-start.12 = (bf16[256,3072]{1,0:T(8,128)(2,1)S(1)}, bf16[256,3072]{1,0:T(8,128)(2,1)S(1)}, u32[]{:S(2)}, u32[]{:S(2)}) collective-permute-start(bf16[256,3072]{1,0:T(8,128)(2,1)S(1)} %slice_dynamic-update-slice_fusion.refs_0_), channel_id=1, source_target_pairs={{0,4},{4,0},{1,5},{5,1},{2,6},{6,2},{3,7},{7,3},{8,12},{12,8},{9,1... | collective-permute-start | bytes 4718600 | tf_op jit(solution)/shard_map/ppermute | solution.py:334
  40.5 27.3 %collective-permute-done.5.refs_2_ = bf16[256,3072]{1,0:T(8,128)(2,1)S(1)} collective-permute-done((bf16[256,3072]{1,0:T(8,128)(2,1)S(1)}, bf16[256,3072]{1,0:T(8,128)(2,1)S(1)}, u32[]{:S(2)}, u32[]{:S(2)}) %collective-permute-start.5) | collective-permute-done | bytes 1572896 | tf_op jit(solution)/shard_map/ppermute | solution.py:20
  70.0 2.1 %collective-permute-start.11 = (bf16[128,3072]{1,0:T(8,128)(2,1)S(1)}, bf16[128,3072]{1,0:T(8,128)(2,1)S(1)}, u32[]{:S(2)}, u32[]{:S(2)}) collective-permute-start(bf16[128,3072]{1,0:T(8,128)(2,1)S(1)} %slice.55), channel_id=1, source_target_pairs={{0,96},{32,0},{64,32},{96,64},{1,97},{33,1},{65,33},{97,65},{2,98}... | collective-permute-start | bytes 2359304 | tf_op jit(solution)/shard_map/ppermute | solution.py:20
  72.3 2.7 %collective-permute-start.9 = (bf16[80,3072]{1,0:T(8,128)(2,1)S(1)}, bf16[80,3072]{1,0:T(8,128)(2,1)S(1)}, u32[]{:S(2)}, u32[]{:S(2)}) collective-permute-start(bf16[80,3072]{1,0:T(8,128)(2,1)S(1)} %slice.57), channel_id=1, source_target_pairs={{0,24},{8,0},{16,8},{24,16},{1,25},{9,1},{17,9},{25,17},{2,26},{10... | collective-permute-start | bytes 1474568 | tf_op jit(solution)/shard_map/ppermute | solution.py:20
  75.6 6.5 %early.1 = (bf16[9,64,128]{2,1,0:T(8,128)(2,1)S(1)}, f32[4,37,64,128]{3,2,1,0:T(8,128)S(1)}) custom-call(s32[4]{0:T(128)S(1)} %pad_add_fusion.meta, s32[17]{0:T(128)S(1)} %get-tuple-element.62.order.order1, bf16[256,3072]{1,0:T(8,128)(2,1)S(1)} %slice_dynamic-update-slice_fusion.refs_0_, bf16[256,3072]{1,0:T(8,128)(2,1)S(1)} %collective-permute-done.4.refs_1_, ...), custom_call_target="tpu_custom_call" | custom-call | flops 3221225472 | bytes 1048576 | tf_op jit(solution)/shard_map/early/pallas_call | solution.py:151
  82.1 3.0 %collective-permute-start.15 = (bf16[9,64,128]{2,1,0:T(8,128)(2,1)S(1)}, bf16[9,64,128]{2,1,0:T(8,128)(2,1)S(1)}, u32[]{:S(2)}, u32[]{:S(2)}) collective-permute-start(bf16[9,64,128]{2,1,0:T(8,128)(2,1)S(1)} %get-tuple-element.67), channel_id=1, source_target_pairs={{0,2},{1,3},{2,0},{3,1},{4,6},{5,7},{6,4},{7,5},{8,10},{9,11},{10,... | collective-permute-start | bytes 442376 | tf_op jit(solution)/shard_map/ppermute | solution.py:20
  85.1 2.0 %collective-permute-done.10.refs_6_.refs_5_ = bf16[128,3072]{1,0:T(8,128)(2,1)S(1)} collective-permute-done((bf16[128,3072]{1,0:T(8,128)(2,1)S(1)}, bf16[128,3072]{1,0:T(8,128)(2,1)S(1)}, u32[]{:S(2)}, u32[]{:S(2)}) %collective-permute-start.10) | collective-permute-done | bytes 786464 | tf_op jit(solution)/shard_map/ppermute | solution.py:20
  87.8 4.9 %collective-permute-start.16 = (bf16[256,3072]{1,0:T(8,128)(2,1)S(1)}, bf16[256,3072]{1,0:T(8,128)(2,1)S(1)}, u32[]{:S(2)}, u32[]{:S(2)}) collective-permute-start(bf16[256,3072]{1,0:T(8,128)(2,1)S(1)} %constant_dynamic-update-slice_fusion.refs_0_), channel_id=1, source_target_pairs={{0,4},{4,0},{1,5},{5,1},{2,6},{6,2},{3,7},{7,3},{8,12},{12,8},{9,1... | collective-permute-start | bytes 4718600 | tf_op jit(solution)/shard_map/ppermute | solution.py:352
  92.7 3.1 %middle.1 = (bf16[16,64,128]{2,1,0:T(8,128)(2,1)S(1)}, bf16[16,64,128]{2,1,0:T(8,128)(2,1)S(1)}, f32[4,37,64,128]{3,2,1,0:T(8,128)S(1)}) custom-call(s32[4]{0:T(128)S(1)} %pad_add_fusion.meta, s32[17]{0:T(128)S(1)} %get-tuple-element.62.order.order1, bf16[256,3072]{1,0:T(8,128)(2,1)S(1)} %slice_dynamic-update-slice_fusion.refs_0_, ...), custom_call_target="tpu_custom_call", output_to_operand_aliasing={{2}: (10, {})} | custom-call | flops 3221225472 | bytes 1048576 | tf_op jit(solution)/shard_map/middle/pallas_call | solution.py:151
  97.2 1.7 %collective-permute-start.18 = (bf16[16,64,128]{2,1,0:T(8,128)(2,1)S(1)}, bf16[16,64,128]{2,1,0:T(8,128)(2,1)S(1)}, u32[]{:S(2)}, u32[]{:S(2)}) collective-permute-start(bf16[16,64,128]{2,1,0:T(8,128)(2,1)S(1)} %get-tuple-element.79), channel_id=1, source_target_pairs={{0,3},{1,0},{2,1},{3,2},{4,7},{5,4},{6,5},{7,6},{8,11},{9,8},{10,9... | collective-permute-start | bytes 786440 | tf_op jit(solution)/shard_map/ppermute | solution.py:20
  98.9 4.2 %late.1 = (bf16[20,64,128]{2,1,0:T(8,128)(2,1)S(1)}, bf16[27,64,128]{2,1,0:T(8,128)(2,1)S(1)}, bf16[20,64,128]{2,1,0:T(8,128)(2,1)S(1)}, f32[4,37,64,128]{3,2,1,0:T(8,128)S(1)}) custom-call(s32[4]{0:T(128)S(1)} %pad_add_fusion.meta, s32[17]{0:T(128)S(1)} %get-tuple-element.62.order.order1, ...), custom_call_target="tpu_custom_call", output_to_operand_aliasing={{3}: (10, {})} | custom-call | flops 3221225472 | bytes 1048576 | tf_op jit(solution)/shard_map/late/pallas_call | solution.py:151
  105.2 2.9 %collective-permute-start.21 = (bf16[20,64,128]{2,1,0:T(8,128)(2,1)S(1)}, bf16[20,64,128]{2,1,0:T(8,128)(2,1)S(1)}, u32[]{:S(2)}, u32[]{:S(2)}) collective-permute-start(bf16[20,64,128]{2,1,0:T(8,128)(2,1)S(1)} %get-tuple-element.84), channel_id=1, source_target_pairs={{0,3},{1,0},{2,1},{3,2},{4,7},{5,4},{6,5},{7,6},{8,11},{9,8},{10,9... | collective-permute-start | bytes 983048 | tf_op jit(solution)/shard_map/ppermute | solution.py:20
  108.1 13.6 %collective-permute-done.21.refs_5_ = bf16[20,64,128]{2,1,0:T(8,128)(2,1)S(1)} collective-permute-done((bf16[20,64,128]{2,1,0:T(8,128)(2,1)S(1)}, bf16[20,64,128]{2,1,0:T(8,128)(2,1)S(1)}, u32[]{:S(2)}, u32[]{:S(2)}) %collective-permute-start.21) | collective-permute-done | bytes 327712 | tf_op jit(solution)/shard_map/ppermute | solution.py:20
  121.7 2.1 %collective-permute-done.19.refs_3_ = bf16[20,64,128]{2,1,0:T(8,128)(2,1)S(1)} collective-permute-done((bf16[20,64,128]{2,1,0:T(8,128)(2,1)S(1)}, bf16[20,64,128]{2,1,0:T(8,128)(2,1)S(1)}, u32[]{:S(2)}, u32[]{:S(2)}) %collective-permute-start.19) | collective-permute-done | bytes 327712 | tf_op jit(solution)/shard_map/ppermute | solution.py:20
  124.8 32.4 %all_to_all.5.got = bf16[32,4,64,128]{3,2,1,0:T(8,128)(2,1)S(1)} all-to-all(bf16[32,4,64,128]{3,2,1,0:T(8,128)(2,1)S(1)} %bitcast.11), channel_id=1, replica_groups=mesh['x'=4,'z'=4,'c'=2,'y'=4] {'x','z','c'}, dimensions={0} | all-to-all | bytes 4194304 | tf_op jit(solution)/shard_map/all_to_all | solution.py:363
  157.2 2.3 %place.1 = f32[4,256,1024]{2,1,0:T(8,128)} custom-call(bf16[32,4,64,128]{3,2,1,0:T(8,128)(2,1)S(1)} %all_to_all.5.got), custom_call_target="tpu_custom_call" | custom-call | tf_op jit(solution)/shard_map/place/pallas_call | solution.py:300
  (54 shorter events, 12.8 us)
Async XLA Ops:
  2.8 28.0 %collective-permute-start = (bf16[128,3072]{1,0:T(8,128)(2,1)S(1)}, bf16[128,3072]{1,0:T(8,128)(2,1)S(1)}, u32[]{:S(2)}, u32[]{:S(2)}) collective-permute-start(bf16[128,3072]{1,0:T(8,128)(2,1)S(1)} %get-tuple-element.47), channel_id=1, source_target_pairs={{0,16},{8,24},{16,0},{24,8},{1,17},{9,25},{17,1},{25,9},{2,18},{10... | collective-permute-start | bytes 2359304 | tf_op jit(solution)/shard_map/ppermute | solution.py:20
  7.3 10.7 %collective-permute-start.1 = (bf16[64,3072]{1,0:T(8,128)(2,1)S(1)}, bf16[64,3072]{1,0:T(8,128)(2,1)S(1)}, u32[]{:S(2)}, u32[]{:S(2)}) collective-permute-start(bf16[64,3072]{1,0:T(8,128)(2,1)S(1)} %get-tuple-element.48), channel_id=1, source_target_pairs={{0,96},{32,0},{64,32},{96,64},{1,97},{33,1},{65,33},{97,65},{2,98}... | collective-permute-start | bytes 1179656 | tf_op jit(solution)/shard_map/ppermute | solution.py:20
  9.8 10.9 %collective-permute-start.2 = (bf16[64,3072]{1,0:T(8,128)(2,1)S(1)}, bf16[64,3072]{1,0:T(8,128)(2,1)S(1)}, u32[]{:S(2)}, u32[]{:S(2)}) collective-permute-start(bf16[64,3072]{1,0:T(8,128)(2,1)S(1)} %get-tuple-element.49), channel_id=1, source_target_pairs={{0,64},{32,96},{64,0},{96,32},{1,65},{33,97},{65,1},{97,33},{2,66}... | collective-permute-start | bytes 1179656 | tf_op jit(solution)/shard_map/ppermute | solution.py:20
  10.3 20.4 %collective-permute-start.3 = (bf16[64,3072]{1,0:T(8,128)(2,1)S(1)}, bf16[64,3072]{1,0:T(8,128)(2,1)S(1)}, u32[]{:S(2)}, u32[]{:S(2)}) collective-permute-start(bf16[64,3072]{1,0:T(8,128)(2,1)S(1)} %get-tuple-element.50), channel_id=1, source_target_pairs={{0,32},{32,64},{64,96},{96,0},{1,33},{33,65},{65,97},{97,1},{2,34}... | collective-permute-start | bytes 1179656 | tf_op jit(solution)/shard_map/ppermute | solution.py:20
  30.9 4.4 %copy-start.2 = (s32[64,2]{0,1:T(2,128)S(1)}, s32[64,2]{0,1:T(2,128)}, u32[]{:S(2)}) copy-start(s32[64,2]{0,1:T(2,128)} %param.6) | copy-start | bytes 1540
  30.9 4.3 %copy-start.1 = (s32[64,1]{0,1:T(1,128)S(1)}, s32[64,1]{0,1:T(1,128)}, u32[]{:S(2)}) copy-start(s32[64,1]{0,1:T(1,128)} %param.7) | copy-start | bytes 772
  31.0 36.8 %collective-permute-start.5 = (bf16[256,3072]{1,0:T(8,128)(2,1)S(1)}, bf16[256,3072]{1,0:T(8,128)(2,1)S(1)}, u32[]{:S(2)}, u32[]{:S(2)}) collective-permute-start(bf16[256,3072]{1,0:T(8,128)(2,1)S(1)} %slice_dynamic-update-slice_fusion.refs_0_), channel_id=1, source_target_pairs={{0,8},{8,16},{16,24},{24,0},{1,9},{9,17},{17,25},{25,1},{2,10},{10... | collective-permute-start | bytes 4718600 | tf_op jit(solution)/shard_map/ppermute | solution.py:20
  31.9 35.9 %collective-permute-start.4 = (bf16[256,3072]{1,0:T(8,128)(2,1)S(1)}, bf16[256,3072]{1,0:T(8,128)(2,1)S(1)}, u32[]{:S(2)}, u32[]{:S(2)}) collective-permute-start(bf16[256,3072]{1,0:T(8,128)(2,1)S(1)} %slice_dynamic-update-slice_fusion.refs_0_), channel_id=1, source_target_pairs={{0,24},{8,0},{16,8},{24,16},{1,25},{9,1},{17,9},{25,17},{2,26},{10... | collective-permute-start | bytes 4718600 | tf_op jit(solution)/shard_map/ppermute | solution.py:20
  33.8 35.4 %collective-permute-start.7 = (bf16[256,3072]{1,0:T(8,128)(2,1)S(1)}, bf16[256,3072]{1,0:T(8,128)(2,1)S(1)}, u32[]{:S(2)}, u32[]{:S(2)}) collective-permute-start(bf16[256,3072]{1,0:T(8,128)(2,1)S(1)} %pad_maximum_fusion.refs_0_.refs_6_.refs_2_), channel_id=1, source_target_pairs={{0,96},{32,0},{64,32},{96,64},{1,97},{33,1},{65,33},{97,65},{2,98}... | collective-permute-start | bytes 4718600 | tf_op jit(solution)/shard_map/ppermute | solution.py:20
  33.8 35.4 %collective-permute-start.6 = (bf16[256,3072]{1,0:T(8,128)(2,1)S(1)}, bf16[256,3072]{1,0:T(8,128)(2,1)S(1)}, u32[]{:S(2)}, u32[]{:S(2)}) collective-permute-start(bf16[256,3072]{1,0:T(8,128)(2,1)S(1)} %pad_maximum_fusion.refs_0_.refs_6_.refs_2_), channel_id=1, source_target_pairs={{0,32},{32,64},{64,96},{96,0},{1,33},{33,65},{65,97},{97,1},{2,34}... | collective-permute-start | bytes 4718600 | tf_op jit(solution)/shard_map/ppermute | solution.py:20
  38.8 33.4 %collective-permute-start.12 = (bf16[256,3072]{1,0:T(8,128)(2,1)S(1)}, bf16[256,3072]{1,0:T(8,128)(2,1)S(1)}, u32[]{:S(2)}, u32[]{:S(2)}) collective-permute-start(bf16[256,3072]{1,0:T(8,128)(2,1)S(1)} %slice_dynamic-update-slice_fusion.refs_0_), channel_id=1, source_target_pairs={{0,4},{4,0},{1,5},{5,1},{2,6},{6,2},{3,7},{7,3},{8,12},{12,8},{9,1... | collective-permute-start | bytes 4718600 | tf_op jit(solution)/shard_map/ppermute | solution.py:334
  67.8 4.5 %collective-permute-start.13 = (bf16[256,3072]{1,0:T(8,128)(2,1)S(1)}, bf16[256,3072]{1,0:T(8,128)(2,1)S(1)}, u32[]{:S(2)}, u32[]{:S(2)}) collective-permute-start(bf16[256,3072]{1,0:T(8,128)(2,1)S(1)} %collective-permute-done.4.refs_1_), channel_id=1, source_target_pairs={{0,4},{4,0},{1,5},{5,1},{2,6},{6,2},{3,7},{7,3},{8,12},{12,8},{9,1... | collective-permute-start | bytes 4718600 | tf_op jit(solution)/shard_map/ppermute | solution.py:341
  69.1 6.5 %collective-permute-start.14 = (bf16[256,3072]{1,0:T(8,128)(2,1)S(1)}, bf16[256,3072]{1,0:T(8,128)(2,1)S(1)}, u32[]{:S(2)}, u32[]{:S(2)}) collective-permute-start(bf16[256,3072]{1,0:T(8,128)(2,1)S(1)} %collective-permute-done.5.refs_2_), channel_id=1, source_target_pairs={{0,4},{4,0},{1,5},{5,1},{2,6},{6,2},{3,7},{7,3},{8,12},{12,8},{9,1... | collective-permute-start | bytes 4718600 | tf_op jit(solution)/shard_map/ppermute | solution.py:341
  69.4 17.7 %collective-permute-start.10 = (bf16[128,3072]{1,0:T(8,128)(2,1)S(1)}, bf16[128,3072]{1,0:T(8,128)(2,1)S(1)}, u32[]{:S(2)}, u32[]{:S(2)}) collective-permute-start(bf16[128,3072]{1,0:T(8,128)(2,1)S(1)} %slice.54), channel_id=1, source_target_pairs={{0,32},{32,64},{64,96},{96,0},{1,33},{33,65},{65,97},{97,1},{2,34}... | collective-permute-start | bytes 2359304 | tf_op jit(solution)/shard_map/ppermute | solution.py:20
  70.0 17.1 %collective-permute-start.11 = (bf16[128,3072]{1,0:T(8,128)(2,1)S(1)}, bf16[128,3072]{1,0:T(8,128)(2,1)S(1)}, u32[]{:S(2)}, u32[]{:S(2)}) collective-permute-start(bf16[128,3072]{1,0:T(8,128)(2,1)S(1)} %slice.55), channel_id=1, source_target_pairs={{0,96},{32,0},{64,32},{96,64},{1,97},{33,1},{65,33},{97,65},{2,98}... | collective-permute-start | bytes 2359304 | tf_op jit(solution)/shard_map/ppermute | solution.py:20
  72.2 12.9 %collective-permute-start.8 = (bf16[80,3072]{1,0:T(8,128)(2,1)S(1)}, bf16[80,3072]{1,0:T(8,128)(2,1)S(1)}, u32[]{:S(2)}, u32[]{:S(2)}) collective-permute-start(bf16[80,3072]{1,0:T(8,128)(2,1)S(1)} %slice.56), channel_id=1, source_target_pairs={{0,8},{8,16},{16,24},{24,0},{1,9},{9,17},{17,25},{25,1},{2,10},{10... | collective-permute-start | bytes 1474568 | tf_op jit(solution)/shard_map/ppermute | solution.py:20
  72.3 12.8 %collective-permute-start.9 = (bf16[80,3072]{1,0:T(8,128)(2,1)S(1)}, bf16[80,3072]{1,0:T(8,128)(2,1)S(1)}, u32[]{:S(2)}, u32[]{:S(2)}) collective-permute-start(bf16[80,3072]{1,0:T(8,128)(2,1)S(1)} %slice.57), channel_id=1, source_target_pairs={{0,24},{8,0},{16,8},{24,16},{1,25},{9,1},{17,9},{25,17},{2,26},{10... | collective-permute-start | bytes 1474568 | tf_op jit(solution)/shard_map/ppermute | solution.py:20
  82.1 5.6 %collective-permute-start.15 = (bf16[9,64,128]{2,1,0:T(8,128)(2,1)S(1)}, bf16[9,64,128]{2,1,0:T(8,128)(2,1)S(1)}, u32[]{:S(2)}, u32[]{:S(2)}) collective-permute-start(bf16[9,64,128]{2,1,0:T(8,128)(2,1)S(1)} %get-tuple-element.67), channel_id=1, source_target_pairs={{0,2},{1,3},{2,0},{3,1},{4,6},{5,7},{6,4},{7,5},{8,10},{9,11},{10,... | collective-permute-start | bytes 442376 | tf_op jit(solution)/shard_map/ppermute | solution.py:20
  87.8 11.1 %collective-permute-start.16 = (bf16[256,3072]{1,0:T(8,128)(2,1)S(1)}, bf16[256,3072]{1,0:T(8,128)(2,1)S(1)}, u32[]{:S(2)}, u32[]{:S(2)}) collective-permute-start(bf16[256,3072]{1,0:T(8,128)(2,1)S(1)} %constant_dynamic-update-slice_fusion.refs_0_), channel_id=1, source_target_pairs={{0,4},{4,0},{1,5},{5,1},{2,6},{6,2},{3,7},{7,3},{8,12},{12,8},{9,1... | collective-permute-start | bytes 4718600 | tf_op jit(solution)/shard_map/ppermute | solution.py:352
  95.9 9.3 %collective-permute-start.17 = (bf16[16,64,128]{2,1,0:T(8,128)(2,1)S(1)}, bf16[16,64,128]{2,1,0:T(8,128)(2,1)S(1)}, u32[]{:S(2)}, u32[]{:S(2)}) collective-permute-start(bf16[16,64,128]{2,1,0:T(8,128)(2,1)S(1)} %get-tuple-element.78), channel_id=1, source_target_pairs={{0,1},{1,2},{2,3},{3,0},{4,5},{5,6},{6,7},{7,4},{8,9},{9,10},{10,1... | collective-permute-start | bytes 786440 | tf_op jit(solution)/shard_map/ppermute | solution.py:20
  97.2 8.0 %collective-permute-start.18 = (bf16[16,64,128]{2,1,0:T(8,128)(2,1)S(1)}, bf16[16,64,128]{2,1,0:T(8,128)(2,1)S(1)}, u32[]{:S(2)}, u32[]{:S(2)}) collective-permute-start(bf16[16,64,128]{2,1,0:T(8,128)(2,1)S(1)} %get-tuple-element.79), channel_id=1, source_target_pairs={{0,3},{1,0},{2,1},{3,2},{4,7},{5,4},{6,5},{7,6},{8,11},{9,8},{10,9... | collective-permute-start | bytes 786440 | tf_op jit(solution)/shard_map/ppermute | solution.py:20
  103.1 20.7 %collective-permute-start.20 = (bf16[27,64,128]{2,1,0:T(8,128)(2,1)S(1)}, bf16[27,64,128]{2,1,0:T(8,128)(2,1)S(1)}, u32[]{:S(2)}, u32[]{:S(2)}) collective-permute-start(bf16[27,64,128]{2,1,0:T(8,128)(2,1)S(1)} %get-tuple-element.83), channel_id=1, source_target_pairs={{0,2},{1,3},{2,0},{3,1},{4,6},{5,7},{6,4},{7,5},{8,10},{9,11},{10,... | collective-permute-start | bytes 1327112 | tf_op jit(solution)/shard_map/ppermute | solution.py:20
  105.2 16.5 %collective-permute-start.21 = (bf16[20,64,128]{2,1,0:T(8,128)(2,1)S(1)}, bf16[20,64,128]{2,1,0:T(8,128)(2,1)S(1)}, u32[]{:S(2)}, u32[]{:S(2)}) collective-permute-start(bf16[20,64,128]{2,1,0:T(8,128)(2,1)S(1)} %get-tuple-element.84), channel_id=1, source_target_pairs={{0,3},{1,0},{2,1},{3,2},{4,7},{5,4},{6,5},{7,6},{8,11},{9,8},{10,9... | collective-permute-start | bytes 983048 | tf_op jit(solution)/shard_map/ppermute | solution.py:20
  108.1 15.7 %collective-permute-start.19 = (bf16[20,64,128]{2,1,0:T(8,128)(2,1)S(1)}, bf16[20,64,128]{2,1,0:T(8,128)(2,1)S(1)}, u32[]{:S(2)}, u32[]{:S(2)}) collective-permute-start(bf16[20,64,128]{2,1,0:T(8,128)(2,1)S(1)} %get-tuple-element.82), channel_id=1, source_target_pairs={{0,1},{1,2},{2,3},{3,0},{4,5},{5,6},{6,7},{7,4},{8,9},{9,10},{10,1... | collective-permute-start | bytes 983048 | tf_op jit(solution)/shard_map/ppermute | solution.py:20
  (1 other events, 1.9 us)

commit v9 on v8

--- a/solution.py
+++ b/solution.py
@@ -321,9 +321,7 @@
     keep, send, *mine = prepare(meta, densities, weights, -(-k // 128) * 128)
     got = shift(send, "z", 2)
     other = [(0, 1), (1, 0)]
-    got, e1, e2, e3 = tie(
-        got, shift(mine[3], "x", 3), shift(mine[2], "x", 2), shift(mine[1], "x", 1)
-    )
+    e1, e2, e3 = shift(mine[3], "x", 3), shift(mine[2], "x", 2), shift(mine[1], "x", 1)
     right = jnp.concatenate([keep, got], 0)
     pieces = [mine[0], e1, e2, e3]
     left = jnp.concatenate([pieces[k][32 * h : 32 * h + 32] for h, k in ORDER], 0)
@@ -343,7 +341,6 @@
     rights = [right, right1, right3]
 
     held = derive(meta, weights, rights)
-    order1, held = tie(order1, held)
     first, second = [meta, order1], [meta, order1, order2]
     near, sums = grams(early_kernel, "early", first, lefts + rights, parts=[NEAR])
     near = shift(near, "y", 2)

time: 160 us -> 158 us (0.988)
  waiting for transfers between devices: 66.2 us -> 63.3 us
    ppermute x1, starting transfers between devices: 4.94 us -> 1.43 us  [on_device(): swap2 = lax.ppermute(left2, 'c', other)]
    ppermute x18, waiting for transfers between devices: 66.2 us -> 63.3 us  [shift(): return lax.ppermute(a, axis, [(i, (i + d) % 4) for i in range(4)])]
    ppermute x18, starting transfers between devices: 28.2 us -> 30.5 us  [shift(): return lax.ppermute(a, axis, [(i, (i + d) % 4) for i in range(4)])]
  transfers between devices with their start and end apart: 22 -> 22, of which waited for: 10 -> 9; matrix products, arithmetic and copies ran while one was open for 0% -> 0% of each run, Pallas kernels for 11% -> 11%
where the time goes in v9:
time: 158 us; the launch traced here: 157 us
  waiting for transfers between devices  63.3 us (40%)
  starting transfers between devices  37.1 us (23%)
  blocking collectives  32.1 us (20%)
  Pallas kernels  22.2 us (14%)
  local copies, waits for them, and re-layouts  2.08 us (1%)
    ppermute x18, waiting for transfers between devices, shift(): return lax.ppermute(a, axis, [(i, (i + d) % 4) for i in range(4)])  63.3 us
    all_to_all x1, blocking collectives, on_device(): arrived = lax.all_to_all(routed, ('x', 'z', 'c'), 0, 0, tiled=True)  32.1 us
    ppermute x18, starting transfers between devices, shift(): return lax.ppermute(a, axis, [(i, (i + d) % 4) for i in range(4)])  30.5 us
    pallas_call x3, Pallas kernels, grams(): pl.pallas_call(kernel, out_shape=shapes, in_specs=[smem] * len(scalars) +...  13.7 us
    pallas_call x1, Pallas kernels, plan(): pl.pallas_call(plan_kernel, out_shape=[jax.ShapeDtypeStruct((n,), jnp.int...  3.48 us
  transfers between devices with their start and end apart: 22, of which 9 were waited for; matrix products, arithmetic and copies ran while one was open for 0% of the time, Pallas kernels for 11%

profile of v9, /device:TPU:1, one launch (start us, length us, event | category | flops | bytes accessed | tf_op | source)
XLA Modules:
  0.0 157.5 jit_solution(8422383034584086696)
XLA Ops:
  2.8 3.4 %collective-permute-start.1 = (bf16[64,3072]{1,0:T(8,128)(2,1)S(1)}, bf16[64,3072]{1,0:T(8,128)(2,1)S(1)}, u32[]{:S(2)}, u32[]{:S(2)}) collective-permute-start(bf16[64,3072]{1,0:T(8,128)(2,1)S(1)} %get-tuple-element.43), channel_id=1, source_target_pairs={{0,96},{32,0},{64,32},{96,64},{1,97},{33,1},{65,33},{97,65},{2,98}... | collective-permute-start | bytes 1179656 | tf_op jit(solution)/shard_map/ppermute | solution.py:20
  7.3 3.6 %collective-permute-start = (bf16[128,3072]{1,0:T(8,128)(2,1)S(1)}, bf16[128,3072]{1,0:T(8,128)(2,1)S(1)}, u32[]{:S(2)}, u32[]{:S(2)}) collective-permute-start(bf16[128,3072]{1,0:T(8,128)(2,1)S(1)} %get-tuple-element.41), channel_id=1, source_target_pairs={{0,16},{8,24},{16,0},{24,8},{1,17},{9,25},{17,1},{25,9},{2,18},{10... | collective-permute-start | bytes 2359304 | tf_op jit(solution)/shard_map/ppermute | solution.py:20
  10.9 4.2 %collective-permute-done.1 = bf16[64,3072]{1,0:T(8,128)(2,1)S(1)} collective-permute-done((bf16[64,3072]{1,0:T(8,128)(2,1)S(1)}, bf16[64,3072]{1,0:T(8,128)(2,1)S(1)}, u32[]{:S(2)}, u32[]{:S(2)}) %collective-permute-start.1) | collective-permute-done | bytes 393248 | tf_op jit(solution)/shard_map/ppermute | solution.py:20
  15.2 2.2 %collective-permute-done.2 = bf16[64,3072]{1,0:T(8,128)(2,1)S(1)} collective-permute-done((bf16[64,3072]{1,0:T(8,128)(2,1)S(1)}, bf16[64,3072]{1,0:T(8,128)(2,1)S(1)}, u32[]{:S(2)}, u32[]{:S(2)}) %collective-permute-start.2) | collective-permute-done | bytes 393248 | tf_op jit(solution)/shard_map/ppermute | solution.py:20
  17.4 9.7 %collective-permute-done.3 = bf16[64,3072]{1,0:T(8,128)(2,1)S(1)} collective-permute-done((bf16[64,3072]{1,0:T(8,128)(2,1)S(1)}, bf16[64,3072]{1,0:T(8,128)(2,1)S(1)}, u32[]{:S(2)}, u32[]{:S(2)}) %collective-permute-start.3) | collective-permute-done | bytes 393248 | tf_op jit(solution)/shard_map/ppermute | solution.py:20
  27.4 3.8 %collective-permute-start.4 = (bf16[256,3072]{1,0:T(8,128)(2,1)S(1)}, bf16[256,3072]{1,0:T(8,128)(2,1)S(1)}, u32[]{:S(2)}, u32[]{:S(2)}) collective-permute-start(bf16[256,3072]{1,0:T(8,128)(2,1)S(1)} %slice_dynamic-update-slice_fusion.refs_0_), channel_id=1, source_target_pairs={{0,24},{8,0},{16,8},{24,16},{1,25},{9,1},{17,9},{25,17},{2,26},{10... | collective-permute-start | bytes 4718600 | tf_op jit(solution)/shard_map/ppermute | solution.py:20
  31.8 2.1 %collective-permute-start.9 = (bf16[256,3072]{1,0:T(8,128)(2,1)S(1)}, bf16[256,3072]{1,0:T(8,128)(2,1)S(1)}, u32[]{:S(2)}, u32[]{:S(2)}) collective-permute-start(bf16[256,3072]{1,0:T(8,128)(2,1)S(1)} %pad_maximum_fusion.refs_6_.refs_0_.refs_2_), channel_id=1, source_target_pairs={{0,96},{32,0},{64,32},{96,64},{1,97},{33,1},{65,33},{97,65},{2,98}... | collective-permute-start | bytes 4718600 | tf_op jit(solution)/shard_map/ppermute | solution.py:20
  33.9 3.5 %plan.1 = (s32[128]{0:T(128)S(1)}, s32[17]{0:T(128)S(1)}, s32[21]{0:T(128)S(1)}) custom-call(s32[4]{0:T(128)S(1)} %pad_add_fusion.meta, s32[64]{0:T(128)S(1)} %get-tuple-element.74.first, s32[64]{0:T(128)S(1)} %get-tuple-element.73.second, s32[64]{0:T(128)S(1)} %bitcast.14), custom_call_target="tpu_custom_call" | custom-call | tf_op jit(solution)/shard_map/plan/pallas_call | solution.py:268
  37.4 2.4 %collective-permute-start.12 = (bf16[256,3072]{1,0:T(8,128)(2,1)S(1)}, bf16[256,3072]{1,0:T(8,128)(2,1)S(1)}, u32[]{:S(2)}, u32[]{:S(2)}) collective-permute-start(bf16[256,3072]{1,0:T(8,128)(2,1)S(1)} %slice_dynamic-update-slice_fusion.refs_0_), channel_id=1, source_target_pairs={{0,4},{4,0},{1,5},{5,1},{2,6},{6,2},{3,7},{7,3},{8,12},{12,8},{9,1... | collective-permute-start | bytes 4718600 | tf_op jit(solution)/shard_map/ppermute | solution.py:332
  39.8 23.6 %collective-permute-done.4.refs_1_ = bf16[256,3072]{1,0:T(8,128)(2,1)S(1)} collective-permute-done((bf16[256,3072]{1,0:T(8,128)(2,1)S(1)}, bf16[256,3072]{1,0:T(8,128)(2,1)S(1)}, u32[]{:S(2)}, u32[]{:S(2)}) %collective-permute-start.4) | collective-permute-done | bytes 1572896 | tf_op jit(solution)/shard_map/ppermute | solution.py:20
  63.4 3.1 %collective-permute-done.5.refs_2_ = bf16[256,3072]{1,0:T(8,128)(2,1)S(1)} collective-permute-done((bf16[256,3072]{1,0:T(8,128)(2,1)S(1)}, bf16[256,3072]{1,0:T(8,128)(2,1)S(1)}, u32[]{:S(2)}, u32[]{:S(2)}) %collective-permute-start.5) | collective-permute-done | bytes 1572896 | tf_op jit(solution)/shard_map/ppermute | solution.py:20
  66.5 2.7 %collective-permute-start.13 = (bf16[256,3072]{1,0:T(8,128)(2,1)S(1)}, bf16[256,3072]{1,0:T(8,128)(2,1)S(1)}, u32[]{:S(2)}, u32[]{:S(2)}) collective-permute-start(bf16[256,3072]{1,0:T(8,128)(2,1)S(1)} %collective-permute-done.4.refs_1_), channel_id=1, source_target_pairs={{0,4},{4,0},{1,5},{5,1},{2,6},{6,2},{3,7},{7,3},{8,12},{12,8},{9,1... | collective-permute-start | bytes 4718600 | tf_op jit(solution)/shard_map/ppermute | solution.py:339
  70.0 2.2 %collective-permute-start.11 = (bf16[128,3072]{1,0:T(8,128)(2,1)S(1)}, bf16[128,3072]{1,0:T(8,128)(2,1)S(1)}, u32[]{:S(2)}, u32[]{:S(2)}) collective-permute-start(bf16[128,3072]{1,0:T(8,128)(2,1)S(1)} %slice.55), channel_id=1, source_target_pairs={{0,96},{32,0},{64,32},{96,64},{1,97},{33,1},{65,33},{97,65},{2,98}... | collective-permute-start | bytes 2359304 | tf_op jit(solution)/shard_map/ppermute | solution.py:20
  72.4 2.7 %collective-permute-start.7 = (bf16[80,3072]{1,0:T(8,128)(2,1)S(1)}, bf16[80,3072]{1,0:T(8,128)(2,1)S(1)}, u32[]{:S(2)}, u32[]{:S(2)}) collective-permute-start(bf16[80,3072]{1,0:T(8,128)(2,1)S(1)} %slice.63), channel_id=1, source_target_pairs={{0,24},{8,0},{16,8},{24,16},{1,25},{9,1},{17,9},{25,17},{2,26},{10... | collective-permute-start | bytes 1474568 | tf_op jit(solution)/shard_map/ppermute | solution.py:20
  75.0 6.5 %early.1 = (bf16[9,64,128]{2,1,0:T(8,128)(2,1)S(1)}, f32[4,37,64,128]{3,2,1,0:T(8,128)S(1)}) custom-call(s32[4]{0:T(128)S(1)} %pad_add_fusion.meta, s32[17]{0:T(128)S(1)} %get-tuple-element.48.order.order1, bf16[256,3072]{1,0:T(8,128)(2,1)S(1)} %slice_dynamic-update-slice_fusion.refs_0_, bf16[256,3072]{1,0:T(8,128)(2,1)S(1)} %collective-permute-done.4.refs_1_, ...), custom_call_target="tpu_custom_call" | custom-call | flops 3221225472 | bytes 1048576 | tf_op jit(solution)/shard_map/early/pallas_call | solution.py:151
  81.5 3.0 %collective-permute-start.15 = (bf16[9,64,128]{2,1,0:T(8,128)(2,1)S(1)}, bf16[9,64,128]{2,1,0:T(8,128)(2,1)S(1)}, u32[]{:S(2)}, u32[]{:S(2)}) collective-permute-start(bf16[9,64,128]{2,1,0:T(8,128)(2,1)S(1)} %get-tuple-element.56), channel_id=1, source_target_pairs={{0,2},{1,3},{2,0},{3,1},{4,6},{5,7},{6,4},{7,5},{8,10},{9,11},{10,... | collective-permute-start | bytes 442376 | tf_op jit(solution)/shard_map/ppermute | solution.py:20
  85.2 4.0 %collective-permute-done.10.refs_6_.refs_5_ = bf16[128,3072]{1,0:T(8,128)(2,1)S(1)} collective-permute-done((bf16[128,3072]{1,0:T(8,128)(2,1)S(1)}, bf16[128,3072]{1,0:T(8,128)(2,1)S(1)}, u32[]{:S(2)}, u32[]{:S(2)}) %collective-permute-start.10) | collective-permute-done | bytes 786464 | tf_op jit(solution)/shard_map/ppermute | solution.py:20
  90.7 3.1 %middle.1 = (bf16[16,64,128]{2,1,0:T(8,128)(2,1)S(1)}, bf16[16,64,128]{2,1,0:T(8,128)(2,1)S(1)}, f32[4,37,64,128]{3,2,1,0:T(8,128)S(1)}) custom-call(s32[4]{0:T(128)S(1)} %pad_add_fusion.meta, s32[17]{0:T(128)S(1)} %get-tuple-element.48.order.order1, bf16[256,3072]{1,0:T(8,128)(2,1)S(1)} %slice_dynamic-update-slice_fusion.refs_0_, ...), custom_call_target="tpu_custom_call", output_to_operand_aliasing={{2}: (10, {})} | custom-call | flops 3221225472 | bytes 1048576 | tf_op jit(solution)/shard_map/middle/pallas_call | solution.py:151
  96.9 4.2 %late.1 = (bf16[20,64,128]{2,1,0:T(8,128)(2,1)S(1)}, bf16[27,64,128]{2,1,0:T(8,128)(2,1)S(1)}, bf16[20,64,128]{2,1,0:T(8,128)(2,1)S(1)}, f32[4,37,64,128]{3,2,1,0:T(8,128)S(1)}) custom-call(s32[4]{0:T(128)S(1)} %pad_add_fusion.meta, s32[17]{0:T(128)S(1)} %get-tuple-element.48.order.order1, ...), custom_call_target="tpu_custom_call", output_to_operand_aliasing={{3}: (10, {})} | custom-call | flops 3221225472 | bytes 1048576 | tf_op jit(solution)/shard_map/late/pallas_call | solution.py:151
  103.2 2.9 %collective-permute-start.21 = (bf16[20,64,128]{2,1,0:T(8,128)(2,1)S(1)}, bf16[20,64,128]{2,1,0:T(8,128)(2,1)S(1)}, u32[]{:S(2)}, u32[]{:S(2)}) collective-permute-start(bf16[20,64,128]{2,1,0:T(8,128)(2,1)S(1)} %get-tuple-element.72), channel_id=1, source_target_pairs={{0,3},{1,0},{2,1},{3,2},{4,7},{5,4},{6,5},{7,6},{8,11},{9,8},{10,9... | collective-permute-start | bytes 983048 | tf_op jit(solution)/shard_map/ppermute | solution.py:20
  106.0 13.6 %collective-permute-done.21.refs_5_ = bf16[20,64,128]{2,1,0:T(8,128)(2,1)S(1)} collective-permute-done((bf16[20,64,128]{2,1,0:T(8,128)(2,1)S(1)}, bf16[20,64,128]{2,1,0:T(8,128)(2,1)S(1)}, u32[]{:S(2)}, u32[]{:S(2)}) %collective-permute-start.21) | collective-permute-done | bytes 327712 | tf_op jit(solution)/shard_map/ppermute | solution.py:20
  119.7 2.1 %collective-permute-done.19.refs_3_ = bf16[20,64,128]{2,1,0:T(8,128)(2,1)S(1)} collective-permute-done((bf16[20,64,128]{2,1,0:T(8,128)(2,1)S(1)}, bf16[20,64,128]{2,1,0:T(8,128)(2,1)S(1)}, u32[]{:S(2)}, u32[]{:S(2)}) %collective-permute-start.19) | collective-permute-done | bytes 327712 | tf_op jit(solution)/shard_map/ppermute | solution.py:20
  122.8 32.1 %all_to_all.5.got = bf16[32,4,64,128]{3,2,1,0:T(8,128)(2,1)S(1)} all-to-all(bf16[32,4,64,128]{3,2,1,0:T(8,128)(2,1)S(1)} %bitcast.11), channel_id=1, replica_groups=mesh['x'=4,'z'=4,'c'=2,'y'=4] {'x','z','c'}, dimensions={0} | all-to-all | bytes 4194304 | tf_op jit(solution)/shard_map/all_to_all | solution.py:360
  155.0 2.3 %place.1 = f32[4,256,1024]{2,1,0:T(8,128)} custom-call(bf16[32,4,64,128]{3,2,1,0:T(8,128)(2,1)S(1)} %all_to_all.5.got), custom_call_target="tpu_custom_call" | custom-call | tf_op jit(solution)/shard_map/place/pallas_call | solution.py:300
  (52 shorter events, 14.1 us)
Async XLA Ops:
  2.8 12.4 %collective-permute-start.1 = (bf16[64,3072]{1,0:T(8,128)(2,1)S(1)}, bf16[64,3072]{1,0:T(8,128)(2,1)S(1)}, u32[]{:S(2)}, u32[]{:S(2)}) collective-permute-start(bf16[64,3072]{1,0:T(8,128)(2,1)S(1)} %get-tuple-element.43), channel_id=1, source_target_pairs={{0,96},{32,0},{64,32},{96,64},{1,97},{33,1},{65,33},{97,65},{2,98}... | collective-permute-start | bytes 1179656 | tf_op jit(solution)/shard_map/ppermute | solution.py:20
  6.2 11.2 %collective-permute-start.2 = (bf16[64,3072]{1,0:T(8,128)(2,1)S(1)}, bf16[64,3072]{1,0:T(8,128)(2,1)S(1)}, u32[]{:S(2)}, u32[]{:S(2)}) collective-permute-start(bf16[64,3072]{1,0:T(8,128)(2,1)S(1)} %get-tuple-element.44), channel_id=1, source_target_pairs={{0,64},{32,96},{64,0},{96,32},{1,65},{33,97},{65,1},{97,33},{2,66}... | collective-permute-start | bytes 1179656 | tf_op jit(solution)/shard_map/ppermute | solution.py:20
  6.7 20.4 %collective-permute-start.3 = (bf16[64,3072]{1,0:T(8,128)(2,1)S(1)}, bf16[64,3072]{1,0:T(8,128)(2,1)S(1)}, u32[]{:S(2)}, u32[]{:S(2)}) collective-permute-start(bf16[64,3072]{1,0:T(8,128)(2,1)S(1)} %get-tuple-element.45), channel_id=1, source_target_pairs={{0,32},{32,64},{64,96},{96,0},{1,33},{33,65},{65,97},{97,1},{2,34}... | collective-permute-start | bytes 1179656 | tf_op jit(solution)/shard_map/ppermute | solution.py:20
  7.3 19.9 %collective-permute-start = (bf16[128,3072]{1,0:T(8,128)(2,1)S(1)}, bf16[128,3072]{1,0:T(8,128)(2,1)S(1)}, u32[]{:S(2)}, u32[]{:S(2)}) collective-permute-start(bf16[128,3072]{1,0:T(8,128)(2,1)S(1)} %get-tuple-element.41), channel_id=1, source_target_pairs={{0,16},{8,24},{16,0},{24,8},{1,17},{9,25},{17,1},{25,9},{2,18},{10... | collective-permute-start | bytes 2359304 | tf_op jit(solution)/shard_map/ppermute | solution.py:20
  27.2 6.6 %copy-start.2 = (s32[64,2]{0,1:T(2,128)S(1)}, s32[64,2]{0,1:T(2,128)}, u32[]{:S(2)}) copy-start(s32[64,2]{0,1:T(2,128)} %param.6) | copy-start | bytes 1540
  27.3 6.6 %copy-start.1 = (s32[64,1]{0,1:T(1,128)S(1)}, s32[64,1]{0,1:T(1,128)}, u32[]{:S(2)}) copy-start(s32[64,1]{0,1:T(1,128)} %param.7) | copy-start | bytes 772
  27.4 36.0 %collective-permute-start.4 = (bf16[256,3072]{1,0:T(8,128)(2,1)S(1)}, bf16[256,3072]{1,0:T(8,128)(2,1)S(1)}, u32[]{:S(2)}, u32[]{:S(2)}) collective-permute-start(bf16[256,3072]{1,0:T(8,128)(2,1)S(1)} %slice_dynamic-update-slice_fusion.refs_0_), channel_id=1, source_target_pairs={{0,24},{8,0},{16,8},{24,16},{1,25},{9,1},{17,9},{25,17},{2,26},{10... | collective-permute-start | bytes 4718600 | tf_op jit(solution)/shard_map/ppermute | solution.py:20
  31.2 35.3 %collective-permute-start.5 = (bf16[256,3072]{1,0:T(8,128)(2,1)S(1)}, bf16[256,3072]{1,0:T(8,128)(2,1)S(1)}, u32[]{:S(2)}, u32[]{:S(2)}) collective-permute-start(bf16[256,3072]{1,0:T(8,128)(2,1)S(1)} %slice_dynamic-update-slice_fusion.refs_0_), channel_id=1, source_target_pairs={{0,8},{8,16},{16,24},{24,0},{1,9},{9,17},{17,25},{25,1},{2,10},{10... | collective-permute-start | bytes 4718600 | tf_op jit(solution)/shard_map/ppermute | solution.py:20
  31.2 38.0 %collective-permute-start.8 = (bf16[256,3072]{1,0:T(8,128)(2,1)S(1)}, bf16[256,3072]{1,0:T(8,128)(2,1)S(1)}, u32[]{:S(2)}, u32[]{:S(2)}) collective-permute-start(bf16[256,3072]{1,0:T(8,128)(2,1)S(1)} %pad_maximum_fusion.refs_6_.refs_0_.refs_2_), channel_id=1, source_target_pairs={{0,32},{32,64},{64,96},{96,0},{1,33},{33,65},{65,97},{97,1},{2,34}... | collective-permute-start | bytes 4718600 | tf_op jit(solution)/shard_map/ppermute | solution.py:20
  31.8 37.4 %collective-permute-start.9 = (bf16[256,3072]{1,0:T(8,128)(2,1)S(1)}, bf16[256,3072]{1,0:T(8,128)(2,1)S(1)}, u32[]{:S(2)}, u32[]{:S(2)}) collective-permute-start(bf16[256,3072]{1,0:T(8,128)(2,1)S(1)} %pad_maximum_fusion.refs_6_.refs_0_.refs_2_), channel_id=1, source_target_pairs={{0,96},{32,0},{64,32},{96,64},{1,97},{33,1},{65,33},{97,65},{2,98}... | collective-permute-start | bytes 4718600 | tf_op jit(solution)/shard_map/ppermute | solution.py:20
  37.4 34.9 %collective-permute-start.12 = (bf16[256,3072]{1,0:T(8,128)(2,1)S(1)}, bf16[256,3072]{1,0:T(8,128)(2,1)S(1)}, u32[]{:S(2)}, u32[]{:S(2)}) collective-permute-start(bf16[256,3072]{1,0:T(8,128)(2,1)S(1)} %slice_dynamic-update-slice_fusion.refs_0_), channel_id=1, source_target_pairs={{0,4},{4,0},{1,5},{5,1},{2,6},{6,2},{3,7},{7,3},{8,12},{12,8},{9,1... | collective-permute-start | bytes 4718600 | tf_op jit(solution)/shard_map/ppermute | solution.py:332
  66.5 5.8 %collective-permute-start.13 = (bf16[256,3072]{1,0:T(8,128)(2,1)S(1)}, bf16[256,3072]{1,0:T(8,128)(2,1)S(1)}, u32[]{:S(2)}, u32[]{:S(2)}) collective-permute-start(bf16[256,3072]{1,0:T(8,128)(2,1)S(1)} %collective-permute-done.4.refs_1_), channel_id=1, source_target_pairs={{0,4},{4,0},{1,5},{5,1},{2,6},{6,2},{3,7},{7,3},{8,12},{12,8},{9,1... | collective-permute-start | bytes 4718600 | tf_op jit(solution)/shard_map/ppermute | solution.py:339
  69.2 5.8 %collective-permute-start.14 = (bf16[256,3072]{1,0:T(8,128)(2,1)S(1)}, bf16[256,3072]{1,0:T(8,128)(2,1)S(1)}, u32[]{:S(2)}, u32[]{:S(2)}) collective-permute-start(bf16[256,3072]{1,0:T(8,128)(2,1)S(1)} %collective-permute-done.5.refs_2_), channel_id=1, source_target_pairs={{0,4},{4,0},{1,5},{5,1},{2,6},{6,2},{3,7},{7,3},{8,12},{12,8},{9,1... | collective-permute-start | bytes 4718600 | tf_op jit(solution)/shard_map/ppermute | solution.py:339
  69.3 19.9 %collective-permute-start.10 = (bf16[128,3072]{1,0:T(8,128)(2,1)S(1)}, bf16[128,3072]{1,0:T(8,128)(2,1)S(1)}, u32[]{:S(2)}, u32[]{:S(2)}) collective-permute-start(bf16[128,3072]{1,0:T(8,128)(2,1)S(1)} %slice.54), channel_id=1, source_target_pairs={{0,32},{32,64},{64,96},{96,0},{1,33},{33,65},{65,97},{97,1},{2,34}... | collective-permute-start | bytes 2359304 | tf_op jit(solution)/shard_map/ppermute | solution.py:20
  70.0 19.2 %collective-permute-start.11 = (bf16[128,3072]{1,0:T(8,128)(2,1)S(1)}, bf16[128,3072]{1,0:T(8,128)(2,1)S(1)}, u32[]{:S(2)}, u32[]{:S(2)}) collective-permute-start(bf16[128,3072]{1,0:T(8,128)(2,1)S(1)} %slice.55), channel_id=1, source_target_pairs={{0,96},{32,0},{64,32},{96,64},{1,97},{33,1},{65,33},{97,65},{2,98}... | collective-permute-start | bytes 2359304 | tf_op jit(solution)/shard_map/ppermute | solution.py:20
  72.3 12.9 %collective-permute-start.6 = (bf16[80,3072]{1,0:T(8,128)(2,1)S(1)}, bf16[80,3072]{1,0:T(8,128)(2,1)S(1)}, u32[]{:S(2)}, u32[]{:S(2)}) collective-permute-start(bf16[80,3072]{1,0:T(8,128)(2,1)S(1)} %slice.62), channel_id=1, source_target_pairs={{0,8},{8,16},{16,24},{24,0},{1,9},{9,17},{17,25},{25,1},{2,10},{10... | collective-permute-start | bytes 1474568 | tf_op jit(solution)/shard_map/ppermute | solution.py:20
  72.4 12.8 %collective-permute-start.7 = (bf16[80,3072]{1,0:T(8,128)(2,1)S(1)}, bf16[80,3072]{1,0:T(8,128)(2,1)S(1)}, u32[]{:S(2)}, u32[]{:S(2)}) collective-permute-start(bf16[80,3072]{1,0:T(8,128)(2,1)S(1)} %slice.63), channel_id=1, source_target_pairs={{0,24},{8,0},{16,8},{24,16},{1,25},{9,1},{17,9},{25,17},{2,26},{10... | collective-permute-start | bytes 1474568 | tf_op jit(solution)/shard_map/ppermute | solution.py:20
  81.5 7.7 %collective-permute-start.15 = (bf16[9,64,128]{2,1,0:T(8,128)(2,1)S(1)}, bf16[9,64,128]{2,1,0:T(8,128)(2,1)S(1)}, u32[]{:S(2)}, u32[]{:S(2)}) collective-permute-start(bf16[9,64,128]{2,1,0:T(8,128)(2,1)S(1)} %get-tuple-element.56), channel_id=1, source_target_pairs={{0,2},{1,3},{2,0},{3,1},{4,6},{5,7},{6,4},{7,5},{8,10},{9,11},{10,... | collective-permute-start | bytes 442376 | tf_op jit(solution)/shard_map/ppermute | solution.py:20
  89.3 7.6 %collective-permute-start.16 = (bf16[256,3072]{1,0:T(8,128)(2,1)S(1)}, bf16[256,3072]{1,0:T(8,128)(2,1)S(1)}, u32[]{:S(2)}, u32[]{:S(2)}) collective-permute-start(bf16[256,3072]{1,0:T(8,128)(2,1)S(1)} %pad_maximum_fusion.1.refs_0_), channel_id=1, source_target_pairs={{0,4},{4,0},{1,5},{5,1},{2,6},{6,2},{3,7},{7,3},{8,12},{12,8},{9,1... | collective-permute-start | bytes 4718600 | tf_op jit(solution)/shard_map/ppermute | solution.py:349
  93.8 9.3 %collective-permute-start.17 = (bf16[16,64,128]{2,1,0:T(8,128)(2,1)S(1)}, bf16[16,64,128]{2,1,0:T(8,128)(2,1)S(1)}, u32[]{:S(2)}, u32[]{:S(2)}) collective-permute-start(bf16[16,64,128]{2,1,0:T(8,128)(2,1)S(1)} %get-tuple-element.66), channel_id=1, source_target_pairs={{0,1},{1,2},{2,3},{3,0},{4,5},{5,6},{6,7},{7,4},{8,9},{9,10},{10,1... | collective-permute-start | bytes 786440 | tf_op jit(solution)/shard_map/ppermute | solution.py:20
  95.2 8.0 %collective-permute-start.18 = (bf16[16,64,128]{2,1,0:T(8,128)(2,1)S(1)}, bf16[16,64,128]{2,1,0:T(8,128)(2,1)S(1)}, u32[]{:S(2)}, u32[]{:S(2)}) collective-permute-start(bf16[16,64,128]{2,1,0:T(8,128)(2,1)S(1)} %get-tuple-element.67), channel_id=1, source_target_pairs={{0,3},{1,0},{2,1},{3,2},{4,7},{5,4},{6,5},{7,6},{8,11},{9,8},{10,9... | collective-permute-start | bytes 786440 | tf_op jit(solution)/shard_map/ppermute | solution.py:20
  101.1 20.7 %collective-permute-start.20 = (bf16[27,64,128]{2,1,0:T(8,128)(2,1)S(1)}, bf16[27,64,128]{2,1,0:T(8,128)(2,1)S(1)}, u32[]{:S(2)}, u32[]{:S(2)}) collective-permute-start(bf16[27,64,128]{2,1,0:T(8,128)(2,1)S(1)} %get-tuple-element.71), channel_id=1, source_target_pairs={{0,2},{1,3},{2,0},{3,1},{4,6},{5,7},{6,4},{7,5},{8,10},{9,11},{10,... | collective-permute-start | bytes 1327112 | tf_op jit(solution)/shard_map/ppermute | solution.py:20
  103.2 16.5 %collective-permute-start.21 = (bf16[20,64,128]{2,1,0:T(8,128)(2,1)S(1)}, bf16[20,64,128]{2,1,0:T(8,128)(2,1)S(1)}, u32[]{:S(2)}, u32[]{:S(2)}) collective-permute-start(bf16[20,64,128]{2,1,0:T(8,128)(2,1)S(1)} %get-tuple-element.72), channel_id=1, source_target_pairs={{0,3},{1,0},{2,1},{3,2},{4,7},{5,4},{6,5},{7,6},{8,11},{9,8},{10,9... | collective-permute-start | bytes 983048 | tf_op jit(solution)/shard_map/ppermute | solution.py:20
  106.0 15.7 %collective-permute-start.19 = (bf16[20,64,128]{2,1,0:T(8,128)(2,1)S(1)}, bf16[20,64,128]{2,1,0:T(8,128)(2,1)S(1)}, u32[]{:S(2)}, u32[]{:S(2)}) collective-permute-start(bf16[20,64,128]{2,1,0:T(8,128)(2,1)S(1)} %get-tuple-element.70), channel_id=1, source_target_pairs={{0,1},{1,2},{2,3},{3,0},{4,5},{5,6},{6,7},{7,4},{8,9},{9,10},{10,1... | collective-permute-start | bytes 983048 | tf_op jit(solution)/shard_map/ppermute | solution.py:20
  (1 other events, 1.9 us)

commit v10 on v9

--- a/solution.py
+++ b/solution.py
@@ -335,7 +335,8 @@
     right2a, right2b = shift(right3[:128], "x", 1), shift(right1[128:], "x", -1)
     late_a, late_b = shift(left3[:SPLIT], "z", 1), shift(left1[SPLIT:END], "z", -1)
     index, order1, order2 = plan(meta, pair_list, owner, 32 * CAP)
-    index, near1, near3 = tie(index, left1, left3)
+    index, near3 = tie(index, left3)
+    near1 = left1
     swap1, swap3 = lax.ppermute(near1, "c", other), lax.ppermute(near3, "c", other)
     lefts = [left, left1, left3, swap0, swap1, swap3]
     rights = [right, right1, right3]

time: 158 us -> 157 us (level)
  waiting for transfers between devices: 63.3 us -> 59.1 us
  starting transfers between devices: 37.1 us -> 40.2 us
    ppermute x18, waiting for transfers between devices: 63.3 us -> 59.1 us  [shift(): return lax.ppermute(a, axis, [(i, (i + d) % 4) for i in range(4)])]
    ppermute x1, starting transfers between devices: 1.43 us -> 4.93 us  [on_device(): swap2 = lax.ppermute(left2, 'c', other)]
    ppermute x1, starting transfers between devices: 2.7 us -> 0.01 us  [on_device(): lax.ppermute(near1, 'c', other)]
    ppermute x1, starting transfers between devices: 0.01 us -> 2.14 us  [on_device(): lax.ppermute(near3, 'c', other)]
where the time goes in v10:
time: 157 us
  waiting for transfers between devices  59.1 us (38%)
  starting transfers between devices  40.2 us (26%)
  blocking collectives  33 us (21%)
  Pallas kernels  22.2 us (14%)
  local copies, waits for them, and re-layouts  2.08 us (1%)
    ppermute x18, waiting for transfers between devices, shift(): return lax.ppermute(a, axis, [(i, (i + d) % 4) for i in range(4)])  59.1 us
    all_to_all x1, blocking collectives, on_device(): arrived = lax.all_to_all(routed, ('x', 'z', 'c'), 0, 0, tiled=True)  33 us
    ppermute x18, starting transfers between devices, shift(): return lax.ppermute(a, axis, [(i, (i + d) % 4) for i in range(4)])  30.7 us
    pallas_call x3, Pallas kernels, grams(): pl.pallas_call(kernel, out_shape=shapes, in_specs=[smem] * len(scalars) +...  13.8 us
    ppermute x1, starting transfers between devices, on_device(): swap2 = lax.ppermute(left2, 'c', other)  4.93 us
    pallas_call x1, Pallas kernels, plan(): pl.pallas_call(plan_kernel, out_shape=[jax.ShapeDtypeStruct((n,), jnp.int...  3.48 us
  transfers between devices with their start and end apart: 22, of which 9 were waited for; matrix products, arithmetic and copies ran while one was open for 0% of the time, Pallas kernels for 11%

profile of v10, /device:TPU:1, one launch (start us, length us, event | category | flops | bytes accessed | tf_op | source)
XLA Modules:
  0.0 157.3 jit_solution(15725728862902823456)
XLA Ops:
  0.0 1.8 %copy.7.dens = bf16[256,3000]{1,0:T(8,128)(2,1)S(1)} copy(bf16[256,3000]{0,1:T(8,128)(2,1)} %param.4) | data formatting | bytes 3072000 | tf_op args[0]
  2.8 3.4 %collective-permute-start.1 = (bf16[64,3072]{1,0:T(8,128)(2,1)S(1)}, bf16[64,3072]{1,0:T(8,128)(2,1)S(1)}, u32[]{:S(2)}, u32[]{:S(2)}) collective-permute-start(bf16[64,3072]{1,0:T(8,128)(2,1)S(1)} %get-tuple-element.42), channel_id=1, source_target_pairs={{0,96},{32,0},{64,32},{96,64},{1,97},{33,1},{65,33},{97,65},{2,98}... | collective-permute-start | bytes 1179656 | tf_op jit(solution)/shard_map/ppermute | solution.py:20
  7.3 3.6 %collective-permute-start = (bf16[128,3072]{1,0:T(8,128)(2,1)S(1)}, bf16[128,3072]{1,0:T(8,128)(2,1)S(1)}, u32[]{:S(2)}, u32[]{:S(2)}) collective-permute-start(bf16[128,3072]{1,0:T(8,128)(2,1)S(1)} %get-tuple-element.40), channel_id=1, source_target_pairs={{0,16},{8,24},{16,0},{24,8},{1,17},{9,25},{17,1},{25,9},{2,18},{10... | collective-permute-start | bytes 2359304 | tf_op jit(solution)/shard_map/ppermute | solution.py:20
  10.9 4.2 %collective-permute-done.1 = bf16[64,3072]{1,0:T(8,128)(2,1)S(1)} collective-permute-done((bf16[64,3072]{1,0:T(8,128)(2,1)S(1)}, bf16[64,3072]{1,0:T(8,128)(2,1)S(1)}, u32[]{:S(2)}, u32[]{:S(2)}) %collective-permute-start.1) | collective-permute-done | bytes 393248 | tf_op jit(solution)/shard_map/ppermute | solution.py:20
  15.2 2.2 %collective-permute-done.2 = bf16[64,3072]{1,0:T(8,128)(2,1)S(1)} collective-permute-done((bf16[64,3072]{1,0:T(8,128)(2,1)S(1)}, bf16[64,3072]{1,0:T(8,128)(2,1)S(1)}, u32[]{:S(2)}, u32[]{:S(2)}) %collective-permute-start.2) | collective-permute-done | bytes 393248 | tf_op jit(solution)/shard_map/ppermute | solution.py:20
  17.4 9.7 %collective-permute-done.3 = bf16[64,3072]{1,0:T(8,128)(2,1)S(1)} collective-permute-done((bf16[64,3072]{1,0:T(8,128)(2,1)S(1)}, bf16[64,3072]{1,0:T(8,128)(2,1)S(1)}, u32[]{:S(2)}, u32[]{:S(2)}) %collective-permute-start.3) | collective-permute-done | bytes 393248 | tf_op jit(solution)/shard_map/ppermute | solution.py:20
  29.1 2.2 %collective-permute-start.6 = (bf16[256,3072]{1,0:T(8,128)(2,1)S(1)}, bf16[256,3072]{1,0:T(8,128)(2,1)S(1)}, u32[]{:S(2)}, u32[]{:S(2)}) collective-permute-start(bf16[256,3072]{1,0:T(8,128)(2,1)S(1)} %slice_dynamic-update-slice_fusion.refs_0_), channel_id=1, source_target_pairs={{0,24},{8,0},{16,8},{24,16},{1,25},{9,1},{17,9},{25,17},{2,26},{10... | collective-permute-start | bytes 4718600 | tf_op jit(solution)/shard_map/ppermute | solution.py:20
  31.9 2.1 %collective-permute-start.9 = (bf16[256,3072]{1,0:T(8,128)(2,1)S(1)}, bf16[256,3072]{1,0:T(8,128)(2,1)S(1)}, u32[]{:S(2)}, u32[]{:S(2)}) collective-permute-start(bf16[256,3072]{1,0:T(8,128)(2,1)S(1)} %pad_maximum_fusion.refs_6_.refs_0_.refs_2_), channel_id=1, source_target_pairs={{0,96},{32,0},{64,32},{96,64},{1,97},{33,1},{65,33},{97,65},{2,98}... | collective-permute-start | bytes 4718600 | tf_op jit(solution)/shard_map/ppermute | solution.py:20
  34.0 3.5 %plan.1 = (s32[128]{0:T(128)S(1)}, s32[17]{0:T(128)S(1)}, s32[21]{0:T(128)S(1)}) custom-call(s32[4]{0:T(128)S(1)} %pad_add_fusion.meta, s32[64]{0:T(128)S(1)} %get-tuple-element.72.first, s32[64]{0:T(128)S(1)} %get-tuple-element.71.second, s32[64]{0:T(128)S(1)} %bitcast.14), custom_call_target="tpu_custom_call" | custom-call | tf_op jit(solution)/shard_map/plan/pallas_call | solution.py:268
  37.5 2.4 %collective-permute-start.12 = (bf16[256,3072]{1,0:T(8,128)(2,1)S(1)}, bf16[256,3072]{1,0:T(8,128)(2,1)S(1)}, u32[]{:S(2)}, u32[]{:S(2)}) collective-permute-start(bf16[256,3072]{1,0:T(8,128)(2,1)S(1)} %slice_dynamic-update-slice_fusion.refs_0_), channel_id=1, source_target_pairs={{0,4},{4,0},{1,5},{5,1},{2,6},{6,2},{3,7},{7,3},{8,12},{12,8},{9,1... | collective-permute-start | bytes 4718600 | tf_op jit(solution)/shard_map/ppermute | solution.py:332
  39.9 24.5 %collective-permute-done.4.refs_2_ = bf16[256,3072]{1,0:T(8,128)(2,1)S(1)} collective-permute-done((bf16[256,3072]{1,0:T(8,128)(2,1)S(1)}, bf16[256,3072]{1,0:T(8,128)(2,1)S(1)}, u32[]{:S(2)}, u32[]{:S(2)}) %collective-permute-start.4) | collective-permute-done | bytes 1572896 | tf_op jit(solution)/shard_map/ppermute | solution.py:20
  64.4 2.1 %collective-permute-start.14 = (bf16[256,3072]{1,0:T(8,128)(2,1)S(1)}, bf16[256,3072]{1,0:T(8,128)(2,1)S(1)}, u32[]{:S(2)}, u32[]{:S(2)}) collective-permute-start(bf16[256,3072]{1,0:T(8,128)(2,1)S(1)} %collective-permute-done.4.refs_2_), channel_id=1, source_target_pairs={{0,4},{4,0},{1,5},{5,1},{2,6},{6,2},{3,7},{7,3},{8,12},{12,8},{9,1... | collective-permute-start | bytes 4718600 | tf_op jit(solution)/shard_map/ppermute | solution.py:340
  67.3 2.2 %collective-permute-start.11 = (bf16[128,3072]{1,0:T(8,128)(2,1)S(1)}, bf16[128,3072]{1,0:T(8,128)(2,1)S(1)}, u32[]{:S(2)}, u32[]{:S(2)}) collective-permute-start(bf16[128,3072]{1,0:T(8,128)(2,1)S(1)} %slice.55), channel_id=1, source_target_pairs={{0,96},{32,0},{64,32},{96,64},{1,97},{33,1},{65,33},{97,65},{2,98}... | collective-permute-start | bytes 2359304 | tf_op jit(solution)/shard_map/ppermute | solution.py:20
  70.6 1.9 %collective-permute-start.7 = (bf16[80,3072]{1,0:T(8,128)(2,1)S(1)}, bf16[80,3072]{1,0:T(8,128)(2,1)S(1)}, u32[]{:S(2)}, u32[]{:S(2)}) collective-permute-start(bf16[80,3072]{1,0:T(8,128)(2,1)S(1)} %slice.63), channel_id=1, source_target_pairs={{0,24},{8,0},{16,8},{24,16},{1,25},{9,1},{17,9},{25,17},{2,26},{10... | collective-permute-start | bytes 1474568 | tf_op jit(solution)/shard_map/ppermute | solution.py:20
  72.5 6.5 %early.1 = (bf16[9,64,128]{2,1,0:T(8,128)(2,1)S(1)}, f32[4,37,64,128]{3,2,1,0:T(8,128)S(1)}) custom-call(s32[4]{0:T(128)S(1)} %pad_add_fusion.meta, s32[17]{0:T(128)S(1)} %get-tuple-element.47.order.order1, bf16[256,3072]{1,0:T(8,128)(2,1)S(1)} %slice_dynamic-update-slice_fusion.refs_0_, bf16[256,3072]{1,0:T(8,128)(2,1)S(1)} %collective-permute-done.6.refs_1_, ...), custom_call_target="tpu_custom_call" | custom-call | flops 3221225472 | bytes 1048576 | tf_op jit(solution)/shard_map/early/pallas_call | solution.py:151
  79.0 3.0 %collective-permute-start.15 = (bf16[9,64,128]{2,1,0:T(8,128)(2,1)S(1)}, bf16[9,64,128]{2,1,0:T(8,128)(2,1)S(1)}, u32[]{:S(2)}, u32[]{:S(2)}) collective-permute-start(bf16[9,64,128]{2,1,0:T(8,128)(2,1)S(1)} %get-tuple-element.54), channel_id=1, source_target_pairs={{0,2},{1,3},{2,0},{3,1},{4,6},{5,7},{6,4},{7,5},{8,10},{9,11},{10,... | collective-permute-start | bytes 442376 | tf_op jit(solution)/shard_map/ppermute | solution.py:20
  84.7 4.9 %collective-permute-start.16 = (bf16[256,3072]{1,0:T(8,128)(2,1)S(1)}, bf16[256,3072]{1,0:T(8,128)(2,1)S(1)}, u32[]{:S(2)}, u32[]{:S(2)}) collective-permute-start(bf16[256,3072]{1,0:T(8,128)(2,1)S(1)} %pad_maximum_fusion.1.refs_0_), channel_id=1, source_target_pairs={{0,4},{4,0},{1,5},{5,1},{2,6},{6,2},{3,7},{7,3},{8,12},{12,8},{9,1... | collective-permute-start | bytes 4718600 | tf_op jit(solution)/shard_map/ppermute | solution.py:350
  89.6 3.1 %middle.1 = (bf16[16,64,128]{2,1,0:T(8,128)(2,1)S(1)}, bf16[16,64,128]{2,1,0:T(8,128)(2,1)S(1)}, f32[4,37,64,128]{3,2,1,0:T(8,128)S(1)}) custom-call(s32[4]{0:T(128)S(1)} %pad_add_fusion.meta, s32[17]{0:T(128)S(1)} %get-tuple-element.47.order.order1, bf16[256,3072]{1,0:T(8,128)(2,1)S(1)} %slice_dynamic-update-slice_fusion.refs_0_, ...), custom_call_target="tpu_custom_call", output_to_operand_aliasing={{2}: (10, {})} | custom-call | flops 3221225472 | bytes 1048576 | tf_op jit(solution)/shard_map/middle/pallas_call | solution.py:151
  95.8 4.2 %late.1 = (bf16[20,64,128]{2,1,0:T(8,128)(2,1)S(1)}, bf16[27,64,128]{2,1,0:T(8,128)(2,1)S(1)}, bf16[20,64,128]{2,1,0:T(8,128)(2,1)S(1)}, f32[4,37,64,128]{3,2,1,0:T(8,128)S(1)}) custom-call(s32[4]{0:T(128)S(1)} %pad_add_fusion.meta, s32[17]{0:T(128)S(1)} %get-tuple-element.47.order.order1, ...), custom_call_target="tpu_custom_call", output_to_operand_aliasing={{3}: (10, {})} | custom-call | flops 3221225472 | bytes 1048576 | tf_op jit(solution)/shard_map/late/pallas_call | solution.py:151
  102.1 2.8 %collective-permute-start.21 = (bf16[20,64,128]{2,1,0:T(8,128)(2,1)S(1)}, bf16[20,64,128]{2,1,0:T(8,128)(2,1)S(1)}, u32[]{:S(2)}, u32[]{:S(2)}) collective-permute-start(bf16[20,64,128]{2,1,0:T(8,128)(2,1)S(1)} %get-tuple-element.70), channel_id=1, source_target_pairs={{0,3},{1,0},{2,1},{3,2},{4,7},{5,4},{6,5},{7,6},{8,11},{9,8},{10,9... | collective-permute-start | bytes 983048 | tf_op jit(solution)/shard_map/ppermute | solution.py:20
  104.9 13.7 %collective-permute-done.21.refs_5_ = bf16[20,64,128]{2,1,0:T(8,128)(2,1)S(1)} collective-permute-done((bf16[20,64,128]{2,1,0:T(8,128)(2,1)S(1)}, bf16[20,64,128]{2,1,0:T(8,128)(2,1)S(1)}, u32[]{:S(2)}, u32[]{:S(2)}) %collective-permute-start.21) | collective-permute-done | bytes 327712 | tf_op jit(solution)/shard_map/ppermute | solution.py:20
  118.6 2.1 %collective-permute-done.19.refs_3_ = bf16[20,64,128]{2,1,0:T(8,128)(2,1)S(1)} collective-permute-done((bf16[20,64,128]{2,1,0:T(8,128)(2,1)S(1)}, bf16[20,64,128]{2,1,0:T(8,128)(2,1)S(1)}, u32[]{:S(2)}, u32[]{:S(2)}) %collective-permute-start.19) | collective-permute-done | bytes 327712 | tf_op jit(solution)/shard_map/ppermute | solution.py:20
  121.7 33.0 %all_to_all.5.got = bf16[32,4,64,128]{3,2,1,0:T(8,128)(2,1)S(1)} all-to-all(bf16[32,4,64,128]{3,2,1,0:T(8,128)(2,1)S(1)} %bitcast.11), channel_id=1, replica_groups=mesh['x'=4,'z'=4,'c'=2,'y'=4] {'x','z','c'}, dimensions={0} | all-to-all | bytes 4194304 | tf_op jit(solution)/shard_map/all_to_all | solution.py:361
  154.8 2.3 %place.1 = f32[4,256,1024]{2,1,0:T(8,128)} custom-call(bf16[32,4,64,128]{3,2,1,0:T(8,128)(2,1)S(1)} %all_to_all.5.got), custom_call_target="tpu_custom_call" | custom-call | tf_op jit(solution)/shard_map/place/pallas_call | solution.py:300
  (52 shorter events, 15.4 us)
Async XLA Ops:
  2.8 12.4 %collective-permute-start.1 = (bf16[64,3072]{1,0:T(8,128)(2,1)S(1)}, bf16[64,3072]{1,0:T(8,128)(2,1)S(1)}, u32[]{:S(2)}, u32[]{:S(2)}) collective-permute-start(bf16[64,3072]{1,0:T(8,128)(2,1)S(1)} %get-tuple-element.42), channel_id=1, source_target_pairs={{0,96},{32,0},{64,32},{96,64},{1,97},{33,1},{65,33},{97,65},{2,98}... | collective-permute-start | bytes 1179656 | tf_op jit(solution)/shard_map/ppermute | solution.py:20
  6.2 11.2 %collective-permute-start.2 = (bf16[64,3072]{1,0:T(8,128)(2,1)S(1)}, bf16[64,3072]{1,0:T(8,128)(2,1)S(1)}, u32[]{:S(2)}, u32[]{:S(2)}) collective-permute-start(bf16[64,3072]{1,0:T(8,128)(2,1)S(1)} %get-tuple-element.43), channel_id=1, source_target_pairs={{0,64},{32,96},{64,0},{96,32},{1,65},{33,97},{65,1},{97,33},{2,66}... | collective-permute-start | bytes 1179656 | tf_op jit(solution)/shard_map/ppermute | solution.py:20
  6.7 20.4 %collective-permute-start.3 = (bf16[64,3072]{1,0:T(8,128)(2,1)S(1)}, bf16[64,3072]{1,0:T(8,128)(2,1)S(1)}, u32[]{:S(2)}, u32[]{:S(2)}) collective-permute-start(bf16[64,3072]{1,0:T(8,128)(2,1)S(1)} %get-tuple-element.44), channel_id=1, source_target_pairs={{0,32},{32,64},{64,96},{96,0},{1,33},{33,65},{65,97},{97,1},{2,34}... | collective-permute-start | bytes 1179656 | tf_op jit(solution)/shard_map/ppermute | solution.py:20
  7.3 19.9 %collective-permute-start = (bf16[128,3072]{1,0:T(8,128)(2,1)S(1)}, bf16[128,3072]{1,0:T(8,128)(2,1)S(1)}, u32[]{:S(2)}, u32[]{:S(2)}) collective-permute-start(bf16[128,3072]{1,0:T(8,128)(2,1)S(1)} %get-tuple-element.40), channel_id=1, source_target_pairs={{0,16},{8,24},{16,0},{24,8},{1,17},{9,25},{17,1},{25,9},{2,18},{10... | collective-permute-start | bytes 2359304 | tf_op jit(solution)/shard_map/ppermute | solution.py:20
  27.2 6.7 %copy-start.2 = (s32[64,2]{0,1:T(2,128)S(1)}, s32[64,2]{0,1:T(2,128)}, u32[]{:S(2)}) copy-start(s32[64,2]{0,1:T(2,128)} %param.6) | copy-start | bytes 1540
  27.3 6.7 %copy-start.1 = (s32[64,1]{0,1:T(1,128)S(1)}, s32[64,1]{0,1:T(1,128)}, u32[]{:S(2)}) copy-start(s32[64,1]{0,1:T(1,128)} %param.7) | copy-start | bytes 772
  27.4 37.0 %collective-permute-start.4 = (bf16[256,3072]{1,0:T(8,128)(2,1)S(1)}, bf16[256,3072]{1,0:T(8,128)(2,1)S(1)}, u32[]{:S(2)}, u32[]{:S(2)}) collective-permute-start(bf16[256,3072]{1,0:T(8,128)(2,1)S(1)} %slice_dynamic-update-slice_fusion.refs_0_), channel_id=1, source_target_pairs={{0,8},{8,16},{16,24},{24,0},{1,9},{9,17},{17,25},{25,1},{2,10},{10... | collective-permute-start | bytes 4718600 | tf_op jit(solution)/shard_map/ppermute | solution.py:20
  29.1 37.5 %collective-permute-start.6 = (bf16[256,3072]{1,0:T(8,128)(2,1)S(1)}, bf16[256,3072]{1,0:T(8,128)(2,1)S(1)}, u32[]{:S(2)}, u32[]{:S(2)}) collective-permute-start(bf16[256,3072]{1,0:T(8,128)(2,1)S(1)} %slice_dynamic-update-slice_fusion.refs_0_), channel_id=1, source_target_pairs={{0,24},{8,0},{16,8},{24,16},{1,25},{9,1},{17,9},{25,17},{2,26},{10... | collective-permute-start | bytes 4718600 | tf_op jit(solution)/shard_map/ppermute | solution.py:20
  31.3 35.3 %collective-permute-start.8 = (bf16[256,3072]{1,0:T(8,128)(2,1)S(1)}, bf16[256,3072]{1,0:T(8,128)(2,1)S(1)}, u32[]{:S(2)}, u32[]{:S(2)}) collective-permute-start(bf16[256,3072]{1,0:T(8,128)(2,1)S(1)} %pad_maximum_fusion.refs_6_.refs_0_.refs_2_), channel_id=1, source_target_pairs={{0,32},{32,64},{64,96},{96,0},{1,33},{33,65},{65,97},{97,1},{2,34}... | collective-permute-start | bytes 4718600 | tf_op jit(solution)/shard_map/ppermute | solution.py:20
  31.9 34.7 %collective-permute-start.9 = (bf16[256,3072]{1,0:T(8,128)(2,1)S(1)}, bf16[256,3072]{1,0:T(8,128)(2,1)S(1)}, u32[]{:S(2)}, u32[]{:S(2)}) collective-permute-start(bf16[256,3072]{1,0:T(8,128)(2,1)S(1)} %pad_maximum_fusion.refs_6_.refs_0_.refs_2_), channel_id=1, source_target_pairs={{0,96},{32,0},{64,32},{96,64},{1,97},{33,1},{65,33},{97,65},{2,98}... | collective-permute-start | bytes 4718600 | tf_op jit(solution)/shard_map/ppermute | solution.py:20
  37.5 32.2 %collective-permute-start.12 = (bf16[256,3072]{1,0:T(8,128)(2,1)S(1)}, bf16[256,3072]{1,0:T(8,128)(2,1)S(1)}, u32[]{:S(2)}, u32[]{:S(2)}) collective-permute-start(bf16[256,3072]{1,0:T(8,128)(2,1)S(1)} %slice_dynamic-update-slice_fusion.refs_0_), channel_id=1, source_target_pairs={{0,4},{4,0},{1,5},{5,1},{2,6},{6,2},{3,7},{7,3},{8,12},{12,8},{9,1... | collective-permute-start | bytes 4718600 | tf_op jit(solution)/shard_map/ppermute | solution.py:332
  64.4 6.2 %collective-permute-start.14 = (bf16[256,3072]{1,0:T(8,128)(2,1)S(1)}, bf16[256,3072]{1,0:T(8,128)(2,1)S(1)}, u32[]{:S(2)}, u32[]{:S(2)}) collective-permute-start(bf16[256,3072]{1,0:T(8,128)(2,1)S(1)} %collective-permute-done.4.refs_2_), channel_id=1, source_target_pairs={{0,4},{4,0},{1,5},{5,1},{2,6},{6,2},{3,7},{7,3},{8,12},{12,8},{9,1... | collective-permute-start | bytes 4718600 | tf_op jit(solution)/shard_map/ppermute | solution.py:340
  66.6 5.9 %collective-permute-start.13 = (bf16[256,3072]{1,0:T(8,128)(2,1)S(1)}, bf16[256,3072]{1,0:T(8,128)(2,1)S(1)}, u32[]{:S(2)}, u32[]{:S(2)}) collective-permute-start(bf16[256,3072]{1,0:T(8,128)(2,1)S(1)} %collective-permute-done.6.refs_1_), channel_id=1, source_target_pairs={{0,4},{4,0},{1,5},{5,1},{2,6},{6,2},{3,7},{7,3},{8,12},{12,8},{9,1... | collective-permute-start | bytes 4718600 | tf_op jit(solution)/shard_map/ppermute | solution.py:340
  66.7 17.6 %collective-permute-start.10 = (bf16[128,3072]{1,0:T(8,128)(2,1)S(1)}, bf16[128,3072]{1,0:T(8,128)(2,1)S(1)}, u32[]{:S(2)}, u32[]{:S(2)}) collective-permute-start(bf16[128,3072]{1,0:T(8,128)(2,1)S(1)} %slice.54), channel_id=1, source_target_pairs={{0,32},{32,64},{64,96},{96,0},{1,33},{33,65},{65,97},{97,1},{2,34}... | collective-permute-start | bytes 2359304 | tf_op jit(solution)/shard_map/ppermute | solution.py:20
  67.3 16.9 %collective-permute-start.11 = (bf16[128,3072]{1,0:T(8,128)(2,1)S(1)}, bf16[128,3072]{1,0:T(8,128)(2,1)S(1)}, u32[]{:S(2)}, u32[]{:S(2)}) collective-permute-start(bf16[128,3072]{1,0:T(8,128)(2,1)S(1)} %slice.55), channel_id=1, source_target_pairs={{0,96},{32,0},{64,32},{96,64},{1,97},{33,1},{65,33},{97,65},{2,98}... | collective-permute-start | bytes 2359304 | tf_op jit(solution)/shard_map/ppermute | solution.py:20
  69.6 13.0 %collective-permute-start.5 = (bf16[80,3072]{1,0:T(8,128)(2,1)S(1)}, bf16[80,3072]{1,0:T(8,128)(2,1)S(1)}, u32[]{:S(2)}, u32[]{:S(2)}) collective-permute-start(bf16[80,3072]{1,0:T(8,128)(2,1)S(1)} %slice.62), channel_id=1, source_target_pairs={{0,8},{8,16},{16,24},{24,0},{1,9},{9,17},{17,25},{25,1},{2,10},{10... | collective-permute-start | bytes 1474568 | tf_op jit(solution)/shard_map/ppermute | solution.py:20
  70.6 12.0 %collective-permute-start.7 = (bf16[80,3072]{1,0:T(8,128)(2,1)S(1)}, bf16[80,3072]{1,0:T(8,128)(2,1)S(1)}, u32[]{:S(2)}, u32[]{:S(2)}) collective-permute-start(bf16[80,3072]{1,0:T(8,128)(2,1)S(1)} %slice.63), channel_id=1, source_target_pairs={{0,24},{8,0},{16,8},{24,16},{1,25},{9,1},{17,9},{25,17},{2,26},{10... | collective-permute-start | bytes 1474568 | tf_op jit(solution)/shard_map/ppermute | solution.py:20
  79.0 5.6 %collective-permute-start.15 = (bf16[9,64,128]{2,1,0:T(8,128)(2,1)S(1)}, bf16[9,64,128]{2,1,0:T(8,128)(2,1)S(1)}, u32[]{:S(2)}, u32[]{:S(2)}) collective-permute-start(bf16[9,64,128]{2,1,0:T(8,128)(2,1)S(1)} %get-tuple-element.54), channel_id=1, source_target_pairs={{0,2},{1,3},{2,0},{3,1},{4,6},{5,7},{6,4},{7,5},{8,10},{9,11},{10,... | collective-permute-start | bytes 442376 | tf_op jit(solution)/shard_map/ppermute | solution.py:20
  84.7 11.1 %collective-permute-start.16 = (bf16[256,3072]{1,0:T(8,128)(2,1)S(1)}, bf16[256,3072]{1,0:T(8,128)(2,1)S(1)}, u32[]{:S(2)}, u32[]{:S(2)}) collective-permute-start(bf16[256,3072]{1,0:T(8,128)(2,1)S(1)} %pad_maximum_fusion.1.refs_0_), channel_id=1, source_target_pairs={{0,4},{4,0},{1,5},{5,1},{2,6},{6,2},{3,7},{7,3},{8,12},{12,8},{9,1... | collective-permute-start | bytes 4718600 | tf_op jit(solution)/shard_map/ppermute | solution.py:350
  92.7 9.3 %collective-permute-start.17 = (bf16[16,64,128]{2,1,0:T(8,128)(2,1)S(1)}, bf16[16,64,128]{2,1,0:T(8,128)(2,1)S(1)}, u32[]{:S(2)}, u32[]{:S(2)}) collective-permute-start(bf16[16,64,128]{2,1,0:T(8,128)(2,1)S(1)} %get-tuple-element.64), channel_id=1, source_target_pairs={{0,1},{1,2},{2,3},{3,0},{4,5},{5,6},{6,7},{7,4},{8,9},{9,10},{10,1... | collective-permute-start | bytes 786440 | tf_op jit(solution)/shard_map/ppermute | solution.py:20
  94.1 8.0 %collective-permute-start.18 = (bf16[16,64,128]{2,1,0:T(8,128)(2,1)S(1)}, bf16[16,64,128]{2,1,0:T(8,128)(2,1)S(1)}, u32[]{:S(2)}, u32[]{:S(2)}) collective-permute-start(bf16[16,64,128]{2,1,0:T(8,128)(2,1)S(1)} %get-tuple-element.65), channel_id=1, source_target_pairs={{0,3},{1,0},{2,1},{3,2},{4,7},{5,4},{6,5},{7,6},{8,11},{9,8},{10,9... | collective-permute-start | bytes 786440 | tf_op jit(solution)/shard_map/ppermute | solution.py:20
  100.0 20.7 %collective-permute-start.20 = (bf16[27,64,128]{2,1,0:T(8,128)(2,1)S(1)}, bf16[27,64,128]{2,1,0:T(8,128)(2,1)S(1)}, u32[]{:S(2)}, u32[]{:S(2)}) collective-permute-start(bf16[27,64,128]{2,1,0:T(8,128)(2,1)S(1)} %get-tuple-element.69), channel_id=1, source_target_pairs={{0,2},{1,3},{2,0},{3,1},{4,6},{5,7},{6,4},{7,5},{8,10},{9,11},{10,... | collective-permute-start | bytes 1327112 | tf_op jit(solution)/shard_map/ppermute | solution.py:20
  102.1 16.5 %collective-permute-start.21 = (bf16[20,64,128]{2,1,0:T(8,128)(2,1)S(1)}, bf16[20,64,128]{2,1,0:T(8,128)(2,1)S(1)}, u32[]{:S(2)}, u32[]{:S(2)}) collective-permute-start(bf16[20,64,128]{2,1,0:T(8,128)(2,1)S(1)} %get-tuple-element.70), channel_id=1, source_target_pairs={{0,3},{1,0},{2,1},{3,2},{4,7},{5,4},{6,5},{7,6},{8,11},{9,8},{10,9... | collective-permute-start | bytes 983048 | tf_op jit(solution)/shard_map/ppermute | solution.py:20
  104.9 15.8 %collective-permute-start.19 = (bf16[20,64,128]{2,1,0:T(8,128)(2,1)S(1)}, bf16[20,64,128]{2,1,0:T(8,128)(2,1)S(1)}, u32[]{:S(2)}, u32[]{:S(2)}) collective-permute-start(bf16[20,64,128]{2,1,0:T(8,128)(2,1)S(1)} %get-tuple-element.68), channel_id=1, source_target_pairs={{0,1},{1,2},{2,3},{3,0},{4,5},{5,6},{6,7},{7,4},{8,9},{9,10},{10,1... | collective-permute-start | bytes 983048 | tf_op jit(solution)/shard_map/ppermute | solution.py:20
  (1 other events, 1.9 us)
